TPU v7x, 32 devices: a whole 2x2x4 slice. The times are simulated.
32 devices in a mesh: dp: 4 (over y, x), context: 2 (over core), tensor: 4 (over z).
Axes of the slice: x: 2, y: 2, z: 4, core: 2. Of those that a mesh axis runs over, the one named last changes fastest.
Arguments:
- inputs: bfloat16 [8, 1024, 2048], P('dp', 'context'), may hold values from -6 to 6
- cotangent: bfloat16 [8, 1024, 2048], P('dp', 'context'), may hold values from -6 to 6
- lengths: int32 [8], P('dp'), may hold values from 256 to 1024, as said below
- w_query: bfloat16 [2048, 2048], P(('dp', 'context'), 'tensor'), may hold values from -0.125 to 0.125
- key_projection_weight: bfloat16 [2048, 512], P(('dp', 'context'), 'tensor'), may hold values from -0.125 to 0.125
- value_projection_weight: bfloat16 [2048, 512], P(('dp', 'context'), 'tensor'), may hold values from -0.125 to 0.125
- w_output: bfloat16 [2048, 2048], P('tensor', ('dp', 'context')), may hold values from -2 to 2
- w_gate: bfloat16 [2048, 8192], P(('dp', 'context'), 'tensor'), may hold values from -0.125 to 0.125
- w_up: bfloat16 [2048, 8192], P(('dp', 'context'), 'tensor'), may hold values from -0.125 to 0.125
- w_down: bfloat16 [8192, 2048], P('tensor', ('dp', 'context')), may hold values from -0.0625 to 0.0625
- attn_gain: bfloat16 [2048], P(('dp', 'context')), may hold values from 0.5 to 1.5
- ffn_gain: bfloat16 [2048], P(('dp', 'context')), may hold values from 0.5 to 1.5
- query_gain: bfloat16 [64], replicated, may hold values from 0.5 to 1.5
- key_gain: bfloat16 [64], replicated, may hold values from 0.5 to 1.5
Outputs:
- output: bfloat16 [8, 1024, 2048], P('dp', ('context', 'tensor'))
- grad_inputs: float32 [8, 1024, 2048], P('dp', ('context', 'tensor'))
- grad_w_query: float32 [2048, 2048], P(('dp', 'context'), 'tensor')
- grad_w_key: float32 [2048, 512], P(('dp', 'context'), 'tensor')
- grad_w_value: float32 [2048, 512], P(('dp', 'context'), 'tensor')
- grad_w_output: float32 [2048, 2048], P('tensor', ('dp', 'context'))
- grad_w_gate: float32 [2048, 8192], P(('dp', 'context'), 'tensor')
- grad_w_up: float32 [2048, 8192], P(('dp', 'context'), 'tensor')
- grad_w_down: float32 [8192, 2048], P('tensor', ('dp', 'context'))
- grad_attn_gain: float32 [2048], P(('dp', 'context'))
- grad_ffn_gain: float32 [2048], P(('dp', 'context'))
- grad_query_gain: float32 [64], replicated
- grad_key_gain: float32 [64], replicated
- rms_values: float32 [3], replicated
Inputs may be any that keep to these rules, and one draw needn't show every extreme that they name: `lengths`: in every draw one sequence, drawn from the seed, has all 1024 slots valid.
All inputs are finite; a program needn't handle non-finite values.
Results may differ from a plain program's by a relative error of at most 0.014.
Values may be sent and summed in bfloat16 or wider, within the bound.
A program may use at most 320 MiB of HBM per device.

v0:
```python
import math

import jax
import jax.numpy as jnp
from jax import lax
from jax.sharding import PartitionSpec as P

epsilon = 1e-05
rope_base = 1000000.0
masked_score = -1e30


def rms_scale(values):
    return lax.rsqrt(jnp.mean(values * values, axis=-1, keepdims=True) + epsilon)


def norm_back(grad_hat, normed_hat, inverse):
    return inverse * (
        grad_hat - normed_hat * jnp.mean(grad_hat * normed_hat, axis=-1, keepdims=True)
    )


def rope_angles(positions, width):
    half = width // 2
    freqs = rope_base ** (-(jnp.arange(half, dtype=jnp.float32) * (2.0 / width)))
    angles = positions.astype(jnp.float32)[:, None] * freqs[None, :]
    return (jnp.cos(angles), jnp.sin(angles))


def rotate(values, cosine, sine):
    half = values.shape[-1] // 2
    first = values[..., :half]
    second = values[..., half:]
    return jnp.concatenate(
        [first * cosine - second * sine, second * cosine + first * sine], axis=-1
    )


def project(left, right):
    return jnp.einsum("src,cd->srd", left, right, preferred_element_type=jnp.float32)


def project_back(left, right):
    return jnp.einsum("src,dc->srd", left, right, preferred_element_type=jnp.float32)


def weight_grad(left, right):
    return jnp.einsum("srd,src->dc", left, right, preferred_element_type=jnp.float32)


def per_device(
    inputs,
    cotangent,
    lengths,
    w_query,
    key_projection_weight,
    value_projection_weight,
    w_output,
    w_gate,
    w_up,
    w_down,
    attn_gain,
    ffn_gain,
    query_gain,
    key_gain,
):
    seq_count, span_len, width = inputs.shape
    head_size = query_gain.shape[0]
    query_heads = w_query.shape[1] // head_size
    kv_heads = key_projection_weight.shape[1] // head_size
    queries_per_group = query_heads // kv_heads
    context_size = lax.axis_size("context")
    tensor_size = lax.axis_size("tensor")
    share_len = span_len // tensor_size
    share_start = lax.axis_index("tensor") * share_len
    positions = lax.axis_index("context") * span_len + jnp.arange(span_len, dtype=jnp.int32)
    key_positions = jnp.arange(span_len * context_size, dtype=jnp.int32)
    row_valid = (positions[None, :] < lengths[:, None]).astype(jnp.float32)
    valid3 = row_valid[:, :, None]
    cosine, sine = rope_angles(positions, head_size)
    cosine = cosine[None, :, None, :]
    sine = sine[None, :, None, :]
    score_scale = 1.0 / math.sqrt(head_size)
    qgain_f = query_gain.astype(jnp.float32)
    kgain_f = key_gain.astype(jnp.float32)

    def cut(values):
        return lax.dynamic_slice_in_dim(values, share_start, share_len, 1)

    resid = inputs.astype(jnp.float32)
    (
        full_query,
        full_key,
        full_value,
        full_output,
        full_gate,
        full_up,
        full_down,
        full_gain1,
        full_gain2,
    ) = (
        lax.all_gather(w_query, ("dp", "context"), axis=0, tiled=True),
        lax.all_gather(key_projection_weight, ("dp", "context"), axis=0, tiled=True),
        lax.all_gather(value_projection_weight, ("dp", "context"), axis=0, tiled=True),
        lax.all_gather(w_output, ("dp", "context"), axis=1, tiled=True),
        lax.all_gather(w_gate, ("dp", "context"), axis=0, tiled=True),
        lax.all_gather(w_up, ("dp", "context"), axis=0, tiled=True),
        lax.all_gather(w_down, ("dp", "context"), axis=1, tiled=True),
        lax.all_gather(attn_gain, ("dp", "context"), axis=0, tiled=True),
        lax.all_gather(ffn_gain, ("dp", "context"), axis=0, tiled=True),
    )
    gain_one = full_gain1.astype(jnp.float32)
    gain_two = full_gain2.astype(jnp.float32)
    inverse1 = rms_scale(resid)
    hat1 = resid * inverse1
    first_normed = (hat1 * gain_one).astype(jnp.bfloat16)
    query_pre = project(first_normed, full_query).reshape(
        seq_count, span_len, query_heads, head_size
    )
    key_before_norm = project(first_normed, full_key).reshape(
        seq_count, span_len, kv_heads, head_size
    )
    value_low = project(first_normed, full_value).astype(jnp.bfloat16)
    query_inverse = rms_scale(query_pre)
    query_hat = query_pre * query_inverse
    query_reduced = rotate(query_hat * qgain_f, cosine, sine).astype(jnp.bfloat16)
    key_inverse = rms_scale(key_before_norm)
    key_hat = key_before_norm * key_inverse
    key_low = rotate(key_hat * kgain_f, cosine, sine).astype(jnp.bfloat16)
    key_send = key_low.reshape(seq_count, span_len, kv_heads * head_size)
    key_whole, value_whole = (
        lax.all_gather(key_send, "context", axis=1, tiled=True),
        lax.all_gather(value_low, "context", axis=1, tiled=True),
    )
    key_whole = key_whole.reshape(seq_count, -1, kv_heads, head_size)
    value_whole = value_whole.reshape(seq_count, -1, kv_heads, head_size)
    query_grouped = query_reduced.reshape(
        seq_count, span_len, kv_heads, queries_per_group, head_size
    )

    def masked_scores(query_part, key_part, length):
        allowed = (key_positions[None, :] <= positions[:, None]) & (key_positions[None, :] < length)
        scores = (
            jnp.einsum("qgre,kge->grqk", query_part, key_part, preferred_element_type=jnp.float32)
            * score_scale
        )
        return jnp.where(allowed[None, None], scores, masked_score)

    def attend_forward(packed):
        query_part, key_part, value_part, length = packed
        scores = masked_scores(query_part, key_part, length)
        peak = jnp.max(scores, axis=-1, keepdims=True)
        log_total = peak + jnp.log(jnp.sum(jnp.exp(scores - peak), axis=-1, keepdims=True))
        probs_low = jnp.exp(scores - log_total).astype(jnp.bfloat16)
        attended = jnp.einsum(
            "grqk,kge->qgre", probs_low, value_part, preferred_element_type=jnp.float32
        )
        return (attended, log_total)

    attended, log_totals = lax.map(attend_forward, (query_grouped, key_whole, value_whole, lengths))
    attended_low = attended.reshape(seq_count, span_len, query_heads * head_size).astype(
        jnp.bfloat16
    )
    attn_branch = lax.psum(project(attended_low, full_output), "tensor")
    hidden_state = resid + attn_branch
    inverse2 = rms_scale(hidden_state)
    hat2 = hidden_state * inverse2
    normed2 = (hat2 * gain_two).astype(jnp.bfloat16)
    gate_value = project(normed2, full_gate)
    up_value = project(normed2, full_up)
    sigmoid_gate = jax.nn.sigmoid(gate_value)
    silu_gate = gate_value * sigmoid_gate
    inner = (silu_gate * up_value).astype(jnp.bfloat16)
    ffn_term = project(inner, full_down)
    ffn_share = cut(lax.psum(ffn_term.astype(jnp.bfloat16), "tensor").astype(jnp.float32))
    hidden_share = cut(hidden_state)
    output = (hidden_share + ffn_share).astype(jnp.bfloat16)
    valid_share = cut(valid3)
    resid_share = cut(resid)
    attn_share = cut(attn_branch)
    squares = jnp.stack(
        [
            jnp.sum(valid_share * resid_share * resid_share),
            jnp.sum(valid_share * attn_share * attn_share),
            jnp.sum(valid_share * ffn_share * ffn_share),
        ]
    )
    share_count = jnp.sum(valid_share)
    grad_out = cotangent.astype(jnp.float32) * valid3
    grad_ffn = grad_out.astype(jnp.bfloat16)
    grad_w_down = weight_grad(inner, grad_ffn)
    grad_inner = project_back(grad_ffn, full_down)
    grad_gate = (
        grad_inner * up_value * sigmoid_gate * (1.0 + gate_value * (1.0 - sigmoid_gate))
    ).astype(jnp.bfloat16)
    grad_up = (grad_inner * silu_gate).astype(jnp.bfloat16)
    grad_w_gate = weight_grad(normed2, grad_gate)
    grad_w_up = weight_grad(normed2, grad_up)
    second_part = project_back(grad_gate, full_gate) + project_back(grad_up, full_up)
    grad_normed2 = lax.psum(second_part, "tensor")
    grad_hidden = grad_out + norm_back(grad_normed2 * gain_two, hat2, inverse2)
    grad_branch = grad_hidden.astype(jnp.bfloat16)
    grad_normed2_share = cut(grad_normed2)
    grad_hidden_share = cut(grad_hidden)
    gain2_term = jnp.sum(grad_normed2_share * cut(hat2), axis=(0, 1))
    grad_w_output = weight_grad(attended_low, grad_branch)
    grad_attended = project_back(grad_branch, full_output).astype(jnp.bfloat16)
    grad_attended = grad_attended.reshape(
        seq_count, span_len, kv_heads, queries_per_group, head_size
    )

    def attend_back(packed):
        query_part, key_part, value_part, grad_part, log_total, length = packed
        probs = jnp.exp(masked_scores(query_part, key_part, length) - log_total)
        grad_probs = jnp.einsum(
            "qgre,kge->grqk", grad_part, value_part, preferred_element_type=jnp.float32
        )
        delta = jnp.sum(probs * grad_probs, axis=-1, keepdims=True)
        grad_scores = (probs * (grad_probs - delta)).astype(jnp.bfloat16)
        grad_query_part = (
            jnp.einsum("grqk,kge->qgre", grad_scores, key_part, preferred_element_type=jnp.float32)
            * score_scale
        )
        grad_key_part = (
            jnp.einsum(
                "grqk,qgre->kge", grad_scores, query_part, preferred_element_type=jnp.float32
            )
            * score_scale
        )
        grad_value_part = jnp.einsum(
            "grqk,qgre->kge",
            probs.astype(jnp.bfloat16),
            grad_part,
            preferred_element_type=jnp.float32,
        )
        return (grad_query_part, grad_key_part, grad_value_part)

    grad_query, grad_key_whole, grad_value_whole = lax.map(
        attend_back, (query_grouped, key_whole, value_whole, grad_attended, log_totals, lengths)
    )
    whole_len = grad_key_whole.shape[1]
    grad_key, grad_value = (
        lax.psum_scatter(
            grad_key_whole.reshape(seq_count, whole_len, kv_heads * head_size),
            "context",
            scatter_dimension=1,
            tiled=True,
        ),
        lax.psum_scatter(
            grad_value_whole.reshape(seq_count, whole_len, kv_heads * head_size),
            "context",
            scatter_dimension=1,
            tiled=True,
        ),
    )
    grad_query = grad_query.reshape(seq_count, span_len, query_heads, head_size)
    grad_query_normed = rotate(grad_query, cosine, -sine)
    query_gain_term = jnp.sum(grad_query_normed * query_hat, axis=(0, 1, 2))
    grad_query_pre = (
        norm_back(grad_query_normed * qgain_f, query_hat, query_inverse)
        .astype(jnp.bfloat16)
        .reshape(seq_count, span_len, query_heads * head_size)
    )
    grad_key_normed = rotate(
        grad_key.reshape(seq_count, span_len, kv_heads, head_size), cosine, -sine
    )
    key_gain_term = jnp.sum(grad_key_normed * key_hat, axis=(0, 1, 2))
    grad_key_pre = (
        norm_back(grad_key_normed * kgain_f, key_hat, key_inverse)
        .astype(jnp.bfloat16)
        .reshape(seq_count, span_len, kv_heads * head_size)
    )
    grad_value_low = grad_value.astype(jnp.bfloat16)
    grad_w_query = weight_grad(first_normed, grad_query_pre)
    grad_w_key = weight_grad(first_normed, grad_key_pre)
    grad_w_value = weight_grad(first_normed, grad_value_low)
    first_part = (
        project_back(grad_query_pre, full_query)
        + project_back(grad_key_pre, full_key)
        + project_back(grad_value_low, full_value)
    )
    grad_normed1_share = cut(lax.psum(first_part, "tensor"))
    hat1_share = cut(hat1)
    gain1_term = jnp.sum(grad_normed1_share * hat1_share, axis=(0, 1))
    grad_inputs = grad_hidden_share + norm_back(
        grad_normed1_share * gain_one, hat1_share, cut(inverse1)
    )
    square_sums, valid_count, grad_query_gain, grad_key_gain, gain1_total, gain2_total = lax.psum(
        (squares, share_count, query_gain_term, key_gain_term, gain1_term, gain2_term),
        ("dp", "context", "tensor"),
    )
    rms_values = jnp.sqrt(square_sums / (valid_count * width))
    gain_piece = attn_gain.shape[0]
    owner_start = lax.axis_index(("dp", "context")) * gain_piece
    grad_attn_gain = lax.dynamic_slice_in_dim(gain1_total, owner_start, gain_piece)
    grad_ffn_gain = lax.dynamic_slice_in_dim(gain2_total, owner_start, gain_piece)
    results = (
        lax.psum_scatter(grad_w_query, ("dp", "context"), scatter_dimension=0, tiled=True),
        lax.psum_scatter(grad_w_key, ("dp", "context"), scatter_dimension=0, tiled=True),
        lax.psum_scatter(grad_w_value, ("dp", "context"), scatter_dimension=0, tiled=True),
        lax.psum_scatter(grad_w_output, ("dp", "context"), scatter_dimension=1, tiled=True),
        lax.psum_scatter(grad_w_gate, ("dp", "context"), scatter_dimension=0, tiled=True),
        lax.psum_scatter(grad_w_up, ("dp", "context"), scatter_dimension=0, tiled=True),
        lax.psum_scatter(grad_w_down, ("dp", "context"), scatter_dimension=1, tiled=True),
    )
    return (
        output,
        grad_inputs,
        results[0],
        results[1],
        results[2],
        results[3],
        results[4],
        results[5],
        results[6],
        grad_attn_gain,
        grad_ffn_gain,
        grad_query_gain,
        grad_key_gain,
        rms_values,
    )


def solution(mesh):
    placed = (
        P("dp", "context", None),
        P("dp", "context", None),
        P("dp"),
        P(("dp", "context"), "tensor"),
        P(("dp", "context"), "tensor"),
        P(("dp", "context"), "tensor"),
        P("tensor", ("dp", "context")),
        P(("dp", "context"), "tensor"),
        P(("dp", "context"), "tensor"),
        P("tensor", ("dp", "context")),
        P(("dp", "context")),
        P(("dp", "context")),
        P(),
        P(),
    )
    return jax.shard_map(
        per_device,
        mesh=mesh,
        in_specs=placed,
        out_specs=(
            P("dp", ("context", "tensor"), None),
            P("dp", ("context", "tensor"), None),
            P(("dp", "context"), "tensor"),
            P(("dp", "context"), "tensor"),
            P(("dp", "context"), "tensor"),
            P("tensor", ("dp", "context")),
            P(("dp", "context"), "tensor"),
            P(("dp", "context"), "tensor"),
            P("tensor", ("dp", "context")),
            P(("dp", "context")),
            P(("dp", "context")),
            P(),
            P(),
            P(),
        ),
        check_vma=False,
    )
```

profile of v0, /device:TPU:0, one launch (start us, length us, event | category | flops | bytes accessed | tf_op | source)
XLA Modules:
  0.0 2064.6 jit_solution(14464854986063575489)
XLA Ops:
  10.6 10.3 all-gather
  25.8 14.5 all_gather.36
  47.8 9.9 all_gather.34
  71.1 59.7 %while.32 = (s32[]{:T(128)}, bf16[2,512,2,4,64]{1,4,3,2,0:T(8,128)(2,1)S(1)}, f32[2,2,4,512,1]{3,2,1,4,0:T(4,128)}, bf16[2,1024,2,64]{1,3,2,0:T(8,128)(2,1)}, s3...) while((s32[]{:T(128)}, ...), condition=%wide.region_6.7_spmd.clone.clone.clone, body=%wide.region_3.6_spmd.clone.clone.sunk.clone | while | flops 1120925184 | bytes 54665832 | solution.py:160
  91.0 10.0 fusion.186
  120.7 10.0 fusion.186
  149.5 280.5 %all-reduce.6.cloned.1.call-done = f32[2,512,2048]{2,1,0:T(8,128)} async-done(((f32[2,512,2048]{2,1,0:T(8,128)}), f32[2,512,2048]{2,1,0:T(8,128)}) %all-reduce.6.cloned.1.call-update) | async-done | bytes 8388624 | tf_op jit(solution)/shard_map/psum | solution.py:164
  446.5 38.7 %all-gather.14.cloned.1.call-done = bf16[2048,2048]{1,0:T(8,128)(2,1)} async-done(((bf16[256,2048]{1,0:T(8,128)(2,1)}), bf16[2048,2048]{1,0:T(8,128)(2,1)}) %all-gather.14.cloned.1.call-update) | async-done | bytes 8388624 | tf_op jit(solution)/shard_map/all_gather | solution.py:107
  485.2 14.4 fusion.75
  499.6 43.3 %all-gather.16.cloned.1.call-done = bf16[2048,2048]{1,0:T(8,128)(2,1)} async-done(((bf16[2048,256]{1,0:T(8,128)(2,1)}), bf16[2048,2048]{1,0:T(8,128)(2,1)}) %all-gather.16.cloned.1.call-update) | async-done | bytes 8388624 | tf_op jit(solution)/shard_map/all_gather | solution.py:108
  542.9 14.5 fusion.69
  557.5 41.6 %all-gather.12.cloned.1.call-done = bf16[2048,2048]{1,0:T(8,128)(2,1)} async-done(((bf16[256,2048]{1,0:T(8,128)(2,1)}), bf16[2048,2048]{1,0:T(8,128)(2,1)}) %all-gather.12.cloned.1.call-update) | async-done | bytes 8388624 | tf_op jit(solution)/shard_map/all_gather | solution.py:106
  599.1 21.7 %multiply_convert_fusion.1 = (bf16[2,512,2048]{2,1,0:T(8,128)(2,1)}, bf16[2,512,2048]{2,1,0:T(8,128)(2,1)S(1)}, bf16[2,512,2048]{2,1,0:T(8,128)(2,1)}) fusion(f32[2,512,2048]{2,1,0:T(8,128)} %fusion.69, f32[2,512,2048]{2,1,0:T(8,128)} %fusion.75, bf16[2,512,2048]{2,1,0:T(8,128)(2,1)} %get-tuple-element.305, bf16[2048,2048]{1,0:T(8,128)(2,1)} %all-gather.12.cloned.1.call-done), kind=kOutput, calls=%fused_computation.96 | convolution fusion | flops 8621391872 | bytes 41943040 | tf_op jit(solution)/shard_map/src,cd->srd/dot_general | solution.py:40
  620.8 14.8 fusion.73
  635.6 14.2 fusion.83
  649.9 290.9 %all-reduce.10.cloned.1.call-done = f32[2,512,2048]{2,1,0:T(8,128)} async-done(((f32[2,512,2048]{2,1,0:T(8,128)}), f32[2,512,2048]{2,1,0:T(8,128)}) %all-reduce.10.cloned.1.call-update) | async-done | bytes 8388624 | tf_op jit(solution)/shard_map/psum | solution.py:200
  961.5 73.4 %while.33 = (s32[]{:T(128)}, f32[2,512,2,4,64]{1,4,3,2,0:T(8,128)}, f32[2,1024,2,64]{1,3,2,0:T(8,128)}, f32[2,1024,2,64]{1,3,2,0:T(8,128)}, bf16[2,1024,2,64]{1,...) while((s32[]{:T(128)}, f32[2,512,2,4,64]{1,4,3,2,0:T(8,128)}, ...), condition=%wide.region_14.15_spmd.clone.clone.clone, body=%wide.region_12.14_spmd.clone.clone.sunk.clone | while | flops 2748708352 | bytes 154070288 | solution.py:238
  967.8 9.5 fusion.197
  1037.6 14.4 fusion.86
  1067.9 10.4 add_add_fusion
  1103.8 15.3 convolution_bitcast_fusion.3
  1119.4 15.2 convolution_bitcast_fusion.2
  1135.4 15.5 convolution_bitcast_fusion.1
  1158.1 55.6 %all-reduce.8.cloned.1.call-done = bf16[2,512,2048]{2,1,0:T(8,128)(2,1)} async-done(((bf16[2,512,2048]{2,1,0:T(8,128)(2,1)}), bf16[2,512,2048]{2,1,0:T(8,128)(2,1)}) %all-reduce.8.cloned.1.call-update) | async-done | bytes 4194320 | tf_op jit(solution)/shard_map/psum | solution.py:175
  1224.1 282.1 %all-reduce.12.cloned.1.call-done = f32[2,512,2048]{2,1,0:T(8,128)} async-done(((f32[2,512,2048]{2,1,0:T(8,128)}), f32[2,512,2048]{2,1,0:T(8,128)}) %all-reduce.12.cloned.1.call-update) | async-done | bytes 8388624 | tf_op jit(solution)/shard_map/psum | solution.py:282
  1508.9 39.8 %all-reduce = (f32[2048]{0:T(1024)S(1)}, f32[2048]{0:T(1024)S(1)}, f32[64]{0:T(128)}, f32[64]{0:T(128)}, f32[3]{0:T(128)S(1)}, /*index=5*/f32[]{:T(128)}) all-reduce(f32[2048]{0:T(1024)S(1)} %get-tuple-element.252, f32[2048]{0:T(1024)S(1)} %multiply_reduce_fusion.3, ...), channel_id=1, replica_groups=mesh['dp'=4,'context'=2,'tensor'=4] {'dp','context','tensor'}, use_global_device_ids=true, to_apply=%region_29.30 | all-reduce | flops 4228 | bytes 33824 | tf_op jit(solution)/shard_map/psum | solution.py:288
  1555.8 29.7 %reduce-scatter.18.cloned.1.call-done = f32[256,128]{1,0:T(8,128)} async-done(((f32[2048,128]{1,0:T(8,128)}), f32[256,128]{1,0:T(8,128)}) %reduce-scatter.18.cloned.1.call-update) | async-done | bytes 131088 | tf_op jit(solution)/shard_map/reduce_scatter | solution.py:300
  1585.5 55.5 %reduce-scatter.20.cloned.1.call-done = f32[512,256]{1,0:T(8,128)} async-done(((f32[512,2048]{1,0:T(8,128)}), f32[512,256]{1,0:T(8,128)}) %reduce-scatter.20.cloned.1.call-update) | async-done | bytes 524304 | tf_op jit(solution)/shard_map/reduce_scatter | solution.py:301
  1641.0 55.1 %reduce-scatter.14.cloned.1.call-done = f32[256,512]{1,0:T(8,128)} async-done(((f32[2048,512]{1,0:T(8,128)}), f32[256,512]{1,0:T(8,128)}) %reduce-scatter.14.cloned.1.call-update) | async-done | bytes 524304 | tf_op jit(solution)/shard_map/reduce_scatter | solution.py:298
  1696.1 120.4 %reduce-scatter.22.cloned.1.call-done = f32[256,2048]{1,0:T(8,128)} async-done(((f32[2048,2048]{1,0:T(8,128)}), f32[256,2048]{1,0:T(8,128)}) %reduce-scatter.22.cloned.1.call-update) | async-done | bytes 2097168 | tf_op jit(solution)/shard_map/reduce_scatter | solution.py:302
  1816.5 120.4 %reduce-scatter.24.cloned.1.call-done = f32[256,2048]{1,0:T(8,128)} async-done(((f32[2048,2048]{1,0:T(8,128)}), f32[256,2048]{1,0:T(8,128)}) %reduce-scatter.24.cloned.1.call-update) | async-done | bytes 2097168 | tf_op jit(solution)/shard_map/reduce_scatter | solution.py:303
  1936.9 120.4 %reduce-scatter.26.cloned.1.call-done = f32[2048,256]{1,0:T(8,128)} async-done(((f32[2048,2048]{1,0:T(8,128)}), f32[2048,256]{1,0:T(8,128)}) %reduce-scatter.26.cloned.1.call-update) | async-done | bytes 2097168 | tf_op jit(solution)/shard_map/reduce_scatter | solution.py:304
  (256 shorter events, 259.0 us)
Async XLA Ops:
  7.2 37.2 %copy-start.44 = (bf16[64]{0:T(256)(128)(2,1)S(1)}, bf16[64]{0:T(256)(128)(2,1)}, u32[]{:S(2)}) copy-start(bf16[64]{0:T(256)(128)(2,1)} %param.31) | copy-start | bytes 388
  7.2 55.1 %all-gather.8.cloned.1.call-start = ((), (), s32[]{:S(2)}) async-start(), calls=%async_computation.9 | async-start | bytes 2359296 | tf_op jit(solution)/shard_map/all_gather | solution.py:102
  9.1 121.7 %all-gather.10.cloned.1.call-start = ((), (), s32[]{:S(2)}) async-start(), calls=%async_computation.10 | async-start | bytes 2359296 | tf_op jit(solution)/shard_map/all_gather | solution.py:105
  9.8 420.2 %all-reduce.6.cloned.1.call-start = ((), (), s32[]{:S(2)}) async-start(), calls=%async_computation.11 | async-start | bytes 16777216 | tf_op jit(solution)/shard_map/psum | solution.py:164
  21.0 41.3 %copy-start.27 = (f32[8,1,256]{2,1,0:T(1,128)}, f32[8,1,256]{2,1,0:T(1,128)S(1)}, u32[]{:S(2)}) copy-start(f32[8,1,256]{2,1,0:T(1,128)S(1)} %convert_element_type.130) | copy-start | bytes 24580
  21.0 26.8 %copy-start.29 = (bf16[256,128]{1,0:T(8,128)(2,1)S(1)}, bf16[256,128]{1,0:T(8,128)(2,1)}, u32[]{:S(2)}) copy-start(bf16[256,128]{1,0:T(8,128)(2,1)} %param.23) | copy-start | bytes 196612
  24.2 405.9 %copy-start.30 = (f32[2,512]{1,0:T(2,128)}, f32[2,512]{1,0:T(2,128)S(1)}, u32[]{:S(2)}) copy-start(f32[2,512]{1,0:T(2,128)S(1)} %add_rsqrt_fusion.3) | copy-start | bytes 12292
  24.8 43.1 %copy-start.36 = (f32[64]{0:T(128)}, f32[64]{0:T(128)S(1)}, u32[]{:S(2)}) copy-start(f32[64]{0:T(128)S(1)} %convert_element_type.108) | copy-start | bytes 772
  25.8 31.9 %copy-start.2 = (bf16[2,512,2048]{2,1,0:T(8,128)(2,1)S(1)}, bf16[2,512,2048]{2,1,0:T(8,128)(2,1)}, u32[]{:S(2)}) copy-start(bf16[2,512,2048]{2,1,0:T(8,128)(2,1)} %param.18) | copy-start | bytes 12582916
  40.3 18.7 copy-start.11
  44.3 14.7 copy-start.7
  45.3 24.3 %copy-start.17 = (f32[512,32]{0,1:T(8,128)}, f32[512,32]{0,1:T(8,128)S(1)}, u32[]{:S(2)}) copy-start(f32[512,32]{0,1:T(8,128)S(1)} %get-tuple-element.336) | copy-start | bytes 196612
  138.4 346.8 %all-gather.14.cloned.1.call-start = ((), (), s32[]{:S(2)}) async-start(), calls=%async_computation.13 | async-start | bytes 9437184 | tf_op jit(solution)/shard_map/all_gather | solution.py:107
  139.0 403.9 %all-gather.16.cloned.1.call-start = ((), (), s32[]{:S(2)}) async-start(), calls=%async_computation.14 | async-start | bytes 9437184 | tf_op jit(solution)/shard_map/all_gather | solution.py:108
  139.6 459.5 %all-gather.12.cloned.1.call-start = ((), (), s32[]{:S(2)}) async-start(), calls=%async_computation.12 | async-start | bytes 9437184 | tf_op jit(solution)/shard_map/all_gather | solution.py:106
  140.1 800.6 %all-reduce.10.cloned.1.call-start = ((), (), s32[]{:S(2)}) async-start(), calls=%async_computation.16 | async-start | bytes 16777216 | tf_op jit(solution)/shard_map/psum | solution.py:200
  149.5 798.1 %copy-start.32 = (f32[2,512]{1,0:T(2,128)}, f32[2,512]{1,0:T(2,128)S(1)}, u32[]{:S(2)}) copy-start(f32[2,512]{1,0:T(2,128)S(1)} %compare_convert_fusion) | copy-start | bytes 12292
  620.8 14.8 copy-start.46
  620.8 14.8 copy-start.40
  649.8 411.9 %reduce-scatter.10.cloned.1.call-start = ((), (), s32[]{:S(2)}) async-start(), calls=%async_computation.17 | async-start | bytes 1572864 | tf_op jit(solution)/shard_map/reduce_scatter | solution.py:243
  1034.9 32.9 %reduce-scatter.12.cloned.1.call-start = ((), (), s32[]{:S(2)}) async-start(), calls=%async_computation.18 | async-start | bytes 1572864 | tf_op jit(solution)/shard_map/reduce_scatter | solution.py:249
  1037.5 176.1 %all-reduce.8.cloned.1.call-start = ((), (), s32[]{:S(2)}) async-start(), calls=%async_computation.15 | async-start | bytes 8388608 | tf_op jit(solution)/shard_map/psum | solution.py:175
  1037.6 14.7 copy-start.18
  1037.6 14.7 copy-start.21
  1052.1 454.1 %all-reduce.12.cloned.1.call-start = ((), (), s32[]{:S(2)}) async-start(), calls=%async_computation.19 | async-start | bytes 16777216 | tf_op jit(solution)/shard_map/psum | solution.py:282
  1078.3 477.5 %reduce-scatter.16.cloned.1.call-start = ((), (), s32[]{:S(2)}) async-start(), calls=%async_computation.21 | async-start | bytes 1179648 | tf_op jit(solution)/shard_map/reduce_scatter | solution.py:299
  1083.9 501.6 %reduce-scatter.18.cloned.1.call-start = ((), (), s32[]{:S(2)}) async-start(), calls=%async_computation.22 | async-start | bytes 1179648 | tf_op jit(solution)/shard_map/reduce_scatter | solution.py:300
  1089.1 551.9 %reduce-scatter.20.cloned.1.call-start = ((), (), s32[]{:S(2)}) async-start(), calls=%async_computation.23 | async-start | bytes 4718592 | tf_op jit(solution)/shard_map/reduce_scatter | solution.py:301
  1096.9 599.3 %reduce-scatter.14.cloned.1.call-start = ((), (), s32[]{:S(2)}) async-start(), calls=%async_computation.20 | async-start | bytes 4718592 | tf_op jit(solution)/shard_map/reduce_scatter | solution.py:298
  1103.8 712.7 %reduce-scatter.22.cloned.1.call-start = ((), (), s32[]{:S(2)}) async-start(), calls=%async_computation.24 | async-start | bytes 18874368 | tf_op jit(solution)/shard_map/reduce_scatter | solution.py:302
  1119.1 817.8 %reduce-scatter.24.cloned.1.call-start = ((), (), s32[]{:S(2)}) async-start(), calls=%async_computation.25 | async-start | bytes 18874368 | tf_op jit(solution)/shard_map/reduce_scatter | solution.py:303
  1134.7 922.6 %reduce-scatter.26.cloned.1.call-start = ((), (), s32[]{:S(2)}) async-start(), calls=%async_computation.26 | async-start | bytes 18874368 | tf_op jit(solution)/shard_map/reduce_scatter | solution.py:304
  (37 other events, 197.7 us)
Sparse Core Ops, SparseCore 0:
  10.5 33.1 all-gather.7
  45.5 28.7 all-gather.9
  138.5 291.4 all-reduce.5
  431.8 53.3 all-gather.13
  486.9 55.9 all-gather.15
  544.7 54.3 all-gather.11
  649.9 290.8 all-reduce.9
  1035.1 7.5 reduce-scatter.9
  1045.6 9.7 reduce-scatter.11
  1057.5 156.1 all-reduce.7
  1216.3 289.8 all-reduce.11
  1510.1 35.1 reduce-scatter.15
  1549.4 36.0 reduce-scatter.17
  1589.6 51.2 reduce-scatter.19
  1644.8 51.3 reduce-scatter.13
  1700.5 115.9 reduce-scatter.21
  1820.9 115.9 reduce-scatter.23
  1941.4 115.9 reduce-scatter.25
where the time goes:
time: 2070 us; the launch traced here: 2060 us
  waiting for transfers between devices  1540 us (74%)
  matrix products  295 us (14%)
  other arithmetic  103 us (5%)
  blocking collectives  88.1 us (4%)
  local copies, waits for them, and re-layouts  24.2 us (1%)
    psum x1, waiting for transfers between devices, per_device(): grad_normed2 = lax.psum(second_part, 'tensor')  291 us
    psum x1, waiting for transfers between devices, per_device(): grad_normed1_share = cut(lax.psum(first_part, 'tensor'))  282 us
    psum x1, waiting for transfers between devices, per_device(): attn_branch = lax.psum(project(attended_low, full_output), 'tensor')  280 us
    reduce_scatter x1, waiting for transfers between devices, per_device(): lax.psum_scatter(grad_w_down, ('dp', 'context'), scatter_dimension=1, til...  120 us
    reduce_scatter x1, waiting for transfers between devices, per_device(): lax.psum_scatter(grad_w_gate, ('dp', 'context'), scatter_dimension=0, til...  120 us
    reduce_scatter x1, waiting for transfers between devices, per_device(): lax.psum_scatter(grad_w_up, ('dp', 'context'), scatter_dimension=0, tiled...  120 us
    dot_general x7, matrix products, weight_grad(): jnp.einsum('srd,src->dc', left, right, preferred_element_type=jnp.float32)  70.4 us
    dot_general x7, matrix products, project(): jnp.einsum('src,cd->srd', left, right, preferred_element_type=jnp.float32)  68.9 us
  transfers between devices with their start and end apart: 18, of which 13 were waited for; matrix products, arithmetic and copies ran while one was open for 13% of the time, Pallas kernels for 0%

commit v1 on v0

v1 whole, which is shorter than its diff:
```python
import functools
import math

import jax
import jax.numpy as jnp
from jax import lax
from jax.experimental import pallas as pl
from jax.experimental.pallas import tpu as pltpu
from jax.sharding import PartitionSpec as P

F32 = jnp.float32
BF16 = jnp.bfloat16
epsilon = 1e-05
rope_base = 1000000.0
log2e = 1.4426950408889634
VMEM_BYTES = 60 * 1024 * 1024
PARAMS = pltpu.CompilerParams(vmem_limit_bytes=VMEM_BYTES)
SMEM = pl.BlockSpec(memory_space=pltpu.SMEM)
SWAP = ((0, 1), (1, 0))


def shape(dims, dtype):
    return jax.ShapeDtypeStruct(tuple(dims), dtype)


def cost(flops, size, exps=0):
    return pl.CostEstimate(flops=int(flops), bytes_accessed=int(size), transcendentals=int(exps))


def dot_nn(a, b):
    return lax.dot_general(a, b, (((1,), (0,)), ((), ())), preferred_element_type=F32)


def dot_nt(a, b):
    return lax.dot_general(a, b, (((1,), (1,)), ((), ())), preferred_element_type=F32)


def dot_tn(a, b):
    return lax.dot_general(a, b, (((0,), (0,)), ((), ())), preferred_element_type=F32)


def inverse_rms(values):
    return lax.rsqrt(jnp.mean(values * values, axis=-1, keepdims=True) + epsilon)


def tie(value, *others):
    return lax.optimization_barrier((value,) + others)[0]


def block_order(dp, row, core):
    if dp == 4:
        return jnp.stack([(row ^ k) * 2 + (core ^ o) for o in range(2) for k in range(dp)]).astype(jnp.int32)
    return jnp.stack([jnp.int32(k) * 2 + (core ^ o) for o in range(2) for k in range(dp)]).astype(jnp.int32)


def to_relative(values, dp, core):
    lead = values.shape[:-1]
    parts = values.reshape(lead + (dp, 2, -1))
    parts = jnp.where(core == 0, parts, parts[..., ::-1, :])
    return jnp.swapaxes(parts, -3, -2).reshape(values.shape)


def to_absolute(values, dp, core):
    lead = values.shape[:-1]
    parts = jnp.swapaxes(values.reshape(lead + (2, dp, -1)), -3, -2)
    return jnp.where(core == 0, parts, parts[..., ::-1, :]).reshape(values.shape)


def over_x(value):
    return lax.ppermute(value, "dp", [(i, i ^ 1) for i in range(4)])


def over_y(value):
    return lax.ppermute(value, "dp", [(i, i ^ 2) for i in range(4)])


def over_core(value):
    return lax.ppermute(value, "context", SWAP)


def gather_blocks(weight, axis, dp):
    if dp == 4:
        from_x = over_x(weight)
        from_y = over_y(weight)
        half = weight.shape[0] // 2
        first = over_x(from_y[:half])
        second = over_y(from_x[half:])
        if axis == 0:
            own = jnp.concatenate([weight, from_x, from_y, first, second], axis=0)
        else:
            diagonal = jnp.concatenate([first, second], axis=0)
            own = jnp.concatenate([weight, from_x, from_y, diagonal], axis=1)
        mark = from_x
    else:
        own = lax.all_gather(weight, "dp", axis=axis, tiled=True)
        mark = own
    return own, over_core(own), mark


def scatter_blocks(total, axis, dp):
    if dp != 4:
        return lax.psum_scatter(total, "dp", scatter_dimension=axis, tiled=True).astype(F32)
    piece = total.shape[axis] // 4
    half = piece // 2 if axis == 0 else total.shape[0] // 2

    def block(k):
        return lax.slice_in_dim(total, k * piece, (k + 1) * piece, axis=axis)

    diagonal = block(3)
    from_x = over_x(diagonal[:half])
    from_y = over_y(diagonal[half:])
    to_y = block(2)
    to_x = block(1)
    to_y = jnp.concatenate([to_y[:half].astype(F32) + from_x.astype(F32), to_y[half:].astype(F32)], axis=0).astype(BF16)
    to_x = jnp.concatenate([to_x[:half].astype(F32), to_x[half:].astype(F32) + from_y.astype(F32)], axis=0).astype(BF16)
    got_x = over_x(to_x)
    got_y = over_y(to_y)
    return block(0).astype(F32) + got_x.astype(F32) + got_y.astype(F32)


def sum_terms(part, tensor):
    if tensor != 4:
        return [lax.psum(part, "tensor")]
    inward = lax.ppermute(part, "tensor", [(0, 1), (3, 2)])
    pair = (part.astype(F32) + inward.astype(F32)).astype(BF16)
    across = lax.ppermute(pair, "tensor", [(1, 2), (2, 1)])
    rest = (part.astype(F32) + across.astype(F32)).astype(BF16)
    outward = lax.ppermute(rest, "tensor", [(1, 0), (2, 3)])
    return [part, inward, across, outward]


def ring_scatter(piece, tensor, rank):
    ring = [(i, (i + 1) % tensor) for i in range(tensor)]
    moving = piece((rank + tensor - 1) % tensor)
    for step in range(1, tensor):
        moving = lax.ppermute(moving, "tensor", ring)
        if step < tensor - 1:
            moving = (moving.astype(F32) + piece((rank + tensor - 1 - step) % tensor).astype(F32)).astype(BF16)
    return moving


def begin_kernel(order, x_ref, cot_ref, gain_ref, scal_ref, xr_ref, n1_ref, gf_ref):
    seq, tile = pl.program_id(0), pl.program_id(1)
    rows, width = x_ref.shape[1:]
    seqs = pl.num_programs(0)
    place = scal_ref[seqs] + tile * rows + lax.broadcasted_iota(jnp.int32, (rows, 1), 0)
    valid = (place < scal_ref[seq]).astype(F32)
    x = x_ref[0].astype(F32)
    inv = inverse_rms(x)
    piece = width // order
    for k in range(order):
        src = pl.ds(pl.multiple_of(scal_ref[seqs + 1 + k] * piece, piece), piece) if order > 1 else slice(0, width)
        dst = slice(k * piece, (k + 1) * piece)
        part = x_ref[0, :, src]
        xr_ref[0, :, dst] = part
        n1_ref[0, :, dst] = (part.astype(F32) * inv * gain_ref[:, dst]).astype(BF16)
        gf_ref[0, :, dst] = (cot_ref[0, :, src].astype(F32) * valid).astype(BF16)


def begin(x, cot, gain, scalars, order):
    seqs, span, width = x.shape
    rows = min(256, span)
    spec = pl.BlockSpec((1, rows, width), lambda s, i: (s, i, 0))
    return pl.pallas_call(
        functools.partial(begin_kernel, order),
        grid=(seqs, span // rows),
        in_specs=[spec, spec, pl.BlockSpec((1, width), lambda s, i: (0, 0)), SMEM],
        out_specs=[spec] * 3,
        out_shape=[shape(x.shape, BF16)] * 3,
        compiler_params=PARAMS,
        cost_estimate=cost(8 * x.size, 10 * x.size),
        name="first_norm",
    )(x, cot, gain, scalars)


def heads_kernel(hd, nq, nk, n1_ref, wo_ref, wx_ref, cos_ref, sin_ref, qg_ref, kg_ref, core_ref, pre_ref, own_ref, oth_ref):
    half = wo_ref.shape[0]
    x = n1_ref[0]
    flat = dot_nn(x[:, :half], wo_ref[...]) + dot_nn(x[:, half:], wx_ref[...])
    turned = flat.T
    span = turned.shape[1]
    normed = turned[: (nq + nk) * hd]
    pre_ref[...] = normed
    core = core_ref[0]
    cosine, sine = cos_ref[...], sin_ref[...]
    done = []
    for h in range(nq + nk):
        v = normed[h * hd : (h + 1) * hd]
        inv = lax.rsqrt(jnp.mean(v * v, axis=0, keepdims=True) + epsilon)
        v = v * inv * (qg_ref[...] if h < nq else kg_ref[...])
        a, b = v[: hd // 2], v[hd // 2 :]
        done.append(jnp.concatenate([a * cosine - b * sine, b * cosine + a * sine], axis=0))
    for h in range(nk):
        lo = (nq + nk + h) * hd
        done.append(turned[lo : lo + hd])
    parts = [[], []]
    for start, count in ((0, nq), (nq, nk), (nq + nk, nk)):
        for side in range(2):
            parts[side] += done[start + side * count // 2 : start + (side + 1) * count // 2]
    low = jnp.concatenate(parts[0], axis=0)
    high = jnp.concatenate(parts[1], axis=0)
    first = core == 0
    own_ref[...] = jnp.where(first, low, high).astype(BF16)
    oth_ref[...] = jnp.where(first, high, low).astype(BF16)


def heads(n1, seq, w_own, w_oth, cosine, sine, qgain, kgain, core, hd, nq, nk):
    span, width = n1.shape[1:]
    sides = (nq + 2 * nk) * hd // 2
    full = pl.BlockSpec(memory_space=pltpu.VMEM)
    whole = lambda a: pl.BlockSpec(a.shape, lambda i: (0,) * a.ndim)
    outs = [shape(((nq + nk) * hd, span), F32), shape((sides, span), BF16), shape((sides, span), BF16)]
    return pl.pallas_call(
        functools.partial(heads_kernel, hd, nq, nk),
        grid=(1,),
        in_specs=[pl.BlockSpec((1, span, width), lambda i: (seq, 0, 0))]
        + [whole(a) for a in (w_own, w_oth, cosine, sine, qgain, kgain)]
        + [SMEM],
        out_specs=[whole(o) for o in outs],
        out_shape=outs,
        compiler_params=PARAMS,
        cost_estimate=cost(2 * span * width * w_own.shape[1], 2 * span * width + 4 * w_own.size),
        name="query_key_value",
    )(n1, w_own, w_oth, cosine, sine, qgain, kgain, core)


def join_positions(core, own, oth):
    first = core == 0
    return jnp.where(first, own, oth), jnp.where(first, oth, own)


def attend_kernel(block, groups, scal_ref, own_ref, got_ref, all_ref, att_ref, inv_ref, ao_ref, ax_ref):
    span = own_ref.shape[1]
    hd = own_ref.shape[0] // (groups + 2)
    length, core = scal_ref[0], scal_ref[1]
    low, high = join_positions(core, own_ref[...], got_ref[...])
    all_ref[:, :span] = low
    all_ref[:, span:] = high
    scale = log2e / math.sqrt(hd)
    krow = lax.broadcasted_iota(jnp.int32, (block, groups * block), 0)
    qcol = lax.broadcasted_iota(jnp.int32, (block, groups * block), 1) % block
    base = groups * hd
    for i in range(2 * span // block):
        cut = slice(i * block, (i + 1) * block)
        q = jnp.concatenate([all_ref[g * hd : (g + 1) * hd, cut] for g in range(groups)], axis=1)
        acc = jnp.zeros((hd, groups * block), F32)
        total = jnp.zeros((1, groups * block), F32)
        for j in range(i + 1):
            kcut = slice(j * block, (j + 1) * block)
            s = dot_tn(all_ref[base : base + hd, kcut], q) * scale
            ok = (krow + j * block) < length
            if j == i:
                ok = ok & (krow <= qcol)
            e = jnp.where(ok, jnp.exp2(s), 0.0)
            total = total + jnp.sum(e, axis=0, keepdims=True)
            acc = acc + dot_nn(all_ref[base + hd : base + 2 * hd, kcut], e.astype(BF16))
        inv = 1.0 / total
        att = (acc * inv).astype(BF16)
        for g in range(groups):
            att_ref[g * hd : (g + 1) * hd, cut] = att[:, g * block : (g + 1) * block]
            inv_ref[g : g + 1, cut] = inv[:, g * block : (g + 1) * block]
    mine, theirs = join_positions(core, att_ref[:, :span], att_ref[:, span:])
    ao_ref[...] = mine
    ax_ref[...] = theirs


def attend(scalars, own, got, groups):
    rows, span = own.shape
    hd = rows // (groups + 2)
    block = min(256, span)
    full = pl.BlockSpec(memory_space=pltpu.VMEM)
    return pl.pallas_call(
        functools.partial(attend_kernel, block, groups),
        in_specs=[SMEM, full, full],
        out_specs=[full] * 5,
        out_shape=[
            shape((rows, 2 * span), BF16),
            shape((groups * hd, 2 * span), BF16),
            shape((groups, 2 * span), F32),
            shape((groups * hd, span), BF16),
            shape((groups * hd, span), BF16),
        ],
        compiler_params=PARAMS,
        cost_estimate=cost(60 * groups * hd * span * span, 12 * rows * span, 4 * groups * span * span),
        name="attend_forward",
    )(scalars, own, got)


def branch_kernel(own_ref, got_ref, wo_ref, wx_ref, core_ref, att_ref, *outs):
    half = wo_ref.shape[1]
    low, high = join_positions(core_ref[0], own_ref[...], got_ref[...])
    att = jnp.concatenate([low, high], axis=0)
    att_ref[...] = att
    rows = outs[0].shape[0]
    for k, out in enumerate(outs):
        part = att[:, k * rows : (k + 1) * rows]
        out[:, :half] = dot_tn(part, wo_ref[...]).astype(BF16)
        out[:, half:] = dot_tn(part, wx_ref[...]).astype(BF16)


def branch(own, got, w_own, w_oth, core, chunks):
    rows, span = own.shape
    width = 2 * w_own.shape[1]
    full = pl.BlockSpec(memory_space=pltpu.VMEM)
    return pl.pallas_call(
        branch_kernel,
        in_specs=[full] * 4 + [SMEM],
        out_specs=[full] * (1 + chunks),
        out_shape=[shape((2 * rows, span), BF16)] + [shape((span // chunks, width), BF16)] * chunks,
        compiler_params=PARAMS,
        cost_estimate=cost(4 * rows * span * width, 4 * rows * width + 2 * span * width),
        name="attention_branch",
    )(own, got, w_own, w_oth, core)


def second_norm_kernel(terms, scal_ref, x_ref, gain_ref, *refs):
    term_refs, (hidden_ref, n2_ref, stat_ref) = refs[:terms], refs[terms:]
    rows = hidden_ref.shape[0]
    branch_sum = term_refs[0][...].astype(F32)
    for ref in term_refs[1:]:
        branch_sum = branch_sum + ref[...].astype(F32)
    resid = x_ref[0].astype(F32)
    hidden = resid + branch_sum
    hidden_ref[...] = hidden
    n2_ref[...] = (hidden * inverse_rms(hidden) * gain_ref[...]).astype(BF16)
    place = scal_ref[1] + lax.broadcasted_iota(jnp.int32, (rows, 1), 0)
    valid = (place < scal_ref[0]).astype(F32)
    first = jnp.sum(valid * resid * resid, keepdims=True)
    second = jnp.sum(valid * branch_sum * branch_sum, keepdims=True)
    line = lax.broadcasted_iota(jnp.int32, (8, 128), 0)
    stat_ref[...] = jnp.where(line == 0, first, second)


def second_norm(scalars, xr, seq, part, gain, terms):
    rows, width = terms[0].shape
    flat = pl.BlockSpec((rows, width), lambda i: (0, 0))
    return pl.pallas_call(
        functools.partial(second_norm_kernel, len(terms)),
        grid=(1,),
        in_specs=[SMEM, pl.BlockSpec((1, rows, width), lambda i: (seq, part, 0)), pl.BlockSpec((1, width), lambda i: (0, 0))]
        + [flat] * len(terms),
        out_specs=[flat, flat, pl.BlockSpec((8, 128), lambda i: (0, 0))],
        out_shape=[shape((rows, width), F32), shape((rows, width), BF16), shape((8, 128), F32)],
        compiler_params=PARAMS,
        cost_estimate=cost(20 * rows * width, (8 + 2 * len(terms)) * rows * width),
        name="second_norm",
    )(scalars, xr, gain, *terms)


def feed_kernel(n_ref, g_ref, wgo, wgx, wuo, wux, wdo, wdx, inner_ref, gg_ref, gu_ref, ffn_ref, gn_ref, facc, gacc):
    step = pl.program_id(0)
    half = wgo.shape[0]
    no, nx = n_ref[:, :half], n_ref[:, half:]
    gate = dot_nn(no, wgo[...]) + dot_nn(nx, wgx[...])
    up = dot_nn(no, wuo[...]) + dot_nn(nx, wux[...])
    gi = dot_nt(g_ref[0, :, :half], wdo[...]) + dot_nt(g_ref[0, :, half:], wdx[...])
    sig = jax.nn.sigmoid(gate)
    silu = gate * sig
    inner = (silu * up).astype(BF16)
    gg = (gi * up * sig * (1.0 + gate * (1.0 - sig))).astype(BF16)
    gu = (gi * silu).astype(BF16)
    inner_ref[...] = inner
    gg_ref[...] = gg
    gu_ref[...] = gu

    @pl.when(step == 0)
    def _():
        facc[...] = jnp.zeros_like(facc)
        gacc[...] = jnp.zeros_like(gacc)

    facc[:, :half] += dot_nn(inner, wdo[...])
    facc[:, half:] += dot_nn(inner, wdx[...])
    gacc[:, :half] += dot_nt(gg, wgo[...]) + dot_nt(gu, wuo[...])
    gacc[:, half:] += dot_nt(gg, wgx[...]) + dot_nt(gu, wux[...])

    @pl.when(step == pl.num_programs(0) - 1)
    def _():
        ffn_ref[...] = facc[...].astype(BF16)
        gn_ref[...] = gacc[...].astype(BF16)


def feed(n2, gf, seq, part, wgo, wgx, wuo, wux, wdo, wdx):
    rows, width = n2.shape
    half, hidden = wgo.shape
    hb = min(512, hidden)
    row = pl.BlockSpec((half, hb), lambda h: (0, h))
    col = pl.BlockSpec((hb, half), lambda h: (h, 0))
    whole = pl.BlockSpec((rows, width), lambda h: (0, 0))
    tile = pl.BlockSpec((rows, hb), lambda h: (0, h))
    return pl.pallas_call(
        feed_kernel,
        grid=(hidden // hb,),
        in_specs=[whole, pl.BlockSpec((1, rows, width), lambda h: (seq, part, 0)), row, row, row, row, col, col],
        out_specs=[tile, tile, tile, whole, whole],
        out_shape=[shape((rows, hidden), BF16)] * 3 + [shape((rows, width), BF16)] * 2,
        scratch_shapes=[pltpu.VMEM((rows, width), F32), pltpu.VMEM((rows, width), F32)],
        compiler_params=PARAMS,
        cost_estimate=cost(12 * rows * width * hidden, 12 * half * hidden + 14 * rows * width, rows * hidden),
        name="feed_forward",
    )(n2, gf, wgo, wgx, wuo, wux, wdo, wdx)


def second_back_kernel(terms, hidden_ref, gf_ref, gain_ref, *refs):
    term_refs, (gb_ref, gh_ref, gain_out) = refs[:terms], refs[terms:]
    e = term_refs[0][...].astype(F32)
    for ref in term_refs[1:]:
        e = e + ref[...].astype(F32)
    hidden = hidden_ref[...]
    inv = inverse_rms(hidden)
    hat = hidden * inv
    eg = e * gain_ref[...]
    gh = gf_ref[0].astype(F32) + inv * (eg - hat * jnp.mean(eg * hat, axis=-1, keepdims=True))
    gh_ref[...] = gh
    gb_ref[...] = gh.astype(BF16)
    gain_out[...] = jnp.sum(e * hat, axis=0, keepdims=True)


def second_back(hidden, gf, seq, part, gain, terms):
    rows, width = hidden.shape
    flat = pl.BlockSpec((rows, width), lambda i: (0, 0))
    line = pl.BlockSpec((1, width), lambda i: (0, 0))
    return pl.pallas_call(
        functools.partial(second_back_kernel, len(terms)),
        grid=(1,),
        in_specs=[flat, pl.BlockSpec((1, rows, width), lambda i: (seq, part, 0)), line] + [flat] * len(terms),
        out_specs=[flat, flat, line],
        out_shape=[shape((rows, width), BF16), shape((rows, width), F32), shape((1, width), F32)],
        compiler_params=PARAMS,
        cost_estimate=cost(20 * rows * width, (12 + 2 * len(terms)) * rows * width),
        name="second_norm_back",
    )(hidden, gf, gain, *terms)


def branch_back_kernel(chunks, *refs):
    gb_refs, (wo_ref, wx_ref, core_ref, own_ref, oth_ref) = refs[:chunks], refs[chunks:]
    half = wo_ref.shape[1]
    rows = gb_refs[0].shape[0]
    heads_half = own_ref.shape[0]
    first = core_ref[0] == 0
    for k, ref in enumerate(gb_refs):
        da = dot_nt(wo_ref[...], ref[:, :half]) + dot_nt(wx_ref[...], ref[:, half:])
        da = da.astype(BF16)
        low, high = da[:heads_half], da[heads_half:]
        cut = slice(k * rows, (k + 1) * rows)
        own_ref[:, cut] = jnp.where(first, low, high)
        oth_ref[:, cut] = jnp.where(first, high, low)


def branch_back(gbs, w_own, w_oth, core):
    chunks = len(gbs)
    rows, width = gbs[0].shape
    dim = w_own.shape[0]
    full = pl.BlockSpec(memory_space=pltpu.VMEM)
    return pl.pallas_call(
        functools.partial(branch_back_kernel, chunks),
        in_specs=[full] * (chunks + 2) + [SMEM],
        out_specs=[full] * 2,
        out_shape=[shape((dim // 2, chunks * rows), BF16)] * 2,
        compiler_params=PARAMS,
        cost_estimate=cost(2 * dim * chunks * rows * width, 2 * dim * width + 2 * chunks * rows * width),
        name="attention_branch_back",
    )(*gbs, w_own, w_oth, core)


def attend_back_kernel(block, groups, scal_ref, all_ref, att_ref, inv_ref, own_ref, got_ref, out_own, out_oth, da_all, grads):
    span = own_ref.shape[1]
    hd = all_ref.shape[0] // (groups + 2)
    length, core = scal_ref[0], scal_ref[1]
    low, high = join_positions(core, own_ref[...], got_ref[...])
    da_all[:, :span] = low
    da_all[:, span:] = high
    scale = log2e / math.sqrt(hd)
    back = 1.0 / math.sqrt(hd)
    krow = lax.broadcasted_iota(jnp.int32, (block, groups * block), 0)
    qcol = lax.broadcasted_iota(jnp.int32, (block, groups * block), 1) % block
    base = groups * hd
    grads[base:, :] = jnp.zeros((2 * hd, 2 * span), F32)
    for i in range(2 * span // block):
        cut = slice(i * block, (i + 1) * block)

        def rows(ref):
            return jnp.concatenate([ref[g * hd : (g + 1) * hd, cut] for g in range(groups)], axis=1)

        q = rows(all_ref)
        da = rows(da_all)
        inv = jnp.concatenate([inv_ref[g : g + 1, cut] for g in range(groups)], axis=1)
        delta = jnp.sum(rows(att_ref).astype(F32) * da.astype(F32), axis=0, keepdims=True)
        dq = jnp.zeros((hd, groups * block), F32)
        for j in range(i + 1):
            kcut = slice(j * block, (j + 1) * block)
            key = all_ref[base : base + hd, kcut]
            s = dot_tn(key, q) * scale
            ok = (krow + j * block) < length
            if j == i:
                ok = ok & (krow <= qcol)
            p = jnp.where(ok, jnp.exp2(s) * inv, 0.0)
            dp = dot_tn(all_ref[base + hd : base + 2 * hd, kcut], da)
            ds = (p * (dp - delta)).astype(BF16)
            dq = dq + dot_nn(key, ds)
            grads[base : base + hd, kcut] += dot_nt(q, ds) * back
            grads[base + hd : base + 2 * hd, kcut] += dot_nt(da, p.astype(BF16))
        dq = dq * back
        for g in range(groups):
            grads[g * hd : (g + 1) * hd, cut] = dq[:, g * block : (g + 1) * block]
    mine, theirs = join_positions(core, grads[:, :span], grads[:, span:])
    out_own[...] = mine.astype(BF16)
    out_oth[...] = theirs.astype(BF16)


def attend_back(scalars, everything, att, inv, own, got, groups):
    rows, slots = everything.shape
    span = slots // 2
    block = min(256, span)
    full = pl.BlockSpec(memory_space=pltpu.VMEM)
    return pl.pallas_call(
        functools.partial(attend_back_kernel, block, groups),
        in_specs=[SMEM] + [full] * 5,
        out_specs=[full] * 2,
        out_shape=[shape((rows, span), BF16)] * 2,
        scratch_shapes=[pltpu.VMEM(att.shape, BF16), pltpu.VMEM((rows, slots), F32)],
        compiler_params=PARAMS,
        cost_estimate=cost(30 * att.shape[0] * slots * slots, 12 * rows * slots, groups * slots * slots),
        name="attend_backward",
    )(scalars, everything, att, inv, own, got)


def heads_back_kernel(hd, nq, nk, own_ref, got_ref, pre_ref, cos_ref, sin_ref, qg_ref, kg_ref, x_ref, wo_ref, wx_ref, core_ref, dpre_ref, first_ref, gain_ref, hgain_ref):
    half = wo_ref.shape[0]
    low, high = join_positions(core_ref[0], own_ref[...].astype(F32), got_ref[...].astype(F32))
    sides = (nq // 2, nk // 2, nk // 2)
    grads = [[], [], []]
    for side in (low, high):
        at = 0
        for kind, count in enumerate(sides):
            for h in range(count):
                grads[kind].append(side[at : at + hd])
                at += hd
    cosine, sine = cos_ref[...], sin_ref[...]
    done = []
    sums = [0.0, 0.0]
    for h in range(nq + nk):
        kind = 0 if h < nq else 1
        g = grads[kind][h - kind * nq]
        a, b = g[: hd // 2], g[hd // 2 :]
        g = jnp.concatenate([a * cosine + b * sine, b * cosine - a * sine], axis=0)
        v = pre_ref[h * hd : (h + 1) * hd, :]
        inv = lax.rsqrt(jnp.mean(v * v, axis=0, keepdims=True) + epsilon)
        hat = v * inv
        sums[kind] = sums[kind] + jnp.sum(g * hat, axis=1, keepdims=True)
        gg = g * (qg_ref[...] if kind == 0 else kg_ref[...])
        done.append(inv * (gg - hat * jnp.mean(gg * hat, axis=0, keepdims=True)))
    done += grads[2]
    hgain_ref[:hd, :] = jnp.broadcast_to(sums[0], (hd, 128))
    hgain_ref[hd:, :] = jnp.broadcast_to(sums[1], (hd, 128))
    dpre = jnp.concatenate(done, axis=0).T.astype(BF16)
    dpre_ref[...] = dpre
    x = x_ref[0].astype(F32)
    hat = x * inverse_rms(x)
    for k, ref in enumerate((wo_ref, wx_ref)):
        cut = slice(k * half, (k + 1) * half)
        part = dot_nt(dpre, ref[...])
        first_ref[:, cut] = part.astype(BF16)
        gain_ref[:, cut] = jnp.sum(part * hat[:, cut], axis=0, keepdims=True)


def heads_back(own, got, pre, cosine, sine, qgain, kgain, xr, seq, w_own, w_oth, core, hd, nq, nk):
    span = own.shape[1]
    half, cols = w_own.shape
    width = 2 * half
    whole = lambda a: pl.BlockSpec(a.shape, lambda i: (0,) * len(a.shape))
    outs = [shape((span, cols), BF16), shape((span, width), BF16), shape((1, width), F32), shape((2 * hd, 128), F32)]
    return pl.pallas_call(
        functools.partial(heads_back_kernel, hd, nq, nk),
        grid=(1,),
        in_specs=[whole(a) for a in (own, got, pre, cosine, sine, qgain, kgain)]
        + [pl.BlockSpec((1, span, width), lambda i: (seq, 0, 0)), whole(w_own), whole(w_oth), SMEM],
        out_specs=[whole(o) for o in outs],
        out_shape=outs,
        compiler_params=PARAMS,
        cost_estimate=cost(2 * span * width * cols, 4 * span * width + 4 * half * cols),
        name="query_key_value_back",
    )(own, got, pre, cosine, sine, qgain, kgain, xr, w_own, w_oth, core)


def place_blocks(order, ids, first_id, value, out_ref):
    piece = value.shape[-1] // order
    for k in range(order):
        if order == 1:
            out_ref[...] = value
        else:
            dst = pl.ds(pl.multiple_of(ids[first_id + k] * piece, piece), piece)
            out_ref[:, dst] = value[:, k * piece : (k + 1) * piece]


def output_kernel(order, scal_ref, got_ref, f0_ref, f1_ref, h0_ref, h1_ref, out_ref, stat_ref):
    low = scal_ref[0] * 2 < scal_ref[3]
    rows = out_ref.shape[0]
    ffn = got_ref[...].astype(F32) + jnp.where(low, f0_ref[...], f1_ref[...]).astype(F32)
    hidden = jnp.where(low, h0_ref[...], h1_ref[...])
    place = scal_ref[2] + lax.broadcasted_iota(jnp.int32, (rows, 1), 0)
    valid = (place < scal_ref[1]).astype(F32)
    stat_ref[...] = jnp.broadcast_to(jnp.sum(valid * ffn * ffn, keepdims=True), (8, 128))
    place_blocks(order, scal_ref, 4, (hidden + ffn).astype(BF16), out_ref)


def share_specs(rows, width, per):
    return [
        pl.BlockSpec((rows, width), lambda i, s: (jnp.minimum(s[0], per - 1), 0)),
        pl.BlockSpec((rows, width), lambda i, s: (jnp.maximum(s[0] - per, 0), 0)),
    ]


def output_share(scalars, got, ffns, hiddens, order):
    rows, width = got.shape
    pair = share_specs(rows, width, ffns[0].shape[0] // rows)
    flat = pl.BlockSpec((rows, width), lambda i, s: (0, 0))
    return pl.pallas_call(
        functools.partial(output_kernel, order),
        grid_spec=pltpu.PrefetchScalarGridSpec(
            num_scalar_prefetch=1,
            grid=(1,),
            in_specs=[flat] + pair + pair,
            out_specs=[flat, pl.BlockSpec((8, 128), lambda i, s: (0, 0))],
        ),
        out_shape=[shape((rows, width), BF16), shape((8, 128), F32)],
        compiler_params=PARAMS,
        cost_estimate=cost(6 * rows * width, 16 * rows * width),
        name="output_share",
    )(scalars, got, *ffns, *hiddens)


def input_kernel(order, scal_ref, got_ref, part_ref, g0_ref, g1_ref, x_ref, gain_ref, out_ref):
    low = scal_ref[0] * 2 < scal_ref[3]
    e = got_ref[...].astype(F32) + part_ref[...].astype(F32)
    gh = jnp.where(low, g0_ref[...], g1_ref[...])
    x = x_ref[0].astype(F32)
    inv = inverse_rms(x)
    hat = x * inv
    eg = e * gain_ref[...]
    value = gh + inv * (eg - hat * jnp.mean(eg * hat, axis=-1, keepdims=True))
    place_blocks(order, scal_ref, 4, value, out_ref)


def input_share(scalars, got, part, ghs, xr, seq, gain, order):
    rows, width = got.shape
    pair = share_specs(rows, width, ghs[0].shape[0] // rows)
    flat = pl.BlockSpec((rows, width), lambda i, s: (0, 0))
    return pl.pallas_call(
        functools.partial(input_kernel, order),
        grid_spec=pltpu.PrefetchScalarGridSpec(
            num_scalar_prefetch=1,
            grid=(1,),
            in_specs=[flat, pl.BlockSpec((rows, width), lambda i, s: (s[0], 0))]
            + pair
            + [pl.BlockSpec((1, rows, width), lambda i, s: (seq, s[0], 0)), pl.BlockSpec((1, width), lambda i, s: (0, 0))],
            out_specs=flat,
        ),
        out_shape=shape((rows, width), F32),
        compiler_params=PARAMS,
        cost_estimate=cost(12 * rows * width, 20 * rows * width),
        name="input_share",
    )(scalars, got, part, *ghs, xr, gain)


def weight_grad_kernel(count, extra, *refs):
    a_refs, b_refs, out = refs[:count], refs[count : 2 * count], refs[-1]
    total = dot_tn(a_refs[0][...], b_refs[0][...])
    for a, b in zip(a_refs[1:], b_refs[1:]):
        total = total + dot_tn(a[...], b[...])
    if extra:
        total = total + refs[2 * count][...].astype(F32)
    out[...] = total.astype(BF16)


def weight_grad(lefts, rights, side, axis, add=None):
    count = len(lefts)
    rows_all, cols_all = lefts[0].shape[1], rights[0].shape[1]
    dims = [rows_all, cols_all]
    dims[axis] //= 2
    rows, cols = min(512, dims[0]), min(2048, dims[1])
    row_at = side * (dims[0] // rows) if axis == 0 else 0
    col_at = side * (dims[1] // cols) if axis == 1 else 0
    specs = [pl.BlockSpec((a.shape[0], rows), lambda j, i: (0, i + row_at)) for a in lefts]
    specs += [pl.BlockSpec((b.shape[0], cols), lambda j, i: (0, j + col_at)) for b in rights]
    tile = pl.BlockSpec((rows, cols), lambda j, i: (i, j))
    tokens = sum(a.shape[0] for a in lefts)
    return pl.pallas_call(
        functools.partial(weight_grad_kernel, count, add is not None),
        grid=(dims[1] // cols, dims[0] // rows),
        in_specs=specs + ([tile] if add is not None else []),
        out_specs=tile,
        out_shape=shape(dims, BF16),
        compiler_params=PARAMS,
        cost_estimate=cost(2 * tokens * dims[0] * dims[1], 2 * tokens * sum(dims) + 2 * dims[0] * dims[1]),
        name="weight_grad",
    )(*lefts, *rights, *([add] if add is not None else []))


def per_device(
    inputs,
    cotangent,
    lengths,
    w_query,
    key_projection_weight,
    value_projection_weight,
    w_output,
    w_gate,
    w_up,
    w_down,
    attn_gain,
    ffn_gain,
    query_gain,
    key_gain,
):
    seqs, span, width = inputs.shape
    hd = query_gain.shape[0]
    nq = w_query.shape[1] // hd
    nk = key_projection_weight.shape[1] // hd
    groups = nq // nk
    dp = lax.axis_size("dp")
    tensor = lax.axis_size("tensor")
    row = lax.axis_index("dp")
    core = lax.axis_index("context")
    rank = lax.axis_index("tensor")
    chunks = 2
    rows = span // chunks
    share = span // tensor
    lengths = lengths.astype(jnp.int32)
    start = (core * span).astype(jnp.int32)
    core1 = core.astype(jnp.int32).reshape(1)
    ids = block_order(dp, row, core)
    order = 2 * dp if (width // (2 * dp)) % 128 == 0 else 1

    positions = start + jnp.arange(span, dtype=jnp.int32)
    freqs = rope_base ** (-(jnp.arange(hd // 2, dtype=F32) * (2.0 / hd)))
    angles = freqs[:, None] * positions.astype(F32)[None, :]
    cosine, sine = jnp.cos(angles), jnp.sin(angles)
    qgain = query_gain.astype(F32).reshape(hd, 1)
    kgain = key_gain.astype(F32).reshape(hd, 1)

    gains = jnp.stack([attn_gain, ffn_gain])
    g_own, g_oth, _ = gather_blocks(gains, 1, dp)
    gains = jnp.concatenate([g_own, g_oth], axis=1).astype(F32)
    gain1, gain2 = gains[0:1], gains[1:2]
    w_qkv = jnp.concatenate([w_query, key_projection_weight, value_projection_weight], axis=1)
    qkv_own, qkv_oth, mark = gather_blocks(w_qkv, 0, dp)
    out_own, out_oth, mark = gather_blocks(tie(w_output, mark), 1, dp)
    gate_own, gate_oth, mark = gather_blocks(tie(w_gate, mark), 0, dp)
    up_own, up_oth, mark = gather_blocks(tie(w_up, mark), 0, dp)
    down_own, down_oth, mark = gather_blocks(tie(w_down, mark), 1, dp)

    scal = jnp.concatenate([lengths, start.reshape(1), ids])
    x_in, cot_in = inputs, cotangent
    if order == 1:
        x_in, cot_in = to_relative(x_in, dp, core), to_relative(cot_in, dp, core)
    xr, n1, gf = begin(x_in, cot_in, gain1, scal, order)

    saved = []
    parts = []
    for s in range(seqs):
        pre, own, oth = heads(n1, s, qkv_own, qkv_oth, cosine, sine, qgain, kgain, core1, hd, nq, nk)
        seq_scal = jnp.stack([lengths[s], core.astype(jnp.int32)])
        everything, att, inv, mine, theirs = attend(seq_scal, own, over_core(oth), groups)
        branched = branch(mine, over_core(theirs), out_own, out_oth, core1, chunks)
        saved.append((pre, everything, att, inv, seq_scal, branched[0]))
        parts.append(branched[1:])

    stats = jnp.zeros((2,), F32)
    ffn_squares = jnp.zeros((), F32)
    hidden, n2, inner, gg, gu, ffn, gn = [[[None] * chunks for _ in range(seqs)] for _ in range(7)]
    out_shares = []
    for s in range(seqs):
        for k in range(chunks):
            terms = sum_terms(parts[s][k], tensor)
            place = jnp.stack([lengths[s], start + k * rows])
            hidden[s][k], n2[s][k], stat = second_norm(place, xr, s, k, gain2, terms)
            stats = stats + stat[:2, 0]
            inner[s][k], gg[s][k], gu[s][k], ffn[s][k], gn[s][k] = feed(
                n2[s][k], gf, s, k, gate_own, gate_oth, up_own, up_oth, down_own, down_oth
            )

    def piece_of(arrays):
        per = arrays[0].shape[0] // share

        def piece(k):
            found = lax.dynamic_slice_in_dim(arrays[0], jnp.minimum(k, per - 1) * share, share, 0)
            for m in range(1, len(arrays)):
                here = lax.dynamic_slice_in_dim(arrays[m], jnp.clip(k - m * per, 0, per - 1) * share, share, 0)
                found = jnp.where(k >= m * per, here, found)
            return found

        return piece

    def share_scalars(s):
        head = jnp.stack([rank.astype(jnp.int32), lengths[s], start + rank.astype(jnp.int32) * share, jnp.int32(tensor)])
        return jnp.concatenate([head, ids])

    gain2_grad = jnp.zeros((1, width), F32)
    gb, gh = [[[None] * chunks for _ in range(seqs)] for _ in range(2)]
    for s in range(seqs):
        for k in range(chunks):
            terms = sum_terms(gn[s][k], tensor)
            gb[s][k], gh[s][k], gain_part = second_back(hidden[s][k], gf, s, k, gain2, terms)
            gain2_grad = gain2_grad + gain_part
    for s in range(seqs):
        got = ring_scatter(piece_of(ffn[s]), tensor, rank)
        out, stat = output_share(share_scalars(s), got, ffn[s], hidden[s], order)
        out_shares.append(out)
        ffn_squares = ffn_squares + stat[0, 0]

    def flat(nested):
        return [item for inner_list in nested for item in inner_list]

    def reduced(lefts, rights, axis):
        oth = weight_grad(lefts, rights, 1, axis)
        own = weight_grad(lefts, rights, 0, axis, over_core(oth))
        return scatter_blocks(own, axis, dp)

    gf_chunks = [gf[s] for s in range(seqs)]
    inner_seq = flat(inner)
    gf_flat = [gf[s, k * rows : (k + 1) * rows] for s in range(seqs) for k in range(chunks)]
    grad_w_down = reduced(inner_seq, gf_flat, 1)
    grad_w_gate = reduced(flat(n2), flat(gg), 0)
    grad_w_up = reduced(flat(n2), flat(gu), 0)

    gain1_grad = jnp.zeros((1, width), F32)
    head_gain = jnp.zeros((2 * hd,), F32)
    dpres, in_shares = [], []
    for s in range(seqs):
        pre, everything, att, inv, seq_scal, att_rows = saved[s]
        da_own, da_oth = branch_back(gb[s], out_own, out_oth, core1)
        d_own, d_oth = attend_back(seq_scal, everything, att, inv, da_own, over_core(da_oth), groups)
        dpre, first, gain_part, hg = heads_back(
            d_own, over_core(d_oth), pre, cosine, sine, qgain, kgain, xr, s, qkv_own, qkv_oth, core1, hd, nq, nk
        )
        gain1_grad = gain1_grad + gain_part
        head_gain = head_gain + hg[:, 0]
        dpres.append(dpre)
        got = ring_scatter(piece_of([first]), tensor, rank)
        in_shares.append(input_share(share_scalars(s), got, first, gh[s], xr, s, gain1, order))

    att_rows = jnp.concatenate([jnp.swapaxes(saved[s][5], 0, 1) for s in range(seqs)], axis=0)
    att_list = [att_rows[i * rows : (i + 1) * rows] for i in range(seqs * chunks)]
    grad_w_output = reduced(att_list, flat(gb), 1)
    grad_qkv = reduced([n1[s] for s in range(seqs)], dpres, 0)
    nqc, nkc = nq * hd, nk * hd
    grad_w_query = grad_qkv[:, :nqc]
    grad_w_key = grad_qkv[:, nqc : nqc + nkc]
    grad_w_value = grad_qkv[:, nqc + nkc :]

    gain2_grad = gain2_grad / tensor
    counts = jnp.sum(jnp.clip(lengths - start, 0, span)).astype(F32) / tensor
    small = jnp.concatenate([head_gain, stats / tensor, ffn_squares.reshape(1), counts.reshape(1)])
    small = jnp.pad(small, (0, (-small.shape[0]) % 128)).reshape(1, -1)
    lines = jnp.concatenate([gain1_grad, gain2_grad], axis=0)
    if dp == 4 and tensor == 4:
        half = width // 2
        quarter = half // 4

        def join(part):
            return jnp.concatenate([part.reshape(1, -1), small], axis=1)

        got = over_core(join(lines[:, half:]))
        lines = lines[:, :half] + got[:, : 2 * half].reshape(2, half)
        small = small + got[:, 2 * half :]
        lines = lines.reshape(2, 4, quarter)
        got = over_x(join(lines[:, 1::2]))
        lines = lines[:, 0::2] + got[:, : 4 * quarter].reshape(2, 2, quarter)
        small = small + got[:, 4 * quarter :]
        got = over_y(join(lines[:, 1]))
        lines = lines[:, 0] + got[:, : 2 * quarter].reshape(2, quarter)
        small = small + got[:, 2 * quarter :]
        for step in (1, 2):
            got = lax.ppermute(join(lines), "tensor", [(i, i ^ step) for i in range(4)])
            lines = lines + got[:, : 2 * quarter].reshape(2, quarter)
            small = small + got[:, 2 * quarter :]
    else:
        piece = width // (2 * dp)
        lines = to_absolute(lines, dp, core) if dp != 4 else lines.reshape(2, 2 * dp, piece)[:, jnp.argsort(ids)].reshape(2, width)
        lines, small = lax.psum((lines, small), ("dp", "context", "tensor"))
        lines = lax.dynamic_slice_in_dim(lines, lax.axis_index(("dp", "context")) * piece, piece, 1)
    small = small[0]
    rms_values = jnp.sqrt(small[2 * hd : 2 * hd + 3] / (small[2 * hd + 3] * width))

    output = jnp.stack(out_shares)
    grad_inputs = jnp.stack(in_shares)
    if order == 1:
        output, grad_inputs = to_absolute(output, dp, core), to_absolute(grad_inputs, dp, core)
    return (
        output,
        grad_inputs,
        grad_w_query,
        grad_w_key,
        grad_w_value,
        grad_w_output,
        grad_w_gate,
        grad_w_up,
        grad_w_down,
        lines[0],
        lines[1],
        small[:hd],
        small[hd : 2 * hd],
        rms_values,
    )


def solution(mesh):
    both = ("dp", "context")
    rows = P(both, "tensor")
    cols = P("tensor", both)
    shares = P("dp", ("context", "tensor"), None)
    acts = P("dp", "context", None)
    return jax.shard_map(
        per_device,
        mesh=mesh,
        in_specs=(acts, acts, P("dp"), rows, rows, rows, cols, rows, rows, cols, P(both), P(both), P(), P()),
        out_specs=(shares, shares, rows, rows, rows, cols, rows, rows, cols, P(both), P(both), P(), P(), P()),
        check_vma=False,
    )
```

time: 2070 us -> 962 us (0.46)
  waiting for transfers between devices: 1540 us -> 342 us
  Pallas kernels: 0 us -> 309 us
  matrix products: 295 us -> 0 us
  starting transfers between devices: 1.2 us -> 138 us
  blocking collectives: 88.1 us -> 0 us
  local copies, waits for them, and re-layouts: 24.2 us -> 79.4 us
    psum x4 -> x0, waiting for transfers between devices: 909 us -> none  [the longest x1 291 us: per_device(): grad_normed2 = lax.psum(second_part, 'tensor')]
    reduce_scatter x9 -> x0, waiting for transfers between devices: 502 us -> none  [the longest x1 120 us: per_device(): lax.psum_scatter(grad_w_down, ('dp', 'context'), scatter_dimension=1, til...]
    ppermute x0 -> x104, waiting for transfers between devices: none -> 342 us  [the longest x8 133 us: sum_terms(): outward = lax.ppermute(rest, 'tensor', [(1, 0), (2, 3)])]
    pallas_call x0 -> x39, Pallas kernels: none -> 309 us  [the longest x4 85 us: feed(): pl.pallas_call(feed_kernel, grid=(hidden // hb,), in_specs=[whole, pl.Blo...]
    dot_general x35 -> x0, matrix products: 295 us -> none  [the longest x7 70.4 us: weight_grad(): jnp.einsum('srd,src->dc', left, right, preferred_element_type=jnp.float32)]
    ppermute x0 -> x104, starting transfers between devices: none -> 138 us  [the longest x12 36.8 us: ring_scatter(): moving = lax.ppermute(moving, 'tensor', ring)]
    all_gather x5 -> x0, waiting for transfers between devices: 124 us -> none  [the longest x1 43.3 us: per_device(): lax.all_gather(w_down, ('dp', 'context'), axis=1, tiled=True)]
    all_gather x6 -> x0, blocking collectives: 48.4 us -> none  [the longest x1 14.5 us: per_device(): lax.all_gather(key_projection_weight, ('dp', 'context'), axis=0, tiled=True)]
  transfers between devices with their start and end apart: 18 -> 104, of which waited for: 13 -> 37; matrix products, arithmetic and copies ran while one was open for 13% -> 15% of each run, Pallas kernels for 0% -> 30%
where the time goes in v1:
time: 962 us; the launch traced here: 956 us
  waiting for transfers between devices  342 us (36%)
  Pallas kernels  309 us (32%)
  starting transfers between devices  138 us (14%)
  other arithmetic  83.6 us (9%)
  local copies, waits for them, and re-layouts  79.4 us (8%)
    ppermute x8, waiting for transfers between devices, sum_terms(): outward = lax.ppermute(rest, 'tensor', [(1, 0), (2, 3)])  133 us
    ppermute x23, waiting for transfers between devices, over_x(): return lax.ppermute(value, 'dp', [(i, i ^ 1) for i in range(4)])  89.5 us
    pallas_call x4, Pallas kernels, feed(): pl.pallas_call(feed_kernel, grid=(hidden // hb,), in_specs=[whole, pl.Blo...  85 us
    pallas_call x10, Pallas kernels, weight_grad(): pl.pallas_call(functools.partial(weight_grad_kernel, count, add is not No...  72.8 us
    ppermute x8, waiting for transfers between devices, sum_terms(): inward = lax.ppermute(part, 'tensor', [(0, 1), (3, 2)])  63 us
    ppermute x12, starting transfers between devices, ring_scatter(): moving = lax.ppermute(moving, 'tensor', ring)  36.8 us
    unnamed x164, local copies, waits for them, and re-layouts  34.3 us
    ppermute x12, waiting for transfers between devices, ring_scatter(): moving = lax.ppermute(moving, 'tensor', ring)  29.3 us
  transfers between devices with their start and end apart: 104, of which 37 were waited for; matrix products, arithmetic and copies ran while one was open for 15% of the time, Pallas kernels for 30%

profile of v1, /device:TPU:0, one launch (start us, length us, event | category | flops | bytes accessed | tf_op | source)
XLA Modules:
  0.0 956.1 jit_solution(7754181040688765002)
XLA Ops:
  50.1 9.8 %first_norm.1 = (bf16[2,512,2048]{2,1,0:T(8,128)(2,1)}, bf16[2,512,2048]{2,1,0:T(8,128)(2,1)}, bf16[2,512,2048]{2,1,0:T(8,128)(2,1)}) custom-call(bf16[2,512,2048]{2,1,0:T(8,128)(2,1)} %x_ref.1, bf16[2,512,2048]{2,1,0:T(8,128)(2,1)} %cot_ref.1, f32[1,2048]{1,0:T(1,128)} %get-tuple-element.251.gain_ref, s32[11]{0:T(128)} %concatenate.115.scal_ref), custom_call_target="tpu_custom_call" | custom-call | flops 16777216 | bytes 20971520 | tf_op jit(solution)/shard_map/first_norm/pallas_call | solution.py:164
  64.0 8.5 collective-permute-done.14
  100.9 11.4 %collective-permute-done.22 = bf16[128,2048]{1,0:T(8,128)(2,1)} collective-permute-done((bf16[128,2048]{1,0:T(8,128)(2,1)}, bf16[128,2048]{1,0:T(8,128)(2,1)}, u32[]{:S(2)}, u32[]{:S(2)}) %collective-permute-start.22) | collective-permute-done | bytes 524320 | tf_op jit(solution)/shard_map/ppermute | solution.py:70
  148.3 19.4 %collective-permute-done.27 = bf16[128,2048]{1,0:T(8,128)(2,1)S(1)} collective-permute-done((bf16[128,2048]{1,0:T(8,128)(2,1)S(1)}, bf16[128,2048]{1,0:T(8,128)(2,1)S(1)}, u32[]{:S(2)}, u32[]{:S(2)}) %collective-permute-start.27) | collective-permute-done | bytes 524320 | tf_op jit(solution)/shard_map/ppermute | solution.py:70
  186.8 8.7 collective-permute-done.46.refs_1_
  196.7 21.4 %collective-permute-done.17.refs_1_ = bf16[256,2048]{1,0:T(8,128)(2,1)S(1)} collective-permute-done((bf16[256,2048]{1,0:T(8,128)(2,1)}, bf16[256,2048]{1,0:T(8,128)(2,1)S(1)}, u32[]{:S(2)}, u32[]{:S(2)}) %collective-permute-start.17) | collective-permute-done | bytes 1048608 | tf_op jit(solution)/shard_map/ppermute | solution.py:124
  219.9 16.4 %maximum_maximum_fusion.wdo = bf16[2048,1024]{1,0:T(8,128)(2,1)} fusion(bf16[1024,256]{1,0:T(8,128)(2,1)S(1)} %collective-permute-done.33, bf16[1024,256]{1,0:T(8,128)(2,1)S(1)} %collective-permute-done.32, bf16[2048,256]{1,0:T(8,128)(2,1)} %collective-permute-done.31, bf16[2048,256]{1,0:T(8,128)(2,1)} %collective-permute-done.30, bf16[2048,256]{1,0:T(8,128)(2,1)} %param.23), kind=kLoop, calls=%fused_computation | loop fusion | flops 20971520 | bytes 8388608 | tf_op jit(solution)/shard_map/concatenate | solution.py:92
  247.0 47.1 %collective-permute-done.45.refs_3_ = bf16[256,2048]{1,0:T(8,128)(2,1)S(1)} collective-permute-done((bf16[256,2048]{1,0:T(8,128)(2,1)S(1)}, bf16[256,2048]{1,0:T(8,128)(2,1)S(1)}, u32[]{:S(2)}, u32[]{:S(2)}) %collective-permute-start.45) | collective-permute-done | bytes 1048608 | tf_op jit(solution)/shard_map/ppermute | solution.py:128
  295.4 22.2 %collective-permute-done.48.refs_3_ = bf16[256,2048]{1,0:T(8,128)(2,1)S(1)} collective-permute-done((bf16[256,2048]{1,0:T(8,128)(2,1)S(1)}, bf16[256,2048]{1,0:T(8,128)(2,1)S(1)}, u32[]{:S(2)}, u32[]{:S(2)}) %collective-permute-start.48) | collective-permute-done | bytes 1048608 | tf_op jit(solution)/shard_map/ppermute | solution.py:128
  346.8 14.8 %collective-permute-done.37.refs_3_ = bf16[256,2048]{1,0:T(8,128)(2,1)S(1)} collective-permute-done((bf16[256,2048]{1,0:T(8,128)(2,1)}, bf16[256,2048]{1,0:T(8,128)(2,1)S(1)}, u32[]{:S(2)}, u32[]{:S(2)}) %collective-permute-start.37) | collective-permute-done | bytes 1048608 | tf_op jit(solution)/shard_map/ppermute | solution.py:128
  369.0 21.4 %feed_forward.5 = (bf16[256,2048]{1,0:T(8,128)(2,1)}, bf16[256,2048]{1,0:T(8,128)(2,1)}, bf16[256,2048]{1,0:T(8,128)(2,1)}, bf16[256,2048]{1,0:T(8,128)(2,1)}, bf16[256,2048]{1,0:T(8,128)(2,1)}) custom-call(bf16[256,2048]{1,0:T(8,128)(2,1)} %get-tuple-element.122.n_ref.refs_0_, bf16[2,512,2048]{2,1,0:T(8,128)(2,1)} %get-tuple-element.116.g_ref.gf_ref, ...), custom_call_target="tpu_custom_call" | custom-call | flops 12884901888 | bytes 32505856 | tf_op jit(solution)/shard_map/feed_forward/pallas_call | solution.py:390
  393.1 21.3 %feed_forward.4 = (bf16[256,2048]{1,0:T(8,128)(2,1)}, bf16[256,2048]{1,0:T(8,128)(2,1)}, bf16[256,2048]{1,0:T(8,128)(2,1)}, bf16[256,2048]{1,0:T(8,128)(2,1)}, bf16[256,2048]{1,0:T(8,128)(2,1)}) custom-call(bf16[256,2048]{1,0:T(8,128)(2,1)} %get-tuple-element.115.n_ref.refs_1_, bf16[2,512,2048]{2,1,0:T(8,128)(2,1)} %get-tuple-element.116.g_ref.gf_ref, ...), custom_call_target="tpu_custom_call" | custom-call | flops 12884901888 | bytes 32505856 | tf_op jit(solution)/shard_map/feed_forward/pallas_call | solution.py:390
  417.9 21.1 %feed_forward.7 = (bf16[256,2048]{1,0:T(8,128)(2,1)}, bf16[256,2048]{1,0:T(8,128)(2,1)}, bf16[256,2048]{1,0:T(8,128)(2,1)}, bf16[256,2048]{1,0:T(8,128)(2,1)}, bf16[256,2048]{1,0:T(8,128)(2,1)}) custom-call(bf16[256,2048]{1,0:T(8,128)(2,1)} %get-tuple-element.135.n_ref.refs_2_, bf16[2,512,2048]{2,1,0:T(8,128)(2,1)} %get-tuple-element.116.g_ref.gf_ref, ...), custom_call_target="tpu_custom_call" | custom-call | flops 12884901888 | bytes 32505856 | tf_op jit(solution)/shard_map/feed_forward/pallas_call | solution.py:390
  439.1 21.2 %feed_forward.6 = (bf16[256,2048]{1,0:T(8,128)(2,1)}, bf16[256,2048]{1,0:T(8,128)(2,1)}, bf16[256,2048]{1,0:T(8,128)(2,1)}, bf16[256,2048]{1,0:T(8,128)(2,1)}, bf16[256,2048]{1,0:T(8,128)(2,1)}) custom-call(bf16[256,2048]{1,0:T(8,128)(2,1)} %get-tuple-element.132.n_ref.refs_3_, bf16[2,512,2048]{2,1,0:T(8,128)(2,1)} %get-tuple-element.116.g_ref.gf_ref, ...), custom_call_target="tpu_custom_call" | custom-call | flops 12884901888 | bytes 32505856 | tf_op jit(solution)/shard_map/feed_forward/pallas_call | solution.py:390
  467.5 8.8 weight_grad.14
  486.7 10.7 %collective-permute-done.63.refs_1_ = bf16[256,2048]{1,0:T(8,128)(2,1)} collective-permute-done((bf16[256,2048]{1,0:T(8,128)(2,1)S(1)}, bf16[256,2048]{1,0:T(8,128)(2,1)}, u32[]{:S(2)}, u32[]{:S(2)}) %collective-permute-start.63) | collective-permute-done | bytes 1048608 | tf_op jit(solution)/shard_map/ppermute | solution.py:124
  499.7 20.1 %collective-permute-done.66.refs_1_ = bf16[256,2048]{1,0:T(8,128)(2,1)S(1)} collective-permute-done((bf16[256,2048]{1,0:T(8,128)(2,1)S(1)}, bf16[256,2048]{1,0:T(8,128)(2,1)S(1)}, u32[]{:S(2)}, u32[]{:S(2)}) %collective-permute-start.66) | collective-permute-done | bytes 1048608 | tf_op jit(solution)/shard_map/ppermute | solution.py:124
  520.9 15.2 %collective-permute-done.39 = bf16[128,2048]{1,0:T(8,128)(2,1)S(1)} collective-permute-done((bf16[128,2048]{1,0:T(8,128)(2,1)S(1)}, bf16[128,2048]{1,0:T(8,128)(2,1)S(1)}, u32[]{:S(2)}, u32[]{:S(2)}) %collective-permute-start.39) | collective-permute-done | bytes 524320 | tf_op jit(solution)/shard_map/ppermute | solution.py:136
  548.9 48.2 %collective-permute-done.54.refs_3_ = bf16[256,2048]{1,0:T(8,128)(2,1)S(1)} collective-permute-done((bf16[256,2048]{1,0:T(8,128)(2,1)S(1)}, bf16[256,2048]{1,0:T(8,128)(2,1)S(1)}, u32[]{:S(2)}, u32[]{:S(2)}) %collective-permute-start.54) | collective-permute-done | bytes 1048608 | tf_op jit(solution)/shard_map/ppermute | solution.py:128
  598.0 32.2 %collective-permute-start.51 = (bf16[128,2048]{1,0:T(8,128)(2,1)S(1)}, bf16[128,2048]{1,0:T(8,128)(2,1)S(1)}, u32[]{:S(2)}, u32[]{:S(2)}) collective-permute-start(bf16[128,2048]{1,0:T(8,128)(2,1)S(1)} %add_convert_fusion.10), channel_id=1, source_target_pairs={{0,1},{1,2},{2,3},{3,0},{4,5},{5,6},{6,7},{7,4},{8,9},{9,10},{10,1... | collective-permute-start | bytes 1572872 | tf_op jit(solution)/shard_map/ppermute | solution.py:136
  630.3 8.7 weight_grad.16
  656.3 8.6 weight_grad.18
  697.9 10.2 %attend_backward.2 = (bf16[384,512]{1,0:T(8,128)(2,1)}, bf16[384,512]{1,0:T(8,128)(2,1)}) custom-call(s32[2]{0:T(128)} %pad_add_fusion.3.scal_ref, bf16[384,1024]{1,0:T(8,128)(2,1)} %get-tuple-element.140.all_ref, bf16[256,1024]{1,0:T(8,128)(2,1)} %get-tuple-element.141.att_ref, f32[4,1024]{1,0:T(4,128)} %get-tuple-element.142.inv_ref, ...), custom_call_target="tpu_custom_call" | custom-call | flops 8053063680 | bytes 4718592 | tf_op jit(solution)/shard_map/attend_backward/pallas_call | solution.py:515
  709.4 9.9 %attend_backward.3 = (bf16[384,512]{1,0:T(8,128)(2,1)}, bf16[384,512]{1,0:T(8,128)(2,1)}) custom-call(s32[2]{0:T(128)} %pad_add_fusion.2.scal_ref, bf16[384,1024]{1,0:T(8,128)(2,1)} %get-tuple-element.155.all_ref, bf16[256,1024]{1,0:T(8,128)(2,1)} %get-tuple-element.156.att_ref, f32[4,1024]{1,0:T(4,128)} %get-tuple-element.157.inv_ref, ...), custom_call_target="tpu_custom_call" | custom-call | flops 8053063680 | bytes 4718592 | tf_op jit(solution)/shard_map/attend_backward/pallas_call | solution.py:515
  728.3 7.7 query_key_value_back.3
  777.1 9.4 weight_grad.17
  787.7 9.4 weight_grad.15
  802.0 9.3 weight_grad.19
  820.8 12.4 %collective-permute-done.83 = bf16[512,256]{1,0:T(8,128)(2,1)S(1)} collective-permute-done((bf16[512,256]{1,0:T(8,128)(2,1)S(1)}, bf16[512,256]{1,0:T(8,128)(2,1)S(1)}, u32[]{:S(2)}, u32[]{:S(2)}) %collective-permute-start.83) | collective-permute-done | bytes 262176 | tf_op jit(solution)/shard_map/ppermute | solution.py:74
  865.7 8.0 collective-permute-done.72
  916.0 12.1 %collective-permute-done.91 = bf16[256,2048]{1,0:T(8,128)(2,1)S(1)} collective-permute-done((bf16[256,2048]{1,0:T(8,128)(2,1)S(1)}, bf16[256,2048]{1,0:T(8,128)(2,1)S(1)}, u32[]{:S(2)}, u32[]{:S(2)}) %collective-permute-start.91) | collective-permute-done | bytes 1048608 | tf_op jit(solution)/shard_map/ppermute | solution.py:70
  933.4 16.6 %collective-permute-done.86 = bf16[256,2048]{1,0:T(8,128)(2,1)S(1)} collective-permute-done((bf16[256,2048]{1,0:T(8,128)(2,1)S(1)}, bf16[256,2048]{1,0:T(8,128)(2,1)S(1)}, u32[]{:S(2)}, u32[]{:S(2)}) %collective-permute-start.86) | collective-permute-done | bytes 1048608 | tf_op jit(solution)/shard_map/ppermute | solution.py:70
  (523 shorter events, 428.8 us)
Async XLA Ops:
  74.9 58.5 %collective-permute-start.16 = (bf16[512,1024]{1,0:T(8,128)(2,1)}, bf16[512,1024]{1,0:T(8,128)(2,1)}, u32[]{:S(2)}, u32[]{:S(2)}) collective-permute-start(bf16[512,1024]{1,0:T(8,128)(2,1)} %maximum_maximum_fusion.1.wo_ref.refs_2_), channel_id=1, source_target_pairs={{0,4},{4,0},{1,5},{5,1},{2,6},{6,2},{3,7},{7,3},{8,12},{12,8},{9,1... | collective-permute-start | bytes 3145736 | tf_op jit(solution)/shard_map/ppermute | solution.py:78
  74.9 56.4 %collective-permute-start.26 = (bf16[256,2048]{1,0:T(8,128)(2,1)}, bf16[256,2048]{1,0:T(8,128)(2,1)}, u32[]{:S(2)}, u32[]{:S(2)}) collective-permute-start(bf16[256,2048]{1,0:T(8,128)(2,1)} %param.22), channel_id=1, source_target_pairs={{0,16},{8,24},{16,0},{24,8},{1,17},{9,25},{17,1},{25,9},{2,18},{10... | collective-permute-start | bytes 3145736 | tf_op jit(solution)/shard_map/ppermute | solution.py:74
  75.4 53.2 %collective-permute-start.25 = (bf16[256,2048]{1,0:T(8,128)(2,1)}, bf16[256,2048]{1,0:T(8,128)(2,1)}, u32[]{:S(2)}, u32[]{:S(2)}) collective-permute-start(bf16[256,2048]{1,0:T(8,128)(2,1)} %param.22), channel_id=1, source_target_pairs={{0,8},{8,0},{16,24},{24,16},{1,9},{9,1},{17,25},{25,17},{2,10},{10... | collective-permute-start | bytes 3145736 | tf_op jit(solution)/shard_map/ppermute | solution.py:70
  128.7 52.6 %collective-permute-start.31 = (bf16[2048,256]{1,0:T(8,128)(2,1)}, bf16[2048,256]{1,0:T(8,128)(2,1)}, u32[]{:S(2)}, u32[]{:S(2)}) collective-permute-start(bf16[2048,256]{1,0:T(8,128)(2,1)} %param.23), channel_id=1, source_target_pairs={{0,16},{8,24},{16,0},{24,8},{1,17},{9,25},{17,1},{25,9},{2,18},{10... | collective-permute-start | bytes 3145736 | tf_op jit(solution)/shard_map/ppermute | solution.py:74
  131.3 52.4 %collective-permute-start.30 = (bf16[2048,256]{1,0:T(8,128)(2,1)}, bf16[2048,256]{1,0:T(8,128)(2,1)}, u32[]{:S(2)}, u32[]{:S(2)}) collective-permute-start(bf16[2048,256]{1,0:T(8,128)(2,1)} %param.23), channel_id=1, source_target_pairs={{0,8},{8,0},{16,24},{24,16},{1,9},{9,1},{17,25},{25,17},{2,10},{10... | collective-permute-start | bytes 3145736 | tf_op jit(solution)/shard_map/ppermute | solution.py:70
  139.4 46.4 %collective-permute-start.43 = (bf16[256,2048]{1,0:T(8,128)(2,1)}, bf16[256,2048]{1,0:T(8,128)(2,1)S(1)}, u32[]{:S(2)}, u32[]{:S(2)}) collective-permute-start(bf16[256,2048]{1,0:T(8,128)(2,1)} %get-tuple-element.131.refs_0_), channel_id=1, source_target_pairs={{0,1},{3,2},{4,5},{7,6},{8,9},{11,10},{12,13},{15,14},{16,17},{19,... | collective-permute-start | bytes 3145736 | tf_op jit(solution)/shard_map/ppermute | solution.py:124
  181.3 57.1 %collective-permute-start.35 = (bf16[256,2048]{1,0:T(8,128)(2,1)S(1)}, bf16[256,2048]{1,0:T(8,128)(2,1)S(1)}, u32[]{:S(2)}, u32[]{:S(2)}) collective-permute-start(bf16[256,2048]{1,0:T(8,128)(2,1)S(1)} %copy-done.8), channel_id=1, source_target_pairs={{0,1},{3,2},{4,5},{7,6},{8,9},{11,10},{12,13},{15,14},{16,17},{19,... | collective-permute-start | bytes 3145736 | tf_op jit(solution)/shard_map/ppermute | solution.py:124
  219.3 149.7 %collective-permute-start.24 = (bf16[1024,2048]{1,0:T(8,128)(2,1)}, bf16[1024,2048]{1,0:T(8,128)(2,1)}, u32[]{:S(2)}, u32[]{:S(2)}) collective-permute-start(bf16[1024,2048]{1,0:T(8,128)(2,1)} %constant_dynamic-update-slice_fusion.15.wgo), channel_id=1, source_target_pairs={{0,4},{4,0},{1,5},{5,1},{2,6},{6,2},{3,7},{7,3},{8,12},{12,8},{9,1... | collective-permute-start | bytes 12582920 | tf_op jit(solution)/shard_map/ppermute | solution.py:78
  219.4 149.6 %collective-permute-start.29 = (bf16[1024,2048]{1,0:T(8,128)(2,1)}, bf16[1024,2048]{1,0:T(8,128)(2,1)}, u32[]{:S(2)}, u32[]{:S(2)}) collective-permute-start(bf16[1024,2048]{1,0:T(8,128)(2,1)} %constant_dynamic-update-slice_fusion.20.wuo), channel_id=1, source_target_pairs={{0,4},{4,0},{1,5},{5,1},{2,6},{6,2},{3,7},{7,3},{8,12},{12,8},{9,1... | collective-permute-start | bytes 12582920 | tf_op jit(solution)/shard_map/ppermute | solution.py:78
  238.4 130.7 %collective-permute-start.34 = (bf16[2048,1024]{1,0:T(8,128)(2,1)}, bf16[2048,1024]{1,0:T(8,128)(2,1)}, u32[]{:S(2)}, u32[]{:S(2)}) collective-permute-start(bf16[2048,1024]{1,0:T(8,128)(2,1)} %maximum_maximum_fusion.wdo), channel_id=1, source_target_pairs={{0,4},{4,0},{1,5},{5,1},{2,6},{6,2},{3,7},{7,3},{8,12},{12,8},{9,1... | collective-permute-start | bytes 12582920 | tf_op jit(solution)/shard_map/ppermute | solution.py:78
  241.7 52.5 %collective-permute-start.45 = (bf16[256,2048]{1,0:T(8,128)(2,1)S(1)}, bf16[256,2048]{1,0:T(8,128)(2,1)S(1)}, u32[]{:S(2)}, u32[]{:S(2)}) collective-permute-start(bf16[256,2048]{1,0:T(8,128)(2,1)S(1)} %fusion.5), channel_id=1, source_target_pairs={{1,0},{2,3},{5,4},{6,7},{9,8},{10,11},{13,12},{14,15},{17,16},{18,... | collective-permute-start | bytes 3145736 | tf_op jit(solution)/shard_map/ppermute | solution.py:128
  243.0 74.7 %collective-permute-start.48 = (bf16[256,2048]{1,0:T(8,128)(2,1)S(1)}, bf16[256,2048]{1,0:T(8,128)(2,1)S(1)}, u32[]{:S(2)}, u32[]{:S(2)}) collective-permute-start(bf16[256,2048]{1,0:T(8,128)(2,1)S(1)} %fusion.7), channel_id=1, source_target_pairs={{1,0},{2,3},{5,4},{6,7},{9,8},{10,11},{13,12},{14,15},{17,16},{18,... | collective-permute-start | bytes 3145736 | tf_op jit(solution)/shard_map/ppermute | solution.py:128
  390.4 90.8 %collective-permute-start.52 = (bf16[256,2048]{1,0:T(8,128)(2,1)}, bf16[256,2048]{1,0:T(8,128)(2,1)}, u32[]{:S(2)}, u32[]{:S(2)}) collective-permute-start(bf16[256,2048]{1,0:T(8,128)(2,1)} %get-tuple-element.143.refs_0_), channel_id=1, source_target_pairs={{0,1},{3,2},{4,5},{7,6},{8,9},{11,10},{12,13},{15,14},{16,17},{19,... | collective-permute-start | bytes 3145736 | tf_op jit(solution)/shard_map/ppermute | solution.py:124
  415.6 60.7 %collective-permute-start.38 = (bf16[128,2048]{1,0:T(8,128)(2,1)S(1)}, bf16[128,2048]{1,0:T(8,128)(2,1)}, u32[]{:S(2)}, u32[]{:S(2)}) collective-permute-start(bf16[128,2048]{1,0:T(8,128)(2,1)S(1)} %dynamic-slice_select_fusion.1), channel_id=1, source_target_pairs={{0,1},{1,2},{2,3},{3,0},{4,5},{5,6},{6,7},{7,4},{8,9},{9,10},{10,1... | collective-permute-start | bytes 1572872 | tf_op jit(solution)/shard_map/ppermute | solution.py:136
  415.6 68.7 %collective-permute-start.55 = (bf16[256,2048]{1,0:T(8,128)(2,1)}, bf16[256,2048]{1,0:T(8,128)(2,1)}, u32[]{:S(2)}, u32[]{:S(2)}) collective-permute-start(bf16[256,2048]{1,0:T(8,128)(2,1)} %get-tuple-element.145.refs_0_), channel_id=1, source_target_pairs={{0,1},{3,2},{4,5},{7,6},{8,9},{11,10},{12,13},{15,14},{16,17},{19,... | collective-permute-start | bytes 3145736 | tf_op jit(solution)/shard_map/ppermute | solution.py:124
  479.9 56.2 %collective-permute-start.39 = (bf16[128,2048]{1,0:T(8,128)(2,1)S(1)}, bf16[128,2048]{1,0:T(8,128)(2,1)S(1)}, u32[]{:S(2)}, u32[]{:S(2)}) collective-permute-start(bf16[128,2048]{1,0:T(8,128)(2,1)S(1)} %add_convert_fusion.13), channel_id=1, source_target_pairs={{0,1},{1,2},{2,3},{3,0},{4,5},{5,6},{6,7},{7,4},{8,9},{9,10},{10,1... | collective-permute-start | bytes 1572872 | tf_op jit(solution)/shard_map/ppermute | solution.py:136
  481.3 66.1 %collective-permute-start.50 = (bf16[128,2048]{1,0:T(8,128)(2,1)S(1)}, bf16[128,2048]{1,0:T(8,128)(2,1)S(1)}, u32[]{:S(2)}, u32[]{:S(2)}) collective-permute-start(bf16[128,2048]{1,0:T(8,128)(2,1)S(1)} %add_convert_fusion.11), channel_id=1, source_target_pairs={{0,1},{1,2},{2,3},{3,0},{4,5},{5,6},{6,7},{7,4},{8,9},{9,10},{10,1... | collective-permute-start | bytes 1572872 | tf_op jit(solution)/shard_map/ppermute | solution.py:136
  484.3 52.8 %collective-permute-start.53 = (bf16[256,2048]{1,0:T(8,128)(2,1)S(1)}, bf16[256,2048]{1,0:T(8,128)(2,1)S(1)}, u32[]{:S(2)}, u32[]{:S(2)}) collective-permute-start(bf16[256,2048]{1,0:T(8,128)(2,1)S(1)} %fusion.8), channel_id=1, source_target_pairs={{1,2},{2,1},{5,6},{6,5},{9,10},{10,9},{13,14},{14,13},{17,18},{18,... | collective-permute-start | bytes 3145736 | tf_op jit(solution)/shard_map/ppermute | solution.py:126
  537.1 127.8 %collective-permute-start.40 = (bf16[128,2048]{1,0:T(8,128)(2,1)S(1)}, bf16[128,2048]{1,0:T(8,128)(2,1)}, u32[]{:S(2)}, u32[]{:S(2)}) collective-permute-start(bf16[128,2048]{1,0:T(8,128)(2,1)S(1)} %add_convert_fusion.12), channel_id=1, source_target_pairs={{0,1},{1,2},{2,3},{3,0},{4,5},{5,6},{6,7},{7,4},{8,9},{9,10},{10,1... | collective-permute-start | bytes 1572872 | tf_op jit(solution)/shard_map/ppermute | solution.py:136
  537.6 59.5 %collective-permute-start.54 = (bf16[256,2048]{1,0:T(8,128)(2,1)S(1)}, bf16[256,2048]{1,0:T(8,128)(2,1)S(1)}, u32[]{:S(2)}, u32[]{:S(2)}) collective-permute-start(bf16[256,2048]{1,0:T(8,128)(2,1)S(1)} %fusion.9), channel_id=1, source_target_pairs={{1,0},{2,3},{5,4},{6,7},{9,8},{10,11},{13,12},{14,15},{17,16},{18,... | collective-permute-start | bytes 3145736 | tf_op jit(solution)/shard_map/ppermute | solution.py:128
  540.3 105.2 %collective-permute-start.57 = (bf16[256,2048]{1,0:T(8,128)(2,1)}, bf16[256,2048]{1,0:T(8,128)(2,1)}, u32[]{:S(2)}, u32[]{:S(2)}) collective-permute-start(bf16[256,2048]{1,0:T(8,128)(2,1)} %fusion.11), channel_id=1, source_target_pairs={{1,0},{2,3},{5,4},{6,7},{9,8},{10,11},{13,12},{14,15},{17,16},{18,... | collective-permute-start | bytes 3145736 | tf_op jit(solution)/shard_map/ppermute | solution.py:128
  542.9 135.1 %collective-permute-start.65 = (bf16[256,2048]{1,0:T(8,128)(2,1)}, bf16[256,2048]{1,0:T(8,128)(2,1)S(1)}, u32[]{:S(2)}, u32[]{:S(2)}) collective-permute-start(bf16[256,2048]{1,0:T(8,128)(2,1)} %fusion.13), channel_id=1, source_target_pairs={{1,0},{2,3},{5,4},{6,7},{9,8},{10,11},{13,12},{14,15},{17,16},{18,... | collective-permute-start | bytes 3145736 | tf_op jit(solution)/shard_map/ppermute | solution.py:128
  547.3 138.1 %collective-permute-start.68 = (bf16[256,2048]{1,0:T(8,128)(2,1)}, bf16[256,2048]{1,0:T(8,128)(2,1)S(1)}, u32[]{:S(2)}, u32[]{:S(2)}) collective-permute-start(bf16[256,2048]{1,0:T(8,128)(2,1)} %fusion.15), channel_id=1, source_target_pairs={{1,0},{2,3},{5,4},{6,7},{9,8},{10,11},{13,12},{14,15},{17,16},{18,... | collective-permute-start | bytes 3145736 | tf_op jit(solution)/shard_map/ppermute | solution.py:128
  598.0 72.6 %collective-permute-start.51 = (bf16[128,2048]{1,0:T(8,128)(2,1)S(1)}, bf16[128,2048]{1,0:T(8,128)(2,1)S(1)}, u32[]{:S(2)}, u32[]{:S(2)}) collective-permute-start(bf16[128,2048]{1,0:T(8,128)(2,1)S(1)} %add_convert_fusion.10), channel_id=1, source_target_pairs={{0,1},{1,2},{2,3},{3,0},{4,5},{5,6},{6,7},{7,4},{8,9},{9,10},{10,1... | collective-permute-start | bytes 1572872 | tf_op jit(solution)/shard_map/ppermute | solution.py:136
  664.9 136.6 %collective-permute-start.94 = (bf16[2048,1024]{1,0:T(8,128)(2,1)}, bf16[2048,1024]{1,0:T(8,128)(2,1)}, u32[]{:S(2)}, u32[]{:S(2)}) collective-permute-start(bf16[2048,1024]{1,0:T(8,128)(2,1)} %weight_grad.18), channel_id=1, source_target_pairs={{0,4},{4,0},{1,5},{5,1},{2,6},{6,2},{3,7},{7,3},{8,12},{12,8},{9,1... | collective-permute-start | bytes 12582920 | tf_op jit(solution)/shard_map/ppermute | solution.py:78
  670.7 106.4 %collective-permute-start.89 = (bf16[1024,2048]{1,0:T(8,128)(2,1)}, bf16[1024,2048]{1,0:T(8,128)(2,1)}, u32[]{:S(2)}, u32[]{:S(2)}) collective-permute-start(bf16[1024,2048]{1,0:T(8,128)(2,1)} %weight_grad.16), channel_id=1, source_target_pairs={{0,4},{4,0},{1,5},{5,1},{2,6},{6,2},{3,7},{7,3},{8,12},{12,8},{9,1... | collective-permute-start | bytes 12582920 | tf_op jit(solution)/shard_map/ppermute | solution.py:78
  678.0 108.6 %collective-permute-start.84 = (bf16[1024,2048]{1,0:T(8,128)(2,1)}, bf16[1024,2048]{1,0:T(8,128)(2,1)}, u32[]{:S(2)}, u32[]{:S(2)}) collective-permute-start(bf16[1024,2048]{1,0:T(8,128)(2,1)} %weight_grad.14), channel_id=1, source_target_pairs={{0,4},{4,0},{1,5},{5,1},{2,6},{6,2},{3,7},{7,3},{8,12},{12,8},{9,1... | collective-permute-start | bytes 12582920 | tf_op jit(solution)/shard_map/ppermute | solution.py:78
  764.8 51.9 %collective-permute-start.60 = (bf16[128,2048]{1,0:T(8,128)(2,1)}, bf16[128,2048]{1,0:T(8,128)(2,1)}, u32[]{:S(2)}, u32[]{:S(2)}) collective-permute-start(bf16[128,2048]{1,0:T(8,128)(2,1)} %constant_dynamic-slice_fusion.1), channel_id=1, source_target_pairs={{0,1},{1,2},{2,3},{3,0},{4,5},{5,6},{6,7},{7,4},{8,9},{9,10},{10,1... | collective-permute-start | bytes 1572872 | tf_op jit(solution)/shard_map/ppermute | solution.py:136
  769.8 48.7 %collective-permute-start.71 = (bf16[128,2048]{1,0:T(8,128)(2,1)}, bf16[128,2048]{1,0:T(8,128)(2,1)}, u32[]{:S(2)}, u32[]{:S(2)}) collective-permute-start(bf16[128,2048]{1,0:T(8,128)(2,1)} %constant_dynamic-slice_fusion), channel_id=1, source_target_pairs={{0,1},{1,2},{2,3},{3,0},{4,5},{5,6},{6,7},{7,4},{8,9},{9,10},{10,1... | collective-permute-start | bytes 1572872 | tf_op jit(solution)/shard_map/ppermute | solution.py:136
  777.1 96.9 %collective-permute-start.74 = (bf16[1024,768]{1,0:T(8,128)(2,1)}, bf16[1024,768]{1,0:T(8,128)(2,1)}, u32[]{:S(2)}, u32[]{:S(2)}) collective-permute-start(bf16[1024,768]{1,0:T(8,128)(2,1)} %weight_grad.10), channel_id=1, source_target_pairs={{0,4},{4,0},{1,5},{5,1},{2,6},{6,2},{3,7},{7,3},{8,12},{12,8},{9,1... | collective-permute-start | bytes 4718600 | tf_op jit(solution)/shard_map/ppermute | solution.py:78
  857.0 52.9 %collective-permute-start.98 = (bf16[2048,256]{1,0:T(8,128)(2,1)}, bf16[2048,256]{1,0:T(8,128)(2,1)}, u32[]{:S(2)}, u32[]{:S(2)}) collective-permute-start(bf16[2048,256]{1,0:T(8,128)(2,1)} %pad_maximum_fusion.7), channel_id=1, source_target_pairs={{0,16},{8,24},{16,0},{24,8},{1,17},{9,25},{17,1},{25,9},{2,18},{10... | collective-permute-start | bytes 3145736 | tf_op jit(solution)/shard_map/ppermute | solution.py:74
  858.6 52.5 %collective-permute-start.96 = (bf16[2048,256]{1,0:T(8,128)(2,1)}, bf16[2048,256]{1,0:T(8,128)(2,1)}, u32[]{:S(2)}, u32[]{:S(2)}) collective-permute-start(bf16[2048,256]{1,0:T(8,128)(2,1)} %pad_maximum_fusion.6), channel_id=1, source_target_pairs={{0,8},{8,0},{16,24},{24,16},{1,9},{9,1},{17,25},{25,17},{2,10},{10... | collective-permute-start | bytes 3145736 | tf_op jit(solution)/shard_map/ppermute | solution.py:70
  (146 other events, 2296.0 us)

commit v2 on v1

--- a/solution.py
+++ b/solution.py
@@ -94,7 +94,7 @@
     else:
         own = lax.all_gather(weight, "dp", axis=axis, tiled=True)
         mark = own
-    return own, over_core(own), mark
+    return jnp.stack([own, over_core(own)]), mark
 
 
 def scatter_blocks(total, axis, dp):
@@ -173,10 +173,10 @@
     )(x, cot, gain, scalars)
 
 
-def heads_kernel(hd, nq, nk, n1_ref, wo_ref, wx_ref, cos_ref, sin_ref, qg_ref, kg_ref, core_ref, pre_ref, own_ref, oth_ref):
-    half = wo_ref.shape[0]
+def heads_kernel(hd, nq, nk, n1_ref, w_ref, cos_ref, sin_ref, qg_ref, kg_ref, core_ref, pre_ref, own_ref, oth_ref):
+    half = w_ref.shape[1]
     x = n1_ref[0]
-    flat = dot_nn(x[:, :half], wo_ref[...]) + dot_nn(x[:, half:], wx_ref[...])
+    flat = dot_nn(x[:, :half], w_ref[0]) + dot_nn(x[:, half:], w_ref[1])
     turned = flat.T
     span = turned.shape[1]
     normed = turned[: (nq + nk) * hd]
@@ -204,7 +204,7 @@
     oth_ref[...] = jnp.where(first, high, low).astype(BF16)
 
 
-def heads(n1, seq, w_own, w_oth, cosine, sine, qgain, kgain, core, hd, nq, nk):
+def heads(n1, seq, weight, cosine, sine, qgain, kgain, core, hd, nq, nk):
     span, width = n1.shape[1:]
     sides = (nq + 2 * nk) * hd // 2
     full = pl.BlockSpec(memory_space=pltpu.VMEM)
@@ -214,14 +214,14 @@
         functools.partial(heads_kernel, hd, nq, nk),
         grid=(1,),
         in_specs=[pl.BlockSpec((1, span, width), lambda i: (seq, 0, 0))]
-        + [whole(a) for a in (w_own, w_oth, cosine, sine, qgain, kgain)]
+        + [whole(a) for a in (weight, cosine, sine, qgain, kgain)]
         + [SMEM],
         out_specs=[whole(o) for o in outs],
         out_shape=outs,
         compiler_params=PARAMS,
-        cost_estimate=cost(2 * span * width * w_own.shape[1], 2 * span * width + 4 * w_own.size),
+        cost_estimate=cost(2 * span * width * weight.shape[2], 2 * span * width + 2 * weight.size),
         name="query_key_value",
-    )(n1, w_own, w_oth, cosine, sine, qgain, kgain, core)
+    )(n1, weight, cosine, sine, qgain, kgain, core)
 
 
 def join_positions(core, own, oth):
@@ -286,31 +286,31 @@
     )(scalars, own, got)
 
 
-def branch_kernel(own_ref, got_ref, wo_ref, wx_ref, core_ref, att_ref, *outs):
-    half = wo_ref.shape[1]
+def branch_kernel(own_ref, got_ref, w_ref, core_ref, att_ref, *outs):
+    half = w_ref.shape[2]
     low, high = join_positions(core_ref[0], own_ref[...], got_ref[...])
     att = jnp.concatenate([low, high], axis=0)
     att_ref[...] = att
     rows = outs[0].shape[0]
     for k, out in enumerate(outs):
         part = att[:, k * rows : (k + 1) * rows]
-        out[:, :half] = dot_tn(part, wo_ref[...]).astype(BF16)
-        out[:, half:] = dot_tn(part, wx_ref[...]).astype(BF16)
-
-
-def branch(own, got, w_own, w_oth, core, chunks):
+        out[:, :half] = dot_tn(part, w_ref[0]).astype(BF16)
+        out[:, half:] = dot_tn(part, w_ref[1]).astype(BF16)
+
+
+def branch(own, got, weight, core, chunks):
     rows, span = own.shape
-    width = 2 * w_own.shape[1]
+    width = 2 * weight.shape[2]
     full = pl.BlockSpec(memory_space=pltpu.VMEM)
     return pl.pallas_call(
         branch_kernel,
-        in_specs=[full] * 4 + [SMEM],
+        in_specs=[full] * 3 + [SMEM],
         out_specs=[full] * (1 + chunks),
         out_shape=[shape((2 * rows, span), BF16)] + [shape((span // chunks, width), BF16)] * chunks,
         compiler_params=PARAMS,
         cost_estimate=cost(4 * rows * span * width, 4 * rows * width + 2 * span * width),
         name="attention_branch",
-    )(own, got, w_own, w_oth, core)
+    )(own, got, weight, core)
 
 
 def second_norm_kernel(terms, scal_ref, x_ref, gain_ref, *refs):
@@ -379,25 +379,25 @@
         gn_ref[...] = gacc[...].astype(BF16)
 
 
-def feed(n2, gf, seq, part, wgo, wgx, wuo, wux, wdo, wdx):
-    rows, width = n2.shape
-    half, hidden = wgo.shape
+def feed(n2, chunk, rows, gf, seq, part, gate, up, down):
+    width = n2.shape[1]
+    _, half, hidden = gate.shape
     hb = min(512, hidden)
-    row = pl.BlockSpec((half, hb), lambda h: (0, h))
-    col = pl.BlockSpec((hb, half), lambda h: (h, 0))
+    row = [pl.BlockSpec((None, half, hb), lambda h, side=side: (side, 0, h)) for side in range(2)]
+    col = [pl.BlockSpec((None, hb, half), lambda h, side=side: (side, h, 0)) for side in range(2)]
     whole = pl.BlockSpec((rows, width), lambda h: (0, 0))
     tile = pl.BlockSpec((rows, hb), lambda h: (0, h))
     return pl.pallas_call(
         feed_kernel,
         grid=(hidden // hb,),
-        in_specs=[whole, pl.BlockSpec((1, rows, width), lambda h: (seq, part, 0)), row, row, row, row, col, col],
+        in_specs=[pl.BlockSpec((rows, width), lambda h: (chunk, 0)), pl.BlockSpec((1, rows, width), lambda h: (seq, part, 0))] + row + row + col,
         out_specs=[tile, tile, tile, whole, whole],
         out_shape=[shape((rows, hidden), BF16)] * 3 + [shape((rows, width), BF16)] * 2,
         scratch_shapes=[pltpu.VMEM((rows, width), F32), pltpu.VMEM((rows, width), F32)],
         compiler_params=PARAMS,
         cost_estimate=cost(12 * rows * width * hidden, 12 * half * hidden + 14 * rows * width, rows * hidden),
         name="feed_forward",
-    )(n2, gf, wgo, wgx, wuo, wux, wdo, wdx)
+    )(n2, gf, gate, gate, up, up, down, down)
 
 
 def second_back_kernel(terms, hidden_ref, gf_ref, gain_ref, *refs):
@@ -415,14 +415,15 @@
     gain_out[...] = jnp.sum(e * hat, axis=0, keepdims=True)
 
 
-def second_back(hidden, gf, seq, part, gain, terms):
-    rows, width = hidden.shape
+def second_back(hidden, chunk, gf, seq, part, gain, terms):
+    rows, width = terms[0].shape
     flat = pl.BlockSpec((rows, width), lambda i: (0, 0))
     line = pl.BlockSpec((1, width), lambda i: (0, 0))
     return pl.pallas_call(
         functools.partial(second_back_kernel, len(terms)),
         grid=(1,),
-        in_specs=[flat, pl.BlockSpec((1, rows, width), lambda i: (seq, part, 0)), line] + [flat] * len(terms),
+        in_specs=[pl.BlockSpec((rows, width), lambda i: (chunk, 0)), pl.BlockSpec((1, rows, width), lambda i: (seq, part, 0)), line]
+        + [flat] * len(terms),
         out_specs=[flat, flat, line],
         out_shape=[shape((rows, width), BF16), shape((rows, width), F32), shape((1, width), F32)],
         compiler_params=PARAMS,
@@ -432,13 +433,13 @@
 
 
 def branch_back_kernel(chunks, *refs):
-    gb_refs, (wo_ref, wx_ref, core_ref, own_ref, oth_ref) = refs[:chunks], refs[chunks:]
-    half = wo_ref.shape[1]
+    gb_refs, (w_ref, core_ref, own_ref, oth_ref) = refs[:chunks], refs[chunks:]
+    half = w_ref.shape[2]
     rows = gb_refs[0].shape[0]
     heads_half = own_ref.shape[0]
     first = core_ref[0] == 0
     for k, ref in enumerate(gb_refs):
-        da = dot_nt(wo_ref[...], ref[:, :half]) + dot_nt(wx_ref[...], ref[:, half:])
+        da = dot_nt(w_ref[0], ref[:, :half]) + dot_nt(w_ref[1], ref[:, half:])
         da = da.astype(BF16)
         low, high = da[:heads_half], da[heads_half:]
         cut = slice(k * rows, (k + 1) * rows)
@@ -446,20 +447,20 @@
         oth_ref[:, cut] = jnp.where(first, high, low)
 
 
-def branch_back(gbs, w_own, w_oth, core):
+def branch_back(gbs, weight, core):
     chunks = len(gbs)
     rows, width = gbs[0].shape
-    dim = w_own.shape[0]
+    dim = weight.shape[1]
     full = pl.BlockSpec(memory_space=pltpu.VMEM)
     return pl.pallas_call(
         functools.partial(branch_back_kernel, chunks),
-        in_specs=[full] * (chunks + 2) + [SMEM],
+        in_specs=[full] * (chunks + 1) + [SMEM],
         out_specs=[full] * 2,
         out_shape=[shape((dim // 2, chunks * rows), BF16)] * 2,
         compiler_params=PARAMS,
         cost_estimate=cost(2 * dim * chunks * rows * width, 2 * dim * width + 2 * chunks * rows * width),
         name="attention_branch_back",
-    )(*gbs, w_own, w_oth, core)
+    )(*gbs, weight, core)
 
 
 def attend_back_kernel(block, groups, scal_ref, all_ref, att_ref, inv_ref, own_ref, got_ref, out_own, out_oth, da_all, grads):
@@ -524,8 +525,8 @@
     )(scalars, everything, att, inv, own, got)
 
 
-def heads_back_kernel(hd, nq, nk, own_ref, got_ref, pre_ref, cos_ref, sin_ref, qg_ref, kg_ref, x_ref, wo_ref, wx_ref, core_ref, dpre_ref, first_ref, gain_ref, hgain_ref):
-    half = wo_ref.shape[0]
+def heads_back_kernel(hd, nq, nk, own_ref, got_ref, pre_ref, cos_ref, sin_ref, qg_ref, kg_ref, x_ref, w_ref, core_ref, dpre_ref, first_ref, gain_ref, hgain_ref):
+    half = w_ref.shape[1]
     low, high = join_positions(core_ref[0], own_ref[...].astype(F32), got_ref[...].astype(F32))
     sides = (nq // 2, nk // 2, nk // 2)
     grads = [[], [], []]
@@ -556,16 +557,16 @@
     dpre_ref[...] = dpre
     x = x_ref[0].astype(F32)
     hat = x * inverse_rms(x)
-    for k, ref in enumerate((wo_ref, wx_ref)):
+    for k in range(2):
         cut = slice(k * half, (k + 1) * half)
-        part = dot_nt(dpre, ref[...])
+        part = dot_nt(dpre, w_ref[k])
         first_ref[:, cut] = part.astype(BF16)
         gain_ref[:, cut] = jnp.sum(part * hat[:, cut], axis=0, keepdims=True)
 
 
-def heads_back(own, got, pre, cosine, sine, qgain, kgain, xr, seq, w_own, w_oth, core, hd, nq, nk):
+def heads_back(own, got, pre, cosine, sine, qgain, kgain, xr, seq, weight, core, hd, nq, nk):
     span = own.shape[1]
-    half, cols = w_own.shape
+    _, half, cols = weight.shape
     width = 2 * half
     whole = lambda a: pl.BlockSpec(a.shape, lambda i: (0,) * len(a.shape))
     outs = [shape((span, cols), BF16), shape((span, width), BF16), shape((1, width), F32), shape((2 * hd, 128), F32)]
@@ -573,13 +574,13 @@
         functools.partial(heads_back_kernel, hd, nq, nk),
         grid=(1,),
         in_specs=[whole(a) for a in (own, got, pre, cosine, sine, qgain, kgain)]
-        + [pl.BlockSpec((1, span, width), lambda i: (seq, 0, 0)), whole(w_own), whole(w_oth), SMEM],
+        + [pl.BlockSpec((1, span, width), lambda i: (seq, 0, 0)), whole(weight), SMEM],
         out_specs=[whole(o) for o in outs],
         out_shape=outs,
         compiler_params=PARAMS,
         cost_estimate=cost(2 * span * width * cols, 4 * span * width + 4 * half * cols),
         name="query_key_value_back",
-    )(own, got, pre, cosine, sine, qgain, kgain, xr, w_own, w_oth, core)
+    )(own, got, pre, cosine, sine, qgain, kgain, xr, weight, core)
 
 
 def place_blocks(order, ids, first_id, value, out_ref):
@@ -694,6 +695,448 @@
         cost_estimate=cost(2 * tokens * dims[0] * dims[1], 2 * tokens * sum(dims) + 2 * dims[0] * dims[1]),
         name="weight_grad",
     )(*lefts, *rights, *([add] if add is not None else []))
+
+
+def xor_one(index):
+    return index + 1 - 2 * (index % 2)
+
+
+def remote(src, dst, send, recv, device):
+    return pltpu.make_async_remote_copy(
+        src_ref=src, dst_ref=dst, send_sem=send, recv_sem=recv, device_id=device, device_id_type=pl.DeviceIdType.MESH
+    )
+
+
+def greet(others):
+    barrier = pltpu.get_barrier_semaphore()
+    count = 0
+    for needed, device in others:
+        if needed is None:
+            pl.semaphore_signal(barrier, inc=1, device_id=device, device_id_type=pl.DeviceIdType.MESH)
+            count = count + 1
+        else:
+
+            @pl.when(needed)
+            def _():
+                pl.semaphore_signal(barrier, inc=1, device_id=device, device_id_type=pl.DeviceIdType.MESH)
+
+            count = count + jnp.where(needed, 1, 0)
+    pl.semaphore_wait(barrier, count)
+
+
+class Gather:
+    def __init__(self, shard, dst, axis, send, recv, local, near_x, near_y, near_core):
+        piece = shard.shape[axis]
+        half = shard.shape[0] // 2
+
+        def block(side, k):
+            cut = pl.ds(k * piece, piece)
+            return dst.at[side, cut, :] if axis == 0 else dst.at[side, :, cut]
+
+        def part(k, h):
+            if axis == 0:
+                return dst.at[0, pl.ds(k * piece + h * half, half), :]
+            return dst.at[0, pl.ds(h * half, half), pl.ds(k * piece, piece)]
+
+        sem = lambda k: (send.at[k], recv.at[k])
+        self.local = pltpu.make_async_copy(shard, block(0, 0), local)
+        self.x = remote(shard, block(0, 1), *sem(0), near_x)
+        self.y = remote(shard, block(0, 2), *sem(1), near_y)
+        self.dx = remote(part(2, 0), part(3, 0), *sem(2), near_x)
+        self.dy = remote(part(1, 1), part(3, 1), *sem(3), near_y)
+        self.cores = [remote(shard, block(1, 0), *sem(4), near_core)]
+        self.cores += [remote(block(0, k), block(1, k), *sem(4 + k), near_core) for k in (1, 2, 3)]
+
+    def first(self):
+        self.x.start()
+        self.y.start()
+        self.cores[0].start()
+        self.local.start()
+
+    def second(self):
+        self.y.wait_recv()
+        self.dx.start()
+        self.cores[2].start()
+        self.x.wait_recv()
+        self.dy.start()
+        self.cores[1].start()
+
+    def third(self):
+        self.dx.wait_recv()
+        self.dy.wait_recv()
+        self.cores[3].start()
+
+    def arrived(self):
+        self.local.wait()
+        for copy in self.cores:
+            copy.wait_recv()
+
+    def sent(self):
+        for copy in [self.x, self.y, self.dx, self.dy] + self.cores:
+            copy.wait_send()
+
+
+def forward_kernel(
+    hd, nq, nk, block, sub,
+    len_ref, x_hbm, cot_hbm, wqkv, wout, wgate, wup, wdown, gain_ref, cos_ref, sin_ref, qg_ref, kg_ref,
+    xr_hbm, n1_hbm, gf_hbm, qkv_hbm, out_hbm, gate_hbm, up_hbm, down_hbm, hidden_hbm, n2_hbm,
+    gains_ref, pre_ref, all_ref, att_ref, inv_ref, tok_ref, stat_ref,
+    xr_v, cot_v, n1_v, qkv_v, out_v, ex_own, ex_send, ex_got, at_own, at_send, at_got,
+    part_v, in_v, back_v, pair_v, total_v, hid_v, norm_v,
+    load_sem, store_sem, wsend, wrecv, wloc, gsend, grecv, exsend, exrecv, zsend, zrecv, hid_sem,
+):
+    seqs, span, width = xr_v.shape
+    groups = nq // nk
+    row, core, rank = lax.axis_index("dp"), lax.axis_index("context"), lax.axis_index("tensor")
+    start = core * span
+    near = [row, xor_one(row), (row + 2) % 4, 3 - row]
+    inner = (rank % 3) != 0
+    outer = (rank % 3) == 0
+    near_x, near_y, near_core = {"dp": near[1]}, {"dp": near[2]}, {"context": 1 - core}
+    z_side, z_mid = {"tensor": xor_one(rank)}, {"tensor": 3 - rank}
+    piece = width // 8
+    total_subs = part_v.shape[0]
+    per = span // sub
+    first_core = core == 0
+
+    loads = []
+    for at, (src, dst) in enumerate(((x_hbm, xr_v), (cot_hbm, cot_v))):
+        for s in range(seqs):
+            for o in range(2):
+                for k in range(4):
+                    b = near[k] * 2 + (core if o == 0 else 1 - core)
+                    cut = pl.ds(pl.multiple_of(b * piece, piece), piece)
+                    loads.append(
+                        pltpu.make_async_copy(
+                            src.at[s, :, cut], dst.at[s, :, pl.ds((o * 4 + k) * piece, piece)], load_sem.at[at, s, o * 4 + k]
+                        )
+                    )
+    for copy in loads:
+        copy.start()
+
+    others = []
+    for o in range(2):
+        for k in range(4):
+            if o or k:
+                others.append((o * 4 + k, {"dp": near[k], "context": core if o == 0 else 1 - core}))
+    greet([(None, d) for _, d in others] + [(None, z_side), (inner, z_mid)])
+
+    gains = [remote(gain_ref, gains_ref.at[b], gsend.at[b], grecv.at[b], d) for b, d in others]
+    for copy in gains:
+        copy.start()
+    weights = [
+        Gather(shard, dst, axis, wsend.at[i], wrecv.at[i], wloc.at[i], near_x, near_y, near_core)
+        for i, (shard, dst, axis) in enumerate(
+            ((wqkv, qkv_v, 0), (wout, out_v, 1), (wgate, gate_hbm, 0), (wup, up_hbm, 0), (wdown, down_hbm, 1))
+        )
+    ]
+    w_qkv, w_out, w_gate, w_up, w_down = weights
+    w_qkv.first()
+    w_out.first()
+    gains_ref[0] = gain_ref[...]
+
+    for copy in loads[len(loads) // 2 :]:
+        copy.wait()
+
+    def mask_rows(i, carry):
+        s, t = i // per, i % per
+        cut = pl.ds(pl.multiple_of(t * sub, sub), sub)
+        place = start + t * sub + lax.broadcasted_iota(jnp.int32, (sub, 1), 0)
+        length = len_ref[s]
+        valid = (place < length).astype(F32)
+        cot_v[s, cut, :] = (cot_v[s, cut, :].astype(F32) * valid).astype(BF16)
+        return carry
+
+    lax.fori_loop(0, total_subs, mask_rows, 0)
+    store_gf = pltpu.make_async_copy(cot_v, gf_hbm, store_sem.at[0])
+    store_gf.start()
+    for copy in loads[: len(loads) // 2]:
+        copy.wait()
+    store_xr = pltpu.make_async_copy(xr_v, xr_hbm, store_sem.at[1])
+    store_xr.start()
+    for copy in gains:
+        copy.wait_recv()
+    gain1 = jnp.concatenate([gains_ref[b, 0:1, :] for b in range(8)], axis=1).astype(F32)
+    gain2 = jnp.concatenate([gains_ref[b, 1:2, :] for b in range(8)], axis=1).astype(F32)
+
+    def norm_rows(i, carry):
+        s, t = i // per, i % per
+        cut = pl.ds(pl.multiple_of(t * sub, sub), sub)
+        x = xr_v[s, cut, :].astype(F32)
+        n1_v[s, cut, :] = (x * inverse_rms(x) * gain1).astype(BF16)
+        return carry
+
+    lax.fori_loop(0, total_subs, norm_rows, 0)
+    store_n1 = pltpu.make_async_copy(n1_v, n1_hbm, store_sem.at[2])
+    store_n1.start()
+    w_qkv.second()
+    w_out.second()
+    w_gate.first()
+    w_qkv.third()
+    w_out.third()
+    w_qkv.arrived()
+    w_up.first()
+
+    cosine, sine = cos_ref[...], sin_ref[...]
+    half = width // 2
+
+    def exchange(s):
+        return remote(ex_send.at[s], ex_got.at[s], exsend.at[0, s], exrecv.at[0, s], near_core)
+
+    def project(s, carry):
+        x = n1_v[s]
+        flat = dot_nn(x[:, :half], qkv_v[0]) + dot_nn(x[:, half:], qkv_v[1])
+        turned = flat.T
+        pre_ref[s] = turned[: (nq + nk) * hd]
+        done = []
+        for h in range(nq + nk):
+            v = turned[h * hd : (h + 1) * hd]
+            inv = lax.rsqrt(jnp.mean(v * v, axis=0, keepdims=True) + epsilon)
+            v = v * inv * (qg_ref[...] if h < nq else kg_ref[...])
+            a, b = v[: hd // 2], v[hd // 2 :]
+            done.append(jnp.concatenate([a * cosine - b * sine, b * cosine + a * sine], axis=0))
+        for h in range(nk):
+            lo = (nq + nk + h) * hd
+            done.append(turned[lo : lo + hd])
+        parts = [[], []]
+        for begin_at, count in ((0, nq), (nq, nk), (nq + nk, nk)):
+            for side in range(2):
+                parts[side] += done[begin_at + side * count // 2 : begin_at + (side + 1) * count // 2]
+        low = jnp.concatenate(parts[0], axis=0)
+        high = jnp.concatenate(parts[1], axis=0)
+        ex_own[s] = jnp.where(first_core, low, high).astype(BF16)
+        ex_send[s] = jnp.where(first_core, high, low).astype(BF16)
+        exchange(s).start()
+        return carry
+
+    lax.fori_loop(0, seqs, project, 0)
+    store_qkv = pltpu.make_async_copy(qkv_v, qkv_hbm, store_sem.at[3])
+    store_qkv.start()
+
+    scale = log2e / math.sqrt(hd)
+    krow = lax.broadcasted_iota(jnp.int32, (block, groups * block), 0)
+    qcol = lax.broadcasted_iota(jnp.int32, (block, groups * block), 1) % block
+    base = groups * hd
+
+    def give(s):
+        return remote(at_send.at[s], at_got.at[s], exsend.at[1, s], exrecv.at[1, s], near_core)
+
+    def attention(s, carry):
+        exchange(s).wait_recv()
+        low, high = join_positions(core, ex_own[s], ex_got[s])
+        all_ref[s, :, :span] = low
+        all_ref[s, :, span:] = high
+        length = len_ref[s]
+        for i in range(2 * span // block):
+            cut = slice(i * block, (i + 1) * block)
+            q = jnp.concatenate([all_ref[s, g * hd : (g + 1) * hd, cut] for g in range(groups)], axis=1)
+            acc = jnp.zeros((hd, groups * block), F32)
+            total = jnp.zeros((1, groups * block), F32)
+            for j in range(i + 1):
+                kcut = slice(j * block, (j + 1) * block)
+                score = dot_tn(all_ref[s, base : base + hd, kcut], q) * scale
+                ok = (krow + j * block) < length
+                if j == i:
+                    ok = ok & (krow <= qcol)
+                e = jnp.where(ok, jnp.exp2(score), 0.0)
+                total = total + jnp.sum(e, axis=0, keepdims=True)
+                acc = acc + dot_nn(all_ref[s, base + hd : base + 2 * hd, kcut], e.astype(BF16))
+            inv = 1.0 / total
+            att = (acc * inv).astype(BF16)
+            for g in range(groups):
+                att_ref[s, g * hd : (g + 1) * hd, cut] = att[:, g * block : (g + 1) * block]
+                inv_ref[s, g : g + 1, cut] = inv[:, g * block : (g + 1) * block]
+        mine, theirs = join_positions(core, att_ref[s, :, :span], att_ref[s, :, span:])
+        at_own[s] = mine
+        at_send[s] = theirs
+        give(s).start()
+        return carry
+
+    lax.fori_loop(0, seqs, attention, 0)
+    w_out.arrived()
+    store_out = pltpu.make_async_copy(out_v, out_hbm, store_sem.at[4])
+    store_out.start()
+
+    def hop_in(u):
+        return remote(part_v.at[u], in_v.at[u], zsend.at[0, u], zrecv.at[0, u], z_side)
+
+    def hop_mid(u):
+        return remote(pair_v.at[u], back_v.at[u], zsend.at[1, u], zrecv.at[1, u], z_mid)
+
+    def hop_out(u):
+        return remote(in_v.at[u], back_v.at[u], zsend.at[2, u], zrecv.at[2, u], z_side)
+
+    def branch_rows(s, carry):
+        give(s).wait_recv()
+        low, high = join_positions(core, at_own[s], at_got[s])
+        att = jnp.concatenate([low, high], axis=0).T
+        tok_ref[s] = att
+        for k in range(per):
+            u = s * per + k
+            rows = att[k * sub : (k + 1) * sub]
+            part_v[u, :, :half] = dot_nn(rows, out_v[0]).astype(BF16)
+            part_v[u, :, half:] = dot_nn(rows, out_v[1]).astype(BF16)
+
+            @pl.when(outer)
+            def _():
+                hop_in(u).start()
+
+        return carry
+
+    lax.fori_loop(0, seqs, branch_rows, 0)
+    w_gate.second()
+    w_down.first()
+    stat_ref[...] = jnp.zeros_like(stat_ref)
+    line = lax.broadcasted_iota(jnp.int32, (8, 128), 0)
+
+    def hidden_store(u):
+        cut = pl.ds(pl.multiple_of(u * sub, sub), sub)
+        return (
+            pltpu.make_async_copy(hid_v.at[u % 2], hidden_hbm.at[cut, :], hid_sem.at[0, u % 2]),
+            pltpu.make_async_copy(norm_v.at[u % 2], n2_hbm.at[cut, :], hid_sem.at[1, u % 2]),
+        )
+
+    def finish(u):
+        s, t = u // per, u % per
+        cut = pl.ds(pl.multiple_of(t * sub, sub), sub)
+
+        @pl.when(inner)
+        def _():
+            total_v[...] = pair_v[u].astype(F32) + back_v[u].astype(F32)
+
+        @pl.when(outer)
+        def _():
+            hop_out(u).wait_recv()
+            total_v[...] = part_v[u].astype(F32) + back_v[u].astype(F32)
+
+        @pl.when(u >= 2)
+        def _():
+            for copy in hidden_store(u - 2):
+                copy.wait()
+
+        total = total_v[...]
+        resid = xr_v[s, cut, :].astype(F32)
+        hidden = resid + total
+        hid_v[u % 2] = hidden
+        norm_v[u % 2] = (hidden * inverse_rms(hidden) * gain2).astype(BF16)
+        for copy in hidden_store(u):
+            copy.start()
+        length = len_ref[s]
+        place = start + t * sub + lax.broadcasted_iota(jnp.int32, (sub, 1), 0)
+        valid = (place < length).astype(F32)
+        one = jnp.sum(valid * resid * resid, keepdims=True)
+        two = jnp.sum(valid * total * total, keepdims=True)
+        stat_ref[...] += jnp.where(line == 0, one, jnp.where(line == 1, two, 0.0))
+
+    def chain(i, carry):
+        @pl.when((i < total_subs) & inner)
+        def _():
+            hop_in(i).wait_recv()
+            pair_v[i] = (part_v[i].astype(F32) + in_v[i].astype(F32)).astype(BF16)
+            hop_mid(i).start()
+
+        @pl.when((i >= 1) & (i < total_subs + 1) & inner)
+        def _():
+            u = i - 1
+            hop_mid(u).wait_recv()
+            in_v[u] = (part_v[u].astype(F32) + back_v[u].astype(F32)).astype(BF16)
+            hop_out(u).start()
+
+        @pl.when(i >= 2)
+        def _():
+            finish(i - 2)
+
+        @pl.when(i == total_subs // 2 - 2)
+        def _():
+            w_gate.third()
+            w_up.second()
+
+        @pl.when(i == total_subs - 1)
+        def _():
+            w_up.third()
+            w_down.second()
+
+        return carry
+
+    lax.fori_loop(0, total_subs + 2, chain, 0)
+    w_down.third()
+    for u in (total_subs - 2, total_subs - 1):
+        for copy in hidden_store(u):
+            copy.wait()
+
+    def settle(u, carry):
+        @pl.when(outer)
+        def _():
+            hop_in(u).wait_send()
+
+        @pl.when(inner)
+        def _():
+            hop_mid(u).wait_send()
+            hop_out(u).wait_send()
+
+        return carry
+
+    lax.fori_loop(0, total_subs, settle, 0)
+    for s in range(seqs):
+        exchange(s).wait_send()
+        give(s).wait_send()
+    for copy in gains:
+        copy.wait_send()
+    for w in weights[2:]:
+        w.arrived()
+    for w in weights:
+        w.sent()
+    for copy in (store_gf, store_xr, store_n1, store_qkv, store_out):
+        copy.wait()
+
+
+def forward(lengths, x, cot, w_qkv, w_out, w_gate, w_up, w_down, gains, cosine, sine, qgain, kgain, hd, nq, nk):
+    seqs, span, width = x.shape
+    half = width // 2
+    groups = nq // nk
+    sub = min(128, span)
+    subs = seqs * span // sub
+    block = min(256, span)
+    hidden = w_gate.shape[1]
+    cols = w_qkv.shape[1]
+    rows = cols // 2
+    any_space = pl.BlockSpec(memory_space=pl.ANY)
+    vmem = pl.BlockSpec(memory_space=pltpu.VMEM)
+    wide = (seqs, span, width)
+    large = [
+        shape(wide, BF16), shape(wide, BF16), shape(wide, BF16),
+        shape((2, half, cols), BF16), shape((2, w_out.shape[0], half), BF16),
+        shape((2, half, hidden), BF16), shape((2, half, hidden), BF16), shape((2, hidden, half), BF16),
+        shape((seqs * span, width), F32), shape((seqs * span, width), BF16),
+    ]
+    small = [
+        shape((8,) + gains.shape, BF16), shape((seqs, (nq + nk) * hd, span), F32), shape((seqs, rows, 2 * span), BF16),
+        shape((seqs, groups * hd, 2 * span), BF16), shape((seqs, groups, 2 * span), F32), shape((seqs, span, nq * hd), BF16),
+        shape((8, 128), F32),
+    ]
+    dma = pltpu.SemaphoreType.DMA
+    ex = pltpu.VMEM((seqs, rows, span), BF16)
+    at = pltpu.VMEM((seqs, groups * hd, span), BF16)
+    moving = pltpu.VMEM((subs, sub, width), BF16)
+    flops = 2 * seqs * span * width * (cols + nq * hd) + 16 * seqs * nq * hd * span * span
+    return pl.pallas_call(
+        functools.partial(forward_kernel, hd, nq, nk, block, sub),
+        in_specs=[SMEM] + [any_space] * 7 + [vmem] * 5,
+        out_specs=[any_space] * len(large) + [vmem] * len(small),
+        out_shape=large + small,
+        scratch_shapes=[
+            pltpu.VMEM(wide, BF16), pltpu.VMEM(wide, BF16), pltpu.VMEM(wide, BF16),
+            pltpu.VMEM((2, half, cols), BF16), pltpu.VMEM((2, w_out.shape[0], half), BF16),
+            ex, ex, ex, at, at, at,
+            moving, moving, moving, moving,
+            pltpu.VMEM((sub, width), F32), pltpu.VMEM((2, sub, width), F32), pltpu.VMEM((2, sub, width), BF16),
+            dma((2, seqs, 8)), dma((5,)), dma((5, 8)), dma((5, 8)), dma((5,)), dma((8,)), dma((8,)),
+            dma((2, seqs)), dma((2, seqs)), dma((3, subs)), dma((3, subs)), dma((2, 2)),
+        ],
+        compiler_params=pltpu.CompilerParams(vmem_limit_bytes=VMEM_BYTES, collective_id=1, has_side_effects=True),
+        cost_estimate=cost(flops, 80 * seqs * span * width),
+        name="attention_forward",
+    )(lengths, x, cot, w_qkv, w_out, w_gate, w_up, w_down, gains, cosine, sine, qgain, kgain)
 
 
 def per_device(
@@ -738,46 +1181,65 @@
     qgain = query_gain.astype(F32).reshape(hd, 1)
     kgain = key_gain.astype(F32).reshape(hd, 1)
 
-    gains = jnp.stack([attn_gain, ffn_gain])
-    g_own, g_oth, _ = gather_blocks(gains, 1, dp)
-    gains = jnp.concatenate([g_own, g_oth], axis=1).astype(F32)
-    gain1, gain2 = gains[0:1], gains[1:2]
     w_qkv = jnp.concatenate([w_query, key_projection_weight, value_projection_weight], axis=1)
-    qkv_own, qkv_oth, mark = gather_blocks(w_qkv, 0, dp)
-    out_own, out_oth, mark = gather_blocks(tie(w_output, mark), 1, dp)
-    gate_own, gate_oth, mark = gather_blocks(tie(w_gate, mark), 0, dp)
-    up_own, up_oth, mark = gather_blocks(tie(w_up, mark), 0, dp)
-    down_own, down_oth, mark = gather_blocks(tie(w_down, mark), 1, dp)
-
-    scal = jnp.concatenate([lengths, start.reshape(1), ids])
-    x_in, cot_in = inputs, cotangent
-    if order == 1:
-        x_in, cot_in = to_relative(x_in, dp, core), to_relative(cot_in, dp, core)
-    xr, n1, gf = begin(x_in, cot_in, gain1, scal, order)
-
     saved = []
-    parts = []
-    for s in range(seqs):
-        pre, own, oth = heads(n1, s, qkv_own, qkv_oth, cosine, sine, qgain, kgain, core1, hd, nq, nk)
-        seq_scal = jnp.stack([lengths[s], core.astype(jnp.int32)])
-        everything, att, inv, mine, theirs = attend(seq_scal, own, over_core(oth), groups)
-        branched = branch(mine, over_core(theirs), out_own, out_oth, core1, chunks)
-        saved.append((pre, everything, att, inv, seq_scal, branched[0]))
-        parts.append(branched[1:])
-
-    stats = jnp.zeros((2,), F32)
+    if dp == 4 and tensor == 4 and order == 8:
+        gains = jnp.pad(jnp.stack([attn_gain, ffn_gain]), ((0, 14), (0, 0)))
+        (xr, n1, gf, qkv, out_w, gate, up, down, hidden_all, n2_all, gains, pre_all, everything_all, att_all, inv_all, tok, stat) = forward(
+            lengths, inputs, cotangent, w_qkv, w_output, w_gate, w_up, w_down, gains, cosine, sine, qgain, kgain, hd, nq, nk
+        )
+        gains = jnp.swapaxes(gains[:, :2], 0, 1).reshape(2, width).astype(F32)
+        gain1, gain2 = gains[0:1], gains[1:2]
+        stats = stat[:2, 0]
+        for s in range(seqs):
+            seq_scal = jnp.stack([lengths[s], core.astype(jnp.int32)])
+            saved.append((pre_all[s], everything_all[s], att_all[s], inv_all[s], seq_scal))
+        tok = tok.reshape(seqs * span, nq * hd)
+    else:
+        gains, _ = gather_blocks(jnp.stack([attn_gain, ffn_gain]), 1, dp)
+        gains = jnp.concatenate([gains[0], gains[1]], axis=1).astype(F32)
+        gain1, gain2 = gains[0:1], gains[1:2]
+        qkv, mark = gather_blocks(w_qkv, 0, dp)
+        out_w, mark = gather_blocks(tie(w_output, mark), 1, dp)
+        gate, mark = gather_blocks(tie(w_gate, mark), 0, dp)
+        up, mark = gather_blocks(tie(w_up, mark), 0, dp)
+        down, mark = gather_blocks(tie(w_down, mark), 1, dp)
+
+        scal = jnp.concatenate([lengths, start.reshape(1), ids])
+        x_in, cot_in = inputs, cotangent
+        if order == 1:
+            x_in, cot_in = to_relative(x_in, dp, core), to_relative(cot_in, dp, core)
+        xr, n1, gf = begin(x_in, cot_in, gain1, scal, order)
+
+        parts, tok = [], []
+        for s in range(seqs):
+            pre, own, oth = heads(n1, s, qkv, cosine, sine, qgain, kgain, core1, hd, nq, nk)
+            seq_scal = jnp.stack([lengths[s], core.astype(jnp.int32)])
+            everything, att, inv, mine, theirs = attend(seq_scal, own, over_core(oth), groups)
+            branched = branch(mine, over_core(theirs), out_w, core1, chunks)
+            saved.append((pre, everything, att, inv, seq_scal))
+            tok.append(jnp.swapaxes(branched[0], 0, 1))
+            parts.append(branched[1:])
+        tok = jnp.concatenate(tok, axis=0)
+
+        stats = jnp.zeros((2,), F32)
+        hidden_all, n2_all = [], []
+        for s in range(seqs):
+            for k in range(chunks):
+                terms = sum_terms(parts[s][k], tensor)
+                place = jnp.stack([lengths[s], start + k * rows])
+                hidden, n2, stat = second_norm(place, xr, s, k, gain2, terms)
+                hidden_all.append(hidden)
+                n2_all.append(n2)
+                stats = stats + stat[:2, 0]
+        hidden_all, n2_all = jnp.concatenate(hidden_all), jnp.concatenate(n2_all)
+
     ffn_squares = jnp.zeros((), F32)
-    hidden, n2, inner, gg, gu, ffn, gn = [[[None] * chunks for _ in range(seqs)] for _ in range(7)]
+    inner, gg, gu, ffn, gn = [[[None] * chunks for _ in range(seqs)] for _ in range(5)]
     out_shares = []
     for s in range(seqs):
         for k in range(chunks):
-            terms = sum_terms(parts[s][k], tensor)
-            place = jnp.stack([lengths[s], start + k * rows])
-            hidden[s][k], n2[s][k], stat = second_norm(place, xr, s, k, gain2, terms)
-            stats = stats + stat[:2, 0]
-            inner[s][k], gg[s][k], gu[s][k], ffn[s][k], gn[s][k] = feed(
-                n2[s][k], gf, s, k, gate_own, gate_oth, up_own, up_oth, down_own, down_oth
-            )
+            inner[s][k], gg[s][k], gu[s][k], ffn[s][k], gn[s][k] = feed(n2_all, s * chunks + k, rows, gf, s, k, gate, up, down)
 
     def piece_of(arrays):
         per = arrays[0].shape[0] // share
@@ -800,11 +1262,12 @@
     for s in range(seqs):
         for k in range(chunks):
             terms = sum_terms(gn[s][k], tensor)
-            gb[s][k], gh[s][k], gain_part = second_back(hidden[s][k], gf, s, k, gain2, terms)
+            gb[s][k], gh[s][k], gain_part = second_back(hidden_all, s * chunks + k, gf, s, k, gain2, terms)
             gain2_grad = gain2_grad + gain_part
     for s in range(seqs):
         got = ring_scatter(piece_of(ffn[s]), tensor, rank)
-        out, stat = output_share(share_scalars(s), got, ffn[s], hidden[s], order)
+        halves = [hidden_all[(s * chunks + k) * rows : (s * chunks + k + 1) * rows] for k in range(chunks)]
+        out, stat = output_share(share_scalars(s), got, ffn[s], halves, order)
         out_shares.append(out)
         ffn_squares = ffn_squares + stat[0, 0]
 
@@ -820,18 +1283,19 @@
     inner_seq = flat(inner)
     gf_flat = [gf[s, k * rows : (k + 1) * rows] for s in range(seqs) for k in range(chunks)]
     grad_w_down = reduced(inner_seq, gf_flat, 1)
-    grad_w_gate = reduced(flat(n2), flat(gg), 0)
-    grad_w_up = reduced(flat(n2), flat(gu), 0)
+    n2_list = [n2_all[i * rows : (i + 1) * rows] for i in range(seqs * chunks)]
+    grad_w_gate = reduced(n2_list, flat(gg), 0)
+    grad_w_up = reduced(n2_list, flat(gu), 0)
 
     gain1_grad = jnp.zeros((1, width), F32)
     head_gain = jnp.zeros((2 * hd,), F32)
     dpres, in_shares = [], []
     for s in range(seqs):
-        pre, everything, att, inv, seq_scal, att_rows = saved[s]
-        da_own, da_oth = branch_back(gb[s], out_own, out_oth, core1)
+        pre, everything, att, inv, seq_scal = saved[s]
+        da_own, da_oth = branch_back(gb[s], out_w, core1)
         d_own, d_oth = attend_back(seq_scal, everything, att, inv, da_own, over_core(da_oth), groups)
         dpre, first, gain_part, hg = heads_back(
-            d_own, over_core(d_oth), pre, cosine, sine, qgain, kgain, xr, s, qkv_own, qkv_oth, core1, hd, nq, nk
+            d_own, over_core(d_oth), pre, cosine, sine, qgain, kgain, xr, s, qkv, core1, hd, nq, nk
         )
         gain1_grad = gain1_grad + gain_part
         head_gain = head_gain + hg[:, 0]
@@ -839,8 +1303,7 @@
         got = ring_scatter(piece_of([first]), tensor, rank)
         in_shares.append(input_share(share_scalars(s), got, first, gh[s], xr, s, gain1, order))
 
-    att_rows = jnp.concatenate([jnp.swapaxes(saved[s][5], 0, 1) for s in range(seqs)], axis=0)
-    att_list = [att_rows[i * rows : (i + 1) * rows] for i in range(seqs * chunks)]
+    att_list = [tok[i * rows : (i + 1) * rows] for i in range(seqs * chunks)]
     grad_w_output = reduced(att_list, flat(gb), 1)
     grad_qkv = reduced([n1[s] for s in range(seqs)], dpres, 0)
     nqc, nkc = nq * hd, nk * hd

time: 962 us -> 833 us (0.87)
  waiting for transfers between devices: 342 us -> 135 us
  Pallas kernels: 309 us -> 410 us
  other arithmetic: 83.6 us -> 58.1 us
  local copies, waits for them, and re-layouts: 79.4 us -> 56.2 us
  starting transfers between devices: 138 us -> 159 us
    ppermute x8 -> x4, waiting for transfers between devices: 133 us -> 4.32 us  [sum_terms(): outward = lax.ppermute(rest, 'tensor', [(1, 0), (2, 3)])]
    pallas_call x15 -> x5, Pallas kernels: 149 us -> 251 us  [the longest x1 165 us: forward(): pl.pallas_call(functools.partial(forward_kernel, hd, nq, nk, block, sub),...]
    ppermute x23 -> x11, waiting for transfers between devices: 89.5 us -> 36.1 us  [over_x(): return lax.ppermute(value, 'dp', [(i, i ^ 1) for i in range(4)])]
    ppermute x12, starting transfers between devices: 36.8 us -> 82.5 us  [ring_scatter(): moving = lax.ppermute(moving, 'tensor', ring)]
    ppermute x8 -> x4, waiting for transfers between devices: 63 us -> 28.9 us  [sum_terms(): inward = lax.ppermute(part, 'tensor', [(0, 1), (3, 2)])]
    unnamed x164 -> x111, local copies, waits for them, and re-layouts: 34.3 us -> 9.72 us
    ppermute x2, starting transfers between devices: 7.82 us -> 30.8 us  [per_device(): got = lax.ppermute(join(lines), 'tensor', [(i, i ^ step) for i in range(4)])]
    concatenate x3 -> x1, other arithmetic: 17.6 us -> 1.8 us  [per_device(): jnp.concatenate([w_query, key_projection_weight, value_projection_weight]...]
  transfers between devices with their start and end apart: 104 -> 58, of which waited for: 37 -> 19; matrix products, arithmetic and copies ran while one was open for 15% -> 11% of each run, Pallas kernels for 30% -> 25%
where the time goes in v2:
time: 833 us; the launch traced here: 823 us
  Pallas kernels  410 us (49%)
  starting transfers between devices  159 us (19%)
  waiting for transfers between devices  135 us (16%)
  other arithmetic  58.1 us (7%)
  local copies, waits for them, and re-layouts  56.2 us (7%)
    pallas_call x1, Pallas kernels, forward(): pl.pallas_call(functools.partial(forward_kernel, hd, nq, nk, block, sub),...  165 us
    pallas_call x4, Pallas kernels, feed(): pl.pallas_call(feed_kernel, grid=(hidden // hb,), in_specs=[pl.BlockSpec(...  85.6 us
    ppermute x12, starting transfers between devices, ring_scatter(): moving = lax.ppermute(moving, 'tensor', ring)  82.5 us
    pallas_call x10, Pallas kernels, weight_grad(): pl.pallas_call(functools.partial(weight_grad_kernel, count, add is not No...  72.6 us
    ppermute x11, waiting for transfers between devices, over_x(): return lax.ppermute(value, 'dp', [(i, i ^ 1) for i in range(4)])  36.1 us
    ppermute x12, waiting for transfers between devices, ring_scatter(): moving = lax.ppermute(moving, 'tensor', ring)  34.8 us
    ppermute x2, starting transfers between devices, per_device(): got = lax.ppermute(join(lines), 'tensor', [(i, i ^ step) for i in range(4)])  30.8 us
    ppermute x11, waiting for transfers between devices, over_y(): return lax.ppermute(value, 'dp', [(i, i ^ 2) for i in range(4)])  29.1 us
  transfers between devices with their start and end apart: 58, of which 19 were waited for; matrix products, arithmetic and copies ran while one was open for 11% of the time, Pallas kernels for 25%

profile of v2, /device:TPU:0, one launch (start us, length us, event | category | flops | bytes accessed | tf_op | source)
XLA Modules:
  0.0 822.8 jit_solution(14855499849339256837)
XLA Ops:
  8.1 165.3 %attention_forward.1 = (bf16[2,512,2048]{2,1,0:T(8,128)(2,1)}, bf16[2,512,2048]{2,1,0:T(8,128)(2,1)}, bf16[2,512,2048]{2,1,0:T(8,128)(2,1)}, bf16[2,1024,768]{2,...) custom-call(s32[2]{0:T(128)} %len_ref.1, ...), custom_call_target="tpu_custom_call" | custom-call | flops 9663676416 | bytes 167772160 | tf_op jit(solution)/shard_map/attention_forward/pallas_call | solution.py:1122
  173.4 21.2 %feed_forward.7 = (bf16[256,2048]{1,0:T(8,128)(2,1)}, bf16[256,2048]{1,0:T(8,128)(2,1)}, bf16[256,2048]{1,0:T(8,128)(2,1)}, bf16[256,2048]{1,0:T(8,128)(2,1)}, bf16[256,2048]{1,0:T(8,128)(2,1)}) custom-call(bf16[1024,2048]{1,0:T(8,128)(2,1)} %get-tuple-element.83.n_ref, bf16[2,512,2048]{2,1,0:T(8,128)(2,1)} %get-tuple-element.84.g_ref.gf_ref, ...), custom_call_target="tpu_custom_call" | custom-call | flops 12884901888 | bytes 32505856 | tf_op jit(solution)/shard_map/feed_forward/pallas_call | solution.py:390
  194.6 21.8 %feed_forward.6 = (bf16[256,2048]{1,0:T(8,128)(2,1)}, bf16[256,2048]{1,0:T(8,128)(2,1)}, bf16[256,2048]{1,0:T(8,128)(2,1)}, bf16[256,2048]{1,0:T(8,128)(2,1)}, bf16[256,2048]{1,0:T(8,128)(2,1)}) custom-call(bf16[1024,2048]{1,0:T(8,128)(2,1)} %get-tuple-element.83.n_ref, bf16[2,512,2048]{2,1,0:T(8,128)(2,1)} %get-tuple-element.84.g_ref.gf_ref, ...), custom_call_target="tpu_custom_call" | custom-call | flops 12884901888 | bytes 32505856 | tf_op jit(solution)/shard_map/feed_forward/pallas_call | solution.py:390
  218.3 21.4 %feed_forward.5 = (bf16[256,2048]{1,0:T(8,128)(2,1)}, bf16[256,2048]{1,0:T(8,128)(2,1)}, bf16[256,2048]{1,0:T(8,128)(2,1)}, bf16[256,2048]{1,0:T(8,128)(2,1)}, bf16[256,2048]{1,0:T(8,128)(2,1)}) custom-call(bf16[1024,2048]{1,0:T(8,128)(2,1)} %get-tuple-element.83.n_ref, bf16[2,512,2048]{2,1,0:T(8,128)(2,1)} %get-tuple-element.84.g_ref.gf_ref, ...), custom_call_target="tpu_custom_call" | custom-call | flops 12884901888 | bytes 32505856 | tf_op jit(solution)/shard_map/feed_forward/pallas_call | solution.py:390
  239.8 21.2 %feed_forward.4 = (bf16[256,2048]{1,0:T(8,128)(2,1)}, bf16[256,2048]{1,0:T(8,128)(2,1)}, bf16[256,2048]{1,0:T(8,128)(2,1)}, bf16[256,2048]{1,0:T(8,128)(2,1)}, bf16[256,2048]{1,0:T(8,128)(2,1)}) custom-call(bf16[1024,2048]{1,0:T(8,128)(2,1)} %get-tuple-element.83.n_ref, bf16[2,512,2048]{2,1,0:T(8,128)(2,1)} %get-tuple-element.84.g_ref.gf_ref, ...), custom_call_target="tpu_custom_call" | custom-call | flops 12884901888 | bytes 32505856 | tf_op jit(solution)/shard_map/feed_forward/pallas_call | solution.py:390
  263.0 5.5 collective-permute-start.17
  280.0 7.2 fusion.18
  298.1 8.7 %weight_grad.14 = bf16[1024,2048]{1,0:T(8,128)(2,1)} custom-call(bf16[256,2048]{1,0:T(8,128)(2,1)} %get-tuple-element.181.refs_0_, bf16[256,2048]{1,0:T(8,128)(2,1)} %get-tuple-element.180.refs_1_, bf16[256,2048]{1,0:T(8,128)(2,1)} %get-tuple-element.179.refs_2_, bf16[256,2048]{1,0:T(8,128)(2,1)} %get-tuple-element.178.refs_3_, ...), custom_call_target="tpu_custom_call" | custom-call | flops 4294967296 | bytes 10485760 | tf_op jit(solution)/shard_map/weight_grad/pallas_call | solution.py:688
  306.8 8.7 %weight_grad.16 = bf16[1024,2048]{1,0:T(8,128)(2,1)} custom-call(bf16[256,2048]{1,0:T(8,128)(2,1)} %get-tuple-element.181.refs_0_, bf16[256,2048]{1,0:T(8,128)(2,1)} %get-tuple-element.180.refs_1_, bf16[256,2048]{1,0:T(8,128)(2,1)} %get-tuple-element.179.refs_2_, bf16[256,2048]{1,0:T(8,128)(2,1)} %get-tuple-element.178.refs_3_, ...), custom_call_target="tpu_custom_call" | custom-call | flops 4294967296 | bytes 10485760 | tf_op jit(solution)/shard_map/weight_grad/pallas_call | solution.py:688
  316.1 8.5 %weight_grad.18 = bf16[2048,1024]{1,0:T(8,128)(2,1)} custom-call(bf16[256,2048]{1,0:T(8,128)(2,1)} %get-tuple-element.137.refs_0_, bf16[256,2048]{1,0:T(8,128)(2,1)} %get-tuple-element.138.refs_1_, bf16[256,2048]{1,0:T(8,128)(2,1)} %get-tuple-element.139.refs_2_, bf16[256,2048]{1,0:T(8,128)(2,1)} %get-tuple-element.140.refs_3_, ...), custom_call_target="tpu_custom_call" | custom-call | flops 4294967296 | bytes 10485760 | tf_op jit(solution)/shard_map/weight_grad/pallas_call | solution.py:688
  334.2 8.8 %collective-permute-done.6.refs_1_ = bf16[256,2048]{1,0:T(8,128)(2,1)} collective-permute-done((bf16[256,2048]{1,0:T(8,128)(2,1)S(1)}, bf16[256,2048]{1,0:T(8,128)(2,1)}, u32[]{:S(2)}, u32[]{:S(2)}) %collective-permute-start.6) | collective-permute-done | bytes 1048608 | tf_op jit(solution)/shard_map/ppermute | solution.py:124
  345.3 20.1 %collective-permute-done.9.refs_1_ = bf16[256,2048]{1,0:T(8,128)(2,1)S(1)} collective-permute-done((bf16[256,2048]{1,0:T(8,128)(2,1)S(1)}, bf16[256,2048]{1,0:T(8,128)(2,1)S(1)}, u32[]{:S(2)}, u32[]{:S(2)}) %collective-permute-start.9) | collective-permute-done | bytes 1048608 | tf_op jit(solution)/shard_map/ppermute | solution.py:124
  383.3 8.4 %collective-permute-done.1 = bf16[128,2048]{1,0:T(8,128)(2,1)S(1)} collective-permute-done((bf16[128,2048]{1,0:T(8,128)(2,1)S(1)}, bf16[128,2048]{1,0:T(8,128)(2,1)S(1)}, u32[]{:S(2)}, u32[]{:S(2)}) %collective-permute-start.1) | collective-permute-done | bytes 524320 | tf_op jit(solution)/shard_map/ppermute | solution.py:136
  391.7 77.6 %collective-permute-start.5 = (bf16[128,2048]{1,0:T(8,128)(2,1)}, bf16[128,2048]{1,0:T(8,128)(2,1)S(1)}, u32[]{:S(2)}, u32[]{:S(2)}) collective-permute-start(bf16[128,2048]{1,0:T(8,128)(2,1)} %add_convert_fusion.10), channel_id=1, source_target_pairs={{0,1},{1,2},{2,3},{3,0},{4,5},{5,6},{6,7},{7,4},{8,9},{9,10},{10,1... | collective-permute-start | bytes 1572872 | tf_op jit(solution)/shard_map/ppermute | solution.py:136
  471.7 6.5 second_norm_back.6
  478.2 6.6 second_norm_back.7
  509.0 6.5 second_norm_back.4
  520.8 6.5 second_norm_back.5
  532.5 9.8 %attend_backward.3 = (bf16[384,512]{1,0:T(8,128)(2,1)}, bf16[384,512]{1,0:T(8,128)(2,1)}) custom-call(s32[2]{0:T(128)} %get-tuple-element.227.scal_ref, bf16[384,1024]{1,0:T(8,128)(2,1)} %get-tuple-element.193.all_ref, bf16[256,1024]{1,0:T(8,128)(2,1)} %get-tuple-element.205.att_ref, f32[4,1024]{1,0:T(4,128)} %get-tuple-element.209.inv_ref, ...), custom_call_target="tpu_custom_call" | custom-call | flops 8053063680 | bytes 4718592 | tf_op jit(solution)/shard_map/attend_backward/pallas_call | solution.py:516
  543.5 10.1 %attend_backward.2 = (bf16[384,512]{1,0:T(8,128)(2,1)}, bf16[384,512]{1,0:T(8,128)(2,1)}) custom-call(s32[2]{0:T(128)} %get-tuple-element.226.scal_ref, bf16[384,1024]{1,0:T(8,128)(2,1)} %get-tuple-element.192.all_ref, bf16[256,1024]{1,0:T(8,128)(2,1)} %get-tuple-element.204.att_ref, f32[4,1024]{1,0:T(4,128)} %get-tuple-element.208.inv_ref, ...), custom_call_target="tpu_custom_call" | custom-call | flops 8053063680 | bytes 4718592 | tf_op jit(solution)/shard_map/attend_backward/pallas_call | solution.py:516
  554.4 7.5 query_key_value_back.3
  562.7 7.6 query_key_value_back.2
  587.1 30.7 %collective-permute-start.57 = (f32[1,768]{1,0:T(1,128)S(1)}, f32[1,768]{1,0:T(1,128)S(1)}, u32[]{:S(2)}, u32[]{:S(2)}) collective-permute-start(f32[1,768]{1,0:T(1,128)S(1)} %pad_maximum_fusion.18), channel_id=1, source_target_pairs={{0,2},{1,3},{2,0},{3,1},{4,6},{5,7},{6,4},{7,5},{8,10},{9,11},{10,... | collective-permute-start | bytes 9224 | tf_op jit(solution)/shard_map/ppermute | solution.py:1337
  634.6 9.4 %weight_grad.15 = bf16[1024,2048]{1,0:T(8,128)(2,1)} custom-call(bf16[256,2048]{1,0:T(8,128)(2,1)} %get-tuple-element.181.refs_0_, bf16[256,2048]{1,0:T(8,128)(2,1)} %get-tuple-element.180.refs_1_, bf16[256,2048]{1,0:T(8,128)(2,1)} %get-tuple-element.179.refs_2_, bf16[256,2048]{1,0:T(8,128)(2,1)} %get-tuple-element.178.refs_3_, ...), custom_call_target="tpu_custom_call" | custom-call | flops 4294967296 | bytes 10485760 | tf_op jit(solution)/shard_map/weight_grad/pallas_call | solution.py:688
  644.7 9.5 %weight_grad.17 = bf16[1024,2048]{1,0:T(8,128)(2,1)} custom-call(bf16[256,2048]{1,0:T(8,128)(2,1)} %get-tuple-element.181.refs_0_, bf16[256,2048]{1,0:T(8,128)(2,1)} %get-tuple-element.180.refs_1_, bf16[256,2048]{1,0:T(8,128)(2,1)} %get-tuple-element.179.refs_2_, bf16[256,2048]{1,0:T(8,128)(2,1)} %get-tuple-element.178.refs_3_, ...), custom_call_target="tpu_custom_call" | custom-call | flops 4294967296 | bytes 10485760 | tf_op jit(solution)/shard_map/weight_grad/pallas_call | solution.py:688
  659.9 9.3 %weight_grad.19 = bf16[2048,1024]{1,0:T(8,128)(2,1)} custom-call(bf16[256,2048]{1,0:T(8,128)(2,1)} %get-tuple-element.137.refs_0_, bf16[256,2048]{1,0:T(8,128)(2,1)} %get-tuple-element.138.refs_1_, bf16[256,2048]{1,0:T(8,128)(2,1)} %get-tuple-element.139.refs_2_, bf16[256,2048]{1,0:T(8,128)(2,1)} %get-tuple-element.140.refs_3_, ...), custom_call_target="tpu_custom_call" | custom-call | flops 4294967296 | bytes 10485760 | tf_op jit(solution)/shard_map/weight_grad/pallas_call | solution.py:688
  678.7 11.8 %collective-permute-done.37 = bf16[512,256]{1,0:T(8,128)(2,1)S(1)} collective-permute-done((bf16[512,256]{1,0:T(8,128)(2,1)S(1)}, bf16[512,256]{1,0:T(8,128)(2,1)S(1)}, u32[]{:S(2)}, u32[]{:S(2)}) %collective-permute-start.37) | collective-permute-done | bytes 262176 | tf_op jit(solution)/shard_map/ppermute | solution.py:74
  699.3 6.0 collective-permute-done.44
  722.2 11.0 %collective-permute-done.15 = bf16[128,2048]{1,0:T(8,128)(2,1)S(1)} collective-permute-done((bf16[128,2048]{1,0:T(8,128)(2,1)S(1)}, bf16[128,2048]{1,0:T(8,128)(2,1)S(1)}, u32[]{:S(2)}, u32[]{:S(2)}) %collective-permute-start.15) | collective-permute-done | bytes 524320 | tf_op jit(solution)/shard_map/ppermute | solution.py:136
  735.9 8.6 %collective-permute-done.27.got_ref = bf16[128,2048]{1,0:T(8,128)(2,1)S(1)} collective-permute-done((bf16[128,2048]{1,0:T(8,128)(2,1)S(1)}, bf16[128,2048]{1,0:T(8,128)(2,1)S(1)}, u32[]{:S(2)}, u32[]{:S(2)}) %collective-permute-start.27) | collective-permute-done | bytes 524320 | tf_op jit(solution)/shard_map/ppermute | solution.py:136
  779.5 17.0 %collective-permute-done.45 = bf16[256,2048]{1,0:T(8,128)(2,1)S(1)} collective-permute-done((bf16[256,2048]{1,0:T(8,128)(2,1)S(1)}, bf16[256,2048]{1,0:T(8,128)(2,1)S(1)}, u32[]{:S(2)}, u32[]{:S(2)}) %collective-permute-start.45) | collective-permute-done | bytes 1048608 | tf_op jit(solution)/shard_map/ppermute | solution.py:70
  799.6 17.1 %collective-permute-done.50 = bf16[2048,256]{1,0:T(8,128)(2,1)S(1)} collective-permute-done((bf16[2048,256]{1,0:T(8,128)(2,1)S(1)}, bf16[2048,256]{1,0:T(8,128)(2,1)S(1)}, u32[]{:S(2)}, u32[]{:S(2)}) %collective-permute-start.50) | collective-permute-done | bytes 1048608 | tf_op jit(solution)/shard_map/ppermute | solution.py:70
  (340 shorter events, 222.3 us)
Async XLA Ops:
  218.3 107.0 %collective-permute-start.3 = (bf16[128,2048]{1,0:T(8,128)(2,1)}, bf16[128,2048]{1,0:T(8,128)(2,1)}, u32[]{:S(2)}, u32[]{:S(2)}) collective-permute-start(bf16[128,2048]{1,0:T(8,128)(2,1)} %dynamic-slice_select_fusion), channel_id=1, source_target_pairs={{0,1},{1,2},{2,3},{3,0},{4,5},{5,6},{6,7},{7,4},{8,9},{9,10},{10,1... | collective-permute-start | bytes 1572872 | tf_op jit(solution)/shard_map/ppermute | solution.py:136
  263.0 65.4 %collective-permute-start = (bf16[128,2048]{1,0:T(8,128)(2,1)}, bf16[128,2048]{1,0:T(8,128)(2,1)}, u32[]{:S(2)}, u32[]{:S(2)}) collective-permute-start(bf16[128,2048]{1,0:T(8,128)(2,1)} %dynamic-slice_select_fusion.1), channel_id=1, source_target_pairs={{0,1},{1,2},{2,3},{3,0},{4,5},{5,6},{6,7},{7,4},{8,9},{9,10},{10,1... | collective-permute-start | bytes 1572872 | tf_op jit(solution)/shard_map/ppermute | solution.py:136
  263.0 66.8 %collective-permute-start.17 = (bf16[256,2048]{1,0:T(8,128)(2,1)}, bf16[256,2048]{1,0:T(8,128)(2,1)}, u32[]{:S(2)}, u32[]{:S(2)}) collective-permute-start(bf16[256,2048]{1,0:T(8,128)(2,1)} %get-tuple-element.114.refs_0_), channel_id=1, source_target_pairs={{0,1},{3,2},{4,5},{7,6},{8,9},{11,10},{12,13},{15,14},{16,17},{19,... | collective-permute-start | bytes 3145736 | tf_op jit(solution)/shard_map/ppermute | solution.py:124
  268.5 63.3 %collective-permute-start.20 = (bf16[256,2048]{1,0:T(8,128)(2,1)S(1)}, bf16[256,2048]{1,0:T(8,128)(2,1)}, u32[]{:S(2)}, u32[]{:S(2)}) collective-permute-start(bf16[256,2048]{1,0:T(8,128)(2,1)S(1)} %copy-done.4), channel_id=1, source_target_pairs={{0,1},{3,2},{4,5},{7,6},{8,9},{11,10},{12,13},{15,14},{16,17},{19,... | collective-permute-start | bytes 3145736 | tf_op jit(solution)/shard_map/ppermute | solution.py:124
  270.9 72.0 %collective-permute-start.6 = (bf16[256,2048]{1,0:T(8,128)(2,1)S(1)}, bf16[256,2048]{1,0:T(8,128)(2,1)}, u32[]{:S(2)}, u32[]{:S(2)}) collective-permute-start(bf16[256,2048]{1,0:T(8,128)(2,1)S(1)} %copy-done.3), channel_id=1, source_target_pairs={{0,1},{3,2},{4,5},{7,6},{8,9},{11,10},{12,13},{15,14},{16,17},{19,... | collective-permute-start | bytes 3145736 | tf_op jit(solution)/shard_map/ppermute | solution.py:124
  325.3 40.1 %collective-permute-start.9 = (bf16[256,2048]{1,0:T(8,128)(2,1)S(1)}, bf16[256,2048]{1,0:T(8,128)(2,1)S(1)}, u32[]{:S(2)}, u32[]{:S(2)}) collective-permute-start(bf16[256,2048]{1,0:T(8,128)(2,1)S(1)} %copy-done.2), channel_id=1, source_target_pairs={{0,1},{3,2},{4,5},{7,6},{8,9},{11,10},{12,13},{15,14},{16,17},{19,... | collective-permute-start | bytes 3145736 | tf_op jit(solution)/shard_map/ppermute | solution.py:124
  328.4 52.5 %collective-permute-start.4 = (bf16[128,2048]{1,0:T(8,128)(2,1)S(1)}, bf16[128,2048]{1,0:T(8,128)(2,1)S(1)}, u32[]{:S(2)}, u32[]{:S(2)}) collective-permute-start(bf16[128,2048]{1,0:T(8,128)(2,1)S(1)} %add_convert_fusion.11), channel_id=1, source_target_pairs={{0,1},{1,2},{2,3},{3,0},{4,5},{5,6},{6,7},{7,4},{8,9},{9,10},{10,1... | collective-permute-start | bytes 1572872 | tf_op jit(solution)/shard_map/ppermute | solution.py:136
  329.8 61.9 %collective-permute-start.1 = (bf16[128,2048]{1,0:T(8,128)(2,1)S(1)}, bf16[128,2048]{1,0:T(8,128)(2,1)S(1)}, u32[]{:S(2)}, u32[]{:S(2)}) collective-permute-start(bf16[128,2048]{1,0:T(8,128)(2,1)S(1)} %add_convert_fusion.13), channel_id=1, source_target_pairs={{0,1},{1,2},{2,3},{3,0},{4,5},{5,6},{6,7},{7,4},{8,9},{9,10},{10,1... | collective-permute-start | bytes 1572872 | tf_op jit(solution)/shard_map/ppermute | solution.py:136
  331.8 34.7 %collective-permute-start.18 = (bf16[256,2048]{1,0:T(8,128)(2,1)S(1)}, bf16[256,2048]{1,0:T(8,128)(2,1)S(1)}, u32[]{:S(2)}, u32[]{:S(2)}) collective-permute-start(bf16[256,2048]{1,0:T(8,128)(2,1)S(1)} %fusion.4), channel_id=1, source_target_pairs={{1,2},{2,1},{5,6},{6,5},{9,10},{10,9},{13,14},{14,13},{17,18},{18,... | collective-permute-start | bytes 3145736 | tf_op jit(solution)/shard_map/ppermute | solution.py:126
  368.9 100.7 %collective-permute-start.19 = (bf16[256,2048]{1,0:T(8,128)(2,1)S(1)}, bf16[256,2048]{1,0:T(8,128)(2,1)S(1)}, u32[]{:S(2)}, u32[]{:S(2)}) collective-permute-start(bf16[256,2048]{1,0:T(8,128)(2,1)S(1)} %fusion.5), channel_id=1, source_target_pairs={{1,0},{2,3},{5,4},{6,7},{9,8},{10,11},{13,12},{14,15},{17,16},{18,... | collective-permute-start | bytes 3145736 | tf_op jit(solution)/shard_map/ppermute | solution.py:128
  371.6 106.6 %collective-permute-start.22 = (bf16[256,2048]{1,0:T(8,128)(2,1)}, bf16[256,2048]{1,0:T(8,128)(2,1)}, u32[]{:S(2)}, u32[]{:S(2)}) collective-permute-start(bf16[256,2048]{1,0:T(8,128)(2,1)} %fusion.7), channel_id=1, source_target_pairs={{1,0},{2,3},{5,4},{6,7},{9,8},{10,11},{13,12},{14,15},{17,16},{18,... | collective-permute-start | bytes 3145736 | tf_op jit(solution)/shard_map/ppermute | solution.py:128
  374.3 134.1 %collective-permute-start.8 = (bf16[256,2048]{1,0:T(8,128)(2,1)}, bf16[256,2048]{1,0:T(8,128)(2,1)}, u32[]{:S(2)}, u32[]{:S(2)}) collective-permute-start(bf16[256,2048]{1,0:T(8,128)(2,1)} %fusion.1), channel_id=1, source_target_pairs={{1,0},{2,3},{5,4},{6,7},{9,8},{10,11},{13,12},{14,15},{17,16},{18,... | collective-permute-start | bytes 3145736 | tf_op jit(solution)/shard_map/ppermute | solution.py:128
  381.0 138.9 %collective-permute-start.11 = (bf16[256,2048]{1,0:T(8,128)(2,1)}, bf16[256,2048]{1,0:T(8,128)(2,1)S(1)}, u32[]{:S(2)}, u32[]{:S(2)}) collective-permute-start(bf16[256,2048]{1,0:T(8,128)(2,1)} %fusion.3), channel_id=1, source_target_pairs={{1,0},{2,3},{5,4},{6,7},{9,8},{10,11},{13,12},{14,15},{17,16},{18,... | collective-permute-start | bytes 3145736 | tf_op jit(solution)/shard_map/ppermute | solution.py:128
  391.7 109.4 %collective-permute-start.5 = (bf16[128,2048]{1,0:T(8,128)(2,1)}, bf16[128,2048]{1,0:T(8,128)(2,1)S(1)}, u32[]{:S(2)}, u32[]{:S(2)}) collective-permute-start(bf16[128,2048]{1,0:T(8,128)(2,1)} %add_convert_fusion.10), channel_id=1, source_target_pairs={{0,1},{1,2},{2,3},{3,0},{4,5},{5,6},{6,7},{7,4},{8,9},{9,10},{10,1... | collective-permute-start | bytes 1572872 | tf_op jit(solution)/shard_map/ppermute | solution.py:136
  489.1 42.7 %collective-permute-start.23 = (bf16[256,512]{1,0:T(8,128)(2,1)}, bf16[256,512]{1,0:T(8,128)(2,1)S(1)}, u32[]{:S(2)}, u32[]{:S(2)}) collective-permute-start(bf16[256,512]{1,0:T(8,128)(2,1)} %get-tuple-element.119), channel_id=1, source_target_pairs={{0,4},{4,0},{1,5},{5,1},{2,6},{6,2},{3,7},{7,3},{8,12},{12,8},{9,1... | collective-permute-start | bytes 786440 | tf_op jit(solution)/shard_map/ppermute | solution.py:78
  495.1 139.4 %collective-permute-start.38 = (bf16[1024,2048]{1,0:T(8,128)(2,1)}, bf16[1024,2048]{1,0:T(8,128)(2,1)}, u32[]{:S(2)}, u32[]{:S(2)}) collective-permute-start(bf16[1024,2048]{1,0:T(8,128)(2,1)} %weight_grad.14), channel_id=1, source_target_pairs={{0,4},{4,0},{1,5},{5,1},{2,6},{6,2},{3,7},{7,3},{8,12},{12,8},{9,1... | collective-permute-start | bytes 12582920 | tf_op jit(solution)/shard_map/ppermute | solution.py:78
  501.1 142.9 %collective-permute-start.43 = (bf16[1024,2048]{1,0:T(8,128)(2,1)}, bf16[1024,2048]{1,0:T(8,128)(2,1)}, u32[]{:S(2)}, u32[]{:S(2)}) collective-permute-start(bf16[1024,2048]{1,0:T(8,128)(2,1)} %weight_grad.16), channel_id=1, source_target_pairs={{0,4},{4,0},{1,5},{5,1},{2,6},{6,2},{3,7},{7,3},{8,12},{12,8},{9,1... | collective-permute-start | bytes 12582920 | tf_op jit(solution)/shard_map/ppermute | solution.py:78
  508.4 150.2 %collective-permute-start.48 = (bf16[2048,1024]{1,0:T(8,128)(2,1)}, bf16[2048,1024]{1,0:T(8,128)(2,1)}, u32[]{:S(2)}, u32[]{:S(2)}) collective-permute-start(bf16[2048,1024]{1,0:T(8,128)(2,1)} %weight_grad.18), channel_id=1, source_target_pairs={{0,4},{4,0},{1,5},{5,1},{2,6},{6,2},{3,7},{7,3},{8,12},{12,8},{9,1... | collective-permute-start | bytes 12582920 | tf_op jit(solution)/shard_map/ppermute | solution.py:78
  579.6 47.6 %collective-permute-start.33 = (bf16[512,1024]{1,0:T(8,128)(2,1)}, bf16[512,1024]{1,0:T(8,128)(2,1)S(1)}, u32[]{:S(2)}, u32[]{:S(2)}) collective-permute-start(bf16[512,1024]{1,0:T(8,128)(2,1)} %weight_grad.12), channel_id=1, source_target_pairs={{0,4},{4,0},{1,5},{5,1},{2,6},{6,2},{3,7},{7,3},{8,12},{12,8},{9,1... | collective-permute-start | bytes 3145736 | tf_op jit(solution)/shard_map/ppermute | solution.py:78
  587.1 35.4 %collective-permute-start.57 = (f32[1,768]{1,0:T(1,128)S(1)}, f32[1,768]{1,0:T(1,128)S(1)}, u32[]{:S(2)}, u32[]{:S(2)}) collective-permute-start(f32[1,768]{1,0:T(1,128)S(1)} %pad_maximum_fusion.18), channel_id=1, source_target_pairs={{0,2},{1,3},{2,0},{3,1},{4,6},{5,7},{6,4},{7,5},{8,10},{9,11},{10,... | collective-permute-start | bytes 9224 | tf_op jit(solution)/shard_map/ppermute | solution.py:1337
  622.5 51.8 %collective-permute-start.25 = (bf16[128,2048]{1,0:T(8,128)(2,1)}, bf16[128,2048]{1,0:T(8,128)(2,1)}, u32[]{:S(2)}, u32[]{:S(2)}) collective-permute-start(bf16[128,2048]{1,0:T(8,128)(2,1)} %constant_dynamic-slice_fusion), channel_id=1, source_target_pairs={{0,1},{1,2},{2,3},{3,0},{4,5},{5,6},{6,7},{7,4},{8,9},{9,10},{10,1... | collective-permute-start | bytes 1572872 | tf_op jit(solution)/shard_map/ppermute | solution.py:136
  627.3 48.9 %collective-permute-start.14 = (bf16[128,2048]{1,0:T(8,128)(2,1)}, bf16[128,2048]{1,0:T(8,128)(2,1)}, u32[]{:S(2)}, u32[]{:S(2)}) collective-permute-start(bf16[128,2048]{1,0:T(8,128)(2,1)} %constant_dynamic-slice_fusion.1), channel_id=1, source_target_pairs={{0,1},{1,2},{2,3},{3,0},{4,5},{5,6},{6,7},{7,4},{8,9},{9,10},{10,1... | collective-permute-start | bytes 1572872 | tf_op jit(solution)/shard_map/ppermute | solution.py:136
  634.6 121.6 %collective-permute-start.28 = (bf16[1024,768]{1,0:T(8,128)(2,1)}, bf16[1024,768]{1,0:T(8,128)(2,1)}, u32[]{:S(2)}, u32[]{:S(2)}) collective-permute-start(bf16[1024,768]{1,0:T(8,128)(2,1)} %weight_grad.10), channel_id=1, source_target_pairs={{0,4},{4,0},{1,5},{5,1},{2,6},{6,2},{3,7},{7,3},{8,12},{12,8},{9,1... | collective-permute-start | bytes 4718600 | tf_op jit(solution)/shard_map/ppermute | solution.py:78
  644.0 27.0 %collective-permute-start.34 = (bf16[256,256]{1,0:T(8,128)(2,1)}, bf16[256,256]{1,0:T(8,128)(2,1)S(1)}, u32[]{:S(2)}, u32[]{:S(2)}) collective-permute-start(bf16[256,256]{1,0:T(8,128)(2,1)} %get-tuple-element.197), channel_id=1, source_target_pairs={{0,16},{8,24},{16,0},{24,8},{1,17},{9,25},{17,1},{25,9},{2,18},{10... | collective-permute-start | bytes 393224 | tf_op jit(solution)/shard_map/ppermute | solution.py:74
  706.1 27.1 %collective-permute-start.15 = (bf16[128,2048]{1,0:T(8,128)(2,1)S(1)}, bf16[128,2048]{1,0:T(8,128)(2,1)S(1)}, u32[]{:S(2)}, u32[]{:S(2)}) collective-permute-start(bf16[128,2048]{1,0:T(8,128)(2,1)S(1)} %add_convert_fusion.9), channel_id=1, source_target_pairs={{0,1},{1,2},{2,3},{3,0},{4,5},{5,6},{6,7},{7,4},{8,9},{9,10},{10,1... | collective-permute-start | bytes 1572872 | tf_op jit(solution)/shard_map/ppermute | solution.py:136
  714.6 58.1 %collective-permute-start.42 = (bf16[256,2048]{1,0:T(8,128)(2,1)}, bf16[256,2048]{1,0:T(8,128)(2,1)}, u32[]{:S(2)}, u32[]{:S(2)}) collective-permute-start(bf16[256,2048]{1,0:T(8,128)(2,1)} %pad_maximum_fusion.3), channel_id=1, source_target_pairs={{0,16},{8,24},{16,0},{24,8},{1,17},{9,25},{17,1},{25,9},{2,18},{10... | collective-permute-start | bytes 3145736 | tf_op jit(solution)/shard_map/ppermute | solution.py:74
  715.3 58.5 %collective-permute-start.40 = (bf16[256,2048]{1,0:T(8,128)(2,1)}, bf16[256,2048]{1,0:T(8,128)(2,1)}, u32[]{:S(2)}, u32[]{:S(2)}) collective-permute-start(bf16[256,2048]{1,0:T(8,128)(2,1)} %pad_maximum_fusion.2), channel_id=1, source_target_pairs={{0,8},{8,0},{16,24},{24,16},{1,9},{9,1},{17,25},{25,17},{2,10},{10... | collective-permute-start | bytes 3145736 | tf_op jit(solution)/shard_map/ppermute | solution.py:70
  745.3 33.4 %collective-permute-start.47 = (bf16[256,2048]{1,0:T(8,128)(2,1)}, bf16[256,2048]{1,0:T(8,128)(2,1)S(1)}, u32[]{:S(2)}, u32[]{:S(2)}) collective-permute-start(bf16[256,2048]{1,0:T(8,128)(2,1)} %pad_maximum_fusion.5), channel_id=1, source_target_pairs={{0,16},{8,24},{16,0},{24,8},{1,17},{9,25},{17,1},{25,9},{2,18},{10... | collective-permute-start | bytes 3145736 | tf_op jit(solution)/shard_map/ppermute | solution.py:74
  771.5 28.1 %collective-permute-start.52 = (bf16[2048,256]{1,0:T(8,128)(2,1)S(1)}, bf16[2048,256]{1,0:T(8,128)(2,1)S(1)}, u32[]{:S(2)}, u32[]{:S(2)}) collective-permute-start(bf16[2048,256]{1,0:T(8,128)(2,1)S(1)} %pad_maximum_fusion.7), channel_id=1, source_target_pairs={{0,16},{8,24},{16,0},{24,8},{1,17},{9,25},{17,1},{25,9},{2,18},{10... | collective-permute-start | bytes 3145736 | tf_op jit(solution)/shard_map/ppermute | solution.py:74
  772.7 44.0 %collective-permute-start.50 = (bf16[2048,256]{1,0:T(8,128)(2,1)S(1)}, bf16[2048,256]{1,0:T(8,128)(2,1)S(1)}, u32[]{:S(2)}, u32[]{:S(2)}) collective-permute-start(bf16[2048,256]{1,0:T(8,128)(2,1)S(1)} %copy-done.28), channel_id=1, source_target_pairs={{0,8},{8,0},{16,24},{24,16},{1,9},{9,1},{17,25},{25,17},{2,10},{10... | collective-permute-start | bytes 3145736 | tf_op jit(solution)/shard_map/ppermute | solution.py:70
  773.9 45.9 %collective-permute-start.32 = (bf16[256,768]{1,0:T(8,128)(2,1)S(1)}, bf16[256,768]{1,0:T(8,128)(2,1)S(1)}, u32[]{:S(2)}, u32[]{:S(2)}) collective-permute-start(bf16[256,768]{1,0:T(8,128)(2,1)S(1)} %pad_maximum_fusion.10), channel_id=1, source_target_pairs={{0,16},{8,24},{16,0},{24,8},{1,17},{9,25},{17,1},{25,9},{2,18},{10... | collective-permute-start | bytes 1179656 | tf_op jit(solution)/shard_map/ppermute | solution.py:74
  778.7 42.3 %collective-permute-start.30 = (bf16[256,768]{1,0:T(8,128)(2,1)S(1)}, bf16[256,768]{1,0:T(8,128)(2,1)S(1)}, u32[]{:S(2)}, u32[]{:S(2)}) collective-permute-start(bf16[256,768]{1,0:T(8,128)(2,1)S(1)} %pad_maximum_fusion.9), channel_id=1, source_target_pairs={{0,8},{8,0},{16,24},{24,16},{1,9},{9,1},{17,25},{25,17},{2,10},{10... | collective-permute-start | bytes 1179656 | tf_op jit(solution)/shard_map/ppermute | solution.py:70
  (81 other events, 747.0 us)

commit v3 on v2

--- a/solution.py
+++ b/solution.py
@@ -14,6 +14,7 @@
 rope_base = 1000000.0
 log2e = 1.4426950408889634
 VMEM_BYTES = 60 * 1024 * 1024
+VMEM_MOST = 63 * 1024 * 1024
 PARAMS = pltpu.CompilerParams(vmem_limit_bytes=VMEM_BYTES)
 SMEM = pl.BlockSpec(memory_space=pltpu.SMEM)
 SWAP = ((0, 1), (1, 0))
@@ -782,7 +783,7 @@
     xr_hbm, n1_hbm, gf_hbm, qkv_hbm, out_hbm, gate_hbm, up_hbm, down_hbm, hidden_hbm, n2_hbm,
     gains_ref, pre_ref, all_ref, att_ref, inv_ref, tok_ref, stat_ref,
     xr_v, cot_v, n1_v, qkv_v, out_v, ex_own, ex_send, ex_got, at_own, at_send, at_got,
-    part_v, in_v, back_v, pair_v, total_v, hid_v, norm_v,
+    part_v, in_v, back_v, total_v, hid_v, norm_v,
     load_sem, store_sem, wsend, wrecv, wloc, gsend, grecv, exsend, exrecv, zsend, zrecv, hid_sem,
 ):
     seqs, span, width = xr_v.shape
@@ -791,7 +792,6 @@
     start = core * span
     near = [row, xor_one(row), (row + 2) % 4, 3 - row]
     inner = (rank % 3) != 0
-    outer = (rank % 3) == 0
     near_x, near_y, near_core = {"dp": near[1]}, {"dp": near[2]}, {"context": 1 - core}
     z_side, z_mid = {"tensor": xor_one(rank)}, {"tensor": 3 - rank}
     piece = width // 8
@@ -839,15 +839,14 @@
         copy.wait()
 
     def mask_rows(i, carry):
-        s, t = i // per, i % per
-        cut = pl.ds(pl.multiple_of(t * sub, sub), sub)
-        place = start + t * sub + lax.broadcasted_iota(jnp.int32, (sub, 1), 0)
-        length = len_ref[s]
-        valid = (place < length).astype(F32)
+        s, t = i // (span // 16), i % (span // 16)
+        cut = pl.ds(pl.multiple_of(t * 16, 16), 16)
+        place = start + t * 16 + lax.broadcasted_iota(jnp.int32, (16, 1), 0)
+        valid = (place < len_ref[s]).astype(F32)
         cot_v[s, cut, :] = (cot_v[s, cut, :].astype(F32) * valid).astype(BF16)
         return carry
 
-    lax.fori_loop(0, total_subs, mask_rows, 0)
+    lax.fori_loop(0, seqs * span // 16, mask_rows, 0)
     store_gf = pltpu.make_async_copy(cot_v, gf_hbm, store_sem.at[0])
     store_gf.start()
     for copy in loads[: len(loads) // 2]:
@@ -860,13 +859,13 @@
     gain2 = jnp.concatenate([gains_ref[b, 1:2, :] for b in range(8)], axis=1).astype(F32)
 
     def norm_rows(i, carry):
-        s, t = i // per, i % per
-        cut = pl.ds(pl.multiple_of(t * sub, sub), sub)
+        s, t = i // (span // 16), i % (span // 16)
+        cut = pl.ds(pl.multiple_of(t * 16, 16), 16)
         x = xr_v[s, cut, :].astype(F32)
         n1_v[s, cut, :] = (x * inverse_rms(x) * gain1).astype(BF16)
         return carry
 
-    lax.fori_loop(0, total_subs, norm_rows, 0)
+    lax.fori_loop(0, seqs * span // 16, norm_rows, 0)
     store_n1 = pltpu.make_async_copy(n1_v, n1_hbm, store_sem.at[2])
     store_n1.start()
     w_qkv.second()
@@ -957,14 +956,7 @@
     store_out = pltpu.make_async_copy(out_v, out_hbm, store_sem.at[4])
     store_out.start()
 
-    def hop_in(u):
-        return remote(part_v.at[u], in_v.at[u], zsend.at[0, u], zrecv.at[0, u], z_side)
-
-    def hop_mid(u):
-        return remote(pair_v.at[u], back_v.at[u], zsend.at[1, u], zrecv.at[1, u], z_mid)
-
-    def hop_out(u):
-        return remote(in_v.at[u], back_v.at[u], zsend.at[2, u], zrecv.at[2, u], z_side)
+    moving = Chain(rank, part_v, in_v, back_v, zsend, zrecv)
 
     def branch_rows(s, carry):
         give(s).wait_recv()
@@ -977,17 +969,13 @@
             part_v[u, :, :half] = dot_nn(rows, out_v[0]).astype(BF16)
             part_v[u, :, half:] = dot_nn(rows, out_v[1]).astype(BF16)
 
-            @pl.when(outer)
-            def _():
-                hop_in(u).start()
-
+            moving.begin(u)
         return carry
 
     lax.fori_loop(0, seqs, branch_rows, 0)
     w_gate.second()
     w_down.first()
     stat_ref[...] = jnp.zeros_like(stat_ref)
-    line = lax.broadcasted_iota(jnp.int32, (8, 128), 0)
 
     def hidden_store(u):
         cut = pl.ds(pl.multiple_of(u * sub, sub), sub)
@@ -1000,47 +988,33 @@
         s, t = u // per, u % per
         cut = pl.ds(pl.multiple_of(t * sub, sub), sub)
 
-        @pl.when(inner)
-        def _():
-            total_v[...] = pair_v[u].astype(F32) + back_v[u].astype(F32)
-
-        @pl.when(outer)
-        def _():
-            hop_out(u).wait_recv()
-            total_v[...] = part_v[u].astype(F32) + back_v[u].astype(F32)
+        moving.total(u, total_v)
 
         @pl.when(u >= 2)
         def _():
             for copy in hidden_store(u - 2):
                 copy.wait()
 
-        total = total_v[...]
-        resid = xr_v[s, cut, :].astype(F32)
-        hidden = resid + total
-        hid_v[u % 2] = hidden
-        norm_v[u % 2] = (hidden * inverse_rms(hidden) * gain2).astype(BF16)
+        length = len_ref[s]
+
+        def body(piece_rows, first):
+            total = total_v[piece_rows, :]
+            resid = xr_v[s, pl.ds(pl.multiple_of(t * sub + first, 16), 16), :].astype(F32)
+            hidden = resid + total
+            hid_v[u % 2, piece_rows, :] = hidden
+            norm_v[u % 2, piece_rows, :] = (hidden * inverse_rms(hidden) * gain2).astype(BF16)
+            place = start + t * sub + first + lax.broadcasted_iota(jnp.int32, (16, 1), 0)
+            valid = (place < length).astype(F32)
+            stat_ref[0] += fold_lanes(valid * resid * resid)
+            stat_ref[1] += fold_lanes(valid * total * total)
+
+        by_pieces(sub, body)
         for copy in hidden_store(u):
             copy.start()
-        length = len_ref[s]
-        place = start + t * sub + lax.broadcasted_iota(jnp.int32, (sub, 1), 0)
-        valid = (place < length).astype(F32)
-        one = jnp.sum(valid * resid * resid, keepdims=True)
-        two = jnp.sum(valid * total * total, keepdims=True)
-        stat_ref[...] += jnp.where(line == 0, one, jnp.where(line == 1, two, 0.0))
 
     def chain(i, carry):
-        @pl.when((i < total_subs) & inner)
-        def _():
-            hop_in(i).wait_recv()
-            pair_v[i] = (part_v[i].astype(F32) + in_v[i].astype(F32)).astype(BF16)
-            hop_mid(i).start()
-
-        @pl.when((i >= 1) & (i < total_subs + 1) & inner)
-        def _():
-            u = i - 1
-            hop_mid(u).wait_recv()
-            in_v[u] = (part_v[u].astype(F32) + back_v[u].astype(F32)).astype(BF16)
-            hop_out(u).start()
+        moving.middle(i)
+        moving.outward(i - 1)
 
         @pl.when(i >= 2)
         def _():
@@ -1064,19 +1038,7 @@
         for copy in hidden_store(u):
             copy.wait()
 
-    def settle(u, carry):
-        @pl.when(outer)
-        def _():
-            hop_in(u).wait_send()
-
-        @pl.when(inner)
-        def _():
-            hop_mid(u).wait_send()
-            hop_out(u).wait_send()
-
-        return carry
-
-    lax.fori_loop(0, total_subs, settle, 0)
+    moving.settle()
     for s in range(seqs):
         exchange(s).wait_send()
         give(s).wait_send()
@@ -1112,7 +1074,7 @@
     small = [
         shape((8,) + gains.shape, BF16), shape((seqs, (nq + nk) * hd, span), F32), shape((seqs, rows, 2 * span), BF16),
         shape((seqs, groups * hd, 2 * span), BF16), shape((seqs, groups, 2 * span), F32), shape((seqs, span, nq * hd), BF16),
-        shape((8, 128), F32),
+        shape((2, 8, 128), F32),
     ]
     dma = pltpu.SemaphoreType.DMA
     ex = pltpu.VMEM((seqs, rows, span), BF16)
@@ -1128,7 +1090,7 @@
             pltpu.VMEM(wide, BF16), pltpu.VMEM(wide, BF16), pltpu.VMEM(wide, BF16),
             pltpu.VMEM((2, half, cols), BF16), pltpu.VMEM((2, w_out.shape[0], half), BF16),
             ex, ex, ex, at, at, at,
-            moving, moving, moving, moving,
+            moving, moving, moving,
             pltpu.VMEM((sub, width), F32), pltpu.VMEM((2, sub, width), F32), pltpu.VMEM((2, sub, width), BF16),
             dma((2, seqs, 8)), dma((5,)), dma((5, 8)), dma((5, 8)), dma((5,)), dma((8,)), dma((8,)),
             dma((2, seqs)), dma((2, seqs)), dma((3, subs)), dma((3, subs)), dma((2, 2)),
@@ -1137,6 +1099,366 @@
         cost_estimate=cost(flops, 80 * seqs * span * width),
         name="attention_forward",
     )(lengths, x, cot, w_qkv, w_out, w_gate, w_up, w_down, gains, cosine, sine, qgain, kgain)
+
+
+def by_pieces(count, body, size=16):
+    def one(p, carry):
+        body(pl.ds(pl.multiple_of(p * size, size), size), p * size)
+        return carry
+
+    lax.fori_loop(0, count // size, one, 0)
+
+
+def fold_lanes(values):
+    tiles = values[:8] + values[8:]
+    return sum(tiles[:, k * 128 : (k + 1) * 128] for k in range(tiles.shape[1] // 128))
+
+
+class Chain:
+    def __init__(self, rank, part, arrive, back, send, recv):
+        self.inner = (rank % 3) != 0
+        self.outer = (rank % 3) == 0
+        self.part, self.arrive, self.back = part, arrive, back
+        self.send, self.recv = send, recv
+        self.side, self.mid = {"tensor": xor_one(rank)}, {"tensor": 3 - rank}
+        self.count = part.shape[0]
+
+    def hop_in(self, u):
+        return remote(self.part.at[u], self.arrive.at[u], self.send.at[0, u], self.recv.at[0, u], self.side)
+
+    def hop_mid(self, u):
+        return remote(self.arrive.at[u], self.back.at[u], self.send.at[1, u], self.recv.at[1, u], self.mid)
+
+    def hop_out(self, u):
+        return remote(self.part.at[u], self.back.at[u], self.send.at[2, u], self.recv.at[2, u], self.side)
+
+    def add(self, into, one, two, u):
+        def body(cut, first):
+            into[u, cut, :] = (one[u, cut, :].astype(F32) + two[u, cut, :].astype(F32)).astype(BF16)
+
+        by_pieces(self.part.shape[1], body)
+
+    def begin(self, u):
+        @pl.when(self.outer)
+        def _():
+            self.hop_in(u).start()
+
+    def middle(self, u):
+        @pl.when((u >= 0) & (u < self.count) & self.inner)
+        def _():
+            self.hop_in(u).wait_recv()
+            self.add(self.arrive, self.part, self.arrive, u)
+            self.hop_mid(u).start()
+
+    def outward(self, u):
+        @pl.when((u >= 0) & (u < self.count) & self.inner)
+        def _():
+            self.hop_mid(u).wait_recv()
+            self.add(self.part, self.part, self.back, u)
+            self.hop_out(u).start()
+
+    def total(self, u, into):
+        @pl.when(self.inner)
+        def _():
+            def body(cut, first):
+                into[cut, :] = self.arrive[u, cut, :].astype(F32) + self.back[u, cut, :].astype(F32)
+
+            by_pieces(self.part.shape[1], body)
+
+        @pl.when(self.outer)
+        def _():
+            self.hop_out(u).wait_recv()
+
+            def body(cut, first):
+                into[cut, :] = self.part[u, cut, :].astype(F32) + self.back[u, cut, :].astype(F32)
+
+            by_pieces(self.part.shape[1], body)
+
+    def settle(self):
+        def one(u, carry):
+            @pl.when(self.outer)
+            def _():
+                self.hop_in(u).wait_send()
+
+            @pl.when(self.inner)
+            def _():
+                self.hop_mid(u).wait_send()
+                self.hop_out(u).wait_send()
+
+            return carry
+
+        lax.fori_loop(0, self.count, one, 0)
+
+
+def feed_both_kernel(
+    hb, sub, rows,
+    n2_hbm, gf_hbm, gate_hbm, up_hbm, down_hbm, hidden_hbm, gain_ref,
+    ffn_hbm, gb_hbm, gh_hbm, dgate_hbm, dup_hbm, ddown_hbm, gain_out,
+    n2_v, gf_v, inner_v, gg_v, gu_v, facc, gacc, wrow, wcol, part_v, in_v, back_v, total_v, hid_v, gh_v, gb_v, ffn_v, stage_row, stage_col,
+    load_sem, wsem, zsend, zrecv, hid_sem, out_sem, ffn_sem, csend, crecv, store_sem, free_sem,
+):
+    core, rank = lax.axis_index("context"), lax.axis_index("tensor")
+    near_core = {"context": 1 - core}
+    tokens, width = n2_v.shape
+    half = width // 2
+    hidden = inner_v.shape[1]
+    hsteps = hidden // hb
+    steps = tokens // rows * hsteps
+    per = rows // sub
+    chain = Chain(rank, part_v, in_v, back_v, zsend, zrecv)
+    subs = chain.count
+
+    def load_weights(i):
+        slot, h = i % 2, i % hsteps
+        cut = pl.ds(pl.multiple_of(h * hb, hb), hb)
+        copies = []
+        for side in range(2):
+            copies.append(pltpu.make_async_copy(gate_hbm.at[side, :, cut], wrow.at[slot, 0, side], wsem.at[slot, side]))
+            copies.append(pltpu.make_async_copy(up_hbm.at[side, :, cut], wrow.at[slot, 1, side], wsem.at[slot, 2 + side]))
+            copies.append(pltpu.make_async_copy(down_hbm.at[side, cut, :], wcol.at[slot, side], wsem.at[slot, 4 + side]))
+        return copies
+
+    def load_hidden(u):
+        cut = pl.ds(pl.multiple_of(u * sub, sub), sub)
+        return pltpu.make_async_copy(hidden_hbm.at[cut, :], hid_v.at[u % 2], hid_sem.at[u % 2])
+
+    loads = [pltpu.make_async_copy(n2_hbm, n2_v, load_sem.at[0]), pltpu.make_async_copy(gf_hbm, gf_v, load_sem.at[1])]
+    for copy in loads + load_weights(0):
+        copy.start()
+    for u in range(2):
+        load_hidden(u).start()
+    greet([(None, chain.side), (chain.inner, chain.mid), (None, near_core)])
+    gain_out[...] = jnp.zeros_like(gain_out)
+    for copy in loads:
+        copy.wait()
+
+    def stores(u):
+        cut = pl.ds(pl.multiple_of(u * sub, sub), sub)
+        return (
+            pltpu.make_async_copy(gh_v.at[u % 2], gh_hbm.at[cut, :], out_sem.at[0, u % 2]),
+            pltpu.make_async_copy(gb_v.at[u % 2], gb_hbm.at[cut, :], out_sem.at[1, u % 2]),
+        )
+
+    def finish(u):
+        chain.total(u, total_v)
+        load_hidden(u).wait()
+
+        @pl.when(u >= 2)
+        def _():
+            for copy in stores(u - 2):
+                copy.wait()
+
+        def body(piece_rows, first):
+            e = total_v[piece_rows, :]
+            hidden_rows = hid_v[u % 2, piece_rows, :]
+            inv = inverse_rms(hidden_rows)
+            hat = hidden_rows * inv
+            eg = e * gain_ref[...]
+            grad = gf_v[pl.ds(pl.multiple_of(u * sub + first, 16), 16), :].astype(F32)
+            gh = grad + inv * (eg - hat * jnp.mean(eg * hat, axis=-1, keepdims=True))
+            gh_v[u % 2, piece_rows, :] = gh
+            gb_v[u % 2, piece_rows, :] = gh.astype(BF16)
+            both = e * hat
+            gain_out[...] += both[:8] + both[8:]
+
+        by_pieces(sub, body)
+        for copy in stores(u):
+            copy.start()
+
+        @pl.when(u + 2 < subs)
+        def _():
+            load_hidden(u + 2).start()
+
+    def serve(k):
+        chain.middle(k - 3)
+        chain.outward(k - 4)
+
+        @pl.when((k >= 5) & (k < 5 + subs))
+        def _():
+            finish(k - 5)
+
+    def store_ffn(c):
+        return pltpu.make_async_copy(ffn_v, ffn_hbm.at[pl.ds(pl.multiple_of(c * rows, rows), rows), :], ffn_sem)
+
+    def step(i, carry):
+        slot, c, h = i % 2, i // hsteps, i % hsteps
+        for copy in load_weights(i):
+            copy.wait()
+
+        @pl.when(i + 1 < steps)
+        def _():
+            for copy in load_weights(i + 1):
+                copy.start()
+
+        here = pl.ds(pl.multiple_of(c * rows, rows), rows)
+        cols = pl.ds(pl.multiple_of(h * hb, hb), hb)
+        n, g = n2_v[here, :], gf_v[here, :]
+        wide = min(256, hb)
+        for q in range(hb // wide):
+            part = slice(q * wide, (q + 1) * wide)
+            gate = dot_nn(n[:, :half], wrow[slot, 0, 0, :, part]) + dot_nn(n[:, half:], wrow[slot, 0, 1, :, part])
+            up = dot_nn(n[:, :half], wrow[slot, 1, 0, :, part]) + dot_nn(n[:, half:], wrow[slot, 1, 1, :, part])
+            gi = dot_nt(g[:, :half], wcol[slot, 0, part, :]) + dot_nt(g[:, half:], wcol[slot, 1, part, :])
+            sig = jax.nn.sigmoid(gate)
+            silu = gate * sig
+            at = pl.ds(pl.multiple_of(h * hb + q * wide, wide), wide)
+            inner_v[here, at] = (silu * up).astype(BF16)
+            gg_v[here, at] = (gi * up * sig * (1.0 + gate * (1.0 - sig))).astype(BF16)
+            gu_v[here, at] = (gi * silu).astype(BF16)
+
+        @pl.when(h == 0)
+        def _():
+            facc[...] = jnp.zeros_like(facc)
+            gacc[...] = jnp.zeros_like(gacc)
+
+        inner, gg, gu = inner_v[here, cols], gg_v[here, cols], gu_v[here, cols]
+        span = min(512, half)
+        for side in range(2):
+            for q in range(half // span):
+                part = slice(q * span, (q + 1) * span)
+                cut = slice(side * half + q * span, side * half + (q + 1) * span)
+                facc[:, cut] += dot_nn(inner, wcol[slot, side, :, part])
+                gacc[:, cut] += dot_nt(gg, wrow[slot, 0, side, part, :]) + dot_nt(gu, wrow[slot, 1, side, part, :])
+
+        @pl.when(h == hsteps - 1)
+        def _():
+            for k in range(per):
+                part_v[c * per + k] = gacc[k * sub : (k + 1) * sub, :].astype(BF16)
+                chain.begin(c * per + k)
+
+            @pl.when(c > 0)
+            def _():
+                store_ffn(c - 1).wait()
+
+            ffn_v[...] = facc[...].astype(BF16)
+            store_ffn(c).start()
+
+        @pl.when(i % 2 == 0)
+        def _():
+            serve(i // 2)
+
+        return carry
+
+    lax.fori_loop(0, steps, step, 0)
+
+    pl.semaphore_signal(free_sem, inc=1, device_id=near_core, device_id_type=pl.DeviceIdType.MESH)
+    outs = (dgate_hbm, dup_hbm, ddown_hbm)
+
+    def landing(w, t):
+        return wrow.at[t // 2, w, t % 2] if w < 2 else wcol.at[t // 2, t % 2]
+
+    def landed(w, t, piece):
+        return wrow[t // 2, w, t % 2, piece, :] if w < 2 else wcol[t // 2, t % 2, piece, :]
+
+    def staging(w):
+        return stage_row if w < 2 else stage_col
+
+    def ship(w, t):
+        return remote(staging(w).at[t % 2], landing(w, t), csend.at[w, t], crecv.at[w, t], near_core)
+
+    def keep(w, t):
+        cut = pl.ds(pl.multiple_of(t * hb, hb), hb)
+        dst = outs[w].at[:, cut] if w < 2 else outs[w].at[cut, :]
+        return pltpu.make_async_copy(staging(w).at[t % 2], dst, store_sem.at[w, t])
+
+    def release(kind, w, t):
+        if kind == 1:
+            ship(w, t).wait_send()
+        else:
+            keep(w, t).wait()
+
+    def group(kind, w, before):
+        def one(t, carry):
+            cut = pl.ds(pl.multiple_of(t * hb, hb), hb)
+            mine = slice(kind * half, (kind + 1) * half)
+            @pl.when(t >= 2)
+            def _():
+                release(kind, w, t - 2)
+
+            if before is not None:
+
+                @pl.when(t < 2)
+                def _():
+                    release(before[0], before[1], t + hsteps - 2)
+
+            if kind == 0:
+                ship(w, t).wait_recv()
+            tall = staging(w).shape[1]
+            size = min(256, tall)
+            for q in range(tall // size):
+                piece = slice(q * size, (q + 1) * size)
+                if w == 2:
+                    left = inner_v[:, pl.ds(pl.multiple_of(t * hb + q * size, size), size)]
+                    value = dot_tn(left, gf_v[:, mine])
+                else:
+                    value = dot_tn(n2_v[:, kind * half + q * size : kind * half + (q + 1) * size], (gg_v, gu_v)[w][:, cut])
+                if kind == 0:
+                    value = value + landed(w, t, piece).astype(F32)
+                staging(w)[t % 2, piece, :] = value.astype(BF16)
+            if kind == 1:
+                ship(w, t).start()
+            else:
+                keep(w, t).start()
+            return carry
+
+        lax.fori_loop(0, hsteps, one, 0)
+
+    done = steps // 2
+    serve(done)
+    pl.semaphore_wait(free_sem, 1)
+    group(1, 0, None)
+    serve(done + 1)
+    group(1, 1, (1, 0))
+    group(0, 0, (1, 1))
+    serve(done + 2)
+    group(1, 2, None)
+    group(0, 1, (0, 0))
+    serve(done + 3)
+    group(0, 2, (1, 2))
+    for k in range(done + 4, 5 + subs):
+        serve(k)
+    for t in range(hsteps - 2, hsteps):
+        keep(1, t).wait()
+        keep(2, t).wait()
+    store_ffn(steps // hsteps - 1).wait()
+    for u in range(subs - 2, subs):
+        for copy in stores(u):
+            copy.wait()
+    chain.settle()
+
+
+def feed_both(n2, gf, gate, up, down, hidden_rows, gain):
+    tokens, width = n2.shape
+    _, half, hidden = gate.shape
+    hb = hidden // 4
+    sub, rows = tokens // 8, tokens // 4
+    any_space = pl.BlockSpec(memory_space=pl.ANY)
+    vmem = pl.BlockSpec(memory_space=pltpu.VMEM)
+    dma = pltpu.SemaphoreType.DMA
+    moving = pltpu.VMEM((8, sub, width), BF16)
+    act = pltpu.VMEM((tokens, hidden), BF16)
+    return pl.pallas_call(
+        functools.partial(feed_both_kernel, hb, sub, rows),
+        in_specs=[any_space] * 6 + [vmem],
+        out_specs=[any_space] * 6 + [vmem],
+        out_shape=[
+            shape((tokens, width), BF16), shape((tokens, width), BF16), shape((tokens, width), F32),
+            shape((half, hidden), BF16), shape((half, hidden), BF16), shape((hidden, half), BF16), shape((8, width), F32),
+        ],
+        scratch_shapes=[
+            pltpu.VMEM((tokens, width), BF16), pltpu.VMEM((tokens, width), BF16), act, act, act,
+            pltpu.VMEM((rows, width), F32), pltpu.VMEM((rows, width), F32),
+            pltpu.VMEM((2, 2, 2, half, hb), BF16), pltpu.VMEM((2, 2, hb, half), BF16),
+            moving, moving, moving, pltpu.VMEM((sub, width), F32),
+            pltpu.VMEM((2, sub, width), F32), pltpu.VMEM((2, sub, width), F32), pltpu.VMEM((2, sub, width), BF16),
+            pltpu.VMEM((rows, width), BF16), pltpu.VMEM((2, half, hb), BF16), pltpu.VMEM((2, hb, half), BF16),
+            dma((2,)), dma((2, 6)), dma((3, 8)), dma((3, 8)), dma((2,)), dma((2, 2)), dma(()), dma((3, 4)), dma((3, 4)),
+            dma((3, 4)), pltpu.SemaphoreType.REGULAR,
+        ],
+        compiler_params=pltpu.CompilerParams(vmem_limit_bytes=VMEM_MOST, collective_id=2, has_side_effects=True),
+        cost_estimate=cost(18 * tokens * width * hidden, 60 * tokens * width),
+        name="feed_forward_both",
+    )(n2, gf, gate, up, down, hidden_rows, gain)
 
 
 def per_device(
@@ -1190,7 +1512,7 @@
         )
         gains = jnp.swapaxes(gains[:, :2], 0, 1).reshape(2, width).astype(F32)
         gain1, gain2 = gains[0:1], gains[1:2]
-        stats = stat[:2, 0]
+        stats = jnp.sum(stat, axis=(1, 2))
         for s in range(seqs):
             seq_scal = jnp.stack([lengths[s], core.astype(jnp.int32)])
             saved.append((pre_all[s], everything_all[s], att_all[s], inv_all[s], seq_scal))
@@ -1235,11 +1557,7 @@
         hidden_all, n2_all = jnp.concatenate(hidden_all), jnp.concatenate(n2_all)
 
     ffn_squares = jnp.zeros((), F32)
-    inner, gg, gu, ffn, gn = [[[None] * chunks for _ in range(seqs)] for _ in range(5)]
     out_shares = []
-    for s in range(seqs):
-        for k in range(chunks):
-            inner[s][k], gg[s][k], gu[s][k], ffn[s][k], gn[s][k] = feed(n2_all, s * chunks + k, rows, gf, s, k, gate, up, down)
 
     def piece_of(arrays):
         per = arrays[0].shape[0] // share
@@ -1257,35 +1575,52 @@
         head = jnp.stack([rank.astype(jnp.int32), lengths[s], start + rank.astype(jnp.int32) * share, jnp.int32(tensor)])
         return jnp.concatenate([head, ids])
 
-    gain2_grad = jnp.zeros((1, width), F32)
-    gb, gh = [[[None] * chunks for _ in range(seqs)] for _ in range(2)]
-    for s in range(seqs):
-        for k in range(chunks):
-            terms = sum_terms(gn[s][k], tensor)
-            gb[s][k], gh[s][k], gain_part = second_back(hidden_all, s * chunks + k, gf, s, k, gain2, terms)
-            gain2_grad = gain2_grad + gain_part
+    def flat(nested):
+        return [item for inner_list in nested for item in inner_list]
+
+    def slices(array, count):
+        size = array.shape[0] // count
+        return [array[i * size : (i + 1) * size] for i in range(count)]
+
+    def reduced(lefts, rights, axis):
+        oth = weight_grad(lefts, rights, 1, axis)
+        own = weight_grad(lefts, rights, 0, axis, over_core(oth))
+        return scatter_blocks(own, axis, dp)
+
+    if dp == 4 and tensor == 4 and order == 8:
+        ffn_all, gb_all, gh_all, d_gate, d_up, d_down, gain2_grad = feed_both(
+            n2_all, gf.reshape(seqs * span, width), gate, up, down, hidden_all, gain2
+        )
+        gain2_grad = jnp.sum(gain2_grad, axis=0, keepdims=True)
+        ffn, gb, gh = [[[a[(s * chunks + k) * rows : (s * chunks + k + 1) * rows] for k in range(chunks)] for s in range(seqs)] for a in (ffn_all, gb_all, gh_all)]
+        grad_w_gate = scatter_blocks(d_gate, 0, dp)
+        grad_w_up = scatter_blocks(d_up, 0, dp)
+        grad_w_down = scatter_blocks(d_down, 1, dp)
+    else:
+        inner, gg, gu, ffn, gn = [[[None] * chunks for _ in range(seqs)] for _ in range(5)]
+        for s in range(seqs):
+            for k in range(chunks):
+                inner[s][k], gg[s][k], gu[s][k], ffn[s][k], gn[s][k] = feed(
+                    n2_all, s * chunks + k, rows, gf, s, k, gate, up, down
+                )
+        gain2_grad = jnp.zeros((1, width), F32)
+        gb, gh = [[[None] * chunks for _ in range(seqs)] for _ in range(2)]
+        for s in range(seqs):
+            for k in range(chunks):
+                terms = sum_terms(gn[s][k], tensor)
+                gb[s][k], gh[s][k], gain_part = second_back(hidden_all, s * chunks + k, gf, s, k, gain2, terms)
+                gain2_grad = gain2_grad + gain_part
+        gf_list = slices(gf.reshape(seqs * span, width), seqs * chunks)
+        n2_list = slices(n2_all, seqs * chunks)
+        grad_w_down = reduced(flat(inner), gf_list, 1)
+        grad_w_gate = reduced(n2_list, flat(gg), 0)
+        grad_w_up = reduced(n2_list, flat(gu), 0)
     for s in range(seqs):
         got = ring_scatter(piece_of(ffn[s]), tensor, rank)
         halves = [hidden_all[(s * chunks + k) * rows : (s * chunks + k + 1) * rows] for k in range(chunks)]
         out, stat = output_share(share_scalars(s), got, ffn[s], halves, order)
         out_shares.append(out)
         ffn_squares = ffn_squares + stat[0, 0]
-
-    def flat(nested):
-        return [item for inner_list in nested for item in inner_list]
-
-    def reduced(lefts, rights, axis):
-        oth = weight_grad(lefts, rights, 1, axis)
-        own = weight_grad(lefts, rights, 0, axis, over_core(oth))
-        return scatter_blocks(own, axis, dp)
-
-    gf_chunks = [gf[s] for s in range(seqs)]
-    inner_seq = flat(inner)
-    gf_flat = [gf[s, k * rows : (k + 1) * rows] for s in range(seqs) for k in range(chunks)]
-    grad_w_down = reduced(inner_seq, gf_flat, 1)
-    n2_list = [n2_all[i * rows : (i + 1) * rows] for i in range(seqs * chunks)]
-    grad_w_gate = reduced(n2_list, flat(gg), 0)
-    grad_w_up = reduced(n2_list, flat(gu), 0)
 
     gain1_grad = jnp.zeros((1, width), F32)
     head_gain = jnp.zeros((2 * hd,), F32)

time: 833 us -> 653 us (0.78)
  starting transfers between devices: 159 us -> 43.7 us
  waiting for transfers between devices: 135 us -> 85.8 us
  Pallas kernels: 410 us -> 395 us
    ppermute x12, starting transfers between devices: 82.5 us -> 14.4 us  [ring_scatter(): moving = lax.ppermute(moving, 'tensor', ring)]
    pallas_call x10 -> x4, Pallas kernels: 72.6 us -> 18.3 us  [weight_grad(): pl.pallas_call(functools.partial(weight_grad_kernel, count, add is not No...]
    pallas_call x8 -> x1, Pallas kernels: 112 us -> 150 us  [feed_both(): pl.pallas_call(functools.partial(feed_both_kernel, hb, sub, rows), in_spe...]
    ppermute x12 -> x0, waiting for transfers between devices: 33.2 us -> none  [the longest x4 28.9 us: sum_terms(): inward = lax.ppermute(part, 'tensor', [(0, 1), (3, 2)])]
    ppermute x2, starting transfers between devices: 30.8 us -> 6.34 us  [per_device(): got = lax.ppermute(join(lines), 'tensor', [(i, i ^ step) for i in range(4)])]
    ppermute x11, waiting for transfers between devices: 29.1 us -> 6.34 us  [over_y(): return lax.ppermute(value, 'dp', [(i, i ^ 2) for i in range(4)])]
    ppermute x12 -> x0, starting transfers between devices: 20.1 us -> none  [the longest x4 11.8 us: sum_terms(): inward = lax.ppermute(part, 'tensor', [(0, 1), (3, 2)])]
    ppermute x2, waiting for transfers between devices: 1.7 us -> 13.5 us  [per_device(): got = lax.ppermute(join(lines), 'tensor', [(i, i ^ step) for i in range(4)])]
  transfers between devices with their start and end apart: 58 -> 43, of which waited for: 19 -> 14; matrix products, arithmetic and copies ran while one was open for 11% -> 14% of each run, Pallas kernels for 25% -> 12%
where the time goes in v3:
time: 653 us; the launch traced here: 643 us
  Pallas kernels  395 us (60%)
  waiting for transfers between devices  85.8 us (13%)
  other arithmetic  57.3 us (9%)
  local copies, waits for them, and re-layouts  56.9 us (9%)
  starting transfers between devices  43.7 us (7%)
    pallas_call x1, Pallas kernels, forward(): pl.pallas_call(functools.partial(forward_kernel, hd, nq, nk, block, sub),...  166 us
    pallas_call x1, Pallas kernels, feed_both(): pl.pallas_call(functools.partial(feed_both_kernel, hb, sub, rows), in_spe...  150 us
    ppermute x11, waiting for transfers between devices, over_x(): return lax.ppermute(value, 'dp', [(i, i ^ 1) for i in range(4)])  42.8 us
    ppermute x12, waiting for transfers between devices, ring_scatter(): moving = lax.ppermute(moving, 'tensor', ring)  23.2 us
    pallas_call x2, Pallas kernels, attend_back(): pl.pallas_call(functools.partial(attend_back_kernel, block, groups), in_s...  19.8 us
    pallas_call x4, Pallas kernels, weight_grad(): pl.pallas_call(functools.partial(weight_grad_kernel, count, add is not No...  18.3 us
    pallas_call x2, Pallas kernels, heads_back(): pl.pallas_call(functools.partial(heads_back_kernel, hd, nq, nk), grid=(1,...  15.1 us
    ppermute x12, starting transfers between devices, ring_scatter(): moving = lax.ppermute(moving, 'tensor', ring)  14.4 us
  transfers between devices with their start and end apart: 43, of which 14 were waited for; matrix products, arithmetic and copies ran while one was open for 14% of the time, Pallas kernels for 12%

profile of v3, /device:TPU:0, one launch (start us, length us, event | category | flops | bytes accessed | tf_op | source)
XLA Modules:
  0.0 643.5 jit_solution(7111424155818558767)
XLA Ops:
  8.1 165.7 %attention_forward.1 = (bf16[2,512,2048]{2,1,0:T(8,128)(2,1)}, bf16[2,512,2048]{2,1,0:T(8,128)(2,1)}, bf16[2,512,2048]{2,1,0:T(8,128)(2,1)}, bf16[2,1024,768]{2,...) custom-call(s32[2]{0:T(128)} %len_ref.1, ...), custom_call_target="tpu_custom_call" | custom-call | flops 9663676416 | bytes 167772160 | tf_op jit(solution)/shard_map/attention_forward/pallas_call | solution.py:1084
  175.2 149.7 %feed_forward_both.1 = (bf16[1024,2048]{1,0:T(8,128)(2,1)}, bf16[1024,2048]{1,0:T(8,128)(2,1)}, f32[1024,2048]{1,0:T(8,128)}, bf16[1024,2048]{1,0:T(8,128)(2,1)}...) custom-call(bf16[1024,2048]{1,0:T(8,128)(2,1)} %get-tuple-element.58.n2_hbm, ...), custom_call_target="tpu_custom_call" | custom-call | flops 77309411328 | bytes 125829120 | tf_op jit(solution)/shard_map/feed_forward_both/pallas_call | solution.py:1440
  324.9 5.6 fusion.15
  330.5 5.4 attention_branch_back.2
  335.9 4.4 attention_branch_back.3
  345.2 4.1 weight_grad.6
  355.1 7.2 %fusion.11 = (f32[256,2048]{1,0:T(8,128)}, f32[256,2048]{1,0:T(8,128)}, f32[256,2048]{1,0:T(8,128)}, f32[256,2048]{1,0:T(8,128)}) fusion(f32[1024,2048]{1,0:T(8,128)} %get-tuple-element.63.hidden_hbm), kind=kLoop, calls=%fused_computation.102 | loop fusion | bytes 16777216 | tf_op jit(solution)/shard_map/slice | solution.py:1620
  363.7 2.8 slice_bitcast_fusion.5
  366.5 3.0 fusion.14
  380.2 3.5 fusion.10
  387.3 9.8 %attend_backward.3 = (bf16[384,512]{1,0:T(8,128)(2,1)}, bf16[384,512]{1,0:T(8,128)(2,1)}) custom-call(s32[2]{0:T(128)} %get-tuple-element.181.scal_ref, bf16[384,1024]{1,0:T(8,128)(2,1)} %get-tuple-element.147.all_ref, bf16[256,1024]{1,0:T(8,128)(2,1)} %get-tuple-element.159.att_ref, f32[4,1024]{1,0:T(4,128)} %get-tuple-element.163.inv_ref, ...), custom_call_target="tpu_custom_call" | custom-call | flops 8053063680 | bytes 4718592 | tf_op jit(solution)/shard_map/attend_backward/pallas_call | solution.py:517
  397.9 10.0 %attend_backward.2 = (bf16[384,512]{1,0:T(8,128)(2,1)}, bf16[384,512]{1,0:T(8,128)(2,1)}) custom-call(s32[2]{0:T(128)} %get-tuple-element.180.scal_ref, bf16[384,1024]{1,0:T(8,128)(2,1)} %get-tuple-element.146.all_ref, bf16[256,1024]{1,0:T(8,128)(2,1)} %get-tuple-element.158.att_ref, f32[4,1024]{1,0:T(4,128)} %get-tuple-element.162.inv_ref, ...), custom_call_target="tpu_custom_call" | custom-call | flops 8053063680 | bytes 4718592 | tf_op jit(solution)/shard_map/attend_backward/pallas_call | solution.py:517
  415.1 7.1 %collective-permute-done.32 = bf16[128,2048]{1,0:T(8,128)(2,1)S(1)} collective-permute-done((bf16[128,2048]{1,0:T(8,128)(2,1)}, bf16[128,2048]{1,0:T(8,128)(2,1)S(1)}, u32[]{:S(2)}, u32[]{:S(2)}) %collective-permute-start.32) | collective-permute-done | bytes 524320 | tf_op jit(solution)/shard_map/ppermute | solution.py:71
  435.4 3.2 collective-permute-start.4
  445.6 7.5 %query_key_value_back.2 = (bf16[512,768]{1,0:T(8,128)(2,1)}, bf16[512,2048]{1,0:T(8,128)(2,1)}, f32[1,2048]{1,0:T(1,128)}, f32[128,128]{1,0:T(8,128)}) custom-call(bf16[384,512]{1,0:T(8,128)(2,1)} %get-tuple-element.75.own_ref, bf16[384,512]{1,0:T(8,128)(2,1)} %copy-done.25, f32[640,512]{1,0:T(8,128)} %get-tuple-element.138.pre_ref, ...), custom_call_target="tpu_custom_call" | custom-call | flops 1610612736 | bytes 7340032 | tf_op jit(solution)/shard_map/query_key_value_back/pallas_call | solution.py:574
  453.8 7.6 %query_key_value_back.3 = (bf16[512,768]{1,0:T(8,128)(2,1)}, bf16[512,2048]{1,0:T(8,128)(2,1)}, f32[1,2048]{1,0:T(1,128)}, f32[128,128]{1,0:T(8,128)}) custom-call(bf16[384,512]{1,0:T(8,128)(2,1)} %get-tuple-element.84.own_ref, bf16[384,512]{1,0:T(8,128)(2,1)} %copy-done.24, f32[640,512]{1,0:T(8,128)} %get-tuple-element.139.pre_ref, ...), custom_call_target="tpu_custom_call" | custom-call | flops 1610612736 | bytes 7340032 | tf_op jit(solution)/shard_map/query_key_value_back/pallas_call | solution.py:574
  467.0 4.7 weight_grad.4
  473.4 4.4 weight_grad.7
  492.4 9.1 %collective-permute-done.8 = bf16[128,2048]{1,0:T(8,128)(2,1)S(1)} collective-permute-done((bf16[128,2048]{1,0:T(8,128)(2,1)S(1)}, bf16[128,2048]{1,0:T(8,128)(2,1)S(1)}, u32[]{:S(2)}, u32[]{:S(2)}) %collective-permute-start.8) | collective-permute-done | bytes 524320 | tf_op jit(solution)/shard_map/ppermute | solution.py:137
  503.2 9.6 %collective-permute-done.5.got_ref = bf16[128,2048]{1,0:T(8,128)(2,1)S(1)} collective-permute-done((bf16[128,2048]{1,0:T(8,128)(2,1)S(1)}, bf16[128,2048]{1,0:T(8,128)(2,1)S(1)}, u32[]{:S(2)}, u32[]{:S(2)}) %collective-permute-start.5) | collective-permute-done | bytes 524320 | tf_op jit(solution)/shard_map/ppermute | solution.py:137
  514.3 4.0 output_share.3
  521.6 4.0 output_share.2
  534.3 3.7 convert_add_fusion.2
  538.1 34.7 %collective-permute-done.39 = f32[1,1280]{1,0:T(1,128)S(1)} collective-permute-done((f32[1,1280]{1,0:T(1,128)S(1)}, f32[1,1280]{1,0:T(1,128)S(1)}, u32[]{:S(2)}, u32[]{:S(2)}) %collective-permute-start.39) | collective-permute-done | bytes 5152 | tf_op jit(solution)/shard_map/ppermute | solution.py:71
  573.8 3.4 convert_add_fusion.1
  580.1 3.5 convert_add_fusion
  583.7 13.0 %collective-permute-done.41 = f32[1,768]{1,0:T(1,128)S(1)} collective-permute-done((f32[1,768]{1,0:T(1,128)S(1)}, f32[1,768]{1,0:T(1,128)S(1)}, u32[]{:S(2)}, u32[]{:S(2)}) %collective-permute-start.41) | collective-permute-done | bytes 3104 | tf_op jit(solution)/shard_map/ppermute | solution.py:1672
  596.7 4.5 collective-permute-start.42
  607.5 5.1 weight_grad.5
  624.3 4.4 input_share.3
  628.7 3.4 collective-permute-done.10.got_ref
  633.0 4.6 input_share.2
  (254 shorter events, 126.5 us)
Async XLA Ops:
  335.9 61.2 %collective-permute-start.6 = (bf16[256,512]{1,0:T(8,128)(2,1)}, bf16[256,512]{1,0:T(8,128)(2,1)S(1)}, u32[]{:S(2)}, u32[]{:S(2)}) collective-permute-start(bf16[256,512]{1,0:T(8,128)(2,1)} %get-tuple-element.74), channel_id=1, source_target_pairs={{0,4},{4,0},{1,5},{5,1},{2,6},{6,2},{3,7},{7,3},{8,12},{12,8},{9,1... | collective-permute-start | bytes 786440 | tf_op jit(solution)/shard_map/ppermute | solution.py:79
  340.3 45.6 %collective-permute-start.11 = (bf16[256,512]{1,0:T(8,128)(2,1)}, bf16[256,512]{1,0:T(8,128)(2,1)}, u32[]{:S(2)}, u32[]{:S(2)}) collective-permute-start(bf16[256,512]{1,0:T(8,128)(2,1)} %get-tuple-element.83), channel_id=1, source_target_pairs={{0,4},{4,0},{1,5},{5,1},{2,6},{6,2},{3,7},{7,3},{8,12},{12,8},{9,1... | collective-permute-start | bytes 786440 | tf_op jit(solution)/shard_map/ppermute | solution.py:79
  342.9 84.4 %collective-permute-start.3 = (bf16[128,2048]{1,0:T(8,128)(2,1)}, bf16[128,2048]{1,0:T(8,128)(2,1)}, u32[]{:S(2)}, u32[]{:S(2)}) collective-permute-start(bf16[128,2048]{1,0:T(8,128)(2,1)} %dynamic-slice_select_fusion), channel_id=1, source_target_pairs={{0,1},{1,2},{2,3},{3,0},{4,5},{5,6},{6,7},{7,4},{8,9},{9,10},{10,1... | collective-permute-start | bytes 1572872 | tf_op jit(solution)/shard_map/ppermute | solution.py:137
  343.8 89.0 %collective-permute-start = (bf16[128,2048]{1,0:T(8,128)(2,1)}, bf16[128,2048]{1,0:T(8,128)(2,1)}, u32[]{:S(2)}, u32[]{:S(2)}) collective-permute-start(bf16[128,2048]{1,0:T(8,128)(2,1)} %dynamic-slice_select_fusion.1), channel_id=1, source_target_pairs={{0,1},{1,2},{2,3},{3,0},{4,5},{5,6},{6,7},{7,4},{8,9},{9,10},{10,1... | collective-permute-start | bytes 1572872 | tf_op jit(solution)/shard_map/ppermute | solution.py:137
  349.3 122.4 %collective-permute-start.21 = (bf16[512,1024]{1,0:T(8,128)(2,1)}, bf16[512,1024]{1,0:T(8,128)(2,1)}, u32[]{:S(2)}, u32[]{:S(2)}) collective-permute-start(bf16[512,1024]{1,0:T(8,128)(2,1)} %weight_grad.6), channel_id=1, source_target_pairs={{0,4},{4,0},{1,5},{5,1},{2,6},{6,2},{3,7},{7,3},{8,12},{12,8},{9,1... | collective-permute-start | bytes 3145736 | tf_op jit(solution)/shard_map/ppermute | solution.py:79
  385.9 21.9 %collective-permute-start.28 = (bf16[128,2048]{1,0:T(8,128)(2,1)}, bf16[128,2048]{1,0:T(8,128)(2,1)S(1)}, u32[]{:S(2)}, u32[]{:S(2)}) collective-permute-start(bf16[128,2048]{1,0:T(8,128)(2,1)} %get-tuple-element.124), channel_id=1, source_target_pairs={{0,8},{8,0},{16,24},{24,16},{1,9},{9,1},{17,25},{25,17},{2,10},{10... | collective-permute-start | bytes 1572872 | tf_op jit(solution)/shard_map/ppermute | solution.py:71
  397.2 14.4 %collective-permute-start.26 = (bf16[128,2048]{1,0:T(8,128)(2,1)}, bf16[128,2048]{1,0:T(8,128)(2,1)}, u32[]{:S(2)}, u32[]{:S(2)}) collective-permute-start(bf16[128,2048]{1,0:T(8,128)(2,1)} %get-tuple-element.125), channel_id=1, source_target_pairs={{0,16},{8,24},{16,0},{24,8},{1,17},{9,25},{17,1},{25,9},{2,18},{10... | collective-permute-start | bytes 1572872 | tf_op jit(solution)/shard_map/ppermute | solution.py:75
  407.9 14.3 %collective-permute-start.32 = (bf16[128,2048]{1,0:T(8,128)(2,1)}, bf16[128,2048]{1,0:T(8,128)(2,1)S(1)}, u32[]{:S(2)}, u32[]{:S(2)}) collective-permute-start(bf16[128,2048]{1,0:T(8,128)(2,1)} %get-tuple-element.118), channel_id=1, source_target_pairs={{0,8},{8,0},{16,24},{24,16},{1,9},{9,1},{17,25},{25,17},{2,10},{10... | collective-permute-start | bytes 1572872 | tf_op jit(solution)/shard_map/ppermute | solution.py:71
  425.0 13.5 %collective-permute-start.34 = (bf16[1024,256]{1,0:T(8,128)(2,1)S(1)}, bf16[1024,256]{1,0:T(8,128)(2,1)S(1)}, u32[]{:S(2)}, u32[]{:S(2)}) collective-permute-start(bf16[1024,256]{1,0:T(8,128)(2,1)S(1)} %copy-done.20), channel_id=1, source_target_pairs={{0,16},{8,24},{16,0},{24,8},{1,17},{9,25},{17,1},{25,9},{2,18},{10... | collective-permute-start | bytes 1572872 | tf_op jit(solution)/shard_map/ppermute | solution.py:75
  427.3 25.8 %collective-permute-start.12 = (bf16[384,512]{1,0:T(8,128)(2,1)}, bf16[384,512]{1,0:T(8,128)(2,1)S(1)}, u32[]{:S(2)}, u32[]{:S(2)}) collective-permute-start(bf16[384,512]{1,0:T(8,128)(2,1)} %get-tuple-element.85), channel_id=1, source_target_pairs={{0,4},{4,0},{1,5},{5,1},{2,6},{6,2},{3,7},{7,3},{8,12},{12,8},{9,1... | collective-permute-start | bytes 1179656 | tf_op jit(solution)/shard_map/ppermute | solution.py:79
  435.4 43.6 %collective-permute-start.4 = (bf16[128,2048]{1,0:T(8,128)(2,1)}, bf16[128,2048]{1,0:T(8,128)(2,1)}, u32[]{:S(2)}, u32[]{:S(2)}) collective-permute-start(bf16[128,2048]{1,0:T(8,128)(2,1)} %add_convert_fusion.11), channel_id=1, source_target_pairs={{0,1},{1,2},{2,3},{3,0},{4,5},{5,6},{6,7},{7,4},{8,9},{9,10},{10,1... | collective-permute-start | bytes 1572872 | tf_op jit(solution)/shard_map/ppermute | solution.py:137
  438.6 42.8 %collective-permute-start.1 = (bf16[128,2048]{1,0:T(8,128)(2,1)}, bf16[128,2048]{1,0:T(8,128)(2,1)}, u32[]{:S(2)}, u32[]{:S(2)}) collective-permute-start(bf16[128,2048]{1,0:T(8,128)(2,1)} %add_convert_fusion.13), channel_id=1, source_target_pairs={{0,1},{1,2},{2,3},{3,0},{4,5},{5,6},{6,7},{7,4},{8,9},{9,10},{10,1... | collective-permute-start | bytes 1572872 | tf_op jit(solution)/shard_map/ppermute | solution.py:137
  444.3 87.9 %collective-permute-start.29 = (bf16[256,2048]{1,0:T(8,128)(2,1)}, bf16[256,2048]{1,0:T(8,128)(2,1)}, u32[]{:S(2)}, u32[]{:S(2)}) collective-permute-start(bf16[256,2048]{1,0:T(8,128)(2,1)} %pad_maximum_fusion.3), channel_id=1, source_target_pairs={{0,16},{8,24},{16,0},{24,8},{1,17},{9,25},{17,1},{25,9},{2,18},{10... | collective-permute-start | bytes 3145736 | tf_op jit(solution)/shard_map/ppermute | solution.py:75
  453.1 80.3 %collective-permute-start.27 = (bf16[256,2048]{1,0:T(8,128)(2,1)}, bf16[256,2048]{1,0:T(8,128)(2,1)}, u32[]{:S(2)}, u32[]{:S(2)}) collective-permute-start(bf16[256,2048]{1,0:T(8,128)(2,1)} %pad_maximum_fusion.2), channel_id=1, source_target_pairs={{0,8},{8,0},{16,24},{24,16},{1,9},{9,1},{17,25},{25,17},{2,10},{10... | collective-permute-start | bytes 3145736 | tf_op jit(solution)/shard_map/ppermute | solution.py:71
  471.7 15.8 %collective-permute-start.13 = (bf16[128,2048]{1,0:T(8,128)(2,1)}, bf16[128,2048]{1,0:T(8,128)(2,1)S(1)}, u32[]{:S(2)}, u32[]{:S(2)}) collective-permute-start(bf16[128,2048]{1,0:T(8,128)(2,1)} %constant_dynamic-slice_fusion), channel_id=1, source_target_pairs={{0,1},{1,2},{2,3},{3,0},{4,5},{5,6},{6,7},{7,4},{8,9},{9,10},{10,1... | collective-permute-start | bytes 1572872 | tf_op jit(solution)/shard_map/ppermute | solution.py:137
  484.8 16.7 %collective-permute-start.8 = (bf16[128,2048]{1,0:T(8,128)(2,1)S(1)}, bf16[128,2048]{1,0:T(8,128)(2,1)S(1)}, u32[]{:S(2)}, u32[]{:S(2)}) collective-permute-start(bf16[128,2048]{1,0:T(8,128)(2,1)S(1)} %copy-done.17), channel_id=1, source_target_pairs={{0,1},{1,2},{2,3},{3,0},{4,5},{5,6},{6,7},{7,4},{8,9},{9,10},{10,1... | collective-permute-start | bytes 1572872 | tf_op jit(solution)/shard_map/ppermute | solution.py:137
  486.4 26.3 %collective-permute-start.5 = (bf16[128,2048]{1,0:T(8,128)(2,1)S(1)}, bf16[128,2048]{1,0:T(8,128)(2,1)S(1)}, u32[]{:S(2)}, u32[]{:S(2)}) collective-permute-start(bf16[128,2048]{1,0:T(8,128)(2,1)S(1)} %add_convert_fusion.10), channel_id=1, source_target_pairs={{0,1},{1,2},{2,3},{3,0},{4,5},{5,6},{6,7},{7,4},{8,9},{9,10},{10,1... | collective-permute-start | bytes 1572872 | tf_op jit(solution)/shard_map/ppermute | solution.py:137
  487.5 33.0 %collective-permute-start.2 = (bf16[128,2048]{1,0:T(8,128)(2,1)}, bf16[128,2048]{1,0:T(8,128)(2,1)}, u32[]{:S(2)}, u32[]{:S(2)}) collective-permute-start(bf16[128,2048]{1,0:T(8,128)(2,1)} %add_convert_fusion.12), channel_id=1, source_target_pairs={{0,1},{1,2},{2,3},{3,0},{4,5},{5,6},{6,7},{7,4},{8,9},{9,10},{10,1... | collective-permute-start | bytes 1572872 | tf_op jit(solution)/shard_map/ppermute | solution.py:137
  501.5 71.3 %collective-permute-start.33 = (bf16[256,2048]{1,0:T(8,128)(2,1)}, bf16[256,2048]{1,0:T(8,128)(2,1)S(1)}, u32[]{:S(2)}, u32[]{:S(2)}) collective-permute-start(bf16[256,2048]{1,0:T(8,128)(2,1)} %pad_maximum_fusion.5), channel_id=1, source_target_pairs={{0,16},{8,24},{16,0},{24,8},{1,17},{9,25},{17,1},{25,9},{2,18},{10... | collective-permute-start | bytes 3145736 | tf_op jit(solution)/shard_map/ppermute | solution.py:75
  513.5 14.6 %collective-permute-start.25 = (bf16[512,256]{1,0:T(8,128)(2,1)}, bf16[512,256]{1,0:T(8,128)(2,1)S(1)}, u32[]{:S(2)}, u32[]{:S(2)}) collective-permute-start(bf16[512,256]{1,0:T(8,128)(2,1)} %pad_maximum_fusion.12), channel_id=1, source_target_pairs={{0,16},{8,24},{16,0},{24,8},{1,17},{9,25},{17,1},{25,9},{2,18},{10... | collective-permute-start | bytes 786440 | tf_op jit(solution)/shard_map/ppermute | solution.py:75
  528.2 44.8 %collective-permute-start.31 = (bf16[256,2048]{1,0:T(8,128)(2,1)}, bf16[256,2048]{1,0:T(8,128)(2,1)}, u32[]{:S(2)}, u32[]{:S(2)}) collective-permute-start(bf16[256,2048]{1,0:T(8,128)(2,1)} %pad_maximum_fusion.4), channel_id=1, source_target_pairs={{0,8},{8,0},{16,24},{24,16},{1,9},{9,1},{17,25},{25,17},{2,10},{10... | collective-permute-start | bytes 3145736 | tf_op jit(solution)/shard_map/ppermute | solution.py:71
  531.0 47.3 %collective-permute-start.37 = (bf16[2048,256]{1,0:T(8,128)(2,1)}, bf16[2048,256]{1,0:T(8,128)(2,1)}, u32[]{:S(2)}, u32[]{:S(2)}) collective-permute-start(bf16[2048,256]{1,0:T(8,128)(2,1)} %pad_maximum_fusion.7), channel_id=1, source_target_pairs={{0,16},{8,24},{16,0},{24,8},{1,17},{9,25},{17,1},{25,9},{2,18},{10... | collective-permute-start | bytes 3145736 | tf_op jit(solution)/shard_map/ppermute | solution.py:75
  532.2 47.9 %collective-permute-start.35 = (bf16[2048,256]{1,0:T(8,128)(2,1)}, bf16[2048,256]{1,0:T(8,128)(2,1)}, u32[]{:S(2)}, u32[]{:S(2)}) collective-permute-start(bf16[2048,256]{1,0:T(8,128)(2,1)} %pad_maximum_fusion.6), channel_id=1, source_target_pairs={{0,8},{8,0},{16,24},{24,16},{1,9},{9,1},{17,25},{25,17},{2,10},{10... | collective-permute-start | bytes 3145736 | tf_op jit(solution)/shard_map/ppermute | solution.py:71
  533.4 39.4 %collective-permute-start.39 = (f32[1,1280]{1,0:T(1,128)S(1)}, f32[1,1280]{1,0:T(1,128)S(1)}, u32[]{:S(2)}, u32[]{:S(2)}) collective-permute-start(f32[1,1280]{1,0:T(1,128)S(1)} %pad_maximum_fusion.15), channel_id=1, source_target_pairs={{0,8},{8,0},{16,24},{24,16},{1,9},{9,1},{17,25},{25,17},{2,10},{10... | collective-permute-start | bytes 15368 | tf_op jit(solution)/shard_map/ppermute | solution.py:71
  572.8 34.7 %collective-permute-start.16 = (bf16[1024,768]{1,0:T(8,128)(2,1)}, bf16[1024,768]{1,0:T(8,128)(2,1)}, u32[]{:S(2)}, u32[]{:S(2)}) collective-permute-start(bf16[1024,768]{1,0:T(8,128)(2,1)} %weight_grad.4), channel_id=1, source_target_pairs={{0,4},{4,0},{1,5},{5,1},{2,6},{6,2},{3,7},{7,3},{8,12},{12,8},{9,1... | collective-permute-start | bytes 4718600 | tf_op jit(solution)/shard_map/ppermute | solution.py:79
  572.9 32.4 %collective-permute-start.14 = (bf16[128,2048]{1,0:T(8,128)(2,1)}, bf16[128,2048]{1,0:T(8,128)(2,1)}, u32[]{:S(2)}, u32[]{:S(2)}) collective-permute-start(bf16[128,2048]{1,0:T(8,128)(2,1)} %add_convert_fusion.7), channel_id=1, source_target_pairs={{0,1},{1,2},{2,3},{3,0},{4,5},{5,6},{6,7},{7,4},{8,9},{9,10},{10,1... | collective-permute-start | bytes 1572872 | tf_op jit(solution)/shard_map/ppermute | solution.py:137
  577.2 38.6 %collective-permute-start.9 = (bf16[128,2048]{1,0:T(8,128)(2,1)}, bf16[128,2048]{1,0:T(8,128)(2,1)S(1)}, u32[]{:S(2)}, u32[]{:S(2)}) collective-permute-start(bf16[128,2048]{1,0:T(8,128)(2,1)} %add_convert_fusion.9), channel_id=1, source_target_pairs={{0,1},{1,2},{2,3},{3,0},{4,5},{5,6},{6,7},{7,4},{8,9},{9,10},{10,1... | collective-permute-start | bytes 1572872 | tf_op jit(solution)/shard_map/ppermute | solution.py:137
  578.3 18.3 %collective-permute-start.41 = (f32[1,768]{1,0:T(1,128)S(1)}, f32[1,768]{1,0:T(1,128)S(1)}, u32[]{:S(2)}, u32[]{:S(2)}) collective-permute-start(f32[1,768]{1,0:T(1,128)S(1)} %pad_maximum_fusion.17), channel_id=1, source_target_pairs={{0,1},{1,0},{2,3},{3,2},{4,5},{5,4},{6,7},{7,6},{8,9},{9,8},{10,11... | collective-permute-start | bytes 9224 | tf_op jit(solution)/shard_map/ppermute | solution.py:1672
  606.6 17.7 %collective-permute-start.15 = (bf16[128,2048]{1,0:T(8,128)(2,1)S(1)}, bf16[128,2048]{1,0:T(8,128)(2,1)}, u32[]{:S(2)}, u32[]{:S(2)}) collective-permute-start(bf16[128,2048]{1,0:T(8,128)(2,1)S(1)} %add_convert_fusion.6), channel_id=1, source_target_pairs={{0,1},{1,2},{2,3},{3,0},{4,5},{5,6},{6,7},{7,4},{8,9},{9,10},{10,1... | collective-permute-start | bytes 1572872 | tf_op jit(solution)/shard_map/ppermute | solution.py:137
  616.0 16.2 %collective-permute-start.10 = (bf16[128,2048]{1,0:T(8,128)(2,1)S(1)}, bf16[128,2048]{1,0:T(8,128)(2,1)S(1)}, u32[]{:S(2)}, u32[]{:S(2)}) collective-permute-start(bf16[128,2048]{1,0:T(8,128)(2,1)S(1)} %add_convert_fusion.8), channel_id=1, source_target_pairs={{0,1},{1,2},{2,3},{3,0},{4,5},{5,6},{6,7},{7,4},{8,9},{9,10},{10,1... | collective-permute-start | bytes 1572872 | tf_op jit(solution)/shard_map/ppermute | solution.py:137
  621.3 19.0 %collective-permute-start.20 = (bf16[256,768]{1,0:T(8,128)(2,1)S(1)}, bf16[256,768]{1,0:T(8,128)(2,1)S(1)}, u32[]{:S(2)}, u32[]{:S(2)}) collective-permute-start(bf16[256,768]{1,0:T(8,128)(2,1)S(1)} %pad_maximum_fusion.10), channel_id=1, source_target_pairs={{0,16},{8,24},{16,0},{24,8},{1,17},{9,25},{17,1},{25,9},{2,18},{10... | collective-permute-start | bytes 1179656 | tf_op jit(solution)/shard_map/ppermute | solution.py:75
  622.7 17.6 %collective-permute-start.18 = (bf16[256,768]{1,0:T(8,128)(2,1)S(1)}, bf16[256,768]{1,0:T(8,128)(2,1)S(1)}, u32[]{:S(2)}, u32[]{:S(2)}) collective-permute-start(bf16[256,768]{1,0:T(8,128)(2,1)S(1)} %pad_maximum_fusion.9), channel_id=1, source_target_pairs={{0,8},{8,0},{16,24},{24,16},{1,9},{9,1},{17,25},{25,17},{2,10},{10... | collective-permute-start | bytes 1179656 | tf_op jit(solution)/shard_map/ppermute | solution.py:71
  (47 other events, 763.9 us)

commit v4 on v3

--- a/solution.py
+++ b/solution.py
@@ -44,13 +44,7 @@
     return lax.rsqrt(jnp.mean(values * values, axis=-1, keepdims=True) + epsilon)
 
 
-def tie(value, *others):
-    return lax.optimization_barrier((value,) + others)[0]
-
-
-def block_order(dp, row, core):
-    if dp == 4:
-        return jnp.stack([(row ^ k) * 2 + (core ^ o) for o in range(2) for k in range(dp)]).astype(jnp.int32)
+def block_order(dp, core):
     return jnp.stack([jnp.int32(k) * 2 + (core ^ o) for o in range(2) for k in range(dp)]).astype(jnp.int32)
 
 
@@ -67,67 +61,17 @@
     return jnp.where(core == 0, parts, parts[..., ::-1, :]).reshape(values.shape)
 
 
-def over_x(value):
-    return lax.ppermute(value, "dp", [(i, i ^ 1) for i in range(4)])
-
-
-def over_y(value):
-    return lax.ppermute(value, "dp", [(i, i ^ 2) for i in range(4)])
-
-
 def over_core(value):
     return lax.ppermute(value, "context", SWAP)
 
 
-def gather_blocks(weight, axis, dp):
-    if dp == 4:
-        from_x = over_x(weight)
-        from_y = over_y(weight)
-        half = weight.shape[0] // 2
-        first = over_x(from_y[:half])
-        second = over_y(from_x[half:])
-        if axis == 0:
-            own = jnp.concatenate([weight, from_x, from_y, first, second], axis=0)
-        else:
-            diagonal = jnp.concatenate([first, second], axis=0)
-            own = jnp.concatenate([weight, from_x, from_y, diagonal], axis=1)
-        mark = from_x
-    else:
-        own = lax.all_gather(weight, "dp", axis=axis, tiled=True)
-        mark = own
-    return jnp.stack([own, over_core(own)]), mark
-
-
-def scatter_blocks(total, axis, dp):
-    if dp != 4:
-        return lax.psum_scatter(total, "dp", scatter_dimension=axis, tiled=True).astype(F32)
-    piece = total.shape[axis] // 4
-    half = piece // 2 if axis == 0 else total.shape[0] // 2
-
-    def block(k):
-        return lax.slice_in_dim(total, k * piece, (k + 1) * piece, axis=axis)
-
-    diagonal = block(3)
-    from_x = over_x(diagonal[:half])
-    from_y = over_y(diagonal[half:])
-    to_y = block(2)
-    to_x = block(1)
-    to_y = jnp.concatenate([to_y[:half].astype(F32) + from_x.astype(F32), to_y[half:].astype(F32)], axis=0).astype(BF16)
-    to_x = jnp.concatenate([to_x[:half].astype(F32), to_x[half:].astype(F32) + from_y.astype(F32)], axis=0).astype(BF16)
-    got_x = over_x(to_x)
-    got_y = over_y(to_y)
-    return block(0).astype(F32) + got_x.astype(F32) + got_y.astype(F32)
-
-
-def sum_terms(part, tensor):
-    if tensor != 4:
-        return [lax.psum(part, "tensor")]
-    inward = lax.ppermute(part, "tensor", [(0, 1), (3, 2)])
-    pair = (part.astype(F32) + inward.astype(F32)).astype(BF16)
-    across = lax.ppermute(pair, "tensor", [(1, 2), (2, 1)])
-    rest = (part.astype(F32) + across.astype(F32)).astype(BF16)
-    outward = lax.ppermute(rest, "tensor", [(1, 0), (2, 3)])
-    return [part, inward, across, outward]
+def gather_blocks(weight, axis):
+    own = lax.all_gather(weight, "dp", axis=axis, tiled=True)
+    return jnp.stack([own, over_core(own)])
+
+
+def scatter_blocks(total, axis):
+    return lax.psum_scatter(total, "dp", scatter_dimension=axis, tiled=True).astype(F32)
 
 
 def ring_scatter(piece, tensor, rank):
@@ -1461,7 +1405,576 @@
     )(n2, gf, gate, up, down, hidden_rows, gain)
 
 
-def per_device(
+class Ring:
+    def __init__(self, rank, source, own, slots, send, recv):
+        self.source, self.own, self.slots, self.send, self.recv = source, own, slots, send, recv
+        self.rank, self.right = rank, {"tensor": (rank + 1) % 4}
+
+    def hop(self, j):
+        src = self.source((self.rank + 3) % 4) if j == 0 else self.slots.at[j - 1]
+        return remote(src, self.slots.at[j], self.send.at[j], self.recv.at[j], self.right)
+
+    def begin(self):
+        self.hop(0).start()
+
+    def step(self, j):
+        self.hop(j - 1).wait_recv()
+        read = self.own((self.rank + 3 - j) % 4)
+
+        def body(cut, first):
+            self.slots[j - 1, cut, :] = (self.slots[j - 1, cut, :].astype(F32) + read(cut).astype(F32)).astype(BF16)
+
+        by_pieces(self.slots.shape[1], body)
+        self.hop(j).start()
+
+    def arrived(self):
+        self.hop(2).wait_recv()
+
+    def settle(self):
+        for j in range(3):
+            self.hop(j).wait_send()
+
+
+def tall(ref):
+    return 16 * max(1, 2048 // ref.shape[1])
+
+
+class Scatter:
+    def __init__(self, block, from_x, from_y, land_x, land_y, temps, send, recv, load, near_x, near_y):
+        self.block, self.from_x, self.from_y, self.land_x, self.land_y = block, from_x, from_y, land_x, land_y
+        self.temps, self.load = temps, load
+        sem = lambda k: (send.at[k], recv.at[k])
+        self.first = [
+            remote(block(3, 0), from_x, *sem(0), near_x),
+            remote(block(3, 1), from_y, *sem(1), near_y),
+            remote(block(1, 0), land_x(0), *sem(2), near_x),
+            remote(block(2, 1), land_y(1), *sem(3), near_y),
+        ]
+        self.second = [
+            remote(from_y, land_x(1), *sem(4), near_x),
+            remote(from_x, land_y(0), *sem(5), near_y),
+        ]
+
+    def begin(self):
+        for copy in self.first:
+            copy.start()
+
+    def pass_on(self):
+        loads = [
+            pltpu.make_async_copy(self.block(1, 1), self.temps.at[0], self.load.at[0]),
+            pltpu.make_async_copy(self.block(2, 0), self.temps.at[1], self.load.at[1]),
+        ]
+        for copy in loads:
+            copy.start()
+        for which, into in ((1, self.from_y), (0, self.from_x)):
+            self.first[which].wait_recv()
+            loads[1 - which].wait()
+            temp = 1 - which
+
+            def body(cut, first):
+                into[cut, :] = (into[cut, :].astype(F32) + self.temps[temp, cut, :].astype(F32)).astype(BF16)
+
+            by_pieces(into.shape[0], body, tall(into))
+            self.second[temp].start()
+
+    def finish(self, stage, out, store):
+        for copy in self.first[2:] + self.second:
+            copy.wait_recv()
+        for h in range(2):
+            loads = [
+                pltpu.make_async_copy(src, self.temps.at[k], self.load.at[k])
+                for k, src in enumerate((self.block(0, h), self.land_x(h), self.land_y(h)))
+            ]
+            for copy in loads:
+                copy.start()
+            for copy in loads:
+                copy.wait()
+
+            def body(cut, first):
+                stage[cut, :] = sum(self.temps[k, cut, :].astype(F32) for k in range(3))
+
+            by_pieces(stage.shape[0], body, tall(stage))
+            keep = pltpu.make_async_copy(stage, out(h), store)
+            keep.start()
+            keep.wait()
+
+    def settle(self):
+        for copy in self.first + self.second:
+            copy.wait_send()
+
+
+def backward_kernel(
+    hd, nq, nk, block,
+    len_ref, gb_hbm, gh_hbm, hidden_hbm, ffn_hbm, xr_hbm, n1_hbm, tok_hbm, outw_hbm, qkvw_hbm, all_hbm, att_hbm, inv_hbm, pre_hbm,
+    dgate_hbm, dup_hbm, ddown_hbm, gain_ref, cos_ref, sin_ref, qg_ref, kg_ref, stat_ref, gain2_ref,
+    out_hbm, gin_hbm, ggate_hbm, gup_hbm, gdown_hbm, gout_hbm, gqkv_hbm, landx0, landy0, landx1, landy1, landx2, landy2,
+    lines_out, small_out,
+    act_v, rows_v, qkvw_v, tok_v, all_v, att_v, inv_v, pre_v, grads, da_all, da_own, da_send, da_got, d_own, d_send, d_got, dpre_v,
+    first_v, slots_v, piece_v, wide_a, wide_b, temp_a, temp_b, stage_a, stage_b,
+    go_v, so_v, wide_o, land_o, temp_o, stage_o, gq_v, sq_v, wide_q, land_q, temp_q, stage_q,
+    tile_v, xtile_v, otile_v, itile_v, lines_v, small_v, lin1, lin2, lin3, lin4, lin5, small_r,
+    load_sem, zsend, zrecv, piece_sem, xsend, xrecv, xload, xstore, exsend, exrecv, osend, orecv, qsend, qrecv,
+    tile_sem, outs_sem, smsend, smrecv,
+):
+    seqs, _, slots = all_v.shape
+    span = slots // 2
+    width = act_v.shape[1]
+    half = width // 2
+    groups = nq // nk
+    share = span // 4
+    row, core, rank = lax.axis_index("dp"), lax.axis_index("context"), lax.axis_index("tensor")
+    start = core * span
+    near = [row, xor_one(row), (row + 2) % 4, 3 - row]
+    near_x, near_y, near_core = {"dp": near[1]}, {"dp": near[2]}, {"context": 1 - core}
+    z_right, z_left, z_far = {"tensor": (rank + 1) % 4}, {"tensor": (rank + 3) % 4}, {"tensor": (rank + 2) % 4}
+    first_core = core == 0
+
+    def load(k, src, dst):
+        copy = pltpu.make_async_copy(src, dst, load_sem.at[k])
+        copy.start()
+        return copy
+
+    load_gb = load(0, gb_hbm, act_v)
+    load_outw = load(1, outw_hbm, rows_v)
+    load_att = [
+        load(2, all_hbm, all_v), load(3, att_hbm, att_v), load(4, inv_hbm, inv_v), load(5, pre_hbm, pre_v),
+    ]
+    load_tok = load(6, tok_hbm, tok_v)
+    load_qkvw = load(7, qkvw_hbm, qkvw_v)
+
+    def piece_rows(s, m):
+        return pl.ds(pl.multiple_of(s * span + m * share, share), share)
+
+    def load_piece(s, m):
+        return pltpu.make_async_copy(ffn_hbm.at[piece_rows(s, m), :], piece_v.at[s], piece_sem.at[s])
+
+    greet([(None, d) for d in (near_x, near_y, near_core, z_right, z_left, z_far)])
+
+    def ffn_own(s):
+        def own(m):
+            load_piece(s, m).wait()
+            return lambda cut: piece_v[s, cut, :]
+
+        return own
+
+    def first_own(s):
+        return lambda m: lambda cut: first_v[s, m, cut, :]
+
+    ffn_rings = [
+        Ring(rank, lambda m, s=s: ffn_hbm.at[piece_rows(s, m), :], ffn_own(s), slots_v.at[s], zsend.at[s], zrecv.at[s])
+        for s in range(seqs)
+    ]
+    first_rings = [
+        Ring(rank, lambda m, s=s: first_v.at[s, m], first_own(s), slots_v.at[seqs + s], zsend.at[seqs + s], zrecv.at[seqs + s])
+        for s in range(seqs)
+    ]
+    for s in range(seqs):
+        ffn_rings[s].begin()
+        load_piece(s, (rank + 2) % 4).start()
+
+    def ffn_step(s, j):
+        ffn_rings[s].step(j)
+        load_piece(s, (rank + 2 - j) % 4).start()
+
+    def in_hbm(ref, axis):
+        size = ref.shape[axis] // 4
+        h2 = (size if axis == 0 else ref.shape[0]) // 2
+
+        def get(k, h):
+            if axis == 0:
+                return ref.at[pl.ds(k * size + h * h2, h2), :]
+            return ref.at[pl.ds(h * h2, h2), pl.ds(k * size, size)]
+
+        return get
+
+    def halves(ref):
+        h2 = ref.shape[0] // 2
+        return lambda h: ref.at[pl.ds(h * h2, h2), :]
+
+    def in_vmem(ref):
+        h2 = ref.shape[1] // 2
+        return lambda k, h: ref.at[k, pl.ds(h * h2, h2), :]
+
+    def scatter(i, get, wide, land_x, land_y, temps):
+        return Scatter(get, wide.at[0], wide.at[1], land_x, land_y, temps, xsend.at[i], xrecv.at[i], xload.at[i], near_x, near_y)
+
+    s_gate = scatter(0, in_hbm(dgate_hbm, 0), wide_a.at[0], halves(landx0), halves(landy0), temp_a)
+    s_up = scatter(1, in_hbm(dup_hbm, 0), wide_a.at[1], halves(landx1), halves(landy1), temp_a)
+    s_down = scatter(2, in_hbm(ddown_hbm, 1), wide_b, halves(landx2), halves(landy2), temp_b)
+    s_out = scatter(3, in_vmem(go_v), wide_o, halves(land_o.at[0]), halves(land_o.at[1]), temp_o)
+    s_qkv = scatter(4, in_vmem(gq_v), wide_q, halves(land_q.at[0]), halves(land_q.at[1]), temp_q)
+    for item in (s_gate, s_up, s_down):
+        item.begin()
+
+    load_gb.wait()
+    load_outw.wait()
+
+    def give(s):
+        return remote(da_send.at[s], da_got.at[s], exsend.at[0, s], exrecv.at[0, s], near_core)
+
+    def exchange(s):
+        return remote(d_send.at[s], d_got.at[s], exsend.at[1, s], exrecv.at[1, s], near_core)
+
+    def branch_rows(s, carry):
+        here = pl.ds(pl.multiple_of(s * span, span), span)
+        parts = []
+        for q in range(2):
+            cut = slice(q * (nq * hd // 2), (q + 1) * (nq * hd // 2))
+            da = dot_nt(rows_v[0, cut, :], act_v[here, :half]) + dot_nt(rows_v[1, cut, :], act_v[here, half:])
+            parts.append(da.astype(BF16))
+        da_own[s] = jnp.where(first_core, parts[0], parts[1])
+        da_send[s] = jnp.where(first_core, parts[1], parts[0])
+        give(s).start()
+        return carry
+
+    lax.fori_loop(0, seqs, branch_rows, 0)
+
+    def load_x(s):
+        return [pltpu.make_async_copy(xr_hbm.at[s, :, pl.ds(k * half, half)], rows_v.at[k], load_sem.at[8 + k]) for k in range(2)]
+
+    for copy in load_x(0):
+        copy.start()
+    for copy in load_att:
+        copy.wait()
+
+    scale = log2e / math.sqrt(hd)
+    back = 1.0 / math.sqrt(hd)
+    krow = lax.broadcasted_iota(jnp.int32, (block, groups * block), 0)
+    qcol = lax.broadcasted_iota(jnp.int32, (block, groups * block), 1) % block
+    base = groups * hd
+
+    def attention(s, carry):
+        give(s).wait_recv()
+        low, high = join_positions(core, da_own[s], da_got[s])
+        da_all[:, :span] = low
+        da_all[:, span:] = high
+        length = len_ref[s]
+        grads[base:, :] = jnp.zeros((2 * hd, slots), F32)
+        for i in range(slots // block):
+            cut = slice(i * block, (i + 1) * block)
+            q = jnp.concatenate([all_v[s, g * hd : (g + 1) * hd, cut] for g in range(groups)], axis=1)
+            da = jnp.concatenate([da_all[g * hd : (g + 1) * hd, cut] for g in range(groups)], axis=1)
+            at = jnp.concatenate([att_v[s, g * hd : (g + 1) * hd, cut] for g in range(groups)], axis=1)
+            inv = jnp.concatenate([inv_v[s, g : g + 1, cut] for g in range(groups)], axis=1)
+            delta = jnp.sum(at.astype(F32) * da.astype(F32), axis=0, keepdims=True)
+            dq = jnp.zeros((hd, groups * block), F32)
+            for j in range(i + 1):
+                kcut = slice(j * block, (j + 1) * block)
+                key = all_v[s, base : base + hd, kcut]
+                score = dot_tn(key, q) * scale
+                ok = (krow + j * block) < length
+                if j == i:
+                    ok = ok & (krow <= qcol)
+                p = jnp.where(ok, jnp.exp2(score) * inv, 0.0)
+                dp = dot_tn(all_v[s, base + hd : base + 2 * hd, kcut], da)
+                ds = (p * (dp - delta)).astype(BF16)
+                dq = dq + dot_nn(key, ds)
+                grads[base : base + hd, kcut] += dot_nt(q, ds) * back
+                grads[base + hd : base + 2 * hd, kcut] += dot_nt(da, p.astype(BF16))
+            dq = dq * back
+            for g in range(groups):
+                grads[g * hd : (g + 1) * hd, cut] = dq[:, g * block : (g + 1) * block]
+        mine, theirs = join_positions(core, grads[:, :span], grads[:, span:])
+        d_own[s] = mine.astype(BF16)
+        d_send[s] = theirs.astype(BF16)
+        exchange(s).start()
+
+        @pl.when(s == 0)
+        def _():
+            ffn_step(0, 1)
+
+        @pl.when(s == seqs - 1)
+        def _():
+            ffn_step(1, 1)
+            s_gate.pass_on()
+
+        return carry
+
+    lax.fori_loop(0, seqs, attention, 0)
+
+    load_tok.wait()
+    blocks_o = [remote(so_v.at[k], go_v.at[k], osend.at[k], orecv.at[k], near_core) for k in range(4)]
+    size_o = half // 4
+    for k in range(4):
+        cut = slice(half + k * size_o, half + (k + 1) * size_o)
+        so_v[k] = dot_tn(tok_v[...], act_v[:, cut]).astype(BF16)
+        blocks_o[k].start()
+
+    cosine, sine = cos_ref[...], sin_ref[...]
+    sides = (nq // 2, nk // 2, nk // 2)
+    lines_v[:8, :] = jnp.zeros((8, width), F32)
+    lines_v[8:, :] = gain2_ref[...] * (1.0 / lax.axis_size("tensor"))
+    small_v[: 2 * hd, :] = jnp.zeros((2 * hd, 128), F32)
+    for k in range(2):
+        small_v[2 * hd + 8 * k : 2 * hd + 8 * k + 8, :] = stat_ref[k] * (1.0 / lax.axis_size("tensor"))
+    small_v[2 * hd + 16 : 2 * hd + 24, :] = jnp.zeros((8, 128), F32)
+    valid_slots = jnp.int32(0)
+    for s in range(seqs):
+        valid_slots = valid_slots + jnp.clip(len_ref[s] - start, 0, span)
+    count = valid_slots.astype(F32) * (1.0 / (1024.0 * lax.axis_size("tensor")))
+    small_v[2 * hd + 24 : 2 * hd + 32, :] = jnp.broadcast_to(count, (8, 128))
+    load_qkvw.wait()
+
+    def fold_columns(values):
+        return sum(values[:, k * 128 : (k + 1) * 128] for k in range(values.shape[1] // 128))
+
+    def heads_rows(s, carry):
+        exchange(s).wait_recv()
+        low, high = join_positions(core, d_own[s].astype(F32), d_got[s].astype(F32))
+        parts = [[], [], []]
+        for side in (low, high):
+            at = 0
+            for kind, number in enumerate(sides):
+                for _ in range(number):
+                    parts[kind].append(side[at : at + hd])
+                    at += hd
+        done = []
+        for h in range(nq + nk):
+            kind = 0 if h < nq else 1
+            g = parts[kind][h - kind * nq]
+            a, b = g[: hd // 2], g[hd // 2 :]
+            g = jnp.concatenate([a * cosine + b * sine, b * cosine - a * sine], axis=0)
+            v = pre_v[s, h * hd : (h + 1) * hd, :]
+            inv = lax.rsqrt(jnp.mean(v * v, axis=0, keepdims=True) + epsilon)
+            hat = v * inv
+            small_v[kind * hd : (kind + 1) * hd, :] += fold_columns(g * hat)
+            gg = g * (qg_ref[...] if kind == 0 else kg_ref[...])
+            done.append(inv * (gg - hat * jnp.mean(gg * hat, axis=0, keepdims=True)))
+        done += parts[2]
+        for h in range(nq + 2 * nk):
+            pair = h % 2
+            if pair == 0:
+                two = jnp.concatenate([done[h], done[h + 1]], axis=0).T.astype(BF16)
+                dpre_v[pl.ds(pl.multiple_of(s * span, span), span), h * hd : (h + 2) * hd] = two
+        for copy in load_x(s):
+            copy.wait()
+        for m in range(4):
+            rows = slice(m * share, (m + 1) * share)
+            xs = [rows_v[k, rows, :].astype(F32) for k in range(2)]
+            mean = sum(jnp.sum(x * x, axis=-1, keepdims=True) for x in xs) * (1.0 / width)
+            inv = lax.rsqrt(mean + epsilon)
+            dpre = dpre_v[pl.ds(pl.multiple_of(s * span + m * share, share), share), :]
+            for k in range(2):
+                part = dot_nt(dpre, qkvw_v[k])
+                cut = slice(k * half, (k + 1) * half)
+                first_v[s, m, :, cut] = part.astype(BF16)
+                both = part * (xs[k] * inv)
+                lines_v[:8, cut] += sum(both[8 * r : 8 * r + 8] for r in range(share // 8))
+
+        @pl.when(s == 0)
+        def _():
+            for copy in load_x(1):
+                copy.start()
+            first_rings[0].begin()
+            ffn_step(0, 2)
+
+        @pl.when(s == seqs - 1)
+        def _():
+            first_rings[1].begin()
+            ffn_step(1, 2)
+            s_up.pass_on()
+
+        return carry
+
+    lax.fori_loop(0, seqs, heads_rows, 0)
+
+    for k in range(4):
+        blocks_o[k].wait_recv()
+        cut = slice(k * size_o, (k + 1) * size_o)
+        go_v[k] = (dot_tn(tok_v[...], act_v[:, cut]) + go_v[k].astype(F32)).astype(BF16)
+    s_out.begin()
+    load_n1 = load(0, n1_hbm, act_v)
+    first_rings[0].step(1)
+    load_n1.wait()
+    blocks_q = [remote(sq_v.at[k], gq_v.at[k], qsend.at[k], qrecv.at[k], near_core) for k in range(4)]
+    size_q = half // 4
+    for k in range(4):
+        cut = slice(half + k * size_q, half + (k + 1) * size_q)
+        sq_v[k] = dot_tn(act_v[:, cut], dpre_v[...]).astype(BF16)
+        blocks_q[k].start()
+    for k in range(4):
+        blocks_q[k].wait_recv()
+        cut = slice(k * size_q, (k + 1) * size_q)
+        gq_v[k] = (dot_tn(act_v[:, cut], dpre_v[...]) + gq_v[k].astype(F32)).astype(BF16)
+    s_qkv.begin()
+
+    piece = width // 8
+
+    def place(tile, dst, s):
+        copies = []
+        for o in range(2):
+            for k in range(4):
+                b = near[k] * 2 + (core if o == 0 else 1 - core)
+                cut = pl.ds(pl.multiple_of(b * piece, piece), piece)
+                copies.append(
+                    pltpu.make_async_copy(tile.at[:, pl.ds((o * 4 + k) * piece, piece)], dst.at[s, :, cut], outs_sem.at[o * 4 + k])
+                )
+        return copies
+
+    def out_share(s):
+        keep = pltpu.make_async_copy(hidden_hbm.at[piece_rows(s, rank), :], tile_v, tile_sem.at[0])
+        keep.start()
+        ffn_rings[s].arrived()
+        read = ffn_rings[s].own(rank)
+        keep.wait()
+
+        def body(cut, first):
+            ffn = slots_v[s, 2, cut, :].astype(F32) + read(cut).astype(F32)
+            otile_v[cut, :] = (tile_v[cut, :] + ffn).astype(BF16)
+            spot = start + rank * share + first + lax.broadcasted_iota(jnp.int32, (16, 1), 0)
+            valid = (spot < len_ref[s]).astype(F32)
+            small_v[2 * hd + 16 : 2 * hd + 24, :] += fold_lanes(valid * ffn * ffn)
+
+        by_pieces(share, body)
+        copies = place(otile_v, out_hbm, s)
+        for copy in copies:
+            copy.start()
+        for copy in copies:
+            copy.wait()
+
+    def in_share(s):
+        loads = [
+            pltpu.make_async_copy(gh_hbm.at[piece_rows(s, rank), :], tile_v, tile_sem.at[0]),
+            pltpu.make_async_copy(xr_hbm.at[s, pl.ds(pl.multiple_of(rank * share, share), share), :], xtile_v, tile_sem.at[1]),
+        ]
+        for copy in loads:
+            copy.start()
+        for copy in loads:
+            copy.wait()
+        first_rings[s].arrived()
+
+        def body(cut, first):
+            e = slots_v[seqs + s, 2, cut, :].astype(F32) + first_v[s, rank, cut, :].astype(F32)
+            x = xtile_v[cut, :].astype(F32)
+            inv = inverse_rms(x)
+            hat = x * inv
+            eg = e * gain_ref[...]
+            itile_v[cut, :] = tile_v[cut, :] + inv * (eg - hat * jnp.mean(eg * hat, axis=-1, keepdims=True))
+
+        by_pieces(share, body)
+        copies = place(itile_v, gin_hbm, s)
+        for copy in copies:
+            copy.start()
+        for copy in copies:
+            copy.wait()
+
+    def lump(n, src, dst, device):
+        return remote(src, dst, smsend.at[n], smrecv.at[n], device)
+
+    def small_hop(n, device, pairs):
+        copies = [lump(2 * n, small_v, small_r.at[n], device)]
+        for i, (src, dst, _) in enumerate(pairs):
+            copies.append(remote(src, dst, smsend.at[2 * n + 1 + 10 * i], smrecv.at[2 * n + 1 + 10 * i], device))
+        for copy in copies:
+            copy.start()
+        for copy in copies:
+            copy.wait()
+        small_v[...] += small_r[n]
+        for _, dst, into in pairs:
+            lines_v[:, into] += dst[...]
+
+    def columns(k):
+        return slice(k * piece, (k + 1) * piece)
+
+    out_share(0)
+    first_rings[1].step(1)
+    s_down.pass_on()
+    out_share(1)
+    first_rings[0].step(2)
+    s_out.pass_on()
+    small_hop(0, near_core, [(lines_v.at[:, pl.ds(half, half)], lin1, slice(0, half))])
+    s_gate.finish(stage_a, in_out(ggate_hbm), xstore.at[0])
+    first_rings[1].step(2)
+    s_qkv.pass_on()
+    small_hop(
+        1, near_x,
+        [(lines_v.at[:, pl.ds(piece, piece)], lin2.at[0], columns(0)), (lines_v.at[:, pl.ds(3 * piece, piece)], lin2.at[1], columns(2))],
+    )
+    small_hop(2, near_y, [(lines_v.at[:, pl.ds(2 * piece, piece)], lin3, columns(0))])
+    s_up.finish(stage_a, in_out(gup_hbm), xstore.at[1])
+    in_share(0)
+    s_down.finish(stage_b, in_out(gdown_hbm), xstore.at[2])
+    small_hop(3, {"tensor": xor_one(rank)}, [(lines_v.at[:, pl.ds(0, piece)], lin4, columns(0))])
+    s_out.finish(stage_o, in_out(gout_hbm), xstore.at[3])
+    small_hop(4, z_far, [(lines_v.at[:, pl.ds(0, piece)], lin5, columns(0))])
+    lines_out[...] = lines_v[:, :piece]
+    small_out[...] = small_v[...]
+    s_qkv.finish(stage_q, in_out(gqkv_hbm), xstore.at[4])
+    in_share(1)
+    for ring in ffn_rings + first_rings:
+        ring.settle()
+    for item in (s_gate, s_up, s_down, s_out, s_qkv):
+        item.settle()
+    for copy in blocks_o + blocks_q:
+        copy.wait_send()
+    for s in range(seqs):
+        give(s).wait_send()
+        exchange(s).wait_send()
+
+
+def in_out(ref):
+    h2 = ref.shape[0] // 2
+    return lambda h: ref.at[pl.ds(h * h2, h2), :]
+
+
+def backward(
+    lengths, gb, gh, hidden_rows, ffn, xr, n1, tok, outw, qkvw, everything, att, inv, pre, dgate, dup, ddown,
+    gain1, cosine, sine, qgain, kgain, stat, gain2_part, hd, nq, nk,
+):
+    seqs, span, width = xr.shape
+    half = width // 2
+    groups = nq // nk
+    share = span // 4
+    piece = width // 8
+    hidden = dgate.shape[1]
+    cols = qkvw.shape[2]
+    feat = nq * hd
+    block = min(256, span)
+    any_space = pl.BlockSpec(memory_space=pl.ANY)
+    vmem = pl.BlockSpec(memory_space=pltpu.VMEM)
+    dma = pltpu.SemaphoreType.DMA
+    hold = lambda *dims: pltpu.VMEM(dims, BF16)
+    wide = lambda *dims: pltpu.VMEM(dims, F32)
+    big = [
+        shape((seqs, share, width), BF16), shape((seqs, share, width), F32),
+        shape((piece, hidden), F32), shape((piece, hidden), F32), shape((hidden, piece), F32), shape((feat, piece), F32), shape((piece, cols), F32),
+    ]
+    big += [shape((piece, hidden), BF16)] * 4 + [shape((hidden, piece), BF16)] * 2
+    small_rows = 2 * hd + 32
+    small = [shape((16, piece), F32), shape((small_rows, 128), F32)]
+    rows = everything.shape[1]
+    scratch = [
+        hold(seqs * span, width), hold(2, span, half), hold(2, half, cols), hold(seqs * span, feat), hold(*everything.shape), hold(*att.shape),
+        wide(*inv.shape), wide(*pre.shape), wide(rows, 2 * span), hold(groups * hd, 2 * span),
+        hold(seqs, feat // 2, span), hold(seqs, feat // 2, span), hold(seqs, feat // 2, span),
+        hold(seqs, rows, span), hold(seqs, rows, span), hold(seqs, rows, span), hold(seqs * span, cols),
+        hold(seqs, 4, share, width), hold(2 * seqs, 3, share, width), hold(seqs, share, width),
+        hold(2, 2, piece // 2, hidden), hold(2, hidden // 2, piece), hold(3, piece // 2, hidden), hold(3, hidden // 2, piece),
+        wide(piece // 2, hidden), wide(hidden // 2, piece),
+        hold(4, feat, piece), hold(4, feat, piece), hold(2, feat // 2, piece), hold(2, feat, piece), hold(3, feat // 2, piece), wide(feat // 2, piece),
+        hold(4, piece, cols), hold(4, piece, cols), hold(2, piece // 2, cols), hold(2, piece, cols), hold(3, piece // 2, cols), wide(piece // 2, cols),
+        wide(share, width), hold(share, width), hold(share, width), wide(share, width),
+        wide(16, width), wide(small_rows, 128), wide(16, half), wide(2, 16, piece), wide(16, piece), wide(16, piece), wide(16, piece), wide(5, small_rows, 128),
+        dma((10,)), dma((2 * seqs, 3)), dma((2 * seqs, 3)), dma((seqs,)), dma((5, 6)), dma((5, 6)), dma((5, 3)), dma((5,)),
+        dma((2, seqs)), dma((2, seqs)), dma((4,)), dma((4,)), dma((4,)), dma((4,)), dma((2,)), dma((8,)), dma((20,)), dma((20,)),
+    ]
+    tokens = seqs * span
+    return pl.pallas_call(
+        functools.partial(backward_kernel, hd, nq, nk, block),
+        in_specs=[SMEM] + [any_space] * 16 + [vmem] * 7,
+        out_specs=[any_space] * len(big) + [vmem] * 2,
+        out_shape=big + small,
+        scratch_shapes=scratch,
+        compiler_params=pltpu.CompilerParams(vmem_limit_bytes=VMEM_MOST, collective_id=3, has_side_effects=True),
+        cost_estimate=cost(4 * tokens * width * (cols + feat), 60 * tokens * width),
+        name="attention_backward",
+    )(
+        lengths, gb, gh, hidden_rows, ffn, xr, n1, tok, outw, qkvw, everything, att, inv, pre, dgate, dup, ddown,
+        gain1, cosine, sine, qgain, kgain, stat, gain2_part,
+    )
+
+
+def per_device_general(
     inputs,
     cotangent,
     lengths,
@@ -1484,7 +1997,6 @@
     groups = nq // nk
     dp = lax.axis_size("dp")
     tensor = lax.axis_size("tensor")
-    row = lax.axis_index("dp")
     core = lax.axis_index("context")
     rank = lax.axis_index("tensor")
     chunks = 2
@@ -1493,7 +2005,7 @@
     lengths = lengths.astype(jnp.int32)
     start = (core * span).astype(jnp.int32)
     core1 = core.astype(jnp.int32).reshape(1)
-    ids = block_order(dp, row, core)
+    ids = block_order(dp, core)
     order = 2 * dp if (width // (2 * dp)) % 128 == 0 else 1
 
     positions = start + jnp.arange(span, dtype=jnp.int32)
@@ -1505,56 +2017,43 @@
 
     w_qkv = jnp.concatenate([w_query, key_projection_weight, value_projection_weight], axis=1)
     saved = []
-    if dp == 4 and tensor == 4 and order == 8:
-        gains = jnp.pad(jnp.stack([attn_gain, ffn_gain]), ((0, 14), (0, 0)))
-        (xr, n1, gf, qkv, out_w, gate, up, down, hidden_all, n2_all, gains, pre_all, everything_all, att_all, inv_all, tok, stat) = forward(
-            lengths, inputs, cotangent, w_qkv, w_output, w_gate, w_up, w_down, gains, cosine, sine, qgain, kgain, hd, nq, nk
-        )
-        gains = jnp.swapaxes(gains[:, :2], 0, 1).reshape(2, width).astype(F32)
-        gain1, gain2 = gains[0:1], gains[1:2]
-        stats = jnp.sum(stat, axis=(1, 2))
-        for s in range(seqs):
-            seq_scal = jnp.stack([lengths[s], core.astype(jnp.int32)])
-            saved.append((pre_all[s], everything_all[s], att_all[s], inv_all[s], seq_scal))
-        tok = tok.reshape(seqs * span, nq * hd)
-    else:
-        gains, _ = gather_blocks(jnp.stack([attn_gain, ffn_gain]), 1, dp)
-        gains = jnp.concatenate([gains[0], gains[1]], axis=1).astype(F32)
-        gain1, gain2 = gains[0:1], gains[1:2]
-        qkv, mark = gather_blocks(w_qkv, 0, dp)
-        out_w, mark = gather_blocks(tie(w_output, mark), 1, dp)
-        gate, mark = gather_blocks(tie(w_gate, mark), 0, dp)
-        up, mark = gather_blocks(tie(w_up, mark), 0, dp)
-        down, mark = gather_blocks(tie(w_down, mark), 1, dp)
-
-        scal = jnp.concatenate([lengths, start.reshape(1), ids])
-        x_in, cot_in = inputs, cotangent
-        if order == 1:
-            x_in, cot_in = to_relative(x_in, dp, core), to_relative(cot_in, dp, core)
-        xr, n1, gf = begin(x_in, cot_in, gain1, scal, order)
-
-        parts, tok = [], []
-        for s in range(seqs):
-            pre, own, oth = heads(n1, s, qkv, cosine, sine, qgain, kgain, core1, hd, nq, nk)
-            seq_scal = jnp.stack([lengths[s], core.astype(jnp.int32)])
-            everything, att, inv, mine, theirs = attend(seq_scal, own, over_core(oth), groups)
-            branched = branch(mine, over_core(theirs), out_w, core1, chunks)
-            saved.append((pre, everything, att, inv, seq_scal))
-            tok.append(jnp.swapaxes(branched[0], 0, 1))
-            parts.append(branched[1:])
-        tok = jnp.concatenate(tok, axis=0)
-
-        stats = jnp.zeros((2,), F32)
-        hidden_all, n2_all = [], []
-        for s in range(seqs):
-            for k in range(chunks):
-                terms = sum_terms(parts[s][k], tensor)
-                place = jnp.stack([lengths[s], start + k * rows])
-                hidden, n2, stat = second_norm(place, xr, s, k, gain2, terms)
-                hidden_all.append(hidden)
-                n2_all.append(n2)
-                stats = stats + stat[:2, 0]
-        hidden_all, n2_all = jnp.concatenate(hidden_all), jnp.concatenate(n2_all)
+    gains = gather_blocks(jnp.stack([attn_gain, ffn_gain]), 1)
+    gains = jnp.concatenate([gains[0], gains[1]], axis=1).astype(F32)
+    gain1, gain2 = gains[0:1], gains[1:2]
+    qkv = gather_blocks(w_qkv, 0)
+    out_w = gather_blocks(w_output, 1)
+    gate = gather_blocks(w_gate, 0)
+    up = gather_blocks(w_up, 0)
+    down = gather_blocks(w_down, 1)
+
+    scal = jnp.concatenate([lengths, start.reshape(1), ids])
+    x_in, cot_in = inputs, cotangent
+    if order == 1:
+        x_in, cot_in = to_relative(x_in, dp, core), to_relative(cot_in, dp, core)
+    xr, n1, gf = begin(x_in, cot_in, gain1, scal, order)
+
+    parts, tok = [], []
+    for s in range(seqs):
+        pre, own, oth = heads(n1, s, qkv, cosine, sine, qgain, kgain, core1, hd, nq, nk)
+        seq_scal = jnp.stack([lengths[s], core.astype(jnp.int32)])
+        everything, att, inv, mine, theirs = attend(seq_scal, own, over_core(oth), groups)
+        branched = branch(mine, over_core(theirs), out_w, core1, chunks)
+        saved.append((pre, everything, att, inv, seq_scal))
+        tok.append(jnp.swapaxes(branched[0], 0, 1))
+        parts.append(branched[1:])
+    tok = jnp.concatenate(tok, axis=0)
+
+    stats = jnp.zeros((2,), F32)
+    hidden_all, n2_all = [], []
+    for s in range(seqs):
+        for k in range(chunks):
+            terms = [lax.psum(parts[s][k], "tensor")]
+            place = jnp.stack([lengths[s], start + k * rows])
+            hidden, n2, stat = second_norm(place, xr, s, k, gain2, terms)
+            hidden_all.append(hidden)
+            n2_all.append(n2)
+            stats = stats + stat[:2, 0]
+    hidden_all, n2_all = jnp.concatenate(hidden_all), jnp.concatenate(n2_all)
 
     ffn_squares = jnp.zeros((), F32)
     out_shares = []
@@ -1585,36 +2084,26 @@
     def reduced(lefts, rights, axis):
         oth = weight_grad(lefts, rights, 1, axis)
         own = weight_grad(lefts, rights, 0, axis, over_core(oth))
-        return scatter_blocks(own, axis, dp)
-
-    if dp == 4 and tensor == 4 and order == 8:
-        ffn_all, gb_all, gh_all, d_gate, d_up, d_down, gain2_grad = feed_both(
-            n2_all, gf.reshape(seqs * span, width), gate, up, down, hidden_all, gain2
-        )
-        gain2_grad = jnp.sum(gain2_grad, axis=0, keepdims=True)
-        ffn, gb, gh = [[[a[(s * chunks + k) * rows : (s * chunks + k + 1) * rows] for k in range(chunks)] for s in range(seqs)] for a in (ffn_all, gb_all, gh_all)]
-        grad_w_gate = scatter_blocks(d_gate, 0, dp)
-        grad_w_up = scatter_blocks(d_up, 0, dp)
-        grad_w_down = scatter_blocks(d_down, 1, dp)
-    else:
-        inner, gg, gu, ffn, gn = [[[None] * chunks for _ in range(seqs)] for _ in range(5)]
-        for s in range(seqs):
-            for k in range(chunks):
-                inner[s][k], gg[s][k], gu[s][k], ffn[s][k], gn[s][k] = feed(
-                    n2_all, s * chunks + k, rows, gf, s, k, gate, up, down
-                )
-        gain2_grad = jnp.zeros((1, width), F32)
-        gb, gh = [[[None] * chunks for _ in range(seqs)] for _ in range(2)]
-        for s in range(seqs):
-            for k in range(chunks):
-                terms = sum_terms(gn[s][k], tensor)
-                gb[s][k], gh[s][k], gain_part = second_back(hidden_all, s * chunks + k, gf, s, k, gain2, terms)
-                gain2_grad = gain2_grad + gain_part
-        gf_list = slices(gf.reshape(seqs * span, width), seqs * chunks)
-        n2_list = slices(n2_all, seqs * chunks)
-        grad_w_down = reduced(flat(inner), gf_list, 1)
-        grad_w_gate = reduced(n2_list, flat(gg), 0)
-        grad_w_up = reduced(n2_list, flat(gu), 0)
+        return scatter_blocks(own, axis)
+
+    inner, gg, gu, ffn, gn = [[[None] * chunks for _ in range(seqs)] for _ in range(5)]
+    for s in range(seqs):
+        for k in range(chunks):
+            inner[s][k], gg[s][k], gu[s][k], ffn[s][k], gn[s][k] = feed(
+                n2_all, s * chunks + k, rows, gf, s, k, gate, up, down
+            )
+    gain2_grad = jnp.zeros((1, width), F32)
+    gb, gh = [[[None] * chunks for _ in range(seqs)] for _ in range(2)]
+    for s in range(seqs):
+        for k in range(chunks):
+            terms = [lax.psum(gn[s][k], "tensor")]
+            gb[s][k], gh[s][k], gain_part = second_back(hidden_all, s * chunks + k, gf, s, k, gain2, terms)
+            gain2_grad = gain2_grad + gain_part
+    gf_list = slices(gf.reshape(seqs * span, width), seqs * chunks)
+    n2_list = slices(n2_all, seqs * chunks)
+    grad_w_down = reduced(flat(inner), gf_list, 1)
+    grad_w_gate = reduced(n2_list, flat(gg), 0)
+    grad_w_up = reduced(n2_list, flat(gu), 0)
     for s in range(seqs):
         got = ring_scatter(piece_of(ffn[s]), tensor, rank)
         halves = [hidden_all[(s * chunks + k) * rows : (s * chunks + k + 1) * rows] for k in range(chunks)]
@@ -1651,32 +2140,10 @@
     small = jnp.concatenate([head_gain, stats / tensor, ffn_squares.reshape(1), counts.reshape(1)])
     small = jnp.pad(small, (0, (-small.shape[0]) % 128)).reshape(1, -1)
     lines = jnp.concatenate([gain1_grad, gain2_grad], axis=0)
-    if dp == 4 and tensor == 4:
-        half = width // 2
-        quarter = half // 4
-
-        def join(part):
-            return jnp.concatenate([part.reshape(1, -1), small], axis=1)
-
-        got = over_core(join(lines[:, half:]))
-        lines = lines[:, :half] + got[:, : 2 * half].reshape(2, half)
-        small = small + got[:, 2 * half :]
-        lines = lines.reshape(2, 4, quarter)
-        got = over_x(join(lines[:, 1::2]))
-        lines = lines[:, 0::2] + got[:, : 4 * quarter].reshape(2, 2, quarter)
-        small = small + got[:, 4 * quarter :]
-        got = over_y(join(lines[:, 1]))
-        lines = lines[:, 0] + got[:, : 2 * quarter].reshape(2, quarter)
-        small = small + got[:, 2 * quarter :]
-        for step in (1, 2):
-            got = lax.ppermute(join(lines), "tensor", [(i, i ^ step) for i in range(4)])
-            lines = lines + got[:, : 2 * quarter].reshape(2, quarter)
-            small = small + got[:, 2 * quarter :]
-    else:
-        piece = width // (2 * dp)
-        lines = to_absolute(lines, dp, core) if dp != 4 else lines.reshape(2, 2 * dp, piece)[:, jnp.argsort(ids)].reshape(2, width)
-        lines, small = lax.psum((lines, small), ("dp", "context", "tensor"))
-        lines = lax.dynamic_slice_in_dim(lines, lax.axis_index(("dp", "context")) * piece, piece, 1)
+    piece = width // (2 * dp)
+    lines = to_absolute(lines, dp, core)
+    lines, small = lax.psum((lines, small), ("dp", "context", "tensor"))
+    lines = lax.dynamic_slice_in_dim(lines, lax.axis_index(("dp", "context")) * piece, piece, 1)
     small = small[0]
     rms_values = jnp.sqrt(small[2 * hd : 2 * hd + 3] / (small[2 * hd + 3] * width))
 
@@ -1702,6 +2169,79 @@
     )
 
 
+def per_device_square(
+    inputs,
+    cotangent,
+    lengths,
+    w_query,
+    key_projection_weight,
+    value_projection_weight,
+    w_output,
+    w_gate,
+    w_up,
+    w_down,
+    attn_gain,
+    ffn_gain,
+    query_gain,
+    key_gain,
+):
+    seqs, span, width = inputs.shape
+    hd = query_gain.shape[0]
+    nq = w_query.shape[1] // hd
+    nk = key_projection_weight.shape[1] // hd
+    lengths = lengths.astype(jnp.int32)
+    positions = lax.axis_index("context") * span + jnp.arange(span, dtype=jnp.int32)
+    freqs = rope_base ** (-(jnp.arange(hd // 2, dtype=F32) * (2.0 / hd)))
+    angles = freqs[:, None] * positions.astype(F32)[None, :]
+    cosine, sine = jnp.cos(angles), jnp.sin(angles)
+    qgain = query_gain.astype(F32).reshape(hd, 1)
+    kgain = key_gain.astype(F32).reshape(hd, 1)
+    w_qkv = jnp.concatenate([w_query, key_projection_weight, value_projection_weight], axis=1)
+    gains = jnp.pad(jnp.stack([attn_gain, ffn_gain]), ((0, 14), (0, 0)))
+
+    (xr, n1, gf, qkv, out_w, gate, up, down, hidden, n2, gains, pre, everything, att, inv, tok, stat) = forward(
+        lengths, inputs, cotangent, w_qkv, w_output, w_gate, w_up, w_down, gains, cosine, sine, qgain, kgain, hd, nq, nk
+    )
+    gains = jnp.swapaxes(gains[:, :2], 0, 1).reshape(2, width).astype(F32)
+    tokens = seqs * span
+    ffn, gb, gh, d_gate, d_up, d_down, gain2_part = feed_both(
+        n2, gf.reshape(tokens, width), gate, up, down, hidden, gains[1:2]
+    )
+    results = backward(
+        lengths, gb, gh, hidden, ffn, xr, n1.reshape(tokens, width), tok.reshape(tokens, nq * hd), out_w, qkv,
+        everything, att, inv, pre, d_gate, d_up, d_down, gains[0:1], cosine, sine, qgain, kgain, stat, gain2_part, hd, nq, nk,
+    )
+    output, grad_inputs, grad_gate, grad_up, grad_down, grad_out, grad_qkv = results[:7]
+    lines, small = results[-2:]
+    nqc, nkc = nq * hd, nk * hd
+    totals = jnp.sum(small[2 * hd :].reshape(4, -1), axis=1)
+    return (
+        output,
+        grad_inputs,
+        grad_qkv[:, :nqc],
+        grad_qkv[:, nqc : nqc + nkc],
+        grad_qkv[:, nqc + nkc :],
+        grad_out,
+        grad_gate,
+        grad_up,
+        grad_down,
+        jnp.sum(lines[:8], axis=0),
+        jnp.sum(lines[8:], axis=0),
+        jnp.sum(small[:hd], axis=1),
+        jnp.sum(small[hd : 2 * hd], axis=1),
+        jnp.sqrt(totals[:3] / (totals[3] * width)),
+    )
+
+
+def per_device(*args):
+    inputs, w_query = args[0], args[3]
+    seqs, span, width = inputs.shape
+    square = lax.axis_size("dp") == 4 and lax.axis_size("tensor") == 4 and lax.axis_size("context") == 2
+    if square and width % 2048 == 0 and span % 512 == 0 and seqs == 2 and w_query.shape[1] == span:
+        return per_device_square(*args)
+    return per_device_general(*args)
+
+
 def solution(mesh):
     both = ("dp", "context")
     rows = P(both, "tensor")

time: 653 us -> 519 us (0.79)
  Pallas kernels: 395 us -> 482 us
  waiting for transfers between devices: 85.8 us -> 0 us
  other arithmetic: 57.3 us -> 9.79 us
  starting transfers between devices: 43.7 us -> 0 us
  local copies, waits for them, and re-layouts: 56.9 us -> 16.1 us
    pallas_call x14 -> x1, Pallas kernels: 80 us -> 167 us  [backward(): pl.pallas_call(functools.partial(backward_kernel, hd, nq, nk, block), in_...]
    ppermute x43 -> x0, waiting for transfers between devices: 85.8 us -> none  [the longest x11 42.8 us: over_x(): return lax.ppermute(value, 'dp', [(i, i ^ 1) for i in range(4)])]
    ppermute x43 -> x0, starting transfers between devices: 43.7 us -> none  [the longest x12 14.4 us: ring_scatter(): moving = lax.ppermute(moving, 'tensor', ring)]
    slice x24 -> x4, local copies, waits for them, and re-layouts: 32.5 us -> 4.9 us  [the longest x1 2.02 us: per_device_square(): grad_qkv[:, :nqc]]
    add x15 -> x0, other arithmetic: 15.3 us -> none  [the longest x5 13.6 us: scatter_blocks(): return block(0).astype(F32) + got_x.astype(F32) + got_y.astype(F32)]
    another operation x9 -> x1, other arithmetic: 13.3 us -> 0.61 us  [per_device_square(): gains = jnp.pad(jnp.stack([attn_gain, ffn_gain]), ((0, 14), (0, 0)))]
    convert_element_type x10 -> x2, other arithmetic: 12.8 us -> 0.77 us  [the longest x1 0.77 us: per_device_square(): gains = jnp.swapaxes(gains[:, :2], 0, 1).reshape(2, width).astype(F32)]
    squeeze x5 -> x0, local copies, waits for them, and re-layouts: 9.81 us -> none  [the longest x1 2.8 us: per_device(): everything_all[s]]
  transfers between devices with their start and end apart: 43 -> 0, of which waited for: 14 -> 0; matrix products, arithmetic and copies ran while one was open for 14% -> 0% of each run, Pallas kernels for 12% -> 0%
where the time goes in v4:
time: 519 us; the launch traced here: 510 us
  Pallas kernels  482 us (93%)
  local copies, waits for them, and re-layouts  16.1 us (3%)
  other arithmetic  9.79 us (2%)
    pallas_call x1, Pallas kernels, backward(): pl.pallas_call(functools.partial(backward_kernel, hd, nq, nk, block), in_...  167 us
    pallas_call x1, Pallas kernels, forward(): pl.pallas_call(functools.partial(forward_kernel, hd, nq, nk, block, sub),...  166 us
    pallas_call x1, Pallas kernels, feed_both(): pl.pallas_call(functools.partial(feed_both_kernel, hb, sub, rows), in_spe...  150 us

profile of v4, /device:TPU:0, one launch (start us, length us, event | category | flops | bytes accessed | tf_op | source)
XLA Modules:
  0.0 509.8 jit_solution(6144220893491212646)
XLA Ops:
  0.6 0.7 bitcast_convert_fusion.1
  1.3 0.7 bitcast_convert_fusion
  2.0 0.7 stack.9
  2.6 0.7 stack.10
  3.3 0.6 fusion.2.gain_ref
  3.9 0.7 copy.29.kg_ref
  4.6 0.7 copy.28.qg_ref
  5.3 1.0 multiply_sine_fusion
  6.3 1.8 pad_maximum_fusion.wqkv
  8.1 165.6 %attention_forward.1 = (bf16[2,512,2048]{2,1,0:T(8,128)(2,1)}, bf16[2,512,2048]{2,1,0:T(8,128)(2,1)}, bf16[2,512,2048]{2,1,0:T(8,128)(2,1)}, bf16[2,1024,768]{2,...) custom-call(s32[2]{0:T(128)} %len_ref.3, ...), custom_call_target="tpu_custom_call" | custom-call | flops 9663676416 | bytes 167772160 | tf_op jit(solution)/shard_map/attention_forward/pallas_call | solution.py:1028
  173.7 0.8 convert_bitcast_fusion
  174.5 0.6 fusion.4
  175.1 149.8 %feed_forward_both.1 = (bf16[1024,2048]{1,0:T(8,128)(2,1)}, bf16[1024,2048]{1,0:T(8,128)(2,1)}, f32[1024,2048]{1,0:T(8,128)}, bf16[1024,2048]{1,0:T(8,128)(2,1)}...) custom-call(bf16[1024,2048]{1,0:T(8,128)(2,1)} %get-tuple-element.47.n2_hbm, ...), custom_call_target="tpu_custom_call" | custom-call | flops 77309411328 | bytes 125829120 | tf_op jit(solution)/shard_map/feed_forward_both/pallas_call | solution.py:1384
  324.9 166.7 %attention_backward.1 = (bf16[2,128,2048]{2,1,0:T(8,128)(2,1)}, f32[2,128,2048]{2,1,0:T(8,128)}, f32[256,2048]{1,0:T(8,128)}, f32[256,2048]{1,0:T(8,128)}, f32[2...) custom-call(s32[2]{0:T(128)} %len_ref.3, ...), custom_call_target="tpu_custom_call" | custom-call | flops 10737418240 | bytes 125829120 | tf_op jit(solution)/shard_map/attention_backward/pallas_call | solution.py:1962
  491.6 0.0 copy-start.3
  491.6 0.0 copy-start.4
  491.6 1.0 slice_reduce_fusion.2
  492.6 1.4 slice_reduce_fusion
  494.0 0.1 reduce_sum.57
  494.1 0.1 reduce_sum.58
  494.2 0.6 slice.59
  495.4 0.5 divide_sqrt_fusion
  496.0 1.3 slice_reduce_fusion.3
  497.2 1.7 fusion.3
  498.9 2.0 slice.50
  501.0 2.3 copy.38
  503.3 1.3 copy.39
  504.6 0.8 copy.40
  505.4 0.0 copy-done.2
  505.4 1.3 copy.41
  506.7 1.3 copy.42
  508.0 1.3 copy.43
  (9 shorter events, 0.0 us)
Async XLA Ops:
  491.6 11.7 %copy-start.3 = (f32[2,128,2048]{2,1,0:T(8,128)S(1)}, f32[2,128,2048]{2,1,0:T(8,128)}, u32[]{:S(2)}) copy-start(f32[2,128,2048]{2,1,0:T(8,128)} %get-tuple-element.105) | copy-start | bytes 6291460
  491.6 13.0 %copy-start.4 = (f32[512,256]{1,0:T(8,128)S(1)}, f32[512,256]{1,0:T(8,128)}, u32[]{:S(2)}) copy-start(f32[512,256]{1,0:T(8,128)} %get-tuple-element.109) | copy-start | bytes 1572868
  498.9 6.4 %copy-start.2 = (f32[256,2048]{1,0:T(8,128)S(1)}, f32[256,2048]{1,0:T(8,128)}, u32[]{:S(2)}) copy-start(f32[256,2048]{1,0:T(8,128)} %get-tuple-element.110) | copy-start | bytes 6291460
  503.3 3.4 copy-start.1
  505.4 2.6 copy-start

commit v5 on v4

--- a/solution.py
+++ b/solution.py
@@ -723,12 +723,12 @@
 
 def forward_kernel(
     hd, nq, nk, block, sub,
-    len_ref, x_hbm, cot_hbm, wqkv, wout, wgate, wup, wdown, gain_ref, cos_ref, sin_ref, qg_ref, kg_ref,
-    xr_hbm, n1_hbm, gf_hbm, qkv_hbm, out_hbm, gate_hbm, up_hbm, down_hbm, hidden_hbm, n2_hbm,
-    gains_ref, pre_ref, all_ref, att_ref, inv_ref, tok_ref, stat_ref,
+    len_ref, x_hbm, cot_hbm, wq_hbm, wk_hbm, wv_hbm, wout, wgate, wup, wdown, small_ref,
+    xr_hbm, n1_hbm, gf_hbm, qkv_hbm, out_hbm, gate_hbm, up_hbm, down_hbm, hidden_hbm, n2_hbm, rest_hbm, gi_hbm, pre_hbm, all_hbm, att_hbm, tok_hbm,
+    gains_ref, table_ref, inv_ref, stat_ref,
     xr_v, cot_v, n1_v, qkv_v, out_v, ex_own, ex_send, ex_got, at_own, at_send, at_got,
-    part_v, in_v, back_v, total_v, hid_v, norm_v,
-    load_sem, store_sem, wsend, wrecv, wloc, gsend, grecv, exsend, exrecv, zsend, zrecv, hid_sem,
+    part_v, in_v, back_v, total_v, hid_v, norm_v, wqkv, gain_ref, down_v, gi_v, pre_ref, all_ref, att_ref, tok_ref,
+    keep_sem, load_sem, store_sem, shard_sem, rest_sem, down_sem, gi_sem, wsend, wrecv, wloc, gsend, grecv, exsend, exrecv, zsend, zrecv, hid_sem,
 ):
     seqs, span, width = xr_v.shape
     groups = nq // nk
@@ -755,8 +755,14 @@
                             src.at[s, :, cut], dst.at[s, :, pl.ds((o * 4 + k) * piece, piece)], load_sem.at[at, s, o * 4 + k]
                         )
                     )
-    for copy in loads:
+    shards, at = [], 0
+    for k, ref in enumerate((wq_hbm, wk_hbm, wv_hbm)):
+        shards.append(pltpu.make_async_copy(ref, wqkv.at[:, pl.ds(at, ref.shape[1])], shard_sem.at[k]))
+        at += ref.shape[1]
+    for copy in shards + loads:
         copy.start()
+    piece = width // 8
+    gain_ref[...] = jnp.concatenate([small_ref[:, :piece], small_ref[:, piece : 2 * piece], jnp.zeros((14, piece), BF16)], axis=0)
 
     others = []
     for o in range(2):
@@ -775,9 +781,21 @@
         )
     ]
     w_qkv, w_out, w_gate, w_up, w_down = weights
+    for copy in shards:
+        copy.wait()
     w_qkv.first()
-    w_out.first()
     gains_ref[0] = gain_ref[...]
+
+    quarter = hd // 2
+    freqs = jnp.exp(lax.broadcasted_iota(jnp.int32, (quarter, span), 0).astype(F32) * (-2.0 * math.log(rope_base) / hd))
+    angles = freqs * (start + lax.broadcasted_iota(jnp.int32, (quarter, span), 1)).astype(F32)
+    cosine, sine = jnp.cos(angles), jnp.sin(angles)
+    both_gains = jnp.broadcast_to(small_ref[:, 2 * piece :].astype(F32), (8, 2 * hd)).T
+    qgain, kgain = both_gains[:hd, 0:1], both_gains[hd:, 0:1]
+    table_ref[:quarter, :] = cosine
+    table_ref[quarter : 2 * quarter, :] = sine
+    table_ref[2 * quarter : 2 * quarter + hd, :128] = jnp.broadcast_to(qgain, (hd, 128))
+    table_ref[2 * quarter + hd :, :128] = jnp.broadcast_to(kgain, (hd, 128))
 
     for copy in loads[len(loads) // 2 :]:
         copy.wait()
@@ -809,24 +827,25 @@
         n1_v[s, cut, :] = (x * inverse_rms(x) * gain1).astype(BF16)
         return carry
 
-    lax.fori_loop(0, seqs * span // 16, norm_rows, 0)
+    lax.fori_loop(0, span // 16, norm_rows, 0)
+    w_qkv.second()
+    w_out.first()
+    lax.fori_loop(span // 16, seqs * span // 16, norm_rows, 0)
     store_n1 = pltpu.make_async_copy(n1_v, n1_hbm, store_sem.at[2])
     store_n1.start()
-    w_qkv.second()
-    w_out.second()
-    w_gate.first()
     w_qkv.third()
-    w_out.third()
     w_qkv.arrived()
-    w_up.first()
-
-    cosine, sine = cos_ref[...], sin_ref[...]
+
     half = width // 2
 
     def exchange(s):
         return remote(ex_send.at[s], ex_got.at[s], exsend.at[0, s], exrecv.at[0, s], near_core)
 
-    def project(s, carry):
+    def keep(k, s):
+        ref, dst = ((pre_ref, pre_hbm), (all_ref, all_hbm), (att_ref, att_hbm), (tok_ref, tok_hbm))[k]
+        return pltpu.make_async_copy(ref.at[s], dst.at[s], keep_sem.at[k, s])
+
+    def project(s):
         x = n1_v[s]
         flat = dot_nn(x[:, :half], qkv_v[0]) + dot_nn(x[:, half:], qkv_v[1])
         turned = flat.T
@@ -835,7 +854,7 @@
         for h in range(nq + nk):
             v = turned[h * hd : (h + 1) * hd]
             inv = lax.rsqrt(jnp.mean(v * v, axis=0, keepdims=True) + epsilon)
-            v = v * inv * (qg_ref[...] if h < nq else kg_ref[...])
+            v = v * inv * (qgain if h < nq else kgain)
             a, b = v[: hd // 2], v[hd // 2 :]
             done.append(jnp.concatenate([a * cosine - b * sine, b * cosine + a * sine], axis=0))
         for h in range(nk):
@@ -850,11 +869,11 @@
         ex_own[s] = jnp.where(first_core, low, high).astype(BF16)
         ex_send[s] = jnp.where(first_core, high, low).astype(BF16)
         exchange(s).start()
-        return carry
-
-    lax.fori_loop(0, seqs, project, 0)
+        keep(0, s).start()
+
     store_qkv = pltpu.make_async_copy(qkv_v, qkv_hbm, store_sem.at[3])
     store_qkv.start()
+    store_out = pltpu.make_async_copy(out_v, out_hbm, store_sem.at[4])
 
     scale = log2e / math.sqrt(hd)
     krow = lax.broadcasted_iota(jnp.int32, (block, groups * block), 0)
@@ -864,7 +883,7 @@
     def give(s):
         return remote(at_send.at[s], at_got.at[s], exsend.at[1, s], exrecv.at[1, s], near_core)
 
-    def attention(s, carry):
+    def attention(s):
         exchange(s).wait_recv()
         low, high = join_positions(core, ex_own[s], ex_got[s])
         all_ref[s, :, :span] = low
@@ -893,32 +912,56 @@
         at_own[s] = mine
         at_send[s] = theirs
         give(s).start()
-        return carry
-
-    lax.fori_loop(0, seqs, attention, 0)
-    w_out.arrived()
-    store_out = pltpu.make_async_copy(out_v, out_hbm, store_sem.at[4])
-    store_out.start()
+        keep(1, s).start()
+        keep(2, s).start()
 
     moving = Chain(rank, part_v, in_v, back_v, zsend, zrecv)
-
-    def branch_rows(s, carry):
+    subs = moving.count
+
+    def branch_rows(s):
         give(s).wait_recv()
         low, high = join_positions(core, at_own[s], at_got[s])
         att = jnp.concatenate([low, high], axis=0).T
         tok_ref[s] = att
-        for k in range(per):
-            u = s * per + k
-            rows = att[k * sub : (k + 1) * sub]
-            part_v[u, :, :half] = dot_nn(rows, out_v[0]).astype(BF16)
-            part_v[u, :, half:] = dot_nn(rows, out_v[1]).astype(BF16)
-
-            moving.begin(u)
+        keep(3, s).start()
+        many = 2
+        for k in range(0, per, many):
+            rows = att[k * sub : (k + many) * sub]
+            for side in range(2):
+                part = dot_nn(rows, out_v[side]).astype(BF16)
+                for m in range(many):
+                    part_v[s * per + k + m, :, side * half : (side + 1) * half] = part[m * sub : (m + 1) * sub]
+            for m in range(many):
+                u = s * per + k + m
+
+                @pl.when(u < subs)
+                def _():
+                    moving.begin(u)
+
+    def sequence(s, carry):
+        project(s)
+
+        @pl.when(s == 0)
+        def _():
+            w_out.second()
+            w_down.first()
+            w_gate.first()
+
+        attention(s)
+
+        @pl.when(s == 0)
+        def _():
+            w_out.third()
+            w_out.arrived()
+            store_out.start()
+
+        branch_rows(s)
         return carry
 
-    lax.fori_loop(0, seqs, branch_rows, 0)
-    w_gate.second()
-    w_down.first()
+    lax.fori_loop(0, seqs, sequence, 0)
+    rest = [pltpu.make_async_copy(part_v.at[u], rest_hbm.at[u - subs], rest_sem.at[u - subs]) for u in range(subs, total_subs)]
+    for copy in rest:
+        copy.start()
     stat_ref[...] = jnp.zeros_like(stat_ref)
 
     def hidden_store(u):
@@ -956,6 +999,37 @@
         for copy in hidden_store(u):
             copy.start()
 
+    hb = down_v.shape[2]
+    blocks = down_hbm.shape[1] // hb
+
+    def load_down(h):
+        cut = pl.ds(pl.multiple_of(h * hb, hb), hb)
+        return [pltpu.make_async_copy(down_hbm.at[side, cut, :], down_v.at[h % 2, side], down_sem.at[h % 2, side]) for side in range(2)]
+
+    def store_gi(h):
+        cut = pl.ds(pl.multiple_of(h * hb, hb), hb)
+        return pltpu.make_async_copy(gi_v.at[h % 2], gi_hbm.at[:, cut], gi_sem.at[h % 2])
+
+    def grad_inner(h):
+        for copy in load_down(h):
+            copy.wait()
+
+        @pl.when(h + 1 < blocks)
+        def _():
+            for copy in load_down(h + 1):
+                copy.start()
+
+        @pl.when(h >= 2)
+        def _():
+            store_gi(h - 2).wait()
+
+        for s in range(seqs):
+            for q in range(span // 256):
+                cut = slice(q * 256, (q + 1) * 256)
+                g = dot_nt(cot_v[s, cut, :half], down_v[h % 2, 0]) + dot_nt(cot_v[s, cut, half:], down_v[h % 2, 1])
+                gi_v[h % 2, s * span + q * 256 : s * span + (q + 1) * 256, :] = g.astype(BF16)
+        store_gi(h).start()
+
     def chain(i, carry):
         moving.middle(i)
         moving.outward(i - 1)
@@ -964,47 +1038,73 @@
         def _():
             finish(i - 2)
 
-        @pl.when(i == total_subs // 2 - 2)
+        @pl.when(i == 1)
+        def _():
+            w_down.second()
+            w_up.first()
+
+        @pl.when(i == 6)
+        def _():
+            w_gate.second()
+
+        @pl.when(i == 8)
+        def _():
+            w_down.third()
+
+        @pl.when(i == 9)
+        def _():
+            w_down.arrived()
+            for copy in load_down(0):
+                copy.start()
+
+        @pl.when((i >= 10) & (i < 10 + blocks))
+        def _():
+            grad_inner(i - 10)
+
+        @pl.when(i == 12)
+        def _():
+            w_up.second()
+
+        @pl.when(i == 14)
         def _():
             w_gate.third()
-            w_up.second()
-
-        @pl.when(i == total_subs - 1)
-        def _():
-            w_up.third()
-            w_down.second()
 
         return carry
 
-    lax.fori_loop(0, total_subs + 2, chain, 0)
-    w_down.third()
-    for u in (total_subs - 2, total_subs - 1):
+    lax.fori_loop(0, subs + 2, chain, 0)
+    w_up.third()
+    for u in (subs - 2, subs - 1):
         for copy in hidden_store(u):
             copy.wait()
-
+    for h in (blocks - 2, blocks - 1):
+        store_gi(h).wait()
     moving.settle()
     for s in range(seqs):
         exchange(s).wait_send()
         give(s).wait_send()
+        for k in range(4):
+            keep(k, s).wait()
     for copy in gains:
         copy.wait_send()
-    for w in weights[2:]:
-        w.arrived()
+    w_gate.arrived()
+    w_up.arrived()
     for w in weights:
         w.sent()
-    for copy in (store_gf, store_xr, store_n1, store_qkv, store_out):
+    for copy in [store_gf, store_xr, store_n1, store_qkv, store_out] + rest:
         copy.wait()
 
 
-def forward(lengths, x, cot, w_qkv, w_out, w_gate, w_up, w_down, gains, cosine, sine, qgain, kgain, hd, nq, nk):
+def forward(lengths, x, cot, w_query, w_key, w_value, w_out, w_gate, w_up, w_down, all_gains, hd, nq, nk):
     seqs, span, width = x.shape
     half = width // 2
     groups = nq // nk
-    sub = min(128, span)
+    sub = span // 8
     subs = seqs * span // sub
+    here = subs - 2
     block = min(256, span)
     hidden = w_gate.shape[1]
-    cols = w_qkv.shape[1]
+    hb = hidden // 4
+    cols = w_query.shape[1] + w_key.shape[1] + w_value.shape[1]
     rows = cols // 2
     any_space = pl.BlockSpec(memory_space=pl.ANY)
     vmem = pl.BlockSpec(memory_space=pltpu.VMEM)
@@ -1013,36 +1113,44 @@
         shape(wide, BF16), shape(wide, BF16), shape(wide, BF16),
         shape((2, half, cols), BF16), shape((2, w_out.shape[0], half), BF16),
         shape((2, half, hidden), BF16), shape((2, half, hidden), BF16), shape((2, hidden, half), BF16),
-        shape((seqs * span, width), F32), shape((seqs * span, width), BF16),
+        shape((seqs * span, width), F32), shape((seqs * span, width), BF16), shape((subs - here, sub, width), BF16),
+        shape((seqs * span, hidden), BF16),
     ]
+    kept = [
+        shape((seqs, (nq + nk) * hd, span), F32), shape((seqs, rows, 2 * span), BF16),
+        shape((seqs, groups * hd, 2 * span), BF16), shape((seqs, span, nq * hd), BF16),
+    ]
+    large += kept
     small = [
-        shape((8,) + gains.shape, BF16), shape((seqs, (nq + nk) * hd, span), F32), shape((seqs, rows, 2 * span), BF16),
-        shape((seqs, groups * hd, 2 * span), BF16), shape((seqs, groups, 2 * span), F32), shape((seqs, span, nq * hd), BF16),
-        shape((2, 8, 128), F32),
+        shape((8, 16, width // 8), BF16), shape((3 * hd, span), F32), shape((seqs, groups, 2 * span), F32), shape((2, 8, 128), F32),
     ]
     dma = pltpu.SemaphoreType.DMA
     ex = pltpu.VMEM((seqs, rows, span), BF16)
     at = pltpu.VMEM((seqs, groups * hd, span), BF16)
     moving = pltpu.VMEM((subs, sub, width), BF16)
+    landing = pltpu.VMEM((here, sub, width), BF16)
     flops = 2 * seqs * span * width * (cols + nq * hd) + 16 * seqs * nq * hd * span * span
     return pl.pallas_call(
         functools.partial(forward_kernel, hd, nq, nk, block, sub),
-        in_specs=[SMEM] + [any_space] * 7 + [vmem] * 5,
+        in_specs=[SMEM] + [any_space] * 9 + [vmem],
         out_specs=[any_space] * len(large) + [vmem] * len(small),
         out_shape=large + small,
         scratch_shapes=[
             pltpu.VMEM(wide, BF16), pltpu.VMEM(wide, BF16), pltpu.VMEM(wide, BF16),
             pltpu.VMEM((2, half, cols), BF16), pltpu.VMEM((2, w_out.shape[0], half), BF16),
             ex, ex, ex, at, at, at,
-            moving, moving, moving,
+            moving, landing, landing,
             pltpu.VMEM((sub, width), F32), pltpu.VMEM((2, sub, width), F32), pltpu.VMEM((2, sub, width), BF16),
-            dma((2, seqs, 8)), dma((5,)), dma((5, 8)), dma((5, 8)), dma((5,)), dma((8,)), dma((8,)),
+            pltpu.VMEM((w_query.shape[0], cols), BF16), pltpu.VMEM((16, width // 8), BF16),
+            pltpu.VMEM((2, 2, hb, half), BF16), pltpu.VMEM((2, seqs * span, hb), BF16),
+            *[pltpu.VMEM(a.shape, a.dtype) for a in kept],
+            dma((4, seqs)), dma((2, seqs, 8)), dma((5,)), dma((3,)), dma((subs - here,)), dma((2, 2)), dma((2,)), dma((5, 8)), dma((5, 8)), dma((5,)), dma((8,)), dma((8,)),
             dma((2, seqs)), dma((2, seqs)), dma((3, subs)), dma((3, subs)), dma((2, 2)),
         ],
-        compiler_params=pltpu.CompilerParams(vmem_limit_bytes=VMEM_BYTES, collective_id=1, has_side_effects=True),
+        compiler_params=pltpu.CompilerParams(vmem_limit_bytes=VMEM_MOST, collective_id=1, has_side_effects=True),
         cost_estimate=cost(flops, 80 * seqs * span * width),
         name="attention_forward",
-    )(lengths, x, cot, w_qkv, w_out, w_gate, w_up, w_down, gains, cosine, sine, qgain, kgain)
+    )(lengths, x, cot, w_query, w_key, w_value, w_out, w_gate, w_up, w_down, all_gains)
 
 
 def by_pieces(count, body, size=16):
@@ -1065,7 +1173,7 @@
         self.part, self.arrive, self.back = part, arrive, back
         self.send, self.recv = send, recv
         self.side, self.mid = {"tensor": xor_one(rank)}, {"tensor": 3 - rank}
-        self.count = part.shape[0]
+        self.count = arrive.shape[0]
 
     def hop_in(self, u):
         return remote(self.part.at[u], self.arrive.at[u], self.send.at[0, u], self.recv.at[0, u], self.side)
@@ -1136,10 +1244,11 @@
 
 def feed_both_kernel(
     hb, sub, rows,
-    n2_hbm, gf_hbm, gate_hbm, up_hbm, down_hbm, hidden_hbm, gain_ref,
-    ffn_hbm, gb_hbm, gh_hbm, dgate_hbm, dup_hbm, ddown_hbm, gain_out,
-    n2_v, gf_v, inner_v, gg_v, gu_v, facc, gacc, wrow, wcol, part_v, in_v, back_v, total_v, hid_v, gh_v, gb_v, ffn_v, stage_row, stage_col,
-    load_sem, wsem, zsend, zrecv, hid_sem, out_sem, ffn_sem, csend, crecv, store_sem, free_sem,
+    len_ref, n2_hbm, gf_hbm, gate_hbm, up_hbm, down_hbm, gi_hbm, rest_hbm, xr_hbm, hidden_in, gains_ref,
+    ffn_hbm, gb_hbm, gh_hbm, dgate_hbm, dup_hbm, ddown_hbm, hidden_hbm, landx, landy, gain_out, stat_ref,
+    n2_v, gf_v, inner_v, gg_v, gu_v, facc, gacc, wrow, wcol, part_v, in_v, back_v, total_v, hid_v, gh_v, gb_v, stage_row, stage_col,
+    late_p, late_a, late_b, xtile_v, gi_v, wide_v, temp_v, gain_ref,
+    load_sem, wsem, zsend, zrecv, hid_sem, out_sem, ffn_sem, csend, crecv, store_sem, lsend, lrecv, xt_sem, xsend, xrecv, xload, free_sem,
 ):
     core, rank = lax.axis_index("context"), lax.axis_index("tensor")
     near_core = {"context": 1 - core}
@@ -1151,11 +1260,15 @@
     per = rows // sub
     chain = Chain(rank, part_v, in_v, back_v, zsend, zrecv)
     subs = chain.count
+    late = Chain(rank, late_p, late_a, late_b, lsend, lrecv)
+    known = subs - late.count
+    start = core * (tokens // 2)
 
     def load_weights(i):
         slot, h = i % 2, i % hsteps
         cut = pl.ds(pl.multiple_of(h * hb, hb), hb)
-        copies = []
+        here = pl.ds(pl.multiple_of(i // hsteps * rows, rows), rows)
+        copies = [pltpu.make_async_copy(gi_hbm.at[here, cut], gi_v.at[slot], wsem.at[slot, 6])]
         for side in range(2):
             copies.append(pltpu.make_async_copy(gate_hbm.at[side, :, cut], wrow.at[slot, 0, side], wsem.at[slot, side]))
             copies.append(pltpu.make_async_copy(up_hbm.at[side, :, cut], wrow.at[slot, 1, side], wsem.at[slot, 2 + side]))
@@ -1164,65 +1277,126 @@
 
     def load_hidden(u):
         cut = pl.ds(pl.multiple_of(u * sub, sub), sub)
-        return pltpu.make_async_copy(hidden_hbm.at[cut, :], hid_v.at[u % 2], hid_sem.at[u % 2])
-
-    loads = [pltpu.make_async_copy(n2_hbm, n2_v, load_sem.at[0]), pltpu.make_async_copy(gf_hbm, gf_v, load_sem.at[1])]
-    for copy in loads + load_weights(0):
+        return pltpu.make_async_copy(hidden_hbm.at[cut, :], hid_v, hid_sem)
+
+    ready = pl.ds(0, known * sub)
+    loads = [
+        pltpu.make_async_copy(n2_hbm.at[ready, :], n2_v.at[ready, :], load_sem.at[0]),
+        pltpu.make_async_copy(rest_hbm, late_p, load_sem.at[1]),
+    ]
+    load_gf = pltpu.make_async_copy(gf_hbm, gf_v, load_sem.at[2])
+    for copy in loads + load_weights(0) + [load_gf]:
         copy.start()
-    for u in range(2):
-        load_hidden(u).start()
-    greet([(None, chain.side), (chain.inner, chain.mid), (None, near_core)])
+    load_hidden(0).start()
+    row = lax.axis_index("dp")
+    near_x, near_y = {"dp": xor_one(row)}, {"dp": (row + 2) % 4}
+    greet([(None, near_core), (None, near_x), (None, near_y), (None, chain.side), (chain.inner, chain.mid)])
+    for b in range(8):
+        gain_ref[:, b * (width // 8) : (b + 1) * (width // 8)] = gains_ref[b, 1:2, :].astype(F32)
     gain_out[...] = jnp.zeros_like(gain_out)
+    stat_ref[...] = jnp.zeros_like(stat_ref)
     for copy in loads:
         copy.wait()
-
-    def stores(u):
+    for u in range(late.count):
+        late.begin(u)
+
+    def load_x(u):
+        at = pl.multiple_of((known + u) * sub, sub)
+        return pltpu.make_async_copy(xr_hbm.at[pl.ds(at, sub), :], xtile_v, xt_sem)
+
+    def late_store(u):
+        return pltpu.make_async_copy(gh_v, hidden_hbm.at[pl.ds(pl.multiple_of((known + u) * sub, sub), sub), :], out_sem.at[0])
+
+    def late_finish(u):
+        load_x(u).start()
+        late.total(u, total_v)
+        load_x(u).wait()
+
+        @pl.when(u >= 1)
+        def _():
+            late_store(u - 1).wait()
+
+        length = len_ref[known * sub // (tokens // 2)]
+        offset = start + known * sub % (tokens // 2) + u * sub
+
+        def body(cut, first):
+            total = total_v[cut, :]
+            resid = xtile_v[cut, :].astype(F32)
+            hidden_rows = resid + total
+            gh_v[cut, :] = hidden_rows
+            normed = (hidden_rows * inverse_rms(hidden_rows) * gain_ref[...]).astype(BF16)
+            n2_v[pl.ds(pl.multiple_of((known + u) * sub + first, 16), 16), :] = normed
+            spot = offset + first + lax.broadcasted_iota(jnp.int32, (16, 1), 0)
+            valid = (spot < length).astype(F32)
+            stat_ref[0] += fold_lanes(valid * resid * resid)
+            stat_ref[1] += fold_lanes(valid * total * total)
+
+        by_pieces(sub, body)
+        late_store(u).start()
+
+    def store_gb(u):
         cut = pl.ds(pl.multiple_of(u * sub, sub), sub)
-        return (
-            pltpu.make_async_copy(gh_v.at[u % 2], gh_hbm.at[cut, :], out_sem.at[0, u % 2]),
-            pltpu.make_async_copy(gb_v.at[u % 2], gb_hbm.at[cut, :], out_sem.at[1, u % 2]),
-        )
+        return pltpu.make_async_copy(gb_v, gb_hbm.at[cut, :], out_sem.at[1])
+
+    def store_gh(u):
+        at = pl.ds(pl.multiple_of(u % 2 * sub, sub), sub)
+        return pltpu.make_async_copy(gh_v, gh_hbm.at[u // 8, at, :], out_sem.at[0])
 
     def finish(u):
         chain.total(u, total_v)
         load_hidden(u).wait()
 
-        @pl.when(u >= 2)
-        def _():
-            for copy in stores(u - 2):
-                copy.wait()
+        @pl.when(u >= 1)
+        def _():
+            store_gb(u - 1).wait()
 
         def body(piece_rows, first):
             e = total_v[piece_rows, :]
-            hidden_rows = hid_v[u % 2, piece_rows, :]
+            hidden_rows = hid_v[piece_rows, :]
             inv = inverse_rms(hidden_rows)
             hat = hidden_rows * inv
             eg = e * gain_ref[...]
             grad = gf_v[pl.ds(pl.multiple_of(u * sub + first, 16), 16), :].astype(F32)
             gh = grad + inv * (eg - hat * jnp.mean(eg * hat, axis=-1, keepdims=True))
-            gh_v[u % 2, piece_rows, :] = gh
-            gb_v[u % 2, piece_rows, :] = gh.astype(BF16)
+            gb_v[piece_rows, :] = gh.astype(BF16)
+
+            @pl.when(u % 8 // 2 == rank)
+            def _():
+                gh_v[piece_rows, :] = gh
+
             both = e * hat
             gain_out[...] += both[:8] + both[8:]
 
         by_pieces(sub, body)
-        for copy in stores(u):
-            copy.start()
-
-        @pl.when(u + 2 < subs)
-        def _():
-            load_hidden(u + 2).start()
-
-    def serve(k):
-        chain.middle(k - 3)
-        chain.outward(k - 4)
-
-        @pl.when((k >= 5) & (k < 5 + subs))
-        def _():
-            finish(k - 5)
+        store_gb(u).start()
+
+        @pl.when(u % 8 // 2 == rank)
+        def _():
+            store_gh(u).start()
+            store_gh(u).wait()
+
+        @pl.when(u + 1 < subs)
+        def _():
+            load_hidden(u + 1).start()
+
+    def serve(n):
+        chain.middle(n)
+        chain.outward(n - 2)
+
+        @pl.when((n >= 4) & (n < 4 + subs))
+        def _():
+            finish(n - 4)
+
+    quarter = width // 4
 
     def store_ffn(c):
-        return pltpu.make_async_copy(ffn_v, ffn_hbm.at[pl.ds(pl.multiple_of(c * rows, rows), rows), :], ffn_sem)
+        here = pl.ds(pl.multiple_of(c * rows, rows), rows)
+        return [
+            pltpu.make_async_copy(
+                stage_row.at[c % 2, pl.ds(k * rows, rows), :], ffn_hbm.at[here, pl.ds(k * quarter, quarter)], ffn_sem.at[c % 2, k]
+            )
+            for k in range(4)
+        ]
 
     def step(i, carry):
         slot, c, h = i % 2, i // hsteps, i % hsteps
@@ -1236,13 +1410,13 @@
 
         here = pl.ds(pl.multiple_of(c * rows, rows), rows)
         cols = pl.ds(pl.multiple_of(h * hb, hb), hb)
-        n, g = n2_v[here, :], gf_v[here, :]
+        n = n2_v[here, :]
         wide = min(256, hb)
         for q in range(hb // wide):
             part = slice(q * wide, (q + 1) * wide)
             gate = dot_nn(n[:, :half], wrow[slot, 0, 0, :, part]) + dot_nn(n[:, half:], wrow[slot, 0, 1, :, part])
             up = dot_nn(n[:, :half], wrow[slot, 1, 0, :, part]) + dot_nn(n[:, half:], wrow[slot, 1, 1, :, part])
-            gi = dot_nt(g[:, :half], wcol[slot, 0, part, :]) + dot_nt(g[:, half:], wcol[slot, 1, part, :])
+            gi = gi_v[slot, :, part].astype(F32)
             sig = jax.nn.sigmoid(gate)
             silu = gate * sig
             at = pl.ds(pl.multiple_of(h * hb + q * wide, wide), wide)
@@ -1264,26 +1438,46 @@
                 facc[:, cut] += dot_nn(inner, wcol[slot, side, :, part])
                 gacc[:, cut] += dot_nt(gg, wrow[slot, 0, side, part, :]) + dot_nt(gu, wrow[slot, 1, side, part, :])
 
+        @pl.when((h == hsteps - 1) & (c >= 2))
+        def _():
+            for copy in store_ffn(c - 2):
+                copy.wait()
+
         @pl.when(h == hsteps - 1)
         def _():
             for k in range(per):
                 part_v[c * per + k] = gacc[k * sub : (k + 1) * sub, :].astype(BF16)
                 chain.begin(c * per + k)
 
-            @pl.when(c > 0)
-            def _():
-                store_ffn(c - 1).wait()
-
-            ffn_v[...] = facc[...].astype(BF16)
-            store_ffn(c).start()
-
-        @pl.when(i % 2 == 0)
-        def _():
-            serve(i // 2)
-
+            for k in range(4):
+                stage_row[c % 2, k * rows : (k + 1) * rows, :] = facc[:, k * quarter : (k + 1) * quarter].astype(BF16)
+            for copy in store_ffn(c):
+                copy.start()
+
+        @pl.when((i >= 2) & (i < 2 + late.count))
+        def _():
+            late.middle(i - 2)
+
+        @pl.when((i >= 4) & (i < 4 + late.count))
+        def _():
+            late.outward(i - 4)
+
+        @pl.when((i >= 6) & (i < 6 + late.count))
+        def _():
+            late_finish(i - 6)
+
+        @pl.when(i == 9)
+        def _():
+            load_gf.wait()
+            late_store(late.count - 1).wait()
+
+        serve(i - 6)
         return carry
 
     lax.fori_loop(0, steps, step, 0)
+    for c in range(2, steps // hsteps):
+        for copy in store_ffn(c):
+            copy.wait()
 
     pl.semaphore_signal(free_sem, inc=1, device_id=near_core, device_id_type=pl.DeviceIdType.MESH)
     outs = (dgate_hbm, dup_hbm, ddown_hbm)
@@ -1311,7 +1505,7 @@
         else:
             keep(w, t).wait()
 
-    def group(kind, w, before):
+    def group(kind, w, before, part):
         def one(t, carry):
             cut = pl.ds(pl.multiple_of(t * hb, hb), hb)
             mine = slice(kind * half, (kind + 1) * half)
@@ -1345,74 +1539,106 @@
                 keep(w, t).start()
             return carry
 
-        lax.fori_loop(0, hsteps, one, 0)
-
-    done = steps // 2
-    serve(done)
+        lax.fori_loop(part * (hsteps // 2), (part + 1) * (hsteps // 2), one, 0)
+
     pl.semaphore_wait(free_sem, 1)
-    group(1, 0, None)
-    serve(done + 1)
-    group(1, 1, (1, 0))
-    group(0, 0, (1, 1))
-    serve(done + 2)
-    group(1, 2, None)
-    group(0, 1, (0, 0))
-    serve(done + 3)
-    group(0, 2, (1, 2))
-    for k in range(done + 4, 5 + subs):
-        serve(k)
+    after = iter(range(steps - 6, subs + 4))
+    done = []
+
+    def both(kind, w, before):
+        for part in range(2):
+            group(kind, w, before, part)
+            done.append(part)
+            if len(done) <= 8 or len(done) % 2 == 0:
+                serve(next(after))
+
+    both(1, 0, None)
+    both(0, 0, (1, 0))
+    for t in range(hsteps - 2, hsteps):
+        keep(0, t).wait()
+    gate_sum = Scatter(
+        row_blocks(dgate_hbm), wide_v.at[0], wide_v.at[1], half_rows(landx), half_rows(landy), temp_v, xsend, xrecv, xload, near_x, near_y
+    )
+    gate_sum.begin()
+    both(1, 1, None)
+    both(1, 2, None)
+    gate_sum.pass_on()
+    both(0, 1, (1, 1))
+    both(0, 2, (1, 2))
+    for n in after:
+        serve(n)
     for t in range(hsteps - 2, hsteps):
         keep(1, t).wait()
         keep(2, t).wait()
-    store_ffn(steps // hsteps - 1).wait()
-    for u in range(subs - 2, subs):
-        for copy in stores(u):
-            copy.wait()
+    store_gb(subs - 1).wait()
+    gate_sum.arrived()
+    gate_sum.settle()
     chain.settle()
-
-
-def feed_both(n2, gf, gate, up, down, hidden_rows, gain):
+    late.settle()
+
+
+def row_blocks(ref):
+    size = ref.shape[0] // 4
+    return lambda k, h: ref.at[pl.ds(k * size + h * (size // 2), size // 2), :]
+
+
+def half_rows(ref):
+    size = ref.shape[0] // 2
+    return lambda h: ref.at[pl.ds(h * size, size), :]
+
+
+def feed_both(lengths, n2, gf, gate, up, down, gi, rest, xr, hidden_rows, gain):
     tokens, width = n2.shape
     _, half, hidden = gate.shape
     hb = hidden // 4
-    sub, rows = tokens // 8, tokens // 4
+    sub, rows = tokens // 16, tokens // 4
+    count = rest.shape[0]
     any_space = pl.BlockSpec(memory_space=pl.ANY)
     vmem = pl.BlockSpec(memory_space=pltpu.VMEM)
     dma = pltpu.SemaphoreType.DMA
-    moving = pltpu.VMEM((8, sub, width), BF16)
+    moving = pltpu.VMEM((16, sub, width), BF16)
+    late = pltpu.VMEM((count, sub, width), BF16)
     act = pltpu.VMEM((tokens, hidden), BF16)
     return pl.pallas_call(
         functools.partial(feed_both_kernel, hb, sub, rows),
-        in_specs=[any_space] * 6 + [vmem],
-        out_specs=[any_space] * 6 + [vmem],
+        in_specs=[SMEM] + [any_space] * 9 + [vmem],
+        out_specs=[any_space] * 9 + [vmem] * 2,
         out_shape=[
-            shape((tokens, width), BF16), shape((tokens, width), BF16), shape((tokens, width), F32),
-            shape((half, hidden), BF16), shape((half, hidden), BF16), shape((hidden, half), BF16), shape((8, width), F32),
+            shape((tokens, width), BF16), shape((tokens, width), BF16), shape((2, 2 * sub, width), F32),
+            shape((half, hidden), BF16), shape((half, hidden), BF16), shape((hidden, half), BF16),
+            shape((tokens, width), F32), shape((half // 4, hidden), BF16), shape((half // 4, hidden), BF16),
+            shape((8, width), F32), shape((2, 8, 128), F32),
         ],
         scratch_shapes=[
             pltpu.VMEM((tokens, width), BF16), pltpu.VMEM((tokens, width), BF16), act, act, act,
             pltpu.VMEM((rows, width), F32), pltpu.VMEM((rows, width), F32),
             pltpu.VMEM((2, 2, 2, half, hb), BF16), pltpu.VMEM((2, 2, hb, half), BF16),
             moving, moving, moving, pltpu.VMEM((sub, width), F32),
-            pltpu.VMEM((2, sub, width), F32), pltpu.VMEM((2, sub, width), F32), pltpu.VMEM((2, sub, width), BF16),
-            pltpu.VMEM((rows, width), BF16), pltpu.VMEM((2, half, hb), BF16), pltpu.VMEM((2, hb, half), BF16),
-            dma((2,)), dma((2, 6)), dma((3, 8)), dma((3, 8)), dma((2,)), dma((2, 2)), dma(()), dma((3, 4)), dma((3, 4)),
-            dma((3, 4)), pltpu.SemaphoreType.REGULAR,
+            pltpu.VMEM((sub, width), F32), pltpu.VMEM((sub, width), F32), pltpu.VMEM((sub, width), BF16),
+            pltpu.VMEM((2, half, hb), BF16), pltpu.VMEM((2, hb, half), BF16),
+            late, late, late, pltpu.VMEM((sub, width), BF16), pltpu.VMEM((2, rows, hb), BF16),
+            pltpu.VMEM((2, half // 8, hidden), BF16), pltpu.VMEM((2, half // 8, hidden), BF16), pltpu.VMEM((1, width), F32),
+            dma((3,)), dma((2, 7)), dma((3, 16)), dma((3, 16)), dma(()), dma((2,)), dma((2, 4)), dma((3, 4)), dma((3, 4)),
+            dma((3, 4)), dma((3, count)), dma((3, count)), dma(()), dma((6,)), dma((6,)), dma((3,)), pltpu.SemaphoreType.REGULAR,
         ],
+        input_output_aliases={9: 6},
         compiler_params=pltpu.CompilerParams(vmem_limit_bytes=VMEM_MOST, collective_id=2, has_side_effects=True),
         cost_estimate=cost(18 * tokens * width * hidden, 60 * tokens * width),
         name="feed_forward_both",
-    )(n2, gf, gate, up, down, hidden_rows, gain)
+    )(lengths, n2, gf, gate, up, down, gi, rest, xr, hidden_rows, gain)
 
 
 class Ring:
-    def __init__(self, rank, source, own, slots, send, recv):
+    def __init__(self, rank, source, own, slots, send, recv, last=None):
         self.source, self.own, self.slots, self.send, self.recv = source, own, slots, send, recv
+        self.last = slots.at[2] if last is None else last
+        self.rows = slots.shape[1]
         self.rank, self.right = rank, {"tensor": (rank + 1) % 4}
 
     def hop(self, j):
         src = self.source((self.rank + 3) % 4) if j == 0 else self.slots.at[j - 1]
-        return remote(src, self.slots.at[j], self.send.at[j], self.recv.at[j], self.right)
+        dst = self.last if j == 2 else self.slots.at[j]
+        return remote(src, dst, self.send.at[j], self.recv.at[j], self.right)
 
     def begin(self):
         self.hop(0).start()
@@ -1424,7 +1650,7 @@
         def body(cut, first):
             self.slots[j - 1, cut, :] = (self.slots[j - 1, cut, :].astype(F32) + read(cut).astype(F32)).astype(BF16)
 
-        by_pieces(self.slots.shape[1], body)
+        by_pieces(self.rows, body)
         self.hop(j).start()
 
     def arrived(self):
@@ -1477,9 +1703,13 @@
             by_pieces(into.shape[0], body, tall(into))
             self.second[temp].start()
 
-    def finish(self, stage, out, store):
+    def arrived(self):
         for copy in self.first[2:] + self.second:
             copy.wait_recv()
+
+    def finish(self, stage, out, store, landed=False):
+        if not landed:
+            self.arrived()
         for h in range(2):
             loads = [
                 pltpu.make_async_copy(src, self.temps.at[k], self.load.at[k])
@@ -1505,15 +1735,15 @@
 
 def backward_kernel(
     hd, nq, nk, block,
-    len_ref, gb_hbm, gh_hbm, hidden_hbm, ffn_hbm, xr_hbm, n1_hbm, tok_hbm, outw_hbm, qkvw_hbm, all_hbm, att_hbm, inv_hbm, pre_hbm,
-    dgate_hbm, dup_hbm, ddown_hbm, gain_ref, cos_ref, sin_ref, qg_ref, kg_ref, stat_ref, gain2_ref,
-    out_hbm, gin_hbm, ggate_hbm, gup_hbm, gdown_hbm, gout_hbm, gqkv_hbm, landx0, landy0, landx1, landy1, landx2, landy2,
+    len_ref, gb_hbm, hidden_hbm, ffn_hbm, xr_hbm, n1_hbm, tok_hbm, outw_hbm, qkvw_hbm, all_hbm, att_hbm, inv_hbm, pre_hbm,
+    dup_hbm, ddown_hbm, table_ref, stat_ref, stat2_ref, gain2_ref,
+    out_hbm, fin_hbm, own_hbm, mine_o, mine_q, landx1, landy1, landx2, landy2, landx3, landy3, landx4, landy4,
     lines_out, small_out,
     act_v, rows_v, qkvw_v, tok_v, all_v, att_v, inv_v, pre_v, grads, da_all, da_own, da_send, da_got, d_own, d_send, d_got, dpre_v,
-    first_v, slots_v, piece_v, wide_a, wide_b, temp_a, temp_b, stage_a, stage_b,
-    go_v, so_v, wide_o, land_o, temp_o, stage_o, gq_v, sq_v, wide_q, land_q, temp_q, stage_q,
-    tile_v, xtile_v, otile_v, itile_v, lines_v, small_v, lin1, lin2, lin3, lin4, lin5, small_r,
-    load_sem, zsend, zrecv, piece_sem, xsend, xrecv, xload, xstore, exsend, exrecv, osend, orecv, qsend, qrecv,
+    first_v, slots_v, piece_v, wide_a, wide_b, temp_a, temp_b,
+    go_v, so_v, wide_o, temp_o, gq_v, sq_v, wide_q, temp_q,
+    tile_v, otile_v, lines_v, small_v, heads_v, lin1, lin2, lin3, small_r,
+    load_sem, zsend, zrecv, piece_sem, xsend, xrecv, xload, own_sem, exsend, exrecv, osend, orecv, qsend, qrecv,
     tile_sem, outs_sem, smsend, smrecv,
 ):
     seqs, _, slots = all_v.shape
@@ -1548,7 +1778,7 @@
     def load_piece(s, m):
         return pltpu.make_async_copy(ffn_hbm.at[piece_rows(s, m), :], piece_v.at[s], piece_sem.at[s])
 
-    greet([(None, d) for d in (near_x, near_y, near_core, z_right, z_left, z_far)])
+    greet([(None, d) for d in (near_x, near_y, {"dp": near[3]}, near_core, z_right, z_left, z_far)])
 
     def ffn_own(s):
         def own(m):
@@ -1565,9 +1795,10 @@
         for s in range(seqs)
     ]
     first_rings = [
-        Ring(rank, lambda m, s=s: first_v.at[s, m], first_own(s), slots_v.at[seqs + s], zsend.at[seqs + s], zrecv.at[seqs + s])
+        Ring(rank, lambda m, s=s: first_v.at[s, m], first_own(s), slots_v.at[seqs + s], zsend.at[seqs + s], zrecv.at[seqs + s], fin_hbm.at[s])
         for s in range(seqs)
     ]
+    last = seqs - 1
     for s in range(seqs):
         ffn_rings[s].begin()
         load_piece(s, (rank + 2) % 4).start()
@@ -1598,13 +1829,11 @@
     def scatter(i, get, wide, land_x, land_y, temps):
         return Scatter(get, wide.at[0], wide.at[1], land_x, land_y, temps, xsend.at[i], xrecv.at[i], xload.at[i], near_x, near_y)
 
-    s_gate = scatter(0, in_hbm(dgate_hbm, 0), wide_a.at[0], halves(landx0), halves(landy0), temp_a)
-    s_up = scatter(1, in_hbm(dup_hbm, 0), wide_a.at[1], halves(landx1), halves(landy1), temp_a)
-    s_down = scatter(2, in_hbm(ddown_hbm, 1), wide_b, halves(landx2), halves(landy2), temp_b)
-    s_out = scatter(3, in_vmem(go_v), wide_o, halves(land_o.at[0]), halves(land_o.at[1]), temp_o)
-    s_qkv = scatter(4, in_vmem(gq_v), wide_q, halves(land_q.at[0]), halves(land_q.at[1]), temp_q)
-    for item in (s_gate, s_up, s_down):
-        item.begin()
+    s_up = scatter(0, in_hbm(dup_hbm, 0), wide_a, halves(landx1), halves(landy1), temp_a)
+    s_down = scatter(1, in_hbm(ddown_hbm, 1), wide_b, halves(landx2), halves(landy2), temp_b)
+    s_out = scatter(2, in_vmem(go_v), wide_o, halves(landx3), halves(landy3), temp_o)
+    s_qkv = scatter(3, in_vmem(gq_v), wide_q, halves(landx4), halves(landy4), temp_q)
+    s_up.begin()
 
     load_gb.wait()
     load_outw.wait()
@@ -1643,7 +1872,7 @@
     qcol = lax.broadcasted_iota(jnp.int32, (block, groups * block), 1) % block
     base = groups * hd
 
-    def attention(s, carry):
+    def attention(s):
         give(s).wait_recv()
         low, high = join_positions(core, da_own[s], da_got[s])
         da_all[:, :span] = low
@@ -1679,46 +1908,29 @@
         d_send[s] = theirs.astype(BF16)
         exchange(s).start()
 
-        @pl.when(s == 0)
-        def _():
-            ffn_step(0, 1)
-
-        @pl.when(s == seqs - 1)
-        def _():
-            ffn_step(1, 1)
-            s_gate.pass_on()
-
-        return carry
-
-    lax.fori_loop(0, seqs, attention, 0)
-
-    load_tok.wait()
-    blocks_o = [remote(so_v.at[k], go_v.at[k], osend.at[k], orecv.at[k], near_core) for k in range(4)]
-    size_o = half // 4
-    for k in range(4):
-        cut = slice(half + k * size_o, half + (k + 1) * size_o)
-        so_v[k] = dot_tn(tok_v[...], act_v[:, cut]).astype(BF16)
-        blocks_o[k].start()
-
-    cosine, sine = cos_ref[...], sin_ref[...]
+    quarter = hd // 2
+    cosine, sine = table_ref[:quarter, :], table_ref[quarter : 2 * quarter, :]
+    qgain, kgain = table_ref[2 * quarter : 2 * quarter + hd, 0:1], table_ref[2 * quarter + hd :, 0:1]
     sides = (nq // 2, nk // 2, nk // 2)
+    copies_in_tensor = 1.0 / lax.axis_size("tensor")
     lines_v[:8, :] = jnp.zeros((8, width), F32)
-    lines_v[8:, :] = gain2_ref[...] * (1.0 / lax.axis_size("tensor"))
-    small_v[: 2 * hd, :] = jnp.zeros((2 * hd, 128), F32)
-    for k in range(2):
-        small_v[2 * hd + 8 * k : 2 * hd + 8 * k + 8, :] = stat_ref[k] * (1.0 / lax.axis_size("tensor"))
-    small_v[2 * hd + 16 : 2 * hd + 24, :] = jnp.zeros((8, 128), F32)
+    lines_v[8:, :] = gain2_ref[...] * copies_in_tensor
+    heads_v[...] = jnp.zeros_like(heads_v)
     valid_slots = jnp.int32(0)
     for s in range(seqs):
         valid_slots = valid_slots + jnp.clip(len_ref[s] - start, 0, span)
-    count = valid_slots.astype(F32) * (1.0 / (1024.0 * lax.axis_size("tensor")))
-    small_v[2 * hd + 24 : 2 * hd + 32, :] = jnp.broadcast_to(count, (8, 128))
+    count = valid_slots.astype(F32) * (copies_in_tensor / 128.0)
+    small_v[...] = jnp.zeros_like(small_v)
+    for k in range(2):
+        both = stat_ref[k] + stat2_ref[k]
+        small_v[1 + k : 2 + k, :] = jnp.sum(both, axis=0, keepdims=True) * copies_in_tensor
+    small_v[4:5, :] = jnp.broadcast_to(count, (1, 128))
     load_qkvw.wait()
 
     def fold_columns(values):
         return sum(values[:, k * 128 : (k + 1) * 128] for k in range(values.shape[1] // 128))
 
-    def heads_rows(s, carry):
+    def heads_rows(s):
         exchange(s).wait_recv()
         low, high = join_positions(core, d_own[s].astype(F32), d_got[s].astype(F32))
         parts = [[], [], []]
@@ -1737,8 +1949,8 @@
             v = pre_v[s, h * hd : (h + 1) * hd, :]
             inv = lax.rsqrt(jnp.mean(v * v, axis=0, keepdims=True) + epsilon)
             hat = v * inv
-            small_v[kind * hd : (kind + 1) * hd, :] += fold_columns(g * hat)
-            gg = g * (qg_ref[...] if kind == 0 else kg_ref[...])
+            heads_v[kind * hd : (kind + 1) * hd, :] += fold_columns(g * hat)
+            gg = g * (qgain if kind == 0 else kgain)
             done.append(inv * (gg - hat * jnp.mean(gg * hat, axis=0, keepdims=True)))
         done += parts[2]
         for h in range(nq + 2 * nk):
@@ -1761,30 +1973,81 @@
                 both = part * (xs[k] * inv)
                 lines_v[:8, cut] += sum(both[8 * r : 8 * r + 8] for r in range(share // 8))
 
+    def sequence(s, carry):
+        attention(s)
+
+        @pl.when(s == last)
+        def _():
+            s_up.pass_on()
+            ffn_step(1, 1)
+
+        heads_rows(s)
+
         @pl.when(s == 0)
         def _():
             for copy in load_x(1):
                 copy.start()
             first_rings[0].begin()
-            ffn_step(0, 2)
-
-        @pl.when(s == seqs - 1)
+            ffn_step(0, 1)
+            s_down.begin()
+
+        @pl.when(s == last)
         def _():
             first_rings[1].begin()
-            ffn_step(1, 2)
-            s_up.pass_on()
 
         return carry
 
-    lax.fori_loop(0, seqs, heads_rows, 0)
-
+    lax.fori_loop(0, seqs, sequence, 0)
+
+    def hop_copies(n, items):
+        return [remote(src, dst, smsend.at[n, i], smrecv.at[n, i], device) for i, (device, src, dst, _) in enumerate(items)]
+
+    def hop_begin(n, items):
+        for copy in hop_copies(n, items):
+            copy.start()
+
+    def hop_end(n, items):
+        for copy in hop_copies(n, items):
+            copy.wait()
+        for _, _, dst, place_to in items:
+            if place_to is None:
+                small_v[...] += dst[...]
+            else:
+                lines_v[:, place_to] += dst[...]
+
+    piece = width // 8
+
+    def columns(k):
+        return slice(k * piece, (k + 1) * piece)
+
+    def view(k, count=1):
+        return lines_v.at[:, pl.ds(k * piece, count * piece)]
+
+    hop_core = [(near_core, view(4, 4), lin1, slice(0, half))]
+    near_all = [near_x, near_y, {"dp": near[3]}]
+    hop_lines = [(near_all[k], view(1 + k), lin2.at[k], columns(0)) for k in range(3)]
+    hop_small = [(near_core, small_v, small_r.at[0], None)]
+    hop_square = [(near_all[k], small_v, small_r.at[1 + k], None) for k in range(3)]
+    z_all = [z_right, z_far, z_left]
+    hop_chain = [(z_all[k], view(0), lin3.at[k], columns(0)) for k in range(3)]
+    hop_chain += [(z_all[k], small_v, small_r.at[4 + k], None) for k in range(3)]
+    hop_begin(0, hop_core)
+
+    load_tok.wait()
+    blocks_o = [remote(so_v.at[k], go_v.at[k], osend.at[k], orecv.at[k], near_core) for k in range(4)]
+    size_o = half // 4
+    for k in range(4):
+        cut = slice(half + k * size_o, half + (k + 1) * size_o)
+        so_v[k] = dot_tn(tok_v[...], act_v[:, cut]).astype(BF16)
+        blocks_o[k].start()
     for k in range(4):
         blocks_o[k].wait_recv()
         cut = slice(k * size_o, (k + 1) * size_o)
         go_v[k] = (dot_tn(tok_v[...], act_v[:, cut]) + go_v[k].astype(F32)).astype(BF16)
     s_out.begin()
     load_n1 = load(0, n1_hbm, act_v)
-    first_rings[0].step(1)
+    hop_end(0, hop_core)
+    hop_begin(1, hop_lines)
     load_n1.wait()
     blocks_q = [remote(sq_v.at[k], gq_v.at[k], qsend.at[k], qrecv.at[k], near_core) for k in range(4)]
     size_q = half // 4
@@ -1797,8 +2060,14 @@
         cut = slice(k * size_q, (k + 1) * size_q)
         gq_v[k] = (dot_tn(act_v[:, cut], dpre_v[...]) + gq_v[k].astype(F32)).astype(BF16)
     s_qkv.begin()
-
-    piece = width // 8
+    keeps = [
+        pltpu.make_async_copy(go_v.at[0], mine_o, own_sem.at[0]),
+        pltpu.make_async_copy(gq_v.at[0], mine_q, own_sem.at[1]),
+    ]
+    keeps += [pltpu.make_async_copy(first_v.at[s, rank], own_hbm.at[s], own_sem.at[2 + s]) for s in range(seqs)]
+    for copy in keeps:
+        copy.start()
+
 
     def place(tile, dst, s):
         copies = []
@@ -1823,7 +2092,7 @@
             otile_v[cut, :] = (tile_v[cut, :] + ffn).astype(BF16)
             spot = start + rank * share + first + lax.broadcasted_iota(jnp.int32, (16, 1), 0)
             valid = (spot < len_ref[s]).astype(F32)
-            small_v[2 * hd + 16 : 2 * hd + 24, :] += fold_lanes(valid * ffn * ffn)
+            small_v[3:4, :] += jnp.sum(fold_lanes(valid * ffn * ffn), axis=0, keepdims=True)
 
         by_pieces(share, body)
         copies = place(otile_v, out_hbm, s)
@@ -1832,78 +2101,36 @@
         for copy in copies:
             copy.wait()
 
-    def in_share(s):
-        loads = [
-            pltpu.make_async_copy(gh_hbm.at[piece_rows(s, rank), :], tile_v, tile_sem.at[0]),
-            pltpu.make_async_copy(xr_hbm.at[s, pl.ds(pl.multiple_of(rank * share, share), share), :], xtile_v, tile_sem.at[1]),
-        ]
-        for copy in loads:
-            copy.start()
-        for copy in loads:
-            copy.wait()
-        first_rings[s].arrived()
-
-        def body(cut, first):
-            e = slots_v[seqs + s, 2, cut, :].astype(F32) + first_v[s, rank, cut, :].astype(F32)
-            x = xtile_v[cut, :].astype(F32)
-            inv = inverse_rms(x)
-            hat = x * inv
-            eg = e * gain_ref[...]
-            itile_v[cut, :] = tile_v[cut, :] + inv * (eg - hat * jnp.mean(eg * hat, axis=-1, keepdims=True))
-
-        by_pieces(share, body)
-        copies = place(itile_v, gin_hbm, s)
-        for copy in copies:
-            copy.start()
-        for copy in copies:
-            copy.wait()
-
-    def lump(n, src, dst, device):
-        return remote(src, dst, smsend.at[n], smrecv.at[n], device)
-
-    def small_hop(n, device, pairs):
-        copies = [lump(2 * n, small_v, small_r.at[n], device)]
-        for i, (src, dst, _) in enumerate(pairs):
-            copies.append(remote(src, dst, smsend.at[2 * n + 1 + 10 * i], smrecv.at[2 * n + 1 + 10 * i], device))
-        for copy in copies:
-            copy.start()
-        for copy in copies:
-            copy.wait()
-        small_v[...] += small_r[n]
-        for _, dst, into in pairs:
-            lines_v[:, into] += dst[...]
-
-    def columns(k):
-        return slice(k * piece, (k + 1) * piece)
-
+    small_v[0:1, :] = jnp.sum(heads_v[...].T, axis=0, keepdims=True)
+    ffn_step(0, 2)
+    ffn_step(1, 2)
+    first_rings[0].step(1)
+    s_down.pass_on()
+    first_rings[1].step(1)
+    s_out.pass_on()
+    s_qkv.pass_on()
+    hop_end(1, hop_lines)
     out_share(0)
-    first_rings[1].step(1)
-    s_down.pass_on()
     out_share(1)
+    hop_begin(2, hop_small)
+    hop_end(2, hop_small)
+    hop_begin(3, hop_square)
+    hop_end(3, hop_square)
+    hop_begin(4, hop_chain)
     first_rings[0].step(2)
-    s_out.pass_on()
-    small_hop(0, near_core, [(lines_v.at[:, pl.ds(half, half)], lin1, slice(0, half))])
-    s_gate.finish(stage_a, in_out(ggate_hbm), xstore.at[0])
     first_rings[1].step(2)
-    s_qkv.pass_on()
-    small_hop(
-        1, near_x,
-        [(lines_v.at[:, pl.ds(piece, piece)], lin2.at[0], columns(0)), (lines_v.at[:, pl.ds(3 * piece, piece)], lin2.at[1], columns(2))],
-    )
-    small_hop(2, near_y, [(lines_v.at[:, pl.ds(2 * piece, piece)], lin3, columns(0))])
-    s_up.finish(stage_a, in_out(gup_hbm), xstore.at[1])
-    in_share(0)
-    s_down.finish(stage_b, in_out(gdown_hbm), xstore.at[2])
-    small_hop(3, {"tensor": xor_one(rank)}, [(lines_v.at[:, pl.ds(0, piece)], lin4, columns(0))])
-    s_out.finish(stage_o, in_out(gout_hbm), xstore.at[3])
-    small_hop(4, z_far, [(lines_v.at[:, pl.ds(0, piece)], lin5, columns(0))])
+    hop_end(4, hop_chain)
     lines_out[...] = lines_v[:, :piece]
     small_out[...] = small_v[...]
-    s_qkv.finish(stage_q, in_out(gqkv_hbm), xstore.at[4])
-    in_share(1)
+    for item in (s_up, s_down, s_out, s_qkv):
+        item.arrived()
+    for ring in first_rings:
+        ring.arrived()
+    for copy in keeps:
+        copy.wait()
     for ring in ffn_rings + first_rings:
         ring.settle()
-    for item in (s_gate, s_up, s_down, s_out, s_qkv):
+    for item in (s_up, s_down, s_out, s_qkv):
         item.settle()
     for copy in blocks_o + blocks_q:
         copy.wait_send()
@@ -1912,21 +2139,16 @@
         exchange(s).wait_send()
 
 
-def in_out(ref):
-    h2 = ref.shape[0] // 2
-    return lambda h: ref.at[pl.ds(h * h2, h2), :]
-
-
 def backward(
-    lengths, gb, gh, hidden_rows, ffn, xr, n1, tok, outw, qkvw, everything, att, inv, pre, dgate, dup, ddown,
-    gain1, cosine, sine, qgain, kgain, stat, gain2_part, hd, nq, nk,
+    lengths, gb, hidden_rows, ffn, xr, n1, tok, outw, qkvw, everything, att, inv, pre, dup, ddown,
+    table, stat, stat2, gain2_part, hd, nq, nk,
 ):
     seqs, span, width = xr.shape
     half = width // 2
     groups = nq // nk
     share = span // 4
     piece = width // 8
-    hidden = dgate.shape[1]
+    hidden = dup.shape[1]
     cols = qkvw.shape[2]
     feat = nq * hd
     block = min(256, span)
@@ -1935,13 +2157,10 @@
     dma = pltpu.SemaphoreType.DMA
     hold = lambda *dims: pltpu.VMEM(dims, BF16)
     wide = lambda *dims: pltpu.VMEM(dims, F32)
-    big = [
-        shape((seqs, share, width), BF16), shape((seqs, share, width), F32),
-        shape((piece, hidden), F32), shape((piece, hidden), F32), shape((hidden, piece), F32), shape((feat, piece), F32), shape((piece, cols), F32),
-    ]
-    big += [shape((piece, hidden), BF16)] * 4 + [shape((hidden, piece), BF16)] * 2
-    small_rows = 2 * hd + 32
-    small = [shape((16, piece), F32), shape((small_rows, 128), F32)]
+    big = [shape((seqs, share, width), BF16)] * 3 + [shape((feat, piece), BF16), shape((piece, cols), BF16)]
+    big += [shape((piece, hidden), BF16)] * 2 + [shape((hidden, piece), BF16)] * 2
+    big += [shape((feat, piece), BF16)] * 2 + [shape((piece, cols), BF16)] * 2
+    small = [shape((16, piece), F32), shape((8, 128), F32)]
     rows = everything.shape[1]
     scratch = [
         hold(seqs * span, width), hold(2, span, half), hold(2, half, cols), hold(seqs * span, feat), hold(*everything.shape), hold(*att.shape),
@@ -1949,19 +2168,18 @@
         hold(seqs, feat // 2, span), hold(seqs, feat // 2, span), hold(seqs, feat // 2, span),
         hold(seqs, rows, span), hold(seqs, rows, span), hold(seqs, rows, span), hold(seqs * span, cols),
         hold(seqs, 4, share, width), hold(2 * seqs, 3, share, width), hold(seqs, share, width),
-        hold(2, 2, piece // 2, hidden), hold(2, hidden // 2, piece), hold(3, piece // 2, hidden), hold(3, hidden // 2, piece),
-        wide(piece // 2, hidden), wide(hidden // 2, piece),
-        hold(4, feat, piece), hold(4, feat, piece), hold(2, feat // 2, piece), hold(2, feat, piece), hold(3, feat // 2, piece), wide(feat // 2, piece),
-        hold(4, piece, cols), hold(4, piece, cols), hold(2, piece // 2, cols), hold(2, piece, cols), hold(3, piece // 2, cols), wide(piece // 2, cols),
-        wide(share, width), hold(share, width), hold(share, width), wide(share, width),
-        wide(16, width), wide(small_rows, 128), wide(16, half), wide(2, 16, piece), wide(16, piece), wide(16, piece), wide(16, piece), wide(5, small_rows, 128),
-        dma((10,)), dma((2 * seqs, 3)), dma((2 * seqs, 3)), dma((seqs,)), dma((5, 6)), dma((5, 6)), dma((5, 3)), dma((5,)),
-        dma((2, seqs)), dma((2, seqs)), dma((4,)), dma((4,)), dma((4,)), dma((4,)), dma((2,)), dma((8,)), dma((20,)), dma((20,)),
+        hold(2, piece // 2, hidden), hold(2, hidden // 2, piece), hold(2, piece // 2, hidden), hold(2, hidden // 2, piece),
+        hold(4, feat, piece), hold(4, feat, piece), hold(2, feat // 2, piece), hold(2, feat // 2, piece),
+        hold(4, piece, cols), hold(4, piece, cols), hold(2, piece // 2, cols), hold(2, piece // 2, cols),
+        wide(share, width), hold(share, width),
+        wide(16, width), wide(8, 128), wide(2 * hd, 128), wide(16, half), wide(3, 16, piece), wide(3, 16, piece), wide(7, 8, 128),
+        dma((10,)), dma((2 * seqs, 3)), dma((2 * seqs, 3)), dma((seqs,)), dma((4, 6)), dma((4, 6)), dma((4, 3)), dma((2 + seqs,)),
+        dma((2, seqs)), dma((2, seqs)), dma((4,)), dma((4,)), dma((4,)), dma((4,)), dma((2,)), dma((8,)), dma((5, 6)), dma((5, 6)),
     ]
     tokens = seqs * span
     return pl.pallas_call(
         functools.partial(backward_kernel, hd, nq, nk, block),
-        in_specs=[SMEM] + [any_space] * 16 + [vmem] * 7,
+        in_specs=[SMEM] + [any_space] * 14 + [vmem] * 4,
         out_specs=[any_space] * len(big) + [vmem] * 2,
         out_shape=big + small,
         scratch_shapes=scratch,
@@ -1969,9 +2187,93 @@
         cost_estimate=cost(4 * tokens * width * (cols + feat), 60 * tokens * width),
         name="attention_backward",
     )(
-        lengths, gb, gh, hidden_rows, ffn, xr, n1, tok, outw, qkvw, everything, att, inv, pre, dgate, dup, ddown,
-        gain1, cosine, sine, qgain, kgain, stat, gain2_part,
+        lengths, gb, hidden_rows, ffn, xr, n1, tok, outw, qkvw, everything, att, inv, pre, dup, ddown,
+        table, stat, stat2, gain2_part,
     )
+
+
+def results_kernel(
+    hd, nqc, nkc, count, scal_ref, dgate, lx0, ly0, dup, lx1, ly1, ddown, lx2, ly2, mine_o, lx3, ly3, mine_q, lx4, ly4,
+    gh_ref, x_ref, fin_ref, own_ref, out_ref, gains_ref, lines_ref, small_ref,
+    output, gin, ggate, gup, gdown, gout, gq, gk, gv, gain_a, gain_b, gain_q, gain_k, rms,
+):
+    def add(*refs):
+        return sum(ref[...].astype(F32) for ref in refs)
+
+    ggate[...] = add(dgate, lx0, ly0)
+    gup[...] = add(dup, lx1, ly1)
+    gdown[...] = add(ddown, lx2, ly2)
+    gout[...] = add(mine_o, lx3, ly3)
+    qkv = add(mine_q, lx4, ly4)
+    gq[...] = qkv[:, :nqc]
+    gk[...] = qkv[:, nqc : nqc + nkc]
+    gv[...] = qkv[:, nqc + nkc :]
+    output[...] = out_ref[...]
+    width = x_ref.shape[-1]
+    piece = width // 8
+    rows = x_ref.shape[1]
+    gain = jnp.concatenate([gains_ref[b, 0:1, :] for b in range(8)], axis=1).astype(F32)
+    for r in range(0, rows, 16):
+        cut = slice(r, r + 16)
+        e = fin_ref[0, cut, :].astype(F32) + own_ref[0, cut, :].astype(F32)
+        x = x_ref[0, cut, :].astype(F32)
+        inv = inverse_rms(x)
+        hat = x * inv
+        eg = e * gain
+        value = gh_ref[0, cut, :] + inv * (eg - hat * jnp.mean(eg * hat, axis=-1, keepdims=True))
+        for k in range(8):
+            gin[0, cut, pl.ds(pl.multiple_of(scal_ref[1 + k] * piece, piece), piece)] = value[:, k * piece : (k + 1) * piece]
+
+    @pl.when(pl.program_id(0) == 0)
+    def _():
+        first = jnp.sum(lines_ref[:8, :], axis=0, keepdims=True)
+        second = jnp.sum(lines_ref[8:, :], axis=0, keepdims=True)
+        gain_a[...] = first.reshape(gain_a.shape)
+        gain_b[...] = second.reshape(gain_b.shape)
+        gain_q[...] = small_ref[0:1, :hd].reshape(gain_q.shape)
+        gain_k[...] = small_ref[0:1, hd : 2 * hd].reshape(gain_k.shape)
+        totals = [jnp.sum(small_ref[k, :]) for k in range(1, 5)]
+        for k in range(3):
+            rms[k] = totals[k] / (totals[3] * count)
+
+
+def finish_results(rank, ids, pairs, mine_o, mine_q, lands_o, lands_q, gh, xr, fin, own, out, gains, lines, small, hd, nqc, nkc):
+    (dgate, lx0, ly0), (dup, lx1, ly1), (ddown, lx2, ly2) = pairs
+    steps = 8
+    seqs, share, width = out.shape
+    hidden = dgate.shape[1]
+    piece = width // 8
+    per = steps // seqs
+    rows = share // per
+    wide = lambda h, w: pl.BlockSpec((h, w), lambda i, s: (i, 0))
+    token = pl.BlockSpec((1, rows, width), lambda i, s: (i // per, i % per, 0))
+    mine = pl.BlockSpec((1, rows, width), lambda i, s: (i // per, s[0] * per + i % per, 0))
+    fixed = lambda a: pl.BlockSpec(a.shape, lambda i, s: (0,) * a.ndim)
+    g = wide(piece // steps, hidden)
+    d = wide(hidden // steps, piece)
+    o = wide(mine_o.shape[0] // steps, piece)
+    q = wide(piece // steps, mine_q.shape[1])
+    outs = [
+        (shape(out.shape, BF16), token), (shape(out.shape, F32), token), (shape((piece, hidden), F32), g), (shape((piece, hidden), F32), g),
+        (shape((hidden, piece), F32), d), (shape(mine_o.shape, F32), o), (shape((piece, nqc), F32), wide(piece // steps, nqc)),
+        (shape((piece, nkc), F32), wide(piece // steps, nkc)), (shape((piece, nkc), F32), wide(piece // steps, nkc)),
+        *[(shape((size,), F32), pl.BlockSpec((size,), lambda i, s: (0,))) for size in (piece, piece, hd, hd)],
+        (shape((3,), F32), pl.BlockSpec(memory_space=pltpu.SMEM)),
+    ]
+    scalars = jnp.concatenate([rank.astype(jnp.int32).reshape(1), ids])
+    return pl.pallas_call(
+        functools.partial(results_kernel, hd, nqc, nkc, float(width)),
+        grid_spec=pltpu.PrefetchScalarGridSpec(
+            num_scalar_prefetch=1,
+            grid=(steps,),
+            in_specs=[g] * 6 + [d] * 3 + [o] * 3 + [q] * 3 + [token, mine, token, token, token, fixed(gains), fixed(lines), fixed(small)],
+            out_specs=[spec for _, spec in outs],
+        ),
+        out_shape=[kind for kind, _ in outs],
+        compiler_params=PARAMS,
+        cost_estimate=cost(30 * piece * hidden, 60 * piece * hidden),
+        name="results",
+    )(scalars, dgate, lx0, ly0, dup, lx1, ly1, ddown, lx2, ly2, mine_o, *lands_o, mine_q, *lands_q, gh, xr, fin, own, out, gains, lines, small)
 
 
 def per_device_general(
@@ -2190,47 +2492,32 @@
     nq = w_query.shape[1] // hd
     nk = key_projection_weight.shape[1] // hd
     lengths = lengths.astype(jnp.int32)
-    positions = lax.axis_index("context") * span + jnp.arange(span, dtype=jnp.int32)
-    freqs = rope_base ** (-(jnp.arange(hd // 2, dtype=F32) * (2.0 / hd)))
-    angles = freqs[:, None] * positions.astype(F32)[None, :]
-    cosine, sine = jnp.cos(angles), jnp.sin(angles)
-    qgain = query_gain.astype(F32).reshape(hd, 1)
-    kgain = key_gain.astype(F32).reshape(hd, 1)
-    w_qkv = jnp.concatenate([w_query, key_projection_weight, value_projection_weight], axis=1)
-    gains = jnp.pad(jnp.stack([attn_gain, ffn_gain]), ((0, 14), (0, 0)))
-
-    (xr, n1, gf, qkv, out_w, gate, up, down, hidden, n2, gains, pre, everything, att, inv, tok, stat) = forward(
-        lengths, inputs, cotangent, w_qkv, w_output, w_gate, w_up, w_down, gains, cosine, sine, qgain, kgain, hd, nq, nk
+    all_gains = jnp.concatenate([attn_gain, ffn_gain, query_gain, key_gain]).reshape(1, -1)
+    (
+        xr, n1, gf, qkv, out_w, gate, up, down, hidden, n2, rest, gi, pre, everything, att, tok, gains, table, inv, stat
+    ) = forward(
+        lengths, inputs, cotangent, w_query, key_projection_weight, value_projection_weight, w_output, w_gate, w_up, w_down,
+        all_gains, hd, nq, nk,
     )
-    gains = jnp.swapaxes(gains[:, :2], 0, 1).reshape(2, width).astype(F32)
     tokens = seqs * span
-    ffn, gb, gh, d_gate, d_up, d_down, gain2_part = feed_both(
-        n2, gf.reshape(tokens, width), gate, up, down, hidden, gains[1:2]
+    flat = lambda a: a.reshape(tokens, -1)
+    ffn, gb, gh, d_gate, d_up, d_down, hidden, landx, landy, gain2_part, stat2 = feed_both(
+        lengths, n2, flat(gf), gate, up, down, gi, rest, flat(xr), hidden, gains
     )
-    results = backward(
-        lengths, gb, gh, hidden, ffn, xr, n1.reshape(tokens, width), tok.reshape(tokens, nq * hd), out_w, qkv,
-        everything, att, inv, pre, d_gate, d_up, d_down, gains[0:1], cosine, sine, qgain, kgain, stat, gain2_part, hd, nq, nk,
+    output, fin, own, mine_o, mine_q, lx1, ly1, lx2, ly2, lx3, ly3, lx4, ly4, lines, small = backward(
+        lengths, gb, hidden, ffn, xr, flat(n1), flat(tok), out_w, qkv,
+        everything, att, inv, pre, d_up, d_down, table, stat, stat2, gain2_part, hd, nq, nk,
     )
-    output, grad_inputs, grad_gate, grad_up, grad_down, grad_out, grad_qkv = results[:7]
-    lines, small = results[-2:]
+    row, core = lax.axis_index("dp"), lax.axis_index("context")
+    near = [row, xor_one(row), (row + 2) % 4, 3 - row]
+    ids = jnp.stack([near[k] * 2 + (core if o == 0 else 1 - core) for o in range(2) for k in range(4)]).astype(jnp.int32)
     nqc, nkc = nq * hd, nk * hd
-    totals = jnp.sum(small[2 * hd :].reshape(4, -1), axis=1)
-    return (
-        output,
-        grad_inputs,
-        grad_qkv[:, :nqc],
-        grad_qkv[:, nqc : nqc + nkc],
-        grad_qkv[:, nqc + nkc :],
-        grad_out,
-        grad_gate,
-        grad_up,
-        grad_down,
-        jnp.sum(lines[:8], axis=0),
-        jnp.sum(lines[8:], axis=0),
-        jnp.sum(small[:hd], axis=1),
-        jnp.sum(small[hd : 2 * hd], axis=1),
-        jnp.sqrt(totals[:3] / (totals[3] * width)),
+    pairs = ((d_gate, landx, landy), (d_up, lx1, ly1), (d_down, lx2, ly2))
+    output, grad_inputs, grad_gate, grad_up, grad_down, grad_out, grad_q, grad_k, grad_v, *small = finish_results(
+        lax.axis_index("tensor"), ids, pairs, mine_o, mine_q, (lx3, ly3), (lx4, ly4), gh, xr, fin, own, output, gains,
+        lines, small, hd, nqc, nkc,
     )
+    return (output, grad_inputs, grad_q, grad_k, grad_v, grad_out, grad_gate, grad_up, grad_down, *small[:4], jnp.sqrt(small[4]))
 
 
 def per_device(*args):

time: 519 us -> 458 us (0.88)
  Pallas kernels: 482 us -> 450 us
  local copies, waits for them, and re-layouts: 16.1 us -> 2.43 us
  other arithmetic: 9.79 us -> 0.78 us
    pallas_call x1, Pallas kernels: 166 us -> 143 us  [forward(): pl.pallas_call(functools.partial(forward_kernel, hd, nq, nk, block, sub),...]
    pallas_call x1, Pallas kernels: 167 us -> 146 us  [backward(): pl.pallas_call(functools.partial(backward_kernel, hd, nq, nk, block), in_...]
    pallas_call x0 -> x1, Pallas kernels: none -> 13.6 us  [finish_results(): pl.pallas_call(functools.partial(results_kernel, hd, nqc, nkc, float(widt...]
    unnamed x16 -> x0, local copies, waits for them, and re-layouts: 8.39 us -> none
where the time goes in v5:
time: 458 us; the launch traced here: 454 us
  Pallas kernels  450 us (98%)
    pallas_call x1, Pallas kernels, feed_both(): pl.pallas_call(functools.partial(feed_both_kernel, hb, sub, rows), in_spe...  148 us
    pallas_call x1, Pallas kernels, backward(): pl.pallas_call(functools.partial(backward_kernel, hd, nq, nk, block), in_...  146 us
    pallas_call x1, Pallas kernels, forward(): pl.pallas_call(functools.partial(forward_kernel, hd, nq, nk, block, sub),...  143 us
    pallas_call x1, Pallas kernels, finish_results(): pl.pallas_call(functools.partial(results_kernel, hd, nqc, nkc, float(widt...  13.6 us

profile of v5, /device:TPU:0, one launch (start us, length us, event | category | flops | bytes accessed | tf_op | source)
XLA Modules:
  0.0 453.7 jit_solution(3900185475915903696)
XLA Ops:
  0.6 0.8 pad_maximum_fusion
  1.4 0.6 reshape.47.small_ref
  2.0 143.0 %attention_forward.1 = (bf16[2,512,2048]{2,1,0:T(8,128)(2,1)}, bf16[2,512,2048]{2,1,0:T(8,128)(2,1)}, bf16[2,512,2048]{2,1,0:T(8,128)(2,1)}, bf16[2,1024,768]{2,...) custom-call(s32[2]{0:T(128)} %len_ref.5, ...), custom_call_target="tpu_custom_call" | custom-call | flops 9663676416 | bytes 167772160 | tf_op jit(solution)/shard_map/attention_forward/pallas_call | solution.py:1133
  145.0 147.5 %feed_forward_both.1 = (bf16[1024,2048]{1,0:T(8,128)(2,1)}, bf16[1024,2048]{1,0:T(8,128)(2,1)}, f32[2,128,2048]{2,1,0:T(8,128)}, bf16[1024,2048]{1,0:T(8,128)(2,...) custom-call(s32[2]{0:T(128)} %len_ref.5, ...), custom_call_target="tpu_custom_call", output_to_operand_aliasing={{6}: (9, {})} | custom-call | flops 77309411328 | bytes 125829120 | tf_op jit(solution)/shard_map/feed_forward_both/pallas_call | solution.py:1602
  292.5 145.5 %attention_backward.1 = (bf16[2,128,2048]{2,1,0:T(8,128)(2,1)}, bf16[2,128,2048]{2,1,0:T(8,128)(2,1)}, bf16[2,128,2048]{2,1,0:T(8,128)(2,1)}, bf16[512,256]{1,0:...) custom-call(s32[2]{0:T(128)} %len_ref.5, ...), custom_call_target="tpu_custom_call" | custom-call | flops 10737418240 | bytes 125829120 | tf_op jit(solution)/shard_map/attention_backward/pallas_call | solution.py:2180
  438.1 0.7 concatenate.6.scal_ref
  438.8 13.6 %results.1 = (bf16[2,128,2048]{2,1,0:T(8,128)(2,1)}, f32[2,128,2048]{2,1,0:T(8,128)}, f32[256,2048]{1,0:T(8,128)}, f32[256,2048]{1,0:T(8,128)}, f32[2048,256]{1,...) custom-call(s32[9]{0:T(128)} %concatenate.6.scal_ref, ...), custom_call_target="tpu_custom_call" | custom-call | flops 15728640 | bytes 31457280 | tf_op jit(solution)/shard_map/results/pallas_call | solution.py:2264
  452.3 1.2 sqrt.3

commit v6 on v5

--- a/solution.py
+++ b/solution.py
@@ -1158,7 +1158,7 @@
         body(pl.ds(pl.multiple_of(p * size, size), size), p * size)
         return carry
 
-    lax.fori_loop(0, count // size, one, 0)
+    lax.fori_loop(0, count // size, one, 0, unroll=2)
 
 
 def fold_lanes(values):
@@ -1245,10 +1245,10 @@
 def feed_both_kernel(
     hb, sub, rows,
     len_ref, n2_hbm, gf_hbm, gate_hbm, up_hbm, down_hbm, gi_hbm, rest_hbm, xr_hbm, hidden_in, gains_ref,
-    ffn_hbm, gb_hbm, gh_hbm, dgate_hbm, dup_hbm, ddown_hbm, hidden_hbm, landx, landy, gain_out, stat_ref,
+    ffn_hbm, gb_hbm, gh_hbm, dgate_hbm, dup_hbm, ddown_hbm, hidden_hbm, landx, landy, ring_hbm, gain_out, stat_ref,
     n2_v, gf_v, inner_v, gg_v, gu_v, facc, gacc, wrow, wcol, part_v, in_v, back_v, total_v, hid_v, gh_v, gb_v, stage_row, stage_col,
     late_p, late_a, late_b, xtile_v, gi_v, wide_v, temp_v, gain_ref,
-    load_sem, wsem, zsend, zrecv, hid_sem, out_sem, ffn_sem, csend, crecv, store_sem, lsend, lrecv, xt_sem, xsend, xrecv, xload, free_sem,
+    load_sem, wsem, zsend, zrecv, hid_sem, out_sem, ffn_sem, csend, crecv, store_sem, lsend, lrecv, xt_sem, xsend, xrecv, xload, rsend, rrecv, free_sem,
 ):
     core, rank = lax.axis_index("context"), lax.axis_index("tensor")
     near_core = {"context": 1 - core}
@@ -1542,6 +1542,11 @@
         lax.fori_loop(part * (hsteps // 2), (part + 1) * (hsteps // 2), one, 0)
 
     pl.semaphore_wait(free_sem, 1)
+
+    def term(m):
+        return ffn_hbm.at[pl.ds(pl.multiple_of(m * (2 * sub), 2 * sub), 2 * sub), :]
+
+    fold = Fold(rank, term, None, ring_hbm, (ring_hbm.at[2], None), rsend, rrecv)
     after = iter(range(steps - 6, subs + 4))
     done = []
 
@@ -1551,6 +1556,8 @@
             done.append(part)
             if len(done) <= 8 or len(done) % 2 == 0:
                 serve(next(after))
+            if len(done) == 5:
+                fold.begin()
 
     both(1, 0, None)
     both(0, 0, (1, 0))
@@ -1574,6 +1581,17 @@
     gate_sum.arrived()
     gate_sum.settle()
     chain.settle()
+
+    @pl.when(fold.inner)
+    def _():
+        for k in range(3):
+            fold.come(k)
+
+    @pl.when(fold.outer)
+    def _():
+        for k in range(3):
+            fold.inward(k).wait_send()
+
     late.settle()
 
 
@@ -1602,12 +1620,12 @@
     return pl.pallas_call(
         functools.partial(feed_both_kernel, hb, sub, rows),
         in_specs=[SMEM] + [any_space] * 9 + [vmem],
-        out_specs=[any_space] * 9 + [vmem] * 2,
+        out_specs=[any_space] * 10 + [vmem] * 2,
         out_shape=[
             shape((tokens, width), BF16), shape((tokens, width), BF16), shape((2, 2 * sub, width), F32),
             shape((half, hidden), BF16), shape((half, hidden), BF16), shape((hidden, half), BF16),
             shape((tokens, width), F32), shape((half // 4, hidden), BF16), shape((half // 4, hidden), BF16),
-            shape((8, width), F32), shape((2, 8, 128), F32),
+            shape((3, 2 * sub, width), BF16), shape((8, width), F32), shape((2, 8, 128), F32),
         ],
         scratch_shapes=[
             pltpu.VMEM((tokens, width), BF16), pltpu.VMEM((tokens, width), BF16), act, act, act,
@@ -1619,7 +1637,7 @@
             late, late, late, pltpu.VMEM((sub, width), BF16), pltpu.VMEM((2, rows, hb), BF16),
             pltpu.VMEM((2, half // 8, hidden), BF16), pltpu.VMEM((2, half // 8, hidden), BF16), pltpu.VMEM((1, width), F32),
             dma((3,)), dma((2, 7)), dma((3, 16)), dma((3, 16)), dma(()), dma((2,)), dma((2, 4)), dma((3, 4)), dma((3, 4)),
-            dma((3, 4)), dma((3, count)), dma((3, count)), dma(()), dma((6,)), dma((6,)), dma((3,)), pltpu.SemaphoreType.REGULAR,
+            dma((3, 4)), dma((3, count)), dma((3, count)), dma(()), dma((6,)), dma((6,)), dma((3,)), dma((6,)), dma((6,)), pltpu.SemaphoreType.REGULAR,
         ],
         input_output_aliases={9: 6},
         compiler_params=pltpu.CompilerParams(vmem_limit_bytes=VMEM_MOST, collective_id=2, has_side_effects=True),
@@ -1628,37 +1646,73 @@
     )(lengths, n2, gf, gate, up, down, gi, rest, xr, hidden_rows, gain)
 
 
-class Ring:
-    def __init__(self, rank, source, own, slots, send, recv, last=None):
-        self.source, self.own, self.slots, self.send, self.recv = source, own, slots, send, recv
-        self.last = slots.at[2] if last is None else last
-        self.rows = slots.shape[1]
-        self.rank, self.right = rank, {"tensor": (rank + 1) % 4}
-
-    def hop(self, j):
-        src = self.source((self.rank + 3) % 4) if j == 0 else self.slots.at[j - 1]
-        dst = self.last if j == 2 else self.slots.at[j]
-        return remote(src, dst, self.send.at[j], self.recv.at[j], self.right)
+class Fold:
+    def __init__(self, rank, source, own, slots, finals, send, recv, landed=None):
+        self.inner, self.outer = (rank % 3) != 0, (rank % 3) == 0
+        self.side, self.mid = {"tensor": xor_one(rank)}, {"tensor": 3 - rank}
+        self.leaving = (3 - rank, xor_one(3 - rank), xor_one(rank))
+        self.added = (xor_one(3 - rank), 3 - rank, xor_one(rank))
+        self.source, self.own, self.slots, self.finals = source, own, slots, finals
+        self.send, self.recv, self.landed = send, recv, landed
+
+    def inward(self, k):
+        dst = self.slots.at[k] if k < 2 else self.finals[0]
+        return remote(self.source(self.leaving[k]), dst, self.send.at[k], self.recv.at[k], self.side)
+
+    def across(self, k):
+        dst = self.slots.at[2] if k == 0 else self.finals[1]
+        return remote(self.slots.at[k], dst, self.send.at[3 + k], self.recv.at[3 + k], self.mid)
+
+    def outward(self):
+        return remote(self.slots.at[2], self.finals[0], self.send.at[5], self.recv.at[5], self.side)
 
     def begin(self):
-        self.hop(0).start()
-
-    def step(self, j):
-        self.hop(j - 1).wait_recv()
-        read = self.own((self.rank + 3 - j) % 4)
-
-        def body(cut, first):
-            self.slots[j - 1, cut, :] = (self.slots[j - 1, cut, :].astype(F32) + read(cut).astype(F32)).astype(BF16)
-
-        by_pieces(self.rows, body)
-        self.hop(j).start()
+        @pl.when(self.outer)
+        def _():
+            for k in range(3):
+                self.inward(k).start()
+
+    def come(self, k):
+        (self.landed[k].wait if self.landed is not None else self.inward(k).wait_recv)()
+
+    def step(self, k):
+        @pl.when(self.inner)
+        def _():
+            if k < 2:
+                self.come(k)
+            else:
+                self.across(0).wait_recv()
+            read = self.own(self.added[k])
+
+            def body(cut, first):
+                self.slots[k, cut, :] = (self.slots[k, cut, :].astype(F32) + read(cut).astype(F32)).astype(BF16)
+
+            by_pieces(self.slots.shape[1], body)
+            (self.across(k) if k < 2 else self.outward()).start()
 
     def arrived(self):
-        self.hop(2).wait_recv()
+        @pl.when(self.inner)
+        def _():
+            self.come(2)
+            self.across(1).wait_recv()
+
+        @pl.when(self.outer)
+        def _():
+            self.outward().wait_recv()
 
     def settle(self):
-        for j in range(3):
-            self.hop(j).wait_send()
+        @pl.when(self.inner)
+        def _():
+            for k in range(2):
+                self.across(k).wait_send()
+            self.outward().wait_send()
+
+        if self.landed is None:
+
+            @pl.when(self.outer)
+            def _():
+                for k in range(3):
+                    self.inward(k).wait_send()
 
 
 def tall(ref):
@@ -1735,12 +1789,12 @@
 
 def backward_kernel(
     hd, nq, nk, block,
-    len_ref, gb_hbm, hidden_hbm, ffn_hbm, xr_hbm, n1_hbm, tok_hbm, outw_hbm, qkvw_hbm, all_hbm, att_hbm, inv_hbm, pre_hbm,
+    len_ref, gb_hbm, hidden_hbm, ffn_hbm, ring_hbm, xr_hbm, n1_hbm, tok_hbm, outw_hbm, qkvw_hbm, all_hbm, att_hbm, inv_hbm, pre_hbm,
     dup_hbm, ddown_hbm, table_ref, stat_ref, stat2_ref, gain2_ref,
-    out_hbm, fin_hbm, own_hbm, mine_o, mine_q, landx1, landy1, landx2, landy2, landx3, landy3, landx4, landy4,
+    out_hbm, fin_hbm, finb_hbm, own_hbm, mine_o, mine_q, landx1, landy1, landx2, landy2, landx3, landy3, landx4, landy4,
     lines_out, small_out,
     act_v, rows_v, qkvw_v, tok_v, all_v, att_v, inv_v, pre_v, grads, da_all, da_own, da_send, da_got, d_own, d_send, d_got, dpre_v,
-    first_v, slots_v, piece_v, wide_a, wide_b, temp_a, temp_b,
+    first_v, slots_v, turns_v, piece_v, wide_a, wide_b, temp_a, temp_b,
     go_v, so_v, wide_o, temp_o, gq_v, sq_v, wide_q, temp_q,
     tile_v, otile_v, lines_v, small_v, heads_v, lin1, lin2, lin3, small_r,
     load_sem, zsend, zrecv, piece_sem, xsend, xrecv, xload, own_sem, exsend, exrecv, osend, orecv, qsend, qrecv,
@@ -1780,6 +1834,17 @@
 
     greet([(None, d) for d in (near_x, near_y, {"dp": near[3]}, near_core, z_right, z_left, z_far)])
 
+    last = seqs - 1
+    inner = (rank % 3) != 0
+    came = []
+    for k, slot in enumerate((0, 1, 3)):
+        came.append(pltpu.make_async_copy(ring_hbm.at[k], slots_v.at[0, slot], load_sem.at[12 + k]))
+
+    @pl.when(inner)
+    def _():
+        for copy in came:
+            copy.start()
+
     def ffn_own(s):
         def own(m):
             load_piece(s, m).wait()
@@ -1791,21 +1856,30 @@
         return lambda m: lambda cut: first_v[s, m, cut, :]
 
     ffn_rings = [
-        Ring(rank, lambda m, s=s: ffn_hbm.at[piece_rows(s, m), :], ffn_own(s), slots_v.at[s], zsend.at[s], zrecv.at[s])
+        Fold(
+            rank, lambda m, s=s: ffn_hbm.at[piece_rows(s, m), :], ffn_own(s), slots_v.at[s], (slots_v.at[s, 3], slots_v.at[s, 4]),
+            zsend.at[s], zrecv.at[s], came if s == 0 else None,
+        )
         for s in range(seqs)
     ]
     first_rings = [
-        Ring(rank, lambda m, s=s: first_v.at[s, m], first_own(s), slots_v.at[seqs + s], zsend.at[seqs + s], zrecv.at[seqs + s], fin_hbm.at[s])
+        Fold(
+            rank, lambda m, s=s: first_v.at[s, m], first_own(s), turns_v.at[s], (fin_hbm.at[s], finb_hbm.at[s]),
+            zsend.at[seqs + s], zrecv.at[seqs + s],
+        )
         for s in range(seqs)
     ]
-    last = seqs - 1
+    for s in range(1, seqs):
+        ffn_rings[s].begin()
     for s in range(seqs):
-        ffn_rings[s].begin()
-        load_piece(s, (rank + 2) % 4).start()
-
-    def ffn_step(s, j):
-        ffn_rings[s].step(j)
-        load_piece(s, (rank + 2 - j) % 4).start()
+        load_piece(s, jnp.where(inner, ffn_rings[s].added[0], rank)).start()
+
+    def ffn_step(s, k):
+        ffn_rings[s].step(k)
+
+        @pl.when(inner)
+        def _():
+            load_piece(s, ffn_rings[s].added[k + 1] if k < 2 else rank).start()
 
     def in_hbm(ref, axis):
         size = ref.shape[axis] // 4
@@ -1834,6 +1908,8 @@
     s_out = scatter(2, in_vmem(go_v), wide_o, halves(landx3), halves(landy3), temp_o)
     s_qkv = scatter(3, in_vmem(gq_v), wide_q, halves(landx4), halves(landy4), temp_q)
     s_up.begin()
+    ffn_step(0, 0)
+    ffn_step(0, 1)
 
     load_gb.wait()
     load_outw.wait()
@@ -1859,7 +1935,7 @@
     lax.fori_loop(0, seqs, branch_rows, 0)
 
     def load_x(s):
-        return [pltpu.make_async_copy(xr_hbm.at[s, :, pl.ds(k * half, half)], rows_v.at[k], load_sem.at[8 + k]) for k in range(2)]
+        return [pltpu.make_async_copy(xr_hbm.at[s, :, pl.ds(k * half, half)], rows_v.at[k], load_sem.at[10 + k]) for k in range(2)]
 
     for copy in load_x(0):
         copy.start()
@@ -1978,8 +2054,8 @@
 
         @pl.when(s == last)
         def _():
+            ffn_step(1, 1)
             s_up.pass_on()
-            ffn_step(1, 1)
 
         heads_rows(s)
 
@@ -1988,7 +2064,8 @@
             for copy in load_x(1):
                 copy.start()
             first_rings[0].begin()
-            ffn_step(0, 1)
+            ffn_step(1, 0)
+            ffn_step(0, 2)
             s_down.begin()
 
         @pl.when(s == last)
@@ -2040,6 +2117,7 @@
         cut = slice(half + k * size_o, half + (k + 1) * size_o)
         so_v[k] = dot_tn(tok_v[...], act_v[:, cut]).astype(BF16)
         blocks_o[k].start()
+    ffn_step(1, 2)
     for k in range(4):
         blocks_o[k].wait_recv()
         cut = slice(k * size_o, (k + 1) * size_o)
@@ -2088,7 +2166,8 @@
         keep.wait()
 
         def body(cut, first):
-            ffn = slots_v[s, 2, cut, :].astype(F32) + read(cut).astype(F32)
+            ffn = slots_v[s, 3, cut, :].astype(F32) + read(cut).astype(F32)
+            ffn = ffn + jnp.where(inner, slots_v[s, 4, cut, :].astype(F32), 0.0)
             otile_v[cut, :] = (tile_v[cut, :] + ffn).astype(BF16)
             spot = start + rank * share + first + lax.broadcasted_iota(jnp.int32, (16, 1), 0)
             valid = (spot < len_ref[s]).astype(F32)
@@ -2102,22 +2181,22 @@
             copy.wait()
 
     small_v[0:1, :] = jnp.sum(heads_v[...].T, axis=0, keepdims=True)
-    ffn_step(0, 2)
-    ffn_step(1, 2)
-    first_rings[0].step(1)
+    first_rings[0].step(0)
+    out_share(0)
     s_down.pass_on()
-    first_rings[1].step(1)
-    s_out.pass_on()
-    s_qkv.pass_on()
+    out_share(1)
     hop_end(1, hop_lines)
-    out_share(0)
-    out_share(1)
     hop_begin(2, hop_small)
     hop_end(2, hop_small)
     hop_begin(3, hop_square)
+    first_rings[0].step(1)
+    first_rings[0].step(2)
+    s_out.pass_on()
+    s_qkv.pass_on()
+    first_rings[1].step(0)
     hop_end(3, hop_square)
     hop_begin(4, hop_chain)
-    first_rings[0].step(2)
+    first_rings[1].step(1)
     first_rings[1].step(2)
     hop_end(4, hop_chain)
     lines_out[...] = lines_v[:, :piece]
@@ -2140,7 +2219,7 @@
 
 
 def backward(
-    lengths, gb, hidden_rows, ffn, xr, n1, tok, outw, qkvw, everything, att, inv, pre, dup, ddown,
+    lengths, gb, hidden_rows, ffn, ring, xr, n1, tok, outw, qkvw, everything, att, inv, pre, dup, ddown,
     table, stat, stat2, gain2_part, hd, nq, nk,
 ):
     seqs, span, width = xr.shape
@@ -2157,7 +2236,7 @@
     dma = pltpu.SemaphoreType.DMA
     hold = lambda *dims: pltpu.VMEM(dims, BF16)
     wide = lambda *dims: pltpu.VMEM(dims, F32)
-    big = [shape((seqs, share, width), BF16)] * 3 + [shape((feat, piece), BF16), shape((piece, cols), BF16)]
+    big = [shape((seqs, share, width), BF16)] * 4 + [shape((feat, piece), BF16), shape((piece, cols), BF16)]
     big += [shape((piece, hidden), BF16)] * 2 + [shape((hidden, piece), BF16)] * 2
     big += [shape((feat, piece), BF16)] * 2 + [shape((piece, cols), BF16)] * 2
     small = [shape((16, piece), F32), shape((8, 128), F32)]
@@ -2167,19 +2246,19 @@
         wide(*inv.shape), wide(*pre.shape), wide(rows, 2 * span), hold(groups * hd, 2 * span),
         hold(seqs, feat // 2, span), hold(seqs, feat // 2, span), hold(seqs, feat // 2, span),
         hold(seqs, rows, span), hold(seqs, rows, span), hold(seqs, rows, span), hold(seqs * span, cols),
-        hold(seqs, 4, share, width), hold(2 * seqs, 3, share, width), hold(seqs, share, width),
+        hold(seqs, 4, share, width), hold(seqs, 5, share, width), hold(seqs, 3, share, width), hold(seqs, share, width),
         hold(2, piece // 2, hidden), hold(2, hidden // 2, piece), hold(2, piece // 2, hidden), hold(2, hidden // 2, piece),
         hold(4, feat, piece), hold(4, feat, piece), hold(2, feat // 2, piece), hold(2, feat // 2, piece),
         hold(4, piece, cols), hold(4, piece, cols), hold(2, piece // 2, cols), hold(2, piece // 2, cols),
         wide(share, width), hold(share, width),
         wide(16, width), wide(8, 128), wide(2 * hd, 128), wide(16, half), wide(3, 16, piece), wide(3, 16, piece), wide(7, 8, 128),
-        dma((10,)), dma((2 * seqs, 3)), dma((2 * seqs, 3)), dma((seqs,)), dma((4, 6)), dma((4, 6)), dma((4, 3)), dma((2 + seqs,)),
+        dma((15,)), dma((2 * seqs, 6)), dma((2 * seqs, 6)), dma((seqs,)), dma((4, 6)), dma((4, 6)), dma((4, 3)), dma((2 + seqs,)),
         dma((2, seqs)), dma((2, seqs)), dma((4,)), dma((4,)), dma((4,)), dma((4,)), dma((2,)), dma((8,)), dma((5, 6)), dma((5, 6)),
     ]
     tokens = seqs * span
     return pl.pallas_call(
         functools.partial(backward_kernel, hd, nq, nk, block),
-        in_specs=[SMEM] + [any_space] * 14 + [vmem] * 4,
+        in_specs=[SMEM] + [any_space] * 15 + [vmem] * 4,
         out_specs=[any_space] * len(big) + [vmem] * 2,
         out_shape=big + small,
         scratch_shapes=scratch,
@@ -2187,93 +2266,126 @@
         cost_estimate=cost(4 * tokens * width * (cols + feat), 60 * tokens * width),
         name="attention_backward",
     )(
-        lengths, gb, hidden_rows, ffn, xr, n1, tok, outw, qkvw, everything, att, inv, pre, dup, ddown,
+        lengths, gb, hidden_rows, ffn, ring, xr, n1, tok, outw, qkvw, everything, att, inv, pre, dup, ddown,
         table, stat, stat2, gain2_part,
     )
 
 
 def results_kernel(
-    hd, nqc, nkc, count, scal_ref, dgate, lx0, ly0, dup, lx1, ly1, ddown, lx2, ly2, mine_o, lx3, ly3, mine_q, lx4, ly4,
-    gh_ref, x_ref, fin_ref, own_ref, out_ref, gains_ref, lines_ref, small_ref,
+    hd, nqc, nkc, count,
+    dgate, lx0, ly0, dup, lx1, ly1, ddown, lx2, ly2, mine_o, lx3, ly3, mine_q, lx4, ly4, gh, xr, fin, finb, own, out, gains_ref, lines_ref, small_ref,
     output, gin, ggate, gup, gdown, gout, gq, gk, gv, gain_a, gain_b, gain_q, gain_k, rms,
+    gate_i, up_i, down_i, o_i, q_i, gate_o, up_o, down_o, o_o, q_o, gh_v, x_v, fin_v, finb_v, own_v, gin_v, out_v, in_sem, token_sem, out_sem, place_sem, copy_sem,
 ):
-    def add(*refs):
-        return sum(ref[...].astype(F32) for ref in refs)
-
-    ggate[...] = add(dgate, lx0, ly0)
-    gup[...] = add(dup, lx1, ly1)
-    gdown[...] = add(ddown, lx2, ly2)
-    gout[...] = add(mine_o, lx3, ly3)
-    qkv = add(mine_q, lx4, ly4)
-    gq[...] = qkv[:, :nqc]
-    gk[...] = qkv[:, nqc : nqc + nkc]
-    gv[...] = qkv[:, nqc + nkc :]
-    output[...] = out_ref[...]
-    width = x_ref.shape[-1]
+    row, core, rank = lax.axis_index("dp"), lax.axis_index("context"), lax.axis_index("tensor")
+    near = [row, xor_one(row), (row + 2) % 4, 3 - row]
+    seqs, share, width = gin_v.shape
     piece = width // 8
-    rows = x_ref.shape[1]
+    sums = (
+        (dgate.at[pl.ds(0, piece), :], lx0, ly0, gate_i, gate_o, ((0, ggate),)),
+        (dup.at[pl.ds(0, piece), :], lx1, ly1, up_i, up_o, ((0, gup),)),
+        (ddown.at[:, pl.ds(0, piece)], lx2, ly2, down_i, down_o, ((0, gdown),)),
+        (mine_o, lx3, ly3, o_i, o_o, ((0, gout),)),
+        (mine_q, lx4, ly4, q_i, q_o, ((0, gq), (nqc, gk), (nqc + nkc, gv))),
+    )
+    into_out = pltpu.make_async_copy(out, out_v, copy_sem.at[0])
+    into_out.start()
+    through = pltpu.make_async_copy(out_v, output, copy_sem.at[1])
+
+    def loads(i):
+        one, two, three, into = sums[i][:4]
+        return [pltpu.make_async_copy(src, into.at[k], in_sem.at[i, k]) for k, src in enumerate((one, two, three))]
+
+    mine = pl.ds(pl.multiple_of(rank * share, share), share)
+    tokens = [
+        pltpu.make_async_copy(src, dst, token_sem.at[k])
+        for k, (src, dst) in enumerate(((gh, gh_v), (xr.at[:, mine, :], x_v), (fin, fin_v), (finb, finb_v), (own, own_v)))
+    ]
+    for copy in tokens:
+        copy.start()
+
+    first = jnp.sum(lines_ref[:8, :], axis=0, keepdims=True)
+    second = jnp.sum(lines_ref[8:, :], axis=0, keepdims=True)
+    gain_a[...] = first.reshape(gain_a.shape)
+    gain_b[...] = second.reshape(gain_b.shape)
+    gain_q[...] = small_ref[0:1, :hd].reshape(gain_q.shape)
+    gain_k[...] = small_ref[0:1, hd : 2 * hd].reshape(gain_k.shape)
+    total = jnp.sum(small_ref[4:5, :], keepdims=True) * count
+    for k in range(3):
+        square = jnp.sum(small_ref[1 + k : 2 + k, :], keepdims=True) / total
+        rms[k] = jnp.max(jnp.sqrt(jnp.broadcast_to(square, (8, 128))))
+
+    into_out.wait()
+    through.start()
     gain = jnp.concatenate([gains_ref[b, 0:1, :] for b in range(8)], axis=1).astype(F32)
-    for r in range(0, rows, 16):
-        cut = slice(r, r + 16)
-        e = fin_ref[0, cut, :].astype(F32) + own_ref[0, cut, :].astype(F32)
-        x = x_ref[0, cut, :].astype(F32)
-        inv = inverse_rms(x)
-        hat = x * inv
-        eg = e * gain
-        value = gh_ref[0, cut, :] + inv * (eg - hat * jnp.mean(eg * hat, axis=-1, keepdims=True))
-        for k in range(8):
-            gin[0, cut, pl.ds(pl.multiple_of(scal_ref[1 + k] * piece, piece), piece)] = value[:, k * piece : (k + 1) * piece]
-
-    @pl.when(pl.program_id(0) == 0)
-    def _():
-        first = jnp.sum(lines_ref[:8, :], axis=0, keepdims=True)
-        second = jnp.sum(lines_ref[8:, :], axis=0, keepdims=True)
-        gain_a[...] = first.reshape(gain_a.shape)
-        gain_b[...] = second.reshape(gain_b.shape)
-        gain_q[...] = small_ref[0:1, :hd].reshape(gain_q.shape)
-        gain_k[...] = small_ref[0:1, hd : 2 * hd].reshape(gain_k.shape)
-        totals = [jnp.sum(small_ref[k, :]) for k in range(1, 5)]
-        for k in range(3):
-            rms[k] = totals[k] / (totals[3] * count)
-
-
-def finish_results(rank, ids, pairs, mine_o, mine_q, lands_o, lands_q, gh, xr, fin, own, out, gains, lines, small, hd, nqc, nkc):
+    for copy in tokens:
+        copy.wait()
+    for i in range(len(sums)):
+        for copy in loads(i):
+            copy.start()
+    inner = (rank % 3) != 0
+    stores = []
+    for s in range(seqs):
+
+        def body(cut, at):
+            e = fin_v[s, cut, :].astype(F32) + own_v[s, cut, :].astype(F32)
+            e = e + jnp.where(inner, finb_v[s, cut, :].astype(F32), 0.0)
+            x = x_v[s, cut, :].astype(F32)
+            inv = inverse_rms(x)
+            hat = x * inv
+            eg = e * gain
+            gin_v[s, cut, :] = gh_v[s, cut, :] + inv * (eg - hat * jnp.mean(eg * hat, axis=-1, keepdims=True))
+
+        by_pieces(share, body)
+        for o in range(2):
+            for k in range(4):
+                b = near[k] * 2 + (core if o == 0 else 1 - core)
+                cut = pl.ds(pl.multiple_of(b * piece, piece), piece)
+                src = gin_v.at[s, :, pl.ds((o * 4 + k) * piece, piece)]
+                stores.append(pltpu.make_async_copy(src, gin.at[s, :, cut], place_sem.at[s, o * 4 + k]))
+                stores[-1].start()
+
+    for i, (_, _, _, came, total_v, parts) in enumerate(sums):
+        for copy in loads(i):
+            copy.wait()
+
+        def body(cut, at):
+            total_v[cut, :] = sum(came[k, cut, :].astype(F32) for k in range(3))
+
+        by_pieces(total_v.shape[0], body, tall(total_v))
+        for n, (at, dst) in enumerate(parts):
+            stores.append(pltpu.make_async_copy(total_v.at[:, pl.ds(at, dst.shape[1])], dst, out_sem.at[i, n]))
+            stores[-1].start()
+    for copy in stores + [through]:
+        copy.wait()
+
+
+def finish_results(pairs, mine_o, mine_q, lands_o, lands_q, gh, xr, fin, finb, own, out, gains, lines, small, hd, nqc, nkc):
     (dgate, lx0, ly0), (dup, lx1, ly1), (ddown, lx2, ly2) = pairs
-    steps = 8
     seqs, share, width = out.shape
     hidden = dgate.shape[1]
     piece = width // 8
-    per = steps // seqs
-    rows = share // per
-    wide = lambda h, w: pl.BlockSpec((h, w), lambda i, s: (i, 0))
-    token = pl.BlockSpec((1, rows, width), lambda i, s: (i // per, i % per, 0))
-    mine = pl.BlockSpec((1, rows, width), lambda i, s: (i // per, s[0] * per + i % per, 0))
-    fixed = lambda a: pl.BlockSpec(a.shape, lambda i, s: (0,) * a.ndim)
-    g = wide(piece // steps, hidden)
-    d = wide(hidden // steps, piece)
-    o = wide(mine_o.shape[0] // steps, piece)
-    q = wide(piece // steps, mine_q.shape[1])
-    outs = [
-        (shape(out.shape, BF16), token), (shape(out.shape, F32), token), (shape((piece, hidden), F32), g), (shape((piece, hidden), F32), g),
-        (shape((hidden, piece), F32), d), (shape(mine_o.shape, F32), o), (shape((piece, nqc), F32), wide(piece // steps, nqc)),
-        (shape((piece, nkc), F32), wide(piece // steps, nkc)), (shape((piece, nkc), F32), wide(piece // steps, nkc)),
-        *[(shape((size,), F32), pl.BlockSpec((size,), lambda i, s: (0,))) for size in (piece, piece, hd, hd)],
-        (shape((3,), F32), pl.BlockSpec(memory_space=pltpu.SMEM)),
-    ]
-    scalars = jnp.concatenate([rank.astype(jnp.int32).reshape(1), ids])
+    any_space = pl.BlockSpec(memory_space=pl.ANY)
+    vmem = pl.BlockSpec(memory_space=pltpu.VMEM)
+    dma = pltpu.SemaphoreType.DMA
+    blocks = [(piece, hidden), (piece, hidden), (hidden, piece), mine_o.shape, mine_q.shape]
+    outs = [shape(out.shape, BF16), shape(out.shape, F32)] + [shape(b, F32) for b in blocks[:4]]
+    outs += [shape((piece, size), F32) for size in (nqc, nkc, nkc)]
+    tiny = [shape((size,), F32) for size in (piece, piece, hd, hd)]
+    token = pltpu.VMEM(out.shape, BF16)
     return pl.pallas_call(
         functools.partial(results_kernel, hd, nqc, nkc, float(width)),
-        grid_spec=pltpu.PrefetchScalarGridSpec(
-            num_scalar_prefetch=1,
-            grid=(steps,),
-            in_specs=[g] * 6 + [d] * 3 + [o] * 3 + [q] * 3 + [token, mine, token, token, token, fixed(gains), fixed(lines), fixed(small)],
-            out_specs=[spec for _, spec in outs],
-        ),
-        out_shape=[kind for kind, _ in outs],
+        in_specs=[any_space] * 21 + [vmem] * 3,
+        out_specs=[any_space] * len(outs) + [vmem] * 4 + [SMEM],
+        out_shape=outs + tiny + [shape((3,), F32)],
+        scratch_shapes=[pltpu.VMEM((3,) + tuple(b), BF16) for b in blocks]
+        + [pltpu.VMEM(b, F32) for b in blocks]
+        + [pltpu.VMEM(out.shape, F32), token, token, token, token, pltpu.VMEM(out.shape, F32), token]
+        + [dma((5, 3)), dma((5,)), dma((5, 3)), dma((seqs, 8)), dma((2,))],
         compiler_params=PARAMS,
         cost_estimate=cost(30 * piece * hidden, 60 * piece * hidden),
         name="results",
-    )(scalars, dgate, lx0, ly0, dup, lx1, ly1, ddown, lx2, ly2, mine_o, *lands_o, mine_q, *lands_q, gh, xr, fin, own, out, gains, lines, small)
+    )(dgate, lx0, ly0, dup, lx1, ly1, ddown, lx2, ly2, mine_o, *lands_o, mine_q, *lands_q, gh, xr, fin, finb, own, out, gains, lines, small)
 
 
 def per_device_general(
@@ -2501,23 +2613,20 @@
     )
     tokens = seqs * span
     flat = lambda a: a.reshape(tokens, -1)
-    ffn, gb, gh, d_gate, d_up, d_down, hidden, landx, landy, gain2_part, stat2 = feed_both(
+    ffn, gb, gh, d_gate, d_up, d_down, hidden, landx, landy, ring, gain2_part, stat2 = feed_both(
         lengths, n2, flat(gf), gate, up, down, gi, rest, flat(xr), hidden, gains
     )
-    output, fin, own, mine_o, mine_q, lx1, ly1, lx2, ly2, lx3, ly3, lx4, ly4, lines, small = backward(
-        lengths, gb, hidden, ffn, xr, flat(n1), flat(tok), out_w, qkv,
+    output, fin, finb, own, mine_o, mine_q, lx1, ly1, lx2, ly2, lx3, ly3, lx4, ly4, lines, small = backward(
+        lengths, gb, hidden, ffn, ring, xr, flat(n1), flat(tok), out_w, qkv,
         everything, att, inv, pre, d_up, d_down, table, stat, stat2, gain2_part, hd, nq, nk,
     )
-    row, core = lax.axis_index("dp"), lax.axis_index("context")
-    near = [row, xor_one(row), (row + 2) % 4, 3 - row]
-    ids = jnp.stack([near[k] * 2 + (core if o == 0 else 1 - core) for o in range(2) for k in range(4)]).astype(jnp.int32)
     nqc, nkc = nq * hd, nk * hd
     pairs = ((d_gate, landx, landy), (d_up, lx1, ly1), (d_down, lx2, ly2))
     output, grad_inputs, grad_gate, grad_up, grad_down, grad_out, grad_q, grad_k, grad_v, *small = finish_results(
-        lax.axis_index("tensor"), ids, pairs, mine_o, mine_q, (lx3, ly3), (lx4, ly4), gh, xr, fin, own, output, gains,
+        pairs, mine_o, mine_q, (lx3, ly3), (lx4, ly4), gh, xr, fin, finb, own, output, gains,
         lines, small, hd, nqc, nkc,
     )
-    return (output, grad_inputs, grad_q, grad_k, grad_v, grad_out, grad_gate, grad_up, grad_down, *small[:4], jnp.sqrt(small[4]))
+    return (output, grad_inputs, grad_q, grad_k, grad_v, grad_out, grad_gate, grad_up, grad_down, *small)
 
 
 def per_device(*args):

time: 458 us -> 424 us (0.926)
  Pallas kernels: 450 us -> 413 us
    pallas_call x1, Pallas kernels: 146 us -> 112 us  [backward(): pl.pallas_call(functools.partial(backward_kernel, hd, nq, nk, block), in_...]
where the time goes in v6:
time: 424 us; the launch traced here: 416 us
  Pallas kernels  413 us (97%)
    pallas_call x1, Pallas kernels, feed_both(): pl.pallas_call(functools.partial(feed_both_kernel, hb, sub, rows), in_spe...  145 us
    pallas_call x1, Pallas kernels, forward(): pl.pallas_call(functools.partial(forward_kernel, hd, nq, nk, block, sub),...  143 us
    pallas_call x1, Pallas kernels, backward(): pl.pallas_call(functools.partial(backward_kernel, hd, nq, nk, block), in_...  112 us
    pallas_call x1, Pallas kernels, finish_results(): pl.pallas_call(functools.partial(results_kernel, hd, nqc, nkc, float(widt...  13.6 us

profile of v6, /device:TPU:0, one launch (start us, length us, event | category | flops | bytes accessed | tf_op | source)
XLA Modules:
  0.0 415.6 jit_solution(14875990015841656253)
XLA Ops:
  0.6 0.8 pad_maximum_fusion
  1.4 0.6 reshape.43.small_ref
  2.0 142.8 %attention_forward.1 = (bf16[2,512,2048]{2,1,0:T(8,128)(2,1)}, bf16[2,512,2048]{2,1,0:T(8,128)(2,1)}, bf16[2,512,2048]{2,1,0:T(8,128)(2,1)}, bf16[2,1024,768]{2,...) custom-call(s32[2]{0:T(128)} %len_ref.5, ...), custom_call_target="tpu_custom_call" | custom-call | flops 9663676416 | bytes 167772160 | tf_op jit(solution)/shard_map/attention_forward/pallas_call | solution.py:1133
  144.8 145.0 %feed_forward_both.1 = (bf16[1024,2048]{1,0:T(8,128)(2,1)}, bf16[1024,2048]{1,0:T(8,128)(2,1)}, f32[2,128,2048]{2,1,0:T(8,128)}, bf16[1024,2048]{1,0:T(8,128)(2,...) custom-call(s32[2]{0:T(128)} %len_ref.5, ...), custom_call_target="tpu_custom_call", output_to_operand_aliasing={{6}: (9, {})} | custom-call | flops 77309411328 | bytes 125829120 | tf_op jit(solution)/shard_map/feed_forward_both/pallas_call | solution.py:1620
  289.8 111.7 %attention_backward.1 = (bf16[2,128,2048]{2,1,0:T(8,128)(2,1)}, bf16[2,128,2048]{2,1,0:T(8,128)(2,1)}, bf16[2,128,2048]{2,1,0:T(8,128)(2,1)}, bf16[2,128,2048]{2...) custom-call(s32[2]{0:T(128)} %len_ref.5, ...), custom_call_target="tpu_custom_call" | custom-call | flops 10737418240 | bytes 125829120 | tf_op jit(solution)/shard_map/attention_backward/pallas_call | solution.py:2259
  401.5 13.6 %results.1 = (bf16[2,128,2048]{2,1,0:T(8,128)(2,1)}, f32[2,128,2048]{2,1,0:T(8,128)}, f32[256,2048]{1,0:T(8,128)}, f32[256,2048]{1,0:T(8,128)}, f32[2048,256]{1,...) custom-call(bf16[1024,2048]{1,0:T(8,128)(2,1)} %get-tuple-element.86, ...), custom_call_target="tpu_custom_call" | custom-call | flops 15728640 | bytes 31457280 | tf_op jit(solution)/shard_map/results/pallas_call | solution.py:2376

commit v7 on v6

--- a/solution.py
+++ b/solution.py
@@ -683,14 +683,18 @@
                 return dst.at[0, pl.ds(k * piece + h * half, half), :]
             return dst.at[0, pl.ds(h * half, half), pl.ds(k * piece, piece)]
 
-        sem = lambda k: (send.at[k], recv.at[k])
+        link, cross = send.at[0], send.at[1]
         self.local = pltpu.make_async_copy(shard, block(0, 0), local)
-        self.x = remote(shard, block(0, 1), *sem(0), near_x)
-        self.y = remote(shard, block(0, 2), *sem(1), near_y)
-        self.dx = remote(part(2, 0), part(3, 0), *sem(2), near_x)
-        self.dy = remote(part(1, 1), part(3, 1), *sem(3), near_y)
-        self.cores = [remote(shard, block(1, 0), *sem(4), near_core)]
-        self.cores += [remote(block(0, k), block(1, k), *sem(4 + k), near_core) for k in (1, 2, 3)]
+        self.x = remote(shard, block(0, 1), link, recv.at[0], near_x)
+        self.y = remote(shard, block(0, 2), link, recv.at[1], near_y)
+        self.dx = remote(part(2, 0), part(3, 0), link, recv.at[2], near_x)
+        self.dy = remote(part(1, 1), part(3, 1), link, recv.at[2], near_y)
+        self.cores = [remote(shard if k == 0 else block(0, k), block(1, k), cross, recv.at[3], near_core) for k in range(4)]
+        cut = pl.ds(0, 3 * piece)
+        three = dst.at[0, cut, :] if axis == 0 else dst.at[0, :, cut]
+        self.all_links = remote(three, three, link, recv.at[0], near_x)
+        self.diagonal = remote(block(0, 3), block(0, 3), link, recv.at[2], near_x)
+        self.all_cores = remote(dst.at[0], dst.at[1], cross, recv.at[3], near_core)
 
     def first(self):
         self.x.start()
@@ -707,23 +711,21 @@
         self.cores[1].start()
 
     def third(self):
-        self.dx.wait_recv()
-        self.dy.wait_recv()
+        self.diagonal.wait_recv()
         self.cores[3].start()
 
     def arrived(self):
         self.local.wait()
-        for copy in self.cores:
-            copy.wait_recv()
+        self.all_cores.wait_recv()
 
     def sent(self):
-        for copy in [self.x, self.y, self.dx, self.dy] + self.cores:
-            copy.wait_send()
+        self.all_links.wait_send()
+        self.all_cores.wait_send()
 
 
 def forward_kernel(
     hd, nq, nk, block, sub,
-    len_ref, x_hbm, cot_hbm, wq_hbm, wk_hbm, wv_hbm, wout, wgate, wup, wdown, small_ref,
+    len_ref, x_hbm, cot_hbm, wq_hbm, wk_hbm, wv_hbm, wout, wgate, wup, wdown, again_ref, fgain_ref, qgain_ref, kgain_ref,
     xr_hbm, n1_hbm, gf_hbm, qkv_hbm, out_hbm, gate_hbm, up_hbm, down_hbm, hidden_hbm, n2_hbm, rest_hbm, gi_hbm, pre_hbm, all_hbm, att_hbm, tok_hbm,
     gains_ref, table_ref, inv_ref, stat_ref,
     xr_v, cot_v, n1_v, qkv_v, out_v, ex_own, ex_send, ex_got, at_own, at_send, at_got,
@@ -752,7 +754,7 @@
                     cut = pl.ds(pl.multiple_of(b * piece, piece), piece)
                     loads.append(
                         pltpu.make_async_copy(
-                            src.at[s, :, cut], dst.at[s, :, pl.ds((o * 4 + k) * piece, piece)], load_sem.at[at, s, o * 4 + k]
+                            src.at[s, :, cut], dst.at[s, :, pl.ds((o * 4 + k) * piece, piece)], load_sem.at[at]
                         )
                     )
     shards, at = [], 0
@@ -762,7 +764,8 @@
     for copy in shards + loads:
         copy.start()
     piece = width // 8
-    gain_ref[...] = jnp.concatenate([small_ref[:, :piece], small_ref[:, piece : 2 * piece], jnp.zeros((14, piece), BF16)], axis=0)
+    wide_gains = [ref[...].astype(F32).reshape(1, piece) for ref in (again_ref, fgain_ref)]
+    gain_ref[...] = jnp.concatenate(wide_gains + [jnp.zeros((14, piece), F32)], axis=0).astype(BF16)
 
     others = []
     for o in range(2):
@@ -771,7 +774,8 @@
                 others.append((o * 4 + k, {"dp": near[k], "context": core if o == 0 else 1 - core}))
     greet([(None, d) for _, d in others] + [(None, z_side), (inner, z_mid)])
 
-    gains = [remote(gain_ref, gains_ref.at[b], gsend.at[b], grecv.at[b], d) for b, d in others]
+    gains = [remote(gain_ref, gains_ref.at[b], gsend, grecv, d) for b, d in others]
+    every_gain = remote(gains_ref.at[pl.ds(1, 7)], gains_ref.at[pl.ds(1, 7)], gsend, grecv, near_core)
     for copy in gains:
         copy.start()
     weights = [
@@ -790,15 +794,14 @@
     freqs = jnp.exp(lax.broadcasted_iota(jnp.int32, (quarter, span), 0).astype(F32) * (-2.0 * math.log(rope_base) / hd))
     angles = freqs * (start + lax.broadcasted_iota(jnp.int32, (quarter, span), 1)).astype(F32)
     cosine, sine = jnp.cos(angles), jnp.sin(angles)
-    both_gains = jnp.broadcast_to(small_ref[:, 2 * piece :].astype(F32), (8, 2 * hd)).T
-    qgain, kgain = both_gains[:hd, 0:1], both_gains[hd:, 0:1]
+    turned = [jnp.broadcast_to(ref[...].astype(F32).reshape(1, hd), (8, hd)).T for ref in (qgain_ref, kgain_ref)]
+    qgain, kgain = turned[0][:, 0:1], turned[1][:, 0:1]
     table_ref[:quarter, :] = cosine
     table_ref[quarter : 2 * quarter, :] = sine
     table_ref[2 * quarter : 2 * quarter + hd, :128] = jnp.broadcast_to(qgain, (hd, 128))
     table_ref[2 * quarter + hd :, :128] = jnp.broadcast_to(kgain, (hd, 128))
 
-    for copy in loads[len(loads) // 2 :]:
-        copy.wait()
+    pltpu.make_async_copy(cot_hbm, cot_v, load_sem.at[1]).wait()
 
     def mask_rows(i, carry):
         s, t = i // (span // 16), i % (span // 16)
@@ -811,12 +814,10 @@
     lax.fori_loop(0, seqs * span // 16, mask_rows, 0)
     store_gf = pltpu.make_async_copy(cot_v, gf_hbm, store_sem.at[0])
     store_gf.start()
-    for copy in loads[: len(loads) // 2]:
-        copy.wait()
+    pltpu.make_async_copy(x_hbm, xr_v, load_sem.at[0]).wait()
     store_xr = pltpu.make_async_copy(xr_v, xr_hbm, store_sem.at[1])
     store_xr.start()
-    for copy in gains:
-        copy.wait_recv()
+    every_gain.wait_recv()
     gain1 = jnp.concatenate([gains_ref[b, 0:1, :] for b in range(8)], axis=1).astype(F32)
     gain2 = jnp.concatenate([gains_ref[b, 1:2, :] for b in range(8)], axis=1).astype(F32)
 
@@ -1034,6 +1035,10 @@
         moving.middle(i)
         moving.outward(i - 1)
 
+        @pl.when(i == subs + 1)
+        def _():
+            w_up.third()
+
         @pl.when(i >= 2)
         def _():
             finish(i - 2)
@@ -1072,7 +1077,6 @@
         return carry
 
     lax.fori_loop(0, subs + 2, chain, 0)
-    w_up.third()
     for u in (subs - 2, subs - 1):
         for copy in hidden_store(u):
             copy.wait()
@@ -1084,8 +1088,7 @@
         give(s).wait_send()
         for k in range(4):
             keep(k, s).wait()
-    for copy in gains:
-        copy.wait_send()
+    every_gain.wait_send()
     w_gate.arrived()
     w_up.arrived()
     for w in weights:
@@ -1132,7 +1135,7 @@
     flops = 2 * seqs * span * width * (cols + nq * hd) + 16 * seqs * nq * hd * span * span
     return pl.pallas_call(
         functools.partial(forward_kernel, hd, nq, nk, block, sub),
-        in_specs=[SMEM] + [any_space] * 9 + [vmem],
+        in_specs=[SMEM] + [any_space] * 9 + [vmem] * 4,
         out_specs=[any_space] * len(large) + [vmem] * len(small),
         out_shape=large + small,
         scratch_shapes=[
@@ -1144,13 +1147,13 @@
             pltpu.VMEM((w_query.shape[0], cols), BF16), pltpu.VMEM((16, width // 8), BF16),
             pltpu.VMEM((2, 2, hb, half), BF16), pltpu.VMEM((2, seqs * span, hb), BF16),
             *[pltpu.VMEM(a.shape, a.dtype) for a in kept],
-            dma((4, seqs)), dma((2, seqs, 8)), dma((5,)), dma((3,)), dma((subs - here,)), dma((2, 2)), dma((2,)), dma((5, 8)), dma((5, 8)), dma((5,)), dma((8,)), dma((8,)),
-            dma((2, seqs)), dma((2, seqs)), dma((3, subs)), dma((3, subs)), dma((2, 2)),
+            dma((4, seqs)), dma((2,)), dma((5,)), dma((3,)), dma((subs - here,)), dma((2, 2)), dma((2,)), dma((5, 2)), dma((5, 4)), dma((5,)), dma(()), dma(()),
+            dma((2, seqs)), dma((2, seqs)), dma((2,)), dma((2, here)), dma((2, 2)),
         ],
         compiler_params=pltpu.CompilerParams(vmem_limit_bytes=VMEM_MOST, collective_id=1, has_side_effects=True),
         cost_estimate=cost(flops, 80 * seqs * span * width),
         name="attention_forward",
-    )(lengths, x, cot, w_query, w_key, w_value, w_out, w_gate, w_up, w_down, all_gains)
+    )(lengths, x, cot, w_query, w_key, w_value, w_out, w_gate, w_up, w_down, *all_gains)
 
 
 def by_pieces(count, body, size=16):
@@ -1176,13 +1179,13 @@
         self.count = arrive.shape[0]
 
     def hop_in(self, u):
-        return remote(self.part.at[u], self.arrive.at[u], self.send.at[0, u], self.recv.at[0, u], self.side)
+        return remote(self.part.at[u], self.arrive.at[u], self.send.at[0], self.recv.at[0, u], self.side)
 
     def hop_mid(self, u):
-        return remote(self.arrive.at[u], self.back.at[u], self.send.at[1, u], self.recv.at[1, u], self.mid)
+        return remote(self.arrive.at[u], self.back.at[u], self.send.at[1], self.recv.at[1, u], self.mid)
 
     def hop_out(self, u):
-        return remote(self.part.at[u], self.back.at[u], self.send.at[2, u], self.recv.at[2, u], self.side)
+        return remote(self.part.at[u], self.back.at[u], self.send.at[0], self.recv.at[0, u], self.side)
 
     def add(self, into, one, two, u):
         def body(cut, first):
@@ -1227,19 +1230,12 @@
             by_pieces(self.part.shape[1], body)
 
     def settle(self):
-        def one(u, carry):
-            @pl.when(self.outer)
-            def _():
-                self.hop_in(u).wait_send()
-
-            @pl.when(self.inner)
-            def _():
-                self.hop_mid(u).wait_send()
-                self.hop_out(u).wait_send()
-
-            return carry
-
-        lax.fori_loop(0, self.count, one, 0)
+        every = self.part.at[pl.ds(0, self.count)]
+        remote(every, self.back, self.send.at[0], self.recv.at[0, 0], self.side).wait_send()
+
+        @pl.when(self.inner)
+        def _():
+            remote(self.arrive, self.back, self.send.at[1], self.recv.at[1, 0], self.mid).wait_send()
 
 
 def feed_both_kernel(
@@ -1589,8 +1585,7 @@
 
     @pl.when(fold.outer)
     def _():
-        for k in range(3):
-            fold.inward(k).wait_send()
+        fold.settle()
 
     late.settle()
 
@@ -1636,8 +1631,8 @@
             pltpu.VMEM((2, half, hb), BF16), pltpu.VMEM((2, hb, half), BF16),
             late, late, late, pltpu.VMEM((sub, width), BF16), pltpu.VMEM((2, rows, hb), BF16),
             pltpu.VMEM((2, half // 8, hidden), BF16), pltpu.VMEM((2, half // 8, hidden), BF16), pltpu.VMEM((1, width), F32),
-            dma((3,)), dma((2, 7)), dma((3, 16)), dma((3, 16)), dma(()), dma((2,)), dma((2, 4)), dma((3, 4)), dma((3, 4)),
-            dma((3, 4)), dma((3, count)), dma((3, count)), dma(()), dma((6,)), dma((6,)), dma((3,)), dma((6,)), dma((6,)), pltpu.SemaphoreType.REGULAR,
+            dma((3,)), dma((2, 7)), dma((2,)), dma((2, 16)), dma(()), dma((2,)), dma((2, 4)), dma((3, 4)), dma((3, 4)),
+            dma((3, 4)), dma((2,)), dma((2, count)), dma(()), dma((6,)), dma((6,)), dma((3,)), dma(()), dma((5,)), pltpu.SemaphoreType.REGULAR,
         ],
         input_output_aliases={9: 6},
         compiler_params=pltpu.CompilerParams(vmem_limit_bytes=VMEM_MOST, collective_id=2, has_side_effects=True),
@@ -1657,14 +1652,14 @@
 
     def inward(self, k):
         dst = self.slots.at[k] if k < 2 else self.finals[0]
-        return remote(self.source(self.leaving[k]), dst, self.send.at[k], self.recv.at[k], self.side)
+        return remote(self.source(self.leaving[k]), dst, self.send, self.recv.at[k], self.side)
 
     def across(self, k):
         dst = self.slots.at[2] if k == 0 else self.finals[1]
-        return remote(self.slots.at[k], dst, self.send.at[3 + k], self.recv.at[3 + k], self.mid)
+        return remote(self.slots.at[k], dst, self.send, self.recv.at[3 + k], self.mid)
 
     def outward(self):
-        return remote(self.slots.at[2], self.finals[0], self.send.at[5], self.recv.at[5], self.side)
+        return remote(self.slots.at[2], self.finals[0], self.send, self.recv.at[0], self.side)
 
     def begin(self):
         @pl.when(self.outer)
@@ -1701,18 +1696,12 @@
             self.outward().wait_recv()
 
     def settle(self):
-        @pl.when(self.inner)
-        def _():
-            for k in range(2):
-                self.across(k).wait_send()
-            self.outward().wait_send()
-
+        three = self.slots.at[pl.ds(0, 3)]
+        every = remote(three, three, self.send, self.recv.at[0], self.side)
         if self.landed is None:
-
-            @pl.when(self.outer)
-            def _():
-                for k in range(3):
-                    self.inward(k).wait_send()
+            every.wait_send()
+        else:
+            pl.when(self.inner)(every.wait_send)
 
 
 def tall(ref):
@@ -1761,9 +1750,7 @@
         for copy in self.first[2:] + self.second:
             copy.wait_recv()
 
-    def finish(self, stage, out, store, landed=False):
-        if not landed:
-            self.arrived()
+    def keep(self, out, store):
         for h in range(2):
             loads = [
                 pltpu.make_async_copy(src, self.temps.at[k], self.load.at[k])
@@ -1775,12 +1762,12 @@
                 copy.wait()
 
             def body(cut, first):
-                stage[cut, :] = sum(self.temps[k, cut, :].astype(F32) for k in range(3))
-
-            by_pieces(stage.shape[0], body, tall(stage))
-            keep = pltpu.make_async_copy(stage, out(h), store)
-            keep.start()
-            keep.wait()
+                self.temps[0, cut, :] = sum(self.temps[k, cut, :].astype(F32) for k in range(3)).astype(BF16)
+
+            by_pieces(self.temps.shape[1], body, tall(self.temps.at[0]))
+            copy = pltpu.make_async_copy(self.temps.at[0], out(h), store)
+            copy.start()
+            copy.wait()
 
     def settle(self):
         for copy in self.first + self.second:
@@ -1790,15 +1777,15 @@
 def backward_kernel(
     hd, nq, nk, block,
     len_ref, gb_hbm, hidden_hbm, ffn_hbm, ring_hbm, xr_hbm, n1_hbm, tok_hbm, outw_hbm, qkvw_hbm, all_hbm, att_hbm, inv_hbm, pre_hbm,
-    dup_hbm, ddown_hbm, table_ref, stat_ref, stat2_ref, gain2_ref,
-    out_hbm, fin_hbm, finb_hbm, own_hbm, mine_o, mine_q, landx1, landy1, landx2, landy2, landx3, landy3, landx4, landy4,
+    gh_hbm, dgate_hbm, landx0, landy0, dup_hbm, ddown_hbm, table_ref, gains_ref, stat_ref, stat2_ref, gain2_ref,
+    out_hbm, gin_hbm, fin_hbm, finb_hbm, own_hbm, sum_gate, sum_up, sum_down, mine_o, mine_q, landx1, landy1, landx2, landy2, landx3, landy3, landx4, landy4,
     lines_out, small_out,
     act_v, rows_v, qkvw_v, tok_v, all_v, att_v, inv_v, pre_v, grads, da_all, da_own, da_send, da_got, d_own, d_send, d_got, dpre_v,
     first_v, slots_v, turns_v, piece_v, wide_a, wide_b, temp_a, temp_b,
     go_v, so_v, wide_o, temp_o, gq_v, sq_v, wide_q, temp_q,
     tile_v, otile_v, lines_v, small_v, heads_v, lin1, lin2, lin3, small_r,
     load_sem, zsend, zrecv, piece_sem, xsend, xrecv, xload, own_sem, exsend, exrecv, osend, orecv, qsend, qrecv,
-    tile_sem, outs_sem, smsend, smrecv,
+    tile_sem, outs_sem, sum_sem, smsend, smrecv,
 ):
     seqs, _, slots = all_v.shape
     span = slots // 2
@@ -1903,6 +1890,7 @@
     def scatter(i, get, wide, land_x, land_y, temps):
         return Scatter(get, wide.at[0], wide.at[1], land_x, land_y, temps, xsend.at[i], xrecv.at[i], xload.at[i], near_x, near_y)
 
+    s_gate = scatter(0, in_hbm(dgate_hbm, 0), wide_a, halves(landx0), halves(landy0), temp_a)
     s_up = scatter(0, in_hbm(dup_hbm, 0), wide_a, halves(landx1), halves(landy1), temp_a)
     s_down = scatter(1, in_hbm(ddown_hbm, 1), wide_b, halves(landx2), halves(landy2), temp_b)
     s_out = scatter(2, in_vmem(go_v), wide_o, halves(landx3), halves(landy3), temp_o)
@@ -2077,7 +2065,10 @@
     lax.fori_loop(0, seqs, sequence, 0)
 
     def hop_copies(n, items):
-        return [remote(src, dst, smsend.at[n, i], smrecv.at[n, i], device) for i, (device, src, dst, _) in enumerate(items)]
+        base_at = (0, 1, 4, 5, 8)[n]
+        return [
+            remote(src, dst, smsend.at[base_at + i], smrecv.at[base_at + i], device) for i, (device, src, dst, _) in enumerate(items)
+        ]
 
     def hop_begin(n, items):
         for copy in hop_copies(n, items):
@@ -2148,15 +2139,12 @@
 
 
     def place(tile, dst, s):
-        copies = []
         for o in range(2):
             for k in range(4):
                 b = near[k] * 2 + (core if o == 0 else 1 - core)
                 cut = pl.ds(pl.multiple_of(b * piece, piece), piece)
-                copies.append(
-                    pltpu.make_async_copy(tile.at[:, pl.ds((o * 4 + k) * piece, piece)], dst.at[s, :, cut], outs_sem.at[o * 4 + k])
-                )
-        return copies
+                pltpu.make_async_copy(tile.at[:, pl.ds((o * 4 + k) * piece, piece)], dst.at[s, :, cut], outs_sem).start()
+        pltpu.make_async_copy(tile, dst.at[s], outs_sem).wait()
 
     def out_share(s):
         keep = pltpu.make_async_copy(hidden_hbm.at[piece_rows(s, rank), :], tile_v, tile_sem.at[0])
@@ -2174,11 +2162,34 @@
             small_v[3:4, :] += jnp.sum(fold_lanes(valid * ffn * ffn), axis=0, keepdims=True)
 
         by_pieces(share, body)
-        copies = place(otile_v, out_hbm, s)
-        for copy in copies:
+        place(otile_v, out_hbm, s)
+
+    def in_share(s):
+        first_rings[s].arrived()
+        tiles = (piece_v.at[0], piece_v.at[1], otile_v)
+        rows = pl.ds(pl.multiple_of(rank * share, share), share)
+        loads = [
+            pltpu.make_async_copy(src, dst, load_sem.at[k])
+            for k, (src, dst) in enumerate(zip((fin_hbm.at[s], finb_hbm.at[s], xr_hbm.at[s, rows, :]), tiles))
+        ]
+        loads.append(pltpu.make_async_copy(gh_hbm.at[s], tile_v, load_sem.at[3]))
+        for copy in loads:
             copy.start()
-        for copy in copies:
+        gain = jnp.concatenate([gains_ref[b, 0:1, :] for b in range(8)], axis=1).astype(F32)
+        for copy in loads:
             copy.wait()
+
+        def body(cut, at):
+            e = piece_v[0, cut, :].astype(F32) + first_v[s, rank, cut, :].astype(F32)
+            e = e + jnp.where(inner, piece_v[1, cut, :].astype(F32), 0.0)
+            x = otile_v[cut, :].astype(F32)
+            inv = inverse_rms(x)
+            hat = x * inv
+            eg = e * gain
+            tile_v[cut, :] = tile_v[cut, :] + inv * (eg - hat * jnp.mean(eg * hat, axis=-1, keepdims=True))
+
+        by_pieces(share, body)
+        place(tile_v, gin_hbm, s)
 
     small_v[0:1, :] = jnp.sum(heads_v[...].T, axis=0, keepdims=True)
     first_rings[0].step(0)
@@ -2193,18 +2204,24 @@
     first_rings[0].step(2)
     s_out.pass_on()
     s_qkv.pass_on()
+    s_gate.keep(halves(sum_gate), sum_sem)
+    s_up.arrived()
+    s_up.keep(halves(sum_up), sum_sem)
     first_rings[1].step(0)
     hop_end(3, hop_square)
     hop_begin(4, hop_chain)
+    s_down.arrived()
+    s_down.keep(halves(sum_down), sum_sem)
     first_rings[1].step(1)
     first_rings[1].step(2)
+    for s in range(last):
+        in_share(s)
     hop_end(4, hop_chain)
     lines_out[...] = lines_v[:, :piece]
     small_out[...] = small_v[...]
-    for item in (s_up, s_down, s_out, s_qkv):
+    for item in (s_out, s_qkv):
         item.arrived()
-    for ring in first_rings:
-        ring.arrived()
+    first_rings[last].arrived()
     for copy in keeps:
         copy.wait()
     for ring in ffn_rings + first_rings:
@@ -2219,8 +2236,8 @@
 
 
 def backward(
-    lengths, gb, hidden_rows, ffn, ring, xr, n1, tok, outw, qkvw, everything, att, inv, pre, dup, ddown,
-    table, stat, stat2, gain2_part, hd, nq, nk,
+    lengths, gb, hidden_rows, ffn, ring, xr, n1, tok, outw, qkvw, everything, att, inv, pre, gh, dgate, landx, landy, dup, ddown,
+    table, gains, stat, stat2, gain2_part, hd, nq, nk,
 ):
     seqs, span, width = xr.shape
     half = width // 2
@@ -2236,7 +2253,9 @@
     dma = pltpu.SemaphoreType.DMA
     hold = lambda *dims: pltpu.VMEM(dims, BF16)
     wide = lambda *dims: pltpu.VMEM(dims, F32)
-    big = [shape((seqs, share, width), BF16)] * 4 + [shape((feat, piece), BF16), shape((piece, cols), BF16)]
+    token = shape((seqs, share, width), BF16)
+    big = [token, shape((seqs - 1, share, width), F32)] + [token] * 3 + [shape((piece, hidden), BF16)] * 2 + [shape((hidden, piece), BF16)]
+    big += [shape((feat, piece), BF16), shape((piece, cols), BF16)]
     big += [shape((piece, hidden), BF16)] * 2 + [shape((hidden, piece), BF16)] * 2
     big += [shape((feat, piece), BF16)] * 2 + [shape((piece, cols), BF16)] * 2
     small = [shape((16, piece), F32), shape((8, 128), F32)]
@@ -2247,18 +2266,18 @@
         hold(seqs, feat // 2, span), hold(seqs, feat // 2, span), hold(seqs, feat // 2, span),
         hold(seqs, rows, span), hold(seqs, rows, span), hold(seqs, rows, span), hold(seqs * span, cols),
         hold(seqs, 4, share, width), hold(seqs, 5, share, width), hold(seqs, 3, share, width), hold(seqs, share, width),
-        hold(2, piece // 2, hidden), hold(2, hidden // 2, piece), hold(2, piece // 2, hidden), hold(2, hidden // 2, piece),
+        hold(2, piece // 2, hidden), hold(2, hidden // 2, piece), hold(3, piece // 2, hidden), hold(3, hidden // 2, piece),
         hold(4, feat, piece), hold(4, feat, piece), hold(2, feat // 2, piece), hold(2, feat // 2, piece),
         hold(4, piece, cols), hold(4, piece, cols), hold(2, piece // 2, cols), hold(2, piece // 2, cols),
         wide(share, width), hold(share, width),
         wide(16, width), wide(8, 128), wide(2 * hd, 128), wide(16, half), wide(3, 16, piece), wide(3, 16, piece), wide(7, 8, 128),
-        dma((15,)), dma((2 * seqs, 6)), dma((2 * seqs, 6)), dma((seqs,)), dma((4, 6)), dma((4, 6)), dma((4, 3)), dma((2 + seqs,)),
-        dma((2, seqs)), dma((2, seqs)), dma((4,)), dma((4,)), dma((4,)), dma((4,)), dma((2,)), dma((8,)), dma((5, 6)), dma((5, 6)),
+        dma((15,)), dma((2 * seqs,)), dma((2 * seqs, 5)), dma((seqs,)), dma((4, 6)), dma((4, 6)), dma((4, 3)), dma((2 + seqs,)),
+        dma((2, seqs)), dma((2, seqs)), dma((4,)), dma((4,)), dma((4,)), dma((4,)), dma((2,)), dma(()), dma(()), dma((14,)), dma((14,)),
     ]
     tokens = seqs * span
     return pl.pallas_call(
         functools.partial(backward_kernel, hd, nq, nk, block),
-        in_specs=[SMEM] + [any_space] * 15 + [vmem] * 4,
+        in_specs=[SMEM] + [any_space] * 19 + [vmem] * 5,
         out_specs=[any_space] * len(big) + [vmem] * 2,
         out_shape=big + small,
         scratch_shapes=scratch,
@@ -2266,42 +2285,49 @@
         cost_estimate=cost(4 * tokens * width * (cols + feat), 60 * tokens * width),
         name="attention_backward",
     )(
-        lengths, gb, hidden_rows, ffn, ring, xr, n1, tok, outw, qkvw, everything, att, inv, pre, dup, ddown,
-        table, stat, stat2, gain2_part,
+        lengths, gb, hidden_rows, ffn, ring, xr, n1, tok, outw, qkvw, everything, att, inv, pre, gh, dgate, landx, landy, dup, ddown,
+        table, gains, stat, stat2, gain2_part,
     )
 
 
 def results_kernel(
     hd, nqc, nkc, count,
-    dgate, lx0, ly0, dup, lx1, ly1, ddown, lx2, ly2, mine_o, lx3, ly3, mine_q, lx4, ly4, gh, xr, fin, finb, own, out, gains_ref, lines_ref, small_ref,
+    sum_gate, sum_up, sum_down, mine_o, lx3, ly3, mine_q, lx4, ly4, gh, xr, fin, finb, own, out, early, gains_ref, lines_ref, small_ref,
     output, gin, ggate, gup, gdown, gout, gq, gk, gv, gain_a, gain_b, gain_q, gain_k, rms,
-    gate_i, up_i, down_i, o_i, q_i, gate_o, up_o, down_o, o_o, q_o, gh_v, x_v, fin_v, finb_v, own_v, gin_v, out_v, in_sem, token_sem, out_sem, place_sem, copy_sem,
+    gate_i, up_i, down_i, o_i, q_i, gate_o, up_o, down_o, o_o, q_o, gh_v, x_v, fin_v, finb_v, own_v, early_v, out_v,
+    in_sem, token_sem, out_sem, place_sem, copy_sem,
 ):
     row, core, rank = lax.axis_index("dp"), lax.axis_index("context"), lax.axis_index("tensor")
     near = [row, xor_one(row), (row + 2) % 4, 3 - row]
-    seqs, share, width = gin_v.shape
+    seqs, share, width = out_v.shape
+    last = seqs - 1
     piece = width // 8
     sums = (
-        (dgate.at[pl.ds(0, piece), :], lx0, ly0, gate_i, gate_o, ((0, ggate),)),
-        (dup.at[pl.ds(0, piece), :], lx1, ly1, up_i, up_o, ((0, gup),)),
-        (ddown.at[:, pl.ds(0, piece)], lx2, ly2, down_i, down_o, ((0, gdown),)),
-        (mine_o, lx3, ly3, o_i, o_o, ((0, gout),)),
-        (mine_q, lx4, ly4, q_i, q_o, ((0, gq), (nqc, gk), (nqc + nkc, gv))),
+        ((sum_gate,), gate_i, gate_o, ((0, ggate),)),
+        ((sum_up,), up_i, up_o, ((0, gup),)),
+        ((sum_down,), down_i, down_o, ((0, gdown),)),
+        ((mine_o, lx3, ly3), o_i, o_o, ((0, gout),)),
+        ((mine_q, lx4, ly4), q_i, q_o, ((0, gq), (nqc, gk), (nqc + nkc, gv))),
     )
-    into_out = pltpu.make_async_copy(out, out_v, copy_sem.at[0])
-    into_out.start()
-    through = pltpu.make_async_copy(out_v, output, copy_sem.at[1])
+    simple = [
+        (pltpu.make_async_copy(out, out_v, copy_sem.at[0]), pltpu.make_async_copy(out_v, output, copy_sem.at[1])),
+        (pltpu.make_async_copy(early, early_v, copy_sem.at[2]), pltpu.make_async_copy(early_v, gin.at[pl.ds(0, last)], copy_sem.at[3])),
+    ]
 
     def loads(i):
-        one, two, three, into = sums[i][:4]
-        return [pltpu.make_async_copy(src, into.at[k], in_sem.at[i, k]) for k, src in enumerate((one, two, three))]
+        return [pltpu.make_async_copy(src, sums[i][1].at[k], in_sem.at[i, k]) for k, src in enumerate(sums[i][0])]
 
     mine = pl.ds(pl.multiple_of(rank * share, share), share)
     tokens = [
         pltpu.make_async_copy(src, dst, token_sem.at[k])
-        for k, (src, dst) in enumerate(((gh, gh_v), (xr.at[:, mine, :], x_v), (fin, fin_v), (finb, finb_v), (own, own_v)))
+        for k, (src, dst) in enumerate(
+            ((gh.at[last], gh_v), (xr.at[last, mine, :], x_v), (fin.at[last], fin_v), (finb.at[last], finb_v), (own.at[last], own_v))
+        )
     ]
-    for copy in tokens:
+    for i in range(len(sums)):
+        for copy in loads(i):
+            copy.start()
+    for copy in tokens + [first for first, _ in simple]:
         copy.start()
 
     first = jnp.sum(lines_ref[:8, :], axis=0, keepdims=True)
@@ -2315,77 +2341,74 @@
         square = jnp.sum(small_ref[1 + k : 2 + k, :], keepdims=True) / total
         rms[k] = jnp.max(jnp.sqrt(jnp.broadcast_to(square, (8, 128))))
 
-    into_out.wait()
-    through.start()
-    gain = jnp.concatenate([gains_ref[b, 0:1, :] for b in range(8)], axis=1).astype(F32)
-    for copy in tokens:
-        copy.wait()
-    for i in range(len(sums)):
-        for copy in loads(i):
-            copy.start()
-    inner = (rank % 3) != 0
     stores = []
-    for s in range(seqs):
-
-        def body(cut, at):
-            e = fin_v[s, cut, :].astype(F32) + own_v[s, cut, :].astype(F32)
-            e = e + jnp.where(inner, finb_v[s, cut, :].astype(F32), 0.0)
-            x = x_v[s, cut, :].astype(F32)
-            inv = inverse_rms(x)
-            hat = x * inv
-            eg = e * gain
-            gin_v[s, cut, :] = gh_v[s, cut, :] + inv * (eg - hat * jnp.mean(eg * hat, axis=-1, keepdims=True))
-
-        by_pieces(share, body)
-        for o in range(2):
-            for k in range(4):
-                b = near[k] * 2 + (core if o == 0 else 1 - core)
-                cut = pl.ds(pl.multiple_of(b * piece, piece), piece)
-                src = gin_v.at[s, :, pl.ds((o * 4 + k) * piece, piece)]
-                stores.append(pltpu.make_async_copy(src, gin.at[s, :, cut], place_sem.at[s, o * 4 + k]))
-                stores[-1].start()
-
-    for i, (_, _, _, came, total_v, parts) in enumerate(sums):
+    for i, (terms, came, total_v, parts) in enumerate(sums):
         for copy in loads(i):
             copy.wait()
 
         def body(cut, at):
-            total_v[cut, :] = sum(came[k, cut, :].astype(F32) for k in range(3))
+            total_v[cut, :] = sum(came[k, cut, :].astype(F32) for k in range(len(terms)))
 
         by_pieces(total_v.shape[0], body, tall(total_v))
         for n, (at, dst) in enumerate(parts):
             stores.append(pltpu.make_async_copy(total_v.at[:, pl.ds(at, dst.shape[1])], dst, out_sem.at[i, n]))
             stores[-1].start()
-    for copy in stores + [through]:
+    for first, second in simple:
+        first.wait()
+        second.start()
+
+    gain = jnp.concatenate([gains_ref[b, 0:1, :] for b in range(8)], axis=1).astype(F32)
+    for copy in tokens:
         copy.wait()
-
-
-def finish_results(pairs, mine_o, mine_q, lands_o, lands_q, gh, xr, fin, finb, own, out, gains, lines, small, hd, nqc, nkc):
-    (dgate, lx0, ly0), (dup, lx1, ly1), (ddown, lx2, ly2) = pairs
+    inner = (rank % 3) != 0
+
+    def body(cut, at):
+        e = fin_v[cut, :].astype(F32) + own_v[cut, :].astype(F32)
+        e = e + jnp.where(inner, finb_v[cut, :].astype(F32), 0.0)
+        x = x_v[cut, :].astype(F32)
+        inv = inverse_rms(x)
+        hat = x * inv
+        eg = e * gain
+        gh_v[cut, :] = gh_v[cut, :] + inv * (eg - hat * jnp.mean(eg * hat, axis=-1, keepdims=True))
+
+    by_pieces(share, body)
+    for o in range(2):
+        for k in range(4):
+            b = near[k] * 2 + (core if o == 0 else 1 - core)
+            cut = pl.ds(pl.multiple_of(b * piece, piece), piece)
+            src = gh_v.at[:, pl.ds((o * 4 + k) * piece, piece)]
+            stores.append(pltpu.make_async_copy(src, gin.at[last, :, cut], place_sem.at[o * 4 + k]))
+            stores[-1].start()
+    for copy in stores + [second for _, second in simple]:
+        copy.wait()
+
+
+def finish_results(sums, mine_o, mine_q, lands_o, lands_q, gh, xr, fin, finb, own, out, early, gains, lines, small, hd, nqc, nkc):
     seqs, share, width = out.shape
-    hidden = dgate.shape[1]
+    hidden = sums[0].shape[1]
     piece = width // 8
     any_space = pl.BlockSpec(memory_space=pl.ANY)
     vmem = pl.BlockSpec(memory_space=pltpu.VMEM)
     dma = pltpu.SemaphoreType.DMA
     blocks = [(piece, hidden), (piece, hidden), (hidden, piece), mine_o.shape, mine_q.shape]
+    terms = (1, 1, 1, 3, 3)
     outs = [shape(out.shape, BF16), shape(out.shape, F32)] + [shape(b, F32) for b in blocks[:4]]
     outs += [shape((piece, size), F32) for size in (nqc, nkc, nkc)]
     tiny = [shape((size,), F32) for size in (piece, piece, hd, hd)]
-    token = pltpu.VMEM(out.shape, BF16)
+    token = pltpu.VMEM((share, width), BF16)
     return pl.pallas_call(
         functools.partial(results_kernel, hd, nqc, nkc, float(width)),
-        in_specs=[any_space] * 21 + [vmem] * 3,
+        in_specs=[any_space] * 16 + [vmem] * 3,
         out_specs=[any_space] * len(outs) + [vmem] * 4 + [SMEM],
         out_shape=outs + tiny + [shape((3,), F32)],
-        scratch_shapes=[pltpu.VMEM((3,) + tuple(b), BF16) for b in blocks]
+        scratch_shapes=[pltpu.VMEM((n,) + tuple(b), BF16) for n, b in zip(terms, blocks)]
         + [pltpu.VMEM(b, F32) for b in blocks]
-        + [pltpu.VMEM(out.shape, F32), token, token, token, token, pltpu.VMEM(out.shape, F32), token]
-        + [dma((5, 3)), dma((5,)), dma((5, 3)), dma((seqs, 8)), dma((2,))],
+        + [pltpu.VMEM((share, width), F32), token, token, token, token, pltpu.VMEM(early.shape, F32), pltpu.VMEM(out.shape, BF16)]
+        + [dma((5, 3)), dma((5,)), dma((5, 3)), dma((8,)), dma((4,))],
         compiler_params=PARAMS,
-        cost_estimate=cost(30 * piece * hidden, 60 * piece * hidden),
+        cost_estimate=cost(30 * piece * hidden, 40 * piece * hidden),
         name="results",
-    )(dgate, lx0, ly0, dup, lx1, ly1, ddown, lx2, ly2, mine_o, *lands_o, mine_q, *lands_q, gh, xr, fin, finb, own, out, gains, lines, small)
+    )(*sums, mine_o, *lands_o, mine_q, *lands_q, gh, xr, fin, finb, own, out, early, gains, lines, small)
 
 
 def per_device_general(
@@ -2604,7 +2627,7 @@
     nq = w_query.shape[1] // hd
     nk = key_projection_weight.shape[1] // hd
     lengths = lengths.astype(jnp.int32)
-    all_gains = jnp.concatenate([attn_gain, ffn_gain, query_gain, key_gain]).reshape(1, -1)
+    all_gains = (attn_gain, ffn_gain, query_gain, key_gain)
     (
         xr, n1, gf, qkv, out_w, gate, up, down, hidden, n2, rest, gi, pre, everything, att, tok, gains, table, inv, stat
     ) = forward(
@@ -2616,14 +2639,15 @@
     ffn, gb, gh, d_gate, d_up, d_down, hidden, landx, landy, ring, gain2_part, stat2 = feed_both(
         lengths, n2, flat(gf), gate, up, down, gi, rest, flat(xr), hidden, gains
     )
-    output, fin, finb, own, mine_o, mine_q, lx1, ly1, lx2, ly2, lx3, ly3, lx4, ly4, lines, small = backward(
+    (
+        output, early, fin, finb, own, sum_gate, sum_up, sum_down, mine_o, mine_q, _, _, _, _, lx3, ly3, lx4, ly4, lines, small
+    ) = backward(
         lengths, gb, hidden, ffn, ring, xr, flat(n1), flat(tok), out_w, qkv,
-        everything, att, inv, pre, d_up, d_down, table, stat, stat2, gain2_part, hd, nq, nk,
+        everything, att, inv, pre, gh, d_gate, landx, landy, d_up, d_down, table, gains, stat, stat2, gain2_part, hd, nq, nk,
     )
     nqc, nkc = nq * hd, nk * hd
-    pairs = ((d_gate, landx, landy), (d_up, lx1, ly1), (d_down, lx2, ly2))
     output, grad_inputs, grad_gate, grad_up, grad_down, grad_out, grad_q, grad_k, grad_v, *small = finish_results(
-        pairs, mine_o, mine_q, (lx3, ly3), (lx4, ly4), gh, xr, fin, finb, own, output, gains,
+        (sum_gate, sum_up, sum_down), mine_o, mine_q, (lx3, ly3), (lx4, ly4), gh, xr, fin, finb, own, output, early, gains,
         lines, small, hd, nqc, nkc,
     )
     return (output, grad_inputs, grad_q, grad_k, grad_v, grad_out, grad_gate, grad_up, grad_down, *small)

time: 424 us -> 415 us (0.979)
  Pallas kernels: 413 us -> 406 us
where the time goes in v7:
time: 415 us; the launch traced here: 407 us
  Pallas kernels  406 us (98%)
    pallas_call x1, Pallas kernels, feed_both(): pl.pallas_call(functools.partial(feed_both_kernel, hb, sub, rows), in_spe...  144 us
    pallas_call x1, Pallas kernels, forward(): pl.pallas_call(functools.partial(forward_kernel, hd, nq, nk, block, sub),...  139 us
    pallas_call x1, Pallas kernels, backward(): pl.pallas_call(functools.partial(backward_kernel, hd, nq, nk, block), in_...  112 us
    pallas_call x1, Pallas kernels, finish_results(): pl.pallas_call(functools.partial(results_kernel, hd, nqc, nkc, float(widt...  10.2 us

profile of v7, /device:TPU:0, one launch (start us, length us, event | category | flops | bytes accessed | tf_op | source)
XLA Modules:
  0.0 407.1 jit_solution(14472019757350353264)
XLA Ops:
  0.7 139.5 %attention_forward.1 = (bf16[2,512,2048]{2,1,0:T(8,128)(2,1)}, bf16[2,512,2048]{2,1,0:T(8,128)(2,1)}, bf16[2,512,2048]{2,1,0:T(8,128)(2,1)}, bf16[2,1024,768]{2,...) custom-call(s32[2]{0:T(128)} %len_ref.5, ...), custom_call_target="tpu_custom_call" | custom-call | flops 9663676416 | bytes 167772160 | tf_op jit(solution)/shard_map/attention_forward/pallas_call | solution.py:1136
  140.2 144.1 %feed_forward_both.1 = (bf16[1024,2048]{1,0:T(8,128)(2,1)}, bf16[1024,2048]{1,0:T(8,128)(2,1)}, f32[2,128,2048]{2,1,0:T(8,128)}, bf16[1024,2048]{1,0:T(8,128)(2,...) custom-call(s32[2]{0:T(128)} %len_ref.5, ...), custom_call_target="tpu_custom_call", output_to_operand_aliasing={{6}: (9, {})} | custom-call | flops 77309411328 | bytes 125829120 | tf_op jit(solution)/shard_map/feed_forward_both/pallas_call | solution.py:1615
  284.3 112.1 %attention_backward.1 = (bf16[2,128,2048]{2,1,0:T(8,128)(2,1)}, f32[1,128,2048]{2,1,0:T(8,128)}, bf16[2,128,2048]{2,1,0:T(8,128)(2,1)}, bf16[2,128,2048]{2,1,0:T...) custom-call(s32[2]{0:T(128)} %len_ref.5, ...), custom_call_target="tpu_custom_call" | custom-call | flops 10737418240 | bytes 125829120 | tf_op jit(solution)/shard_map/attention_backward/pallas_call | solution.py:2278
  396.4 10.2 %results.1 = (bf16[2,128,2048]{2,1,0:T(8,128)(2,1)}, f32[2,128,2048]{2,1,0:T(8,128)}, f32[256,2048]{1,0:T(8,128)}, f32[256,2048]{1,0:T(8,128)}, f32[2048,256]{1,...) custom-call(bf16[256,2048]{1,0:T(8,128)(2,1)} %get-tuple-element.108, ...), custom_call_target="tpu_custom_call" | custom-call | flops 15728640 | bytes 20971520 | tf_op jit(solution)/shard_map/results/pallas_call | solution.py:2399

commit v8 on v7

--- a/solution.py
+++ b/solution.py
@@ -726,10 +726,10 @@
 def forward_kernel(
     hd, nq, nk, block, sub,
     len_ref, x_hbm, cot_hbm, wq_hbm, wk_hbm, wv_hbm, wout, wgate, wup, wdown, again_ref, fgain_ref, qgain_ref, kgain_ref,
-    xr_hbm, n1_hbm, gf_hbm, qkv_hbm, out_hbm, gate_hbm, up_hbm, down_hbm, hidden_hbm, n2_hbm, rest_hbm, gi_hbm, pre_hbm, all_hbm, att_hbm, tok_hbm,
+    xr_hbm, n1_hbm, gf_hbm, qkv_hbm, out_hbm, gate_hbm, up_hbm, down_hbm, hidden_hbm, n2_hbm, rest_hbm, resta_hbm, gi_hbm, pre_hbm, all_hbm, att_hbm, tok_hbm,
     gains_ref, table_ref, inv_ref, stat_ref,
     xr_v, cot_v, n1_v, qkv_v, out_v, ex_own, ex_send, ex_got, at_own, at_send, at_got,
-    part_v, in_v, back_v, total_v, hid_v, norm_v, wqkv, gain_ref, down_v, gi_v, pre_ref, all_ref, att_ref, tok_ref,
+    part_v, in_v, back_v, hid_v, norm_v, wqkv, gain_ref, down_v, gi_v, pre_ref, all_ref, att_ref, tok_ref,
     keep_sem, load_sem, store_sem, shard_sem, rest_sem, down_sem, gi_sem, wsend, wrecv, wloc, gsend, grecv, exsend, exrecv, zsend, zrecv, hid_sem,
 ):
     seqs, span, width = xr_v.shape
@@ -788,6 +788,7 @@
     for copy in shards:
         copy.wait()
     w_qkv.first()
+    w_out.first()
     gains_ref[0] = gain_ref[...]
 
     quarter = hd // 2
@@ -830,10 +831,12 @@
 
     lax.fori_loop(0, span // 16, norm_rows, 0)
     w_qkv.second()
-    w_out.first()
     lax.fori_loop(span // 16, seqs * span // 16, norm_rows, 0)
     store_n1 = pltpu.make_async_copy(n1_v, n1_hbm, store_sem.at[2])
     store_n1.start()
+    w_out.second()
+    w_down.first()
+    w_gate.first()
     w_qkv.third()
     w_qkv.arrived()
 
@@ -935,18 +938,10 @@
             for m in range(many):
                 u = s * per + k + m
 
-                @pl.when(u < subs)
-                def _():
-                    moving.begin(u)
+                moving.begin(u)
 
     def sequence(s, carry):
         project(s)
-
-        @pl.when(s == 0)
-        def _():
-            w_out.second()
-            w_down.first()
-            w_gate.first()
 
         attention(s)
 
@@ -960,9 +955,9 @@
         return carry
 
     lax.fori_loop(0, seqs, sequence, 0)
-    rest = [pltpu.make_async_copy(part_v.at[u], rest_hbm.at[u - subs], rest_sem.at[u - subs]) for u in range(subs, total_subs)]
-    for copy in rest:
-        copy.start()
+    tail = pl.ds(subs, total_subs - subs)
+    rest = [pltpu.make_async_copy(part_v.at[tail], rest_hbm, rest_sem.at[0])]
+    rest[0].start()
     stat_ref[...] = jnp.zeros_like(stat_ref)
 
     def hidden_store(u):
@@ -976,7 +971,7 @@
         s, t = u // per, u % per
         cut = pl.ds(pl.multiple_of(t * sub, sub), sub)
 
-        moving.total(u, total_v)
+        moving.ready(u)
 
         @pl.when(u >= 2)
         def _():
@@ -986,7 +981,7 @@
         length = len_ref[s]
 
         def body(piece_rows, first):
-            total = total_v[piece_rows, :]
+            total = moving.total(u, piece_rows)
             resid = xr_v[s, pl.ds(pl.multiple_of(t * sub + first, 16), 16), :].astype(F32)
             hidden = resid + total
             hid_v[u % 2, piece_rows, :] = hidden
@@ -1035,14 +1030,6 @@
         moving.middle(i)
         moving.outward(i - 1)
 
-        @pl.when(i == subs + 1)
-        def _():
-            w_up.third()
-
-        @pl.when(i >= 2)
-        def _():
-            finish(i - 2)
-
         @pl.when(i == 1)
         def _():
             w_down.second()
@@ -1052,31 +1039,41 @@
         def _():
             w_gate.second()
 
+        @pl.when(i == 7)
+        def _():
+            w_down.third()
+
         @pl.when(i == 8)
-        def _():
-            w_down.third()
-
-        @pl.when(i == 9)
         def _():
             w_down.arrived()
             for copy in load_down(0):
                 copy.start()
 
-        @pl.when((i >= 10) & (i < 10 + blocks))
-        def _():
-            grad_inner(i - 10)
-
-        @pl.when(i == 12)
+        @pl.when(i == 10)
         def _():
             w_up.second()
 
-        @pl.when(i == 14)
-        def _():
-            w_gate.third()
+        @pl.when(i >= 2)
+        def _():
+            finish(i - 2)
+
+        @pl.when((i >= 9) & (i < 9 + blocks))
+        def _():
+            grad_inner(i - 9)
 
         return carry
 
     lax.fori_loop(0, subs + 2, chain, 0)
+    w_gate.third()
+    came = pltpu.make_async_copy(in_v.at[tail], resta_hbm, rest_sem.at[1])
+
+    @pl.when(inner)
+    def _():
+        for u in range(subs, total_subs):
+            moving.hop_in(u).wait_recv()
+        came.start()
+
+    w_up.third()
     for u in (subs - 2, subs - 1):
         for copy in hidden_store(u):
             copy.wait()
@@ -1091,6 +1088,7 @@
     every_gain.wait_send()
     w_gate.arrived()
     w_up.arrived()
+    pl.when(inner)(came.wait)
     for w in weights:
         w.sent()
     for copy in [store_gf, store_xr, store_n1, store_qkv, store_out] + rest:
@@ -1103,7 +1101,7 @@
     groups = nq // nk
     sub = span // 8
     subs = seqs * span // sub
-    here = subs - 2
+    here = subs - 4
     block = min(256, span)
     hidden = w_gate.shape[1]
     hb = hidden // 4
@@ -1117,7 +1115,7 @@
         shape((2, half, cols), BF16), shape((2, w_out.shape[0], half), BF16),
         shape((2, half, hidden), BF16), shape((2, half, hidden), BF16), shape((2, hidden, half), BF16),
         shape((seqs * span, width), F32), shape((seqs * span, width), BF16), shape((subs - here, sub, width), BF16),
-        shape((seqs * span, hidden), BF16),
+        shape((subs - here, sub, width), BF16), shape((seqs * span, hidden), BF16),
     ]
     kept = [
         shape((seqs, (nq + nk) * hd, span), F32), shape((seqs, rows, 2 * span), BF16),
@@ -1132,6 +1130,7 @@
     at = pltpu.VMEM((seqs, groups * hd, span), BF16)
     moving = pltpu.VMEM((subs, sub, width), BF16)
     landing = pltpu.VMEM((here, sub, width), BF16)
+    arriving = pltpu.VMEM((subs, sub, width), BF16)
     flops = 2 * seqs * span * width * (cols + nq * hd) + 16 * seqs * nq * hd * span * span
     return pl.pallas_call(
         functools.partial(forward_kernel, hd, nq, nk, block, sub),
@@ -1142,13 +1141,13 @@
             pltpu.VMEM(wide, BF16), pltpu.VMEM(wide, BF16), pltpu.VMEM(wide, BF16),
             pltpu.VMEM((2, half, cols), BF16), pltpu.VMEM((2, w_out.shape[0], half), BF16),
             ex, ex, ex, at, at, at,
-            moving, landing, landing,
-            pltpu.VMEM((sub, width), F32), pltpu.VMEM((2, sub, width), F32), pltpu.VMEM((2, sub, width), BF16),
+            moving, arriving, landing,
+            pltpu.VMEM((2, sub, width), F32), pltpu.VMEM((2, sub, width), BF16),
             pltpu.VMEM((w_query.shape[0], cols), BF16), pltpu.VMEM((16, width // 8), BF16),
             pltpu.VMEM((2, 2, hb, half), BF16), pltpu.VMEM((2, seqs * span, hb), BF16),
             *[pltpu.VMEM(a.shape, a.dtype) for a in kept],
-            dma((4, seqs)), dma((2,)), dma((5,)), dma((3,)), dma((subs - here,)), dma((2, 2)), dma((2,)), dma((5, 2)), dma((5, 4)), dma((5,)), dma(()), dma(()),
-            dma((2, seqs)), dma((2, seqs)), dma((2,)), dma((2, here)), dma((2, 2)),
+            dma((4, seqs)), dma((2,)), dma((5,)), dma((3,)), dma((2,)), dma((2, 2)), dma((2,)), dma((5, 2)), dma((5, 4)), dma((5,)), dma(()), dma(()),
+            dma((2, seqs)), dma((2, seqs)), dma((2,)), dma((2, subs)), dma((2, 2)),
         ],
         compiler_params=pltpu.CompilerParams(vmem_limit_bytes=VMEM_MOST, collective_id=1, has_side_effects=True),
         cost_estimate=cost(flops, 80 * seqs * span * width),
@@ -1170,13 +1169,14 @@
 
 
 class Chain:
-    def __init__(self, rank, part, arrive, back, send, recv):
+    def __init__(self, rank, part, arrive, back, send, recv, landed=False):
+        self.landed = landed
         self.inner = (rank % 3) != 0
         self.outer = (rank % 3) == 0
         self.part, self.arrive, self.back = part, arrive, back
         self.send, self.recv = send, recv
         self.side, self.mid = {"tensor": xor_one(rank)}, {"tensor": 3 - rank}
-        self.count = arrive.shape[0]
+        self.count = back.shape[0]
 
     def hop_in(self, u):
         return remote(self.part.at[u], self.arrive.at[u], self.send.at[0], self.recv.at[0, u], self.side)
@@ -1201,7 +1201,8 @@
     def middle(self, u):
         @pl.when((u >= 0) & (u < self.count) & self.inner)
         def _():
-            self.hop_in(u).wait_recv()
+            if not self.landed:
+                self.hop_in(u).wait_recv()
             self.add(self.arrive, self.part, self.arrive, u)
             self.hop_mid(u).start()
 
@@ -1212,39 +1213,39 @@
             self.add(self.part, self.part, self.back, u)
             self.hop_out(u).start()
 
-    def total(self, u, into):
+    def ready(self, u):
+        @pl.when(self.outer)
+        def _():
+            self.hop_out(u).wait_recv()
+
+    def total(self, u, cut):
+        near = jnp.where(self.inner, self.arrive[u, cut, :], self.part[u, cut, :])
+        return near.astype(F32) + self.back[u, cut, :].astype(F32)
+
+    def settle(self):
+        def all_sent(ref, count, sem):
+            every = ref.at[pl.ds(0, count)]
+            remote(every, every, self.send.at[sem], self.recv.at[0, 0], self.side).wait_send()
+
         @pl.when(self.inner)
         def _():
-            def body(cut, first):
-                into[cut, :] = self.arrive[u, cut, :].astype(F32) + self.back[u, cut, :].astype(F32)
-
-            by_pieces(self.part.shape[1], body)
-
-        @pl.when(self.outer)
-        def _():
-            self.hop_out(u).wait_recv()
-
-            def body(cut, first):
-                into[cut, :] = self.part[u, cut, :].astype(F32) + self.back[u, cut, :].astype(F32)
-
-            by_pieces(self.part.shape[1], body)
-
-    def settle(self):
-        every = self.part.at[pl.ds(0, self.count)]
-        remote(every, self.back, self.send.at[0], self.recv.at[0, 0], self.side).wait_send()
-
-        @pl.when(self.inner)
-        def _():
-            remote(self.arrive, self.back, self.send.at[1], self.recv.at[1, 0], self.mid).wait_send()
+            all_sent(self.part, self.count, 0)
+            all_sent(self.arrive, self.count, 1)
+
+        if not self.landed:
+
+            @pl.when(self.outer)
+            def _():
+                all_sent(self.part, self.arrive.shape[0], 0)
 
 
 def feed_both_kernel(
     hb, sub, rows,
-    len_ref, n2_hbm, gf_hbm, gate_hbm, up_hbm, down_hbm, gi_hbm, rest_hbm, xr_hbm, hidden_in, gains_ref,
+    len_ref, n2_hbm, gf_hbm, gate_hbm, up_hbm, down_hbm, gi_hbm, rest_hbm, resta_hbm, xr_hbm, hidden_in, gains_ref,
     ffn_hbm, gb_hbm, gh_hbm, dgate_hbm, dup_hbm, ddown_hbm, hidden_hbm, landx, landy, ring_hbm, gain_out, stat_ref,
-    n2_v, gf_v, inner_v, gg_v, gu_v, facc, gacc, wrow, wcol, part_v, in_v, back_v, total_v, hid_v, gh_v, gb_v, stage_row, stage_col,
-    late_p, late_a, late_b, xtile_v, gi_v, wide_v, temp_v, gain_ref,
-    load_sem, wsem, zsend, zrecv, hid_sem, out_sem, ffn_sem, csend, crecv, store_sem, lsend, lrecv, xt_sem, xsend, xrecv, xload, rsend, rrecv, free_sem,
+    n2_v, gf_v, inner_v, gg_v, gu_v, facc, gacc, wrow, wcol, part_v, in_v, back_v, hid_v, gh_v, gb_v, stage_row, stage_col,
+    xtile_v, gi_v, wide_v, temp_v, gain_ref,
+    load_sem, wsem, zsend, zrecv, hid_sem, out_sem, ffn_sem, csend, crecv, store_sem, lsend, lrecv, xt_sem, xsend, xrecv, xload, rsend, rrecv, free_sem, done_sem,
 ):
     core, rank = lax.axis_index("context"), lax.axis_index("tensor")
     near_core = {"context": 1 - core}
@@ -1256,8 +1257,9 @@
     per = rows // sub
     chain = Chain(rank, part_v, in_v, back_v, zsend, zrecv)
     subs = chain.count
-    late = Chain(rank, late_p, late_a, late_b, lsend, lrecv)
-    known = subs - late.count
+    known = subs - rest_hbm.shape[0]
+    tail = pl.ds(known, subs - known)
+    late = Chain(rank, part_v.at[tail], in_v.at[tail], back_v.at[tail], lsend, lrecv, True)
     start = core * (tokens // 2)
 
     def load_weights(i):
@@ -1275,13 +1277,16 @@
         cut = pl.ds(pl.multiple_of(u * sub, sub), sub)
         return pltpu.make_async_copy(hidden_hbm.at[cut, :], hid_v, hid_sem)
 
-    ready = pl.ds(0, known * sub)
+    ready = pl.ds(rows, known * sub - rows)
+    head = pl.ds(0, rows)
+    load_head = pltpu.make_async_copy(n2_hbm.at[head, :], n2_v.at[head, :], load_sem.at[4])
     loads = [
         pltpu.make_async_copy(n2_hbm.at[ready, :], n2_v.at[ready, :], load_sem.at[0]),
-        pltpu.make_async_copy(rest_hbm, late_p, load_sem.at[1]),
+        pltpu.make_async_copy(rest_hbm, late.part, load_sem.at[1]),
+        pltpu.make_async_copy(resta_hbm, late.arrive, load_sem.at[3]),
     ]
     load_gf = pltpu.make_async_copy(gf_hbm, gf_v, load_sem.at[2])
-    for copy in loads + load_weights(0) + [load_gf]:
+    for copy in load_weights(0) + [load_head] + loads + [load_gf]:
         copy.start()
     load_hidden(0).start()
     row = lax.axis_index("dp")
@@ -1291,10 +1296,7 @@
         gain_ref[:, b * (width // 8) : (b + 1) * (width // 8)] = gains_ref[b, 1:2, :].astype(F32)
     gain_out[...] = jnp.zeros_like(gain_out)
     stat_ref[...] = jnp.zeros_like(stat_ref)
-    for copy in loads:
-        copy.wait()
-    for u in range(late.count):
-        late.begin(u)
+    load_head.wait()
 
     def load_x(u):
         at = pl.multiple_of((known + u) * sub, sub)
@@ -1305,7 +1307,7 @@
 
     def late_finish(u):
         load_x(u).start()
-        late.total(u, total_v)
+        late.ready(u)
         load_x(u).wait()
 
         @pl.when(u >= 1)
@@ -1316,7 +1318,7 @@
         offset = start + known * sub % (tokens // 2) + u * sub
 
         def body(cut, first):
-            total = total_v[cut, :]
+            total = late.total(u, cut)
             resid = xtile_v[cut, :].astype(F32)
             hidden_rows = resid + total
             gh_v[cut, :] = hidden_rows
@@ -1339,7 +1341,7 @@
         return pltpu.make_async_copy(gh_v, gh_hbm.at[u // 8, at, :], out_sem.at[0])
 
     def finish(u):
-        chain.total(u, total_v)
+        chain.ready(u)
         load_hidden(u).wait()
 
         @pl.when(u >= 1)
@@ -1347,7 +1349,7 @@
             store_gb(u - 1).wait()
 
         def body(piece_rows, first):
-            e = total_v[piece_rows, :]
+            e = chain.total(u, piece_rows)
             hidden_rows = hid_v[piece_rows, :]
             inv = inverse_rms(hidden_rows)
             hat = hidden_rows * inv
@@ -1422,22 +1424,15 @@
 
         @pl.when(h == 0)
         def _():
-            facc[...] = jnp.zeros_like(facc)
             gacc[...] = jnp.zeros_like(gacc)
 
-        inner, gg, gu = inner_v[here, cols], gg_v[here, cols], gu_v[here, cols]
+        gg, gu = gg_v[here, cols], gu_v[here, cols]
         span = min(512, half)
         for side in range(2):
             for q in range(half // span):
                 part = slice(q * span, (q + 1) * span)
                 cut = slice(side * half + q * span, side * half + (q + 1) * span)
-                facc[:, cut] += dot_nn(inner, wcol[slot, side, :, part])
                 gacc[:, cut] += dot_nt(gg, wrow[slot, 0, side, part, :]) + dot_nt(gu, wrow[slot, 1, side, part, :])
-
-        @pl.when((h == hsteps - 1) & (c >= 2))
-        def _():
-            for copy in store_ffn(c - 2):
-                copy.wait()
 
         @pl.when(h == hsteps - 1)
         def _():
@@ -1445,18 +1440,44 @@
                 part_v[c * per + k] = gacc[k * sub : (k + 1) * sub, :].astype(BF16)
                 chain.begin(c * per + k)
 
-            for k in range(4):
-                stage_row[c % 2, k * rows : (k + 1) * rows, :] = facc[:, k * quarter : (k + 1) * quarter].astype(BF16)
-            for copy in store_ffn(c):
-                copy.start()
-
-        @pl.when((i >= 2) & (i < 2 + late.count))
-        def _():
-            late.middle(i - 2)
-
-        @pl.when((i >= 4) & (i < 4 + late.count))
-        def _():
-            late.outward(i - 4)
+        @pl.when(c % 2 == 1)
+        def _():
+            pair = pl.ds(pl.multiple_of((c - 1) * rows, rows), 2 * rows)
+            inner = inner_v[pair, cols]
+
+            @pl.when(h == 0)
+            def _():
+                facc[...] = jnp.zeros_like(facc)
+
+            for side in range(2):
+                for q in range(half // span):
+                    part = slice(q * span, (q + 1) * span)
+                    cut = slice(side * half + q * span, side * half + (q + 1) * span)
+                    facc[:, cut] += dot_nn(inner, wcol[slot, side, :, part])
+
+            @pl.when(h == hsteps - 1)
+            def _():
+                for m in range(2):
+
+                    @pl.when(c >= 2)
+                    def _():
+                        for copy in store_ffn(c - 3 + m):
+                            copy.wait()
+
+                    for k in range(4):
+                        stage_row[m, k * rows : (k + 1) * rows, :] = facc[
+                            m * rows : (m + 1) * rows, k * quarter : (k + 1) * quarter
+                        ].astype(BF16)
+                    for copy in store_ffn(c - 1 + m):
+                        copy.start()
+
+        @pl.when(i == 0)
+        def _():
+            for copy in loads:
+                copy.wait()
+
+        late.middle(i)
+        late.outward(i - 3)
 
         @pl.when((i >= 6) & (i < 6 + late.count))
         def _():
@@ -1466,6 +1487,16 @@
         def _():
             load_gf.wait()
             late_store(late.count - 1).wait()
+            late.settle()
+            pl.semaphore_signal(done_sem, inc=1, device_id=chain.side, device_id_type=pl.DeviceIdType.MESH)
+
+            @pl.when(chain.inner)
+            def _():
+                pl.semaphore_signal(done_sem, inc=1, device_id=chain.mid, device_id_type=pl.DeviceIdType.MESH)
+
+        @pl.when(i == steps - 2)
+        def _():
+            pl.semaphore_wait(done_sem, jnp.where(chain.inner, 2, 1))
 
         serve(i - 6)
         return carry
@@ -1587,8 +1618,6 @@
     def _():
         fold.settle()
 
-    late.settle()
-
 
 def row_blocks(ref):
     size = ref.shape[0] // 4
@@ -1600,7 +1629,7 @@
     return lambda h: ref.at[pl.ds(h * size, size), :]
 
 
-def feed_both(lengths, n2, gf, gate, up, down, gi, rest, xr, hidden_rows, gain):
+def feed_both(lengths, n2, gf, gate, up, down, gi, rest, came, xr, hidden_rows, gain):
     tokens, width = n2.shape
     _, half, hidden = gate.shape
     hb = hidden // 4
@@ -1610,11 +1639,10 @@
     vmem = pl.BlockSpec(memory_space=pltpu.VMEM)
     dma = pltpu.SemaphoreType.DMA
     moving = pltpu.VMEM((16, sub, width), BF16)
-    late = pltpu.VMEM((count, sub, width), BF16)
     act = pltpu.VMEM((tokens, hidden), BF16)
     return pl.pallas_call(
         functools.partial(feed_both_kernel, hb, sub, rows),
-        in_specs=[SMEM] + [any_space] * 9 + [vmem],
+        in_specs=[SMEM] + [any_space] * 10 + [vmem],
         out_specs=[any_space] * 10 + [vmem] * 2,
         out_shape=[
             shape((tokens, width), BF16), shape((tokens, width), BF16), shape((2, 2 * sub, width), F32),
@@ -1624,21 +1652,21 @@
         ],
         scratch_shapes=[
             pltpu.VMEM((tokens, width), BF16), pltpu.VMEM((tokens, width), BF16), act, act, act,
-            pltpu.VMEM((rows, width), F32), pltpu.VMEM((rows, width), F32),
+            pltpu.VMEM((2 * rows, width), F32), pltpu.VMEM((rows, width), F32),
             pltpu.VMEM((2, 2, 2, half, hb), BF16), pltpu.VMEM((2, 2, hb, half), BF16),
-            moving, moving, moving, pltpu.VMEM((sub, width), F32),
+            moving, moving, moving,
             pltpu.VMEM((sub, width), F32), pltpu.VMEM((sub, width), F32), pltpu.VMEM((sub, width), BF16),
             pltpu.VMEM((2, half, hb), BF16), pltpu.VMEM((2, hb, half), BF16),
-            late, late, late, pltpu.VMEM((sub, width), BF16), pltpu.VMEM((2, rows, hb), BF16),
+            pltpu.VMEM((sub, width), BF16), pltpu.VMEM((2, rows, hb), BF16),
             pltpu.VMEM((2, half // 8, hidden), BF16), pltpu.VMEM((2, half // 8, hidden), BF16), pltpu.VMEM((1, width), F32),
-            dma((3,)), dma((2, 7)), dma((2,)), dma((2, 16)), dma(()), dma((2,)), dma((2, 4)), dma((3, 4)), dma((3, 4)),
-            dma((3, 4)), dma((2,)), dma((2, count)), dma(()), dma((6,)), dma((6,)), dma((3,)), dma(()), dma((5,)), pltpu.SemaphoreType.REGULAR,
+            dma((5,)), dma((2, 7)), dma((2,)), dma((2, 16)), dma(()), dma((2,)), dma((2, 4)), dma((3, 4)), dma((3, 4)),
+            dma((3, 4)), dma((2,)), dma((2, count)), dma(()), dma((6,)), dma((6,)), dma((3,)), dma(()), dma((5,)), pltpu.SemaphoreType.REGULAR, pltpu.SemaphoreType.REGULAR,
         ],
-        input_output_aliases={9: 6},
+        input_output_aliases={10: 6},
         compiler_params=pltpu.CompilerParams(vmem_limit_bytes=VMEM_MOST, collective_id=2, has_side_effects=True),
         cost_estimate=cost(18 * tokens * width * hidden, 60 * tokens * width),
         name="feed_forward_both",
-    )(lengths, n2, gf, gate, up, down, gi, rest, xr, hidden_rows, gain)
+    )(lengths, n2, gf, gate, up, down, gi, rest, came, xr, hidden_rows, gain)
 
 
 class Fold:
@@ -2629,7 +2657,7 @@
     lengths = lengths.astype(jnp.int32)
     all_gains = (attn_gain, ffn_gain, query_gain, key_gain)
     (
-        xr, n1, gf, qkv, out_w, gate, up, down, hidden, n2, rest, gi, pre, everything, att, tok, gains, table, inv, stat
+        xr, n1, gf, qkv, out_w, gate, up, down, hidden, n2, rest, came, gi, pre, everything, att, tok, gains, table, inv, stat
     ) = forward(
         lengths, inputs, cotangent, w_query, key_projection_weight, value_projection_weight, w_output, w_gate, w_up, w_down,
         all_gains, hd, nq, nk,
@@ -2637,7 +2665,7 @@
     tokens = seqs * span
     flat = lambda a: a.reshape(tokens, -1)
     ffn, gb, gh, d_gate, d_up, d_down, hidden, landx, landy, ring, gain2_part, stat2 = feed_both(
-        lengths, n2, flat(gf), gate, up, down, gi, rest, flat(xr), hidden, gains
+        lengths, n2, flat(gf), gate, up, down, gi, rest, came, flat(xr), hidden, gains
     )
     (
         output, early, fin, finb, own, sum_gate, sum_up, sum_down, mine_o, mine_q, _, _, _, _, lx3, ly3, lx4, ly4, lines, small

time: 415 us -> 411 us (level)
    pallas_call x1, Pallas kernels: 139 us -> 135 us  [forward(): pl.pallas_call(functools.partial(forward_kernel, hd, nq, nk, block, sub),...]
where the time goes in v8:
time: 411 us; the launch traced here: 403 us
  Pallas kernels  402 us (98%)
    pallas_call x1, Pallas kernels, feed_both(): pl.pallas_call(functools.partial(feed_both_kernel, hb, sub, rows), in_spe...  146 us
    pallas_call x1, Pallas kernels, forward(): pl.pallas_call(functools.partial(forward_kernel, hd, nq, nk, block, sub),...  135 us
    pallas_call x1, Pallas kernels, backward(): pl.pallas_call(functools.partial(backward_kernel, hd, nq, nk, block), in_...  111 us
    pallas_call x1, Pallas kernels, finish_results(): pl.pallas_call(functools.partial(results_kernel, hd, nqc, nkc, float(widt...  10.2 us

profile of v8, /device:TPU:0, one launch (start us, length us, event | category | flops | bytes accessed | tf_op | source)
XLA Modules:
  0.0 403.1 jit_solution(17400105609650299028)
XLA Ops:
  0.7 134.9 %attention_forward.1 = (bf16[2,512,2048]{2,1,0:T(8,128)(2,1)}, bf16[2,512,2048]{2,1,0:T(8,128)(2,1)}, bf16[2,512,2048]{2,1,0:T(8,128)(2,1)}, bf16[2,1024,768]{2,...) custom-call(s32[2]{0:T(128)} %len_ref.5, ...), custom_call_target="tpu_custom_call" | custom-call | flops 9663676416 | bytes 167772160 | tf_op jit(solution)/shard_map/attention_forward/pallas_call | solution.py:1135
  135.5 145.7 %feed_forward_both.1 = (bf16[1024,2048]{1,0:T(8,128)(2,1)}, bf16[1024,2048]{1,0:T(8,128)(2,1)}, f32[2,128,2048]{2,1,0:T(8,128)}, bf16[1024,2048]{1,0:T(8,128)(2,...) custom-call(s32[2]{0:T(128)} %len_ref.5, ...), custom_call_target="tpu_custom_call", output_to_operand_aliasing={{6}: (10, {})} | custom-call | flops 77309411328 | bytes 125829120 | tf_op jit(solution)/shard_map/feed_forward_both/pallas_call | solution.py:1643
  281.3 111.1 %attention_backward.1 = (bf16[2,128,2048]{2,1,0:T(8,128)(2,1)}, f32[1,128,2048]{2,1,0:T(8,128)}, bf16[2,128,2048]{2,1,0:T(8,128)(2,1)}, bf16[2,128,2048]{2,1,0:T...) custom-call(s32[2]{0:T(128)} %len_ref.5, ...), custom_call_target="tpu_custom_call" | custom-call | flops 10737418240 | bytes 125829120 | tf_op jit(solution)/shard_map/attention_backward/pallas_call | solution.py:2306
  392.4 10.2 %results.1 = (bf16[2,128,2048]{2,1,0:T(8,128)(2,1)}, f32[2,128,2048]{2,1,0:T(8,128)}, f32[256,2048]{1,0:T(8,128)}, f32[256,2048]{1,0:T(8,128)}, f32[2048,256]{1,...) custom-call(bf16[256,2048]{1,0:T(8,128)(2,1)} %get-tuple-element.110, ...), custom_call_target="tpu_custom_call" | custom-call | flops 15728640 | bytes 20971520 | tf_op jit(solution)/shard_map/results/pallas_call | solution.py:2427

commit v9 on v8

--- a/solution.py
+++ b/solution.py
@@ -1270,8 +1270,12 @@
         for side in range(2):
             copies.append(pltpu.make_async_copy(gate_hbm.at[side, :, cut], wrow.at[slot, 0, side], wsem.at[slot, side]))
             copies.append(pltpu.make_async_copy(up_hbm.at[side, :, cut], wrow.at[slot, 1, side], wsem.at[slot, 2 + side]))
-            copies.append(pltpu.make_async_copy(down_hbm.at[side, cut, :], wcol.at[slot, side], wsem.at[slot, 4 + side]))
         return copies
+
+    def load_down(i):
+        slot, h = i % 2, i % hsteps
+        cut = pl.ds(pl.multiple_of(h * hb, hb), hb)
+        return [pltpu.make_async_copy(down_hbm.at[side, cut, :], wcol.at[slot, side], wsem.at[slot, 4 + side]) for side in range(2)]
 
     def load_hidden(u):
         cut = pl.ds(pl.multiple_of(u * sub, sub), sub)
@@ -1406,6 +1410,11 @@
             for copy in load_weights(i + 1):
                 copy.start()
 
+            @pl.when((i + 1) // hsteps % 2 == 1)
+            def _():
+                for copy in load_down(i + 1):
+                    copy.start()
+
         here = pl.ds(pl.multiple_of(c * rows, rows), rows)
         cols = pl.ds(pl.multiple_of(h * hb, hb), hb)
         n = n2_v[here, :]
@@ -1444,6 +1453,8 @@
         def _():
             pair = pl.ds(pl.multiple_of((c - 1) * rows, rows), 2 * rows)
             inner = inner_v[pair, cols]
+            for copy in load_down(i):
+                copy.wait()
 
             @pl.when(h == 0)
             def _():
@@ -1583,7 +1594,7 @@
             done.append(part)
             if len(done) <= 8 or len(done) % 2 == 0:
                 serve(next(after))
-            if len(done) == 5:
+            if len(done) == 4:
                 fold.begin()
 
     both(1, 0, None)

time: 411 us -> 410 us (level)
  no operation moved by 1% of the time
where the time goes in v9:
time: 410 us; the launch traced here: 402 us
  Pallas kernels  401 us (98%)
    pallas_call x1, Pallas kernels, feed_both(): pl.pallas_call(functools.partial(feed_both_kernel, hb, sub, rows), in_spe...  143 us
    pallas_call x1, Pallas kernels, forward(): pl.pallas_call(functools.partial(forward_kernel, hd, nq, nk, block, sub),...  135 us
    pallas_call x1, Pallas kernels, backward(): pl.pallas_call(functools.partial(backward_kernel, hd, nq, nk, block), in_...  112 us
    pallas_call x1, Pallas kernels, finish_results(): pl.pallas_call(functools.partial(results_kernel, hd, nqc, nkc, float(widt...  10.2 us

profile of v9, /device:TPU:0, one launch (start us, length us, event | category | flops | bytes accessed | tf_op | source)
XLA Modules:
  0.0 401.9 jit_solution(17512845268673650904)
XLA Ops:
  0.7 134.9 %attention_forward.1 = (bf16[2,512,2048]{2,1,0:T(8,128)(2,1)}, bf16[2,512,2048]{2,1,0:T(8,128)(2,1)}, bf16[2,512,2048]{2,1,0:T(8,128)(2,1)}, bf16[2,1024,768]{2,...) custom-call(s32[2]{0:T(128)} %len_ref.5, ...), custom_call_target="tpu_custom_call" | custom-call | flops 9663676416 | bytes 167772160 | tf_op jit(solution)/shard_map/attention_forward/pallas_call | solution.py:1135
  135.5 143.5 %feed_forward_both.1 = (bf16[1024,2048]{1,0:T(8,128)(2,1)}, bf16[1024,2048]{1,0:T(8,128)(2,1)}, f32[2,128,2048]{2,1,0:T(8,128)}, bf16[1024,2048]{1,0:T(8,128)(2,...) custom-call(s32[2]{0:T(128)} %len_ref.5, ...), custom_call_target="tpu_custom_call", output_to_operand_aliasing={{6}: (10, {})} | custom-call | flops 77309411328 | bytes 125829120 | tf_op jit(solution)/shard_map/feed_forward_both/pallas_call | solution.py:1654
  279.0 112.2 %attention_backward.1 = (bf16[2,128,2048]{2,1,0:T(8,128)(2,1)}, f32[1,128,2048]{2,1,0:T(8,128)}, bf16[2,128,2048]{2,1,0:T(8,128)(2,1)}, bf16[2,128,2048]{2,1,0:T...) custom-call(s32[2]{0:T(128)} %len_ref.5, ...), custom_call_target="tpu_custom_call" | custom-call | flops 10737418240 | bytes 125829120 | tf_op jit(solution)/shard_map/attention_backward/pallas_call | solution.py:2317
  391.2 10.2 %results.1 = (bf16[2,128,2048]{2,1,0:T(8,128)(2,1)}, f32[2,128,2048]{2,1,0:T(8,128)}, f32[256,2048]{1,0:T(8,128)}, f32[256,2048]{1,0:T(8,128)}, f32[2048,256]{1,...) custom-call(bf16[256,2048]{1,0:T(8,128)(2,1)} %get-tuple-element.110, ...), custom_call_target="tpu_custom_call" | custom-call | flops 15728640 | bytes 20971520 | tf_op jit(solution)/shard_map/results/pallas_call | solution.py:2438

commit v10 on v9

--- a/solution.py
+++ b/solution.py
@@ -1290,7 +1290,7 @@
         pltpu.make_async_copy(resta_hbm, late.arrive, load_sem.at[3]),
     ]
     load_gf = pltpu.make_async_copy(gf_hbm, gf_v, load_sem.at[2])
-    for copy in load_weights(0) + [load_head] + loads + [load_gf]:
+    for copy in load_weights(0) + [load_head] + loads[1:]:
         copy.start()
     load_hidden(0).start()
     row = lax.axis_index("dp")
@@ -1484,8 +1484,17 @@
 
         @pl.when(i == 0)
         def _():
-            for copy in loads:
+            for copy in loads[1:]:
                 copy.wait()
+
+        @pl.when(i == 1)
+        def _():
+            loads[0].start()
+
+        @pl.when(i == hsteps - 1)
+        def _():
+            loads[0].wait()
+            load_gf.start()
 
         late.middle(i)
         late.outward(i - 3)

time: 410 us -> 409 us (level)
  no operation moved by 1% of the time
where the time goes in v10:
time: 409 us; the launch traced here: 401 us
  Pallas kernels  400 us (98%)
    pallas_call x1, Pallas kernels, feed_both(): pl.pallas_call(functools.partial(feed_both_kernel, hb, sub, rows), in_spe...  142 us
    pallas_call x1, Pallas kernels, forward(): pl.pallas_call(functools.partial(forward_kernel, hd, nq, nk, block, sub),...  135 us
    pallas_call x1, Pallas kernels, backward(): pl.pallas_call(functools.partial(backward_kernel, hd, nq, nk, block), in_...  112 us
    pallas_call x1, Pallas kernels, finish_results(): pl.pallas_call(functools.partial(results_kernel, hd, nqc, nkc, float(widt...  10.2 us

profile of v10, /device:TPU:0, one launch (start us, length us, event | category | flops | bytes accessed | tf_op | source)
XLA Modules:
  0.0 400.8 jit_solution(13397847334201433763)
XLA Ops:
  0.7 134.9 %attention_forward.1 = (bf16[2,512,2048]{2,1,0:T(8,128)(2,1)}, bf16[2,512,2048]{2,1,0:T(8,128)(2,1)}, bf16[2,512,2048]{2,1,0:T(8,128)(2,1)}, bf16[2,1024,768]{2,...) custom-call(s32[2]{0:T(128)} %len_ref.5, ...), custom_call_target="tpu_custom_call" | custom-call | flops 9663676416 | bytes 167772160 | tf_op jit(solution)/shard_map/attention_forward/pallas_call | solution.py:1135
  135.5 142.3 %feed_forward_both.1 = (bf16[1024,2048]{1,0:T(8,128)(2,1)}, bf16[1024,2048]{1,0:T(8,128)(2,1)}, f32[2,128,2048]{2,1,0:T(8,128)}, bf16[1024,2048]{1,0:T(8,128)(2,...) custom-call(s32[2]{0:T(128)} %len_ref.5, ...), custom_call_target="tpu_custom_call", output_to_operand_aliasing={{6}: (10, {})} | custom-call | flops 77309411328 | bytes 125829120 | tf_op jit(solution)/shard_map/feed_forward_both/pallas_call | solution.py:1663
  277.8 112.2 %attention_backward.1 = (bf16[2,128,2048]{2,1,0:T(8,128)(2,1)}, f32[1,128,2048]{2,1,0:T(8,128)}, bf16[2,128,2048]{2,1,0:T(8,128)(2,1)}, bf16[2,128,2048]{2,1,0:T...) custom-call(s32[2]{0:T(128)} %len_ref.5, ...), custom_call_target="tpu_custom_call" | custom-call | flops 10737418240 | bytes 125829120 | tf_op jit(solution)/shard_map/attention_backward/pallas_call | solution.py:2326
  390.1 10.2 %results.1 = (bf16[2,128,2048]{2,1,0:T(8,128)(2,1)}, f32[2,128,2048]{2,1,0:T(8,128)}, f32[256,2048]{1,0:T(8,128)}, f32[256,2048]{1,0:T(8,128)}, f32[2048,256]{1,...) custom-call(bf16[256,2048]{1,0:T(8,128)(2,1)} %get-tuple-element.110, ...), custom_call_target="tpu_custom_call" | custom-call | flops 15728640 | bytes 20971520 | tf_op jit(solution)/shard_map/results/pallas_call | solution.py:2447
